TPU v7x, 256 devices: a whole 4x4x8 slice. The times are simulated.
256 devices in a mesh: wide: 16 (over x, y), narrow: 16 (over z, core).
Axes of the slice: x: 4, y: 4, z: 8, core: 2. Of those that a mesh axis runs over, the one named last changes fastest.
Arguments:
- amplitudes: bfloat16 [4096, 32768], P('narrow', 'wide'), may hold values from -12 to 12
- integrals: bfloat16 [32768, 4096], P('wide'), may hold values from -0.046875 to 0.046875
- pair_integrals: bfloat16 [4096, 4096], P('narrow'), may hold values from -0.09375 to 0.09375
- slab_index: int32 [4096], replicated, may hold values from 0 to 32767, as said below
- occupied_energy: float32 [4096], P('narrow'), may hold values from -3 to -0.5
- virtual_energy: float32 [4096], P('wide'), may hold values from 1.5 to 6
Outputs:
- updated: float32 [4096, 4096], P('narrow', 'wide')
Inputs may be any that keep to these rules, and one draw needn't show every extreme that they name: `slab_index`: distinct indices of cd pairs; at most 512 of them lie in any one aligned block of 2048 cd pairs, and one such block holds exactly that many.
All inputs are finite; a program needn't handle non-finite values.
Results may differ from a plain program's by a relative error of at most 0.0003.
Values may be sent and summed in bfloat16 or wider, within the bound.
No kernel may reach another device: no remote copies, remote signals or barrier semaphores. Data moves between devices by JAX's collectives and lax.ppermute only.
A program may use at most 128 MiB of HBM per device.

v0:
```python
import jax
import jax.numpy as jnp
from jax import lax
from jax.sharding import PartitionSpec as P


def on_device(amplitudes, integrals, pair_integrals, slab_index, occupied_energy, virtual_energy):
    wide_count = lax.axis_size("wide")
    wide_index = lax.axis_index("wide")
    height, span_local = amplitudes.shape
    slab_total = integrals.shape[1]
    slot_count = slab_total // wide_count
    capacity = 2 * slot_count
    ladder = jnp.dot(amplitudes, integrals, preferred_element_type=jnp.float32)
    owners = slab_index // span_local
    one_hot = (owners[:, None] == jnp.arange(wide_count, dtype=jnp.int32)[None, :]).astype(
        jnp.int32
    )
    earlier = jnp.cumsum(one_hot, axis=0) - one_hot
    ranking = jnp.sum(earlier * one_hot, axis=1)
    held_here = owners == wide_index
    position = jnp.where(held_here, ranking, capacity)
    local_col = jnp.where(held_here, slab_index - wide_index * span_local, 0)
    columns = jnp.zeros((capacity,), jnp.int32).at[position].set(local_col, mode="drop")
    filled = (
        jnp.zeros((capacity,), jnp.bfloat16)
        .at[position]
        .set(jnp.ones((slab_total,), jnp.bfloat16), mode="drop")
    )
    owned_cols = jnp.take(amplitudes, columns, axis=1) * filled[None, :]
    gathered = lax.all_gather(owned_cols, "wide", axis=1, tiled=True)
    first_slot = wide_index * slot_count
    slot_owner = lax.dynamic_slice_in_dim(owners, first_slot, slot_count)
    slot_rank = lax.dynamic_slice_in_dim(ranking, first_slot, slot_count)
    chosen = jnp.take(gathered, slot_owner * capacity + slot_rank, axis=1)
    late_term = jnp.dot(
        pair_integrals,
        lax.all_gather(chosen, "narrow", axis=0, tiled=True),
        preferred_element_type=jnp.float32,
    )
    summed = lax.psum_scatter(ladder, "wide", scatter_dimension=1, tiled=True) + late_term
    denominator = virtual_energy[None, :] - occupied_energy[:, None]
    return summed / denominator


def solution(mesh):
    placed = (P("narrow", "wide"), P("wide", None), P("narrow", None), P(), P("narrow"), P("wide"))
    return jax.shard_map(
        on_device, mesh=mesh, in_specs=placed, out_specs=P("narrow", "wide"), check_vma=False
    )
```

profile of v0, /device:TPU:1, one launch (start us, length us, event | category | flops | bytes accessed | tf_op | source)
XLA Modules:
  0.0 260.4 jit_solution(13297128873175259026)
XLA Ops:
  6.5 0.9 subtract_select_fusion
  7.5 4.6 %reduce-window.6 = s32[16,32,128]{2,1,0:T(8,128)S(1)} reduce-window(s32[16,32,128]{2,1,0:T(8,128)S(1)} %fusion.5, s32[]{:T(128)} %constant.35.clone.1), window={size=1x1x128 pad=0_0x0_0x127_0}, to_apply=%region_1.2 | reduce-window | flops 8323072 | bytes 524292 | tf_op jit(solution)/shard_map/reduce-window
  12.1 0.5 slice_reduce_fusion
  12.5 0.2 reduce-window.9
  12.7 0.1 broadcast_add_fusion
  12.9 0.2 fusion.4
  13.1 15.5 %scatter_custom_fusion = s32[512]{0:T(512)S(1)} fusion(s32[4096]{0:T(1024)S(1)} %compare_select_fusion, s32[4096]{0:T(1024)S(1)} %get-tuple-element.7, s32[]{:T(128)} %constant.35.clone.1), kind=kCustom, calls=%fused_computation.34 | custom fusion | bytes 2052 | tf_op jit(solution)/shard_map/scatter | solution.py:24
  28.6 1.5 copy.9
  30.1 2.0 gather_fusion
  32.1 28.5 %scatter_custom_fusion.1 = bf16[512]{0:T(512)(128)(2,1)S(1)} fusion(s32[4096]{0:T(1024)S(1)} %compare_select_fusion, bf16[4096]{0:T(1024)(128)(2,1)S(1)} %broadcast.36, bf16[]{:T(256)} %constant.66.clone.1), kind=kCustom, calls=%fused_computation.36 | custom fusion | bytes 1026 | tf_op jit(solution)/shard_map/scatter | solution.py:28
  60.7 0.9 multiply_bitcast_fusion
  61.6 0.0 all-gather.3.cloned.1.call-update
  61.6 0.0 reduce-scatter.2.cloned.1.call-start
  61.6 12.5 %fusion.12 = f32[256,4096]{1,0:T(8,128)} fusion(bf16[256,2048]{1,0:T(8,128)(2,1)} %param.6, bf16[2048,4096]{1,0:T(8,128)(2,1)} %param.7), kind=kOutput, calls=%fused_computation.38 | convolution fusion | flops 4294967296 | bytes 22020096 | tf_op jit(solution)/shard_map/dot_general | solution.py:14
  74.2 0.0 reduce-scatter.2.cloned.1.call-update
  74.2 0.0 all-gather.5.cloned.1.call-start
  74.2 0.1 compare_and_fusion.1
  74.3 47.7 %all-gather.3.cloned.1.call-done = bf16[256,8192]{0,1:T(8,128)(2,1)} async-done(((bf16[256,512]{0,1:T(8,128)(2,1)}), bf16[256,8192]{0,1:T(8,128)(2,1)}) %all-gather.3.cloned.1.call-update) | async-done | bytes 4194320 | tf_op jit(solution)/shard_map/all_gather | solution.py:31
  122.1 3.7 %gather_fusion.1 = bf16[256,256]{1,0:T(8,128)(2,1)S(1)} fusion(bf16[256,8192]{0,1:T(8,128)(2,1)} %all-gather.3.cloned.1.call-done, s32[1024]{0:T(1024)S(1)} %pad_clamp_fusion), kind=kCustom, calls=%fused_computation.1 | custom fusion | bytes 263168 | tf_op jit(solution)/shard_map/jit(_take)/gather | solution.py:35
  125.8 0.8 select_bitcast_fusion
  126.5 0.0 all-gather.5.cloned.1.call-update
  126.6 79.9 %reduce-scatter.2.cloned.1.call-done = f32[256,256]{1,0:T(8,128)} async-done(((f32[256,4096]{1,0:T(8,128)}), f32[256,256]{1,0:T(8,128)}) %reduce-scatter.2.cloned.1.call-update) | async-done | bytes 262160 | tf_op jit(solution)/shard_map/reduce_scatter | solution.py:41
  206.5 44.4 %all-gather.5.cloned.1.call-done = bf16[4096,256]{0,1:T(8,128)(2,1)} async-done(((bf16[256,256]{0,1:T(8,128)(2,1)}), bf16[4096,256]{0,1:T(8,128)(2,1)}) %all-gather.5.cloned.1.call-update) | async-done | bytes 2097168 | tf_op jit(solution)/shard_map/all_gather | solution.py:38
  250.8 3.0 %fusion.1 = f32[256,256]{1,0:T(8,128)} fusion(f32[256,256]{1,0:T(8,128)} %reduce-scatter.2.cloned.1.call-done, bf16[4096,256]{0,1:T(8,128)(2,1)} %all-gather.5.cloned.1.call-done, bf16[256,4096]{1,0:T(8,128)(2,1)S(1)} %copy-done, f32[256]{0:T(256)S(1)} %copy-done.1, f32[256]{0:T(256)S(1)} %copy-done.2), kind=kOutput, calls=%fused_computation.6 | convolution fusion | flops 537067520 | bytes 4720640 | tf_op jit(solution)/shard_map/dot_general | solution.py:36
  (14 shorter events, 0.1 us)
Async XLA Ops:
  6.5 244.3 %copy-start = (bf16[256,4096]{1,0:T(8,128)(2,1)S(1)}, bf16[256,4096]{1,0:T(8,128)(2,1)}, u32[]{:S(2)}) copy-start(bf16[256,4096]{1,0:T(8,128)(2,1)} %param.8) | copy-start | bytes 6291460
  6.5 115.6 %all-gather.3.cloned.1.call-start = ((), (), s32[]{:S(2)}) async-start(), calls=%async_computation.2 | async-start | bytes 4456448 | tf_op jit(solution)/shard_map/all_gather | solution.py:31
  61.6 144.9 %reduce-scatter.2.cloned.1.call-start = ((), (), s32[]{:S(2)}) async-start(), calls=%async_computation.1 | async-start | bytes 4456448 | tf_op jit(solution)/shard_map/reduce_scatter | solution.py:41
  74.2 176.7 %copy-start.1 = (f32[256]{0:T(256)S(1)}, f32[256]{0:T(256)}, u32[]{:S(2)}) copy-start(f32[256]{0:T(256)} %param.10) | copy-start | bytes 3076
  74.2 176.7 %copy-start.2 = (f32[256]{0:T(256)S(1)}, f32[256]{0:T(256)}, u32[]{:S(2)}) copy-start(f32[256]{0:T(256)} %param.11) | copy-start | bytes 3076
  74.2 176.6 %all-gather.5.cloned.1.call-start = ((), (), s32[]{:S(2)}) async-start(), calls=%async_computation.3 | async-start | bytes 2228224 | tf_op jit(solution)/shard_map/all_gather | solution.py:38
Sparse Core Ops, SparseCore 0:
  61.7 60.3 all-gather.2
  125.7 80.6 reduce-scatter.1
  208.3 42.4 all-gather.4
where the time goes:
time: 261 us; the launch traced here: 260 us
  waiting for transfers between devices  172 us (66%)
  local copies, waits for them, and re-layouts  51.7 us (20%)
  matrix products  15.6 us (6%)
  between operations  13.2 us (5%)
  other arithmetic  7.83 us (3%)
    reduce_scatter x1, waiting for transfers between devices, on_device(): lax.psum_scatter(ladder, 'wide', scatter_dimension=1, tiled=True)  79.9 us
    all_gather x1, waiting for transfers between devices, on_device(): gathered = lax.all_gather(owned_cols, 'wide', axis=1, tiled=True)  47.7 us
    all_gather x1, waiting for transfers between devices, on_device(): lax.all_gather(chosen, 'narrow', axis=0, tiled=True)  44.4 us
    scatter x1, local copies, waits for them, and re-layouts, on_device(): filled = jnp.zeros((capacity,), jnp.bfloat16).at[position].set(jnp.ones((...  28.5 us
    scatter x1, local copies, waits for them, and re-layouts, on_device(): jnp.zeros((capacity,), jnp.int32).at[position].set(local_col, mode='drop')  15.5 us
    dot_general x1, matrix products, on_device(): ladder = jnp.dot(amplitudes, integrals, preferred_element_type=jnp.float32)  12.5 us
  transfers between devices with their start and end apart: 3, of which 3 were waited for; matrix products, arithmetic and copies ran while one was open for 7% of the time, Pallas kernels for 0%

commit v1 on v0

v1 whole, which is shorter than its diff:
```python
import jax
import jax.numpy as jnp
from jax import lax
from jax.experimental import pallas as pl
from jax.experimental.pallas import tpu as pltpu
from jax.sharding import PartitionSpec as P

CHUNKS = 16
DEPTH = 32
LANES = 256
CODE_ROWS = 16
STEPS = 256.0
TOP = 32760.0
VMEM = pl.BlockSpec(memory_space=pltpu.VMEM)
SMEM = pl.BlockSpec(memory_space=pltpu.SMEM)


def iota(shape, dim):
    return lax.broadcasted_iota(jnp.int32, shape, dim)


def ones_where(mask):
    return jnp.where(mask, 1.0, 0.0)


def bdot(left, right, dims=((1,), (0,))):
    return lax.dot_general(
        left.astype(jnp.bfloat16),
        right.astype(jnp.bfloat16),
        (dims, ((), ())),
        preferred_element_type=jnp.float32,
    )


def count_before(classes):
    member = jnp.concatenate(
        [ones_where(classes[c : c + 1, :] == iota((CHUNKS, LANES), 0)) for c in range(CHUNKS)], 0
    )
    earlier = ones_where(iota((LANES, LANES), 0) < iota((LANES, LANES), 1))
    return member, bdot(member, earlier)


def pick(member, table):
    return jnp.sum((member * table).reshape(CHUNKS, CHUNKS, LANES), axis=1).astype(jnp.int32)


def select_kernel(shift, here_ref, index_ref, amp_ref, sent_ref, rank_ref):
    index = index_ref[...]
    here = here_ref[0]
    owner = jnp.right_shift(index, shift)
    member, within = count_before(owner)
    r, c = iota((LANES, LANES), 0), iota((LANES, LANES), 1)
    ahead = ones_where(((r & 15) == (c & 15)) & (jnp.right_shift(c, 4) < jnp.right_shift(r, 4)))
    base = jnp.sum(bdot(ahead, member), axis=1, keepdims=True)
    rank = pick(member, within + base)
    rank_ref[...] = rank
    middle, depth = rank & 15, jnp.right_shift(rank, 4)
    column = index & ((1 << shift) - 1)
    high, low = jnp.right_shift(column, 6).astype(jnp.float32), (column & 63).astype(jnp.float32)
    lefts, rights = [], []
    for k in range(CHUNKS):
        one = slice(k, k + 1)
        hit = ones_where((depth[one] == iota((DEPTH, LANES), 0)) & (owner[one] == here))
        lefts.append(jnp.concatenate([hit * high[one], hit * low[one]], 0))
        rights.append(ones_where(middle[one] == iota((CHUNKS, LANES), 0)))
    found = bdot(jnp.concatenate(lefts, 1), jnp.concatenate(rights, 1), ((1,), (1,)))
    columns = (found[:DEPTH] * 64.0 + found[DEPTH:]).astype(jnp.int32)
    span = amp_ref.shape[1]
    lane = iota((DEPTH, span), 1)
    for k in range(0, CHUNKS, 4):
        chosen = jnp.concatenate(
            [
                ones_where(lane == columns[:, j : j + 1]).astype(jnp.bfloat16)
                for j in range(k, k + 4)
            ],
            0,
        )
        got = bdot(chosen, amp_ref[...], ((1,), (1,))).astype(jnp.bfloat16)
        sent_ref[k : k + 4] = got.reshape(4, DEPTH, got.shape[1])


def route_kernel(shift, here_ref, index_ref, rank_ref, forward_ref, settle_ref):
    index, rank, here = index_ref[...], rank_ref[...], here_ref[0]
    owner = jnp.right_shift(index, shift)
    middle, depth = rank & 15, jnp.right_shift(rank, 4)
    member, within = count_before(middle)
    place = pick(member, within)
    source = (owner * DEPTH + depth).astype(jnp.float32)
    lane = iota((DEPTH, CHUNKS * DEPTH), 1)
    for k in range(CHUNKS):
        one = slice(k, k + 1)
        hit = (place[one] == iota((DEPTH, LANES), 0)) & (middle[one] == here)
        row = jnp.sum(jnp.where(hit, source[one], 0.0), axis=1, keepdims=True).astype(jnp.int32)
        forward_ref[k * DEPTH : (k + 1) * DEPTH, :] = ones_where(lane == row).astype(jnp.bfloat16)
    arrived = (middle * DEPTH + place).astype(jnp.float32)
    own = iota((CHUNKS, LANES), 0) == here
    wanted = jnp.sum(jnp.where(own, arrived, 0.0), axis=0, keepdims=True).astype(jnp.int32)
    settle_ref[...] = ones_where(iota((CHUNKS * DEPTH, LANES), 0) == wanted).astype(jnp.bfloat16)


def ladder_kernel(amp_ref, int_ref, coded_ref):
    height = amp_ref.shape[0]
    for k in range(coded_ref.shape[0]):
        part = jnp.dot(
            amp_ref[...],
            int_ref[:, k * LANES : (k + 1) * LANES],
            preferred_element_type=jnp.float32,
        )
        largest = jnp.max(jnp.abs(part), axis=0, keepdims=True)
        code = jnp.ceil(jnp.log2(jnp.maximum(largest, 2.0**-120)) * STEPS) + 1.0
        shrunk = part * jnp.exp2(code * (-1.0 / STEPS)) * TOP
        coded_ref[k, :height, :] = jnp.round(shrunk).astype(jnp.int32).astype(jnp.int16)
        coded_ref[k, height:, :] = jnp.broadcast_to(
            code.astype(jnp.int32), (CODE_ROWS, LANES)
        ).astype(jnp.int16)


def decode_kernel(coded_ref, sum_ref):
    height = sum_ref.shape[0]
    total = jnp.zeros(sum_ref.shape, jnp.float32)
    for k in range(CHUNKS):
        code = coded_ref[k, height:, :].astype(jnp.int32).astype(jnp.float32)[:1, :]
        values = coded_ref[k, :height, :].astype(jnp.int32).astype(jnp.float32)
        total = total + values * jnp.exp2(code * (1.0 / STEPS))
    sum_ref[...] = total * (1.0 / TOP)


def finish_kernel(place_ref, pair_ref, ladder_ref, occ_ref, virt_ref, own_ref, far_ref, sib_ref, sibfar_ref, out_ref):
    z, core = place_ref[0], place_ref[1]
    rows = out_ref.shape[0]
    half = rows // 2
    total = ladder_ref[...]

    def add(total, away, which, start, block):
        n = jnp.bitwise_and(z - away + 8, 7) * 2 + which
        columns = pl.ds(pl.multiple_of(n * rows + start, 128), block.shape[0])
        return total + jnp.dot(pair_ref[:, columns], block, preferred_element_type=jnp.float32)

    for near, far, which in ((own_ref, far_ref, core), (sib_ref, sibfar_ref, 1 - core)):
        for k, away in enumerate((0, 1, -1, 2, -2)):
            total = add(total, away, which, 0, near[k * rows : (k + 1) * rows])
        total = add(total, 3, which, 0, far[:rows])
        total = add(total, -3, which, 0, far[rows : 2 * rows])
        total = add(total, 4, which, 0, far[2 * rows : 2 * rows + half])
        total = add(total, 4, which, half, far[2 * rows + half :])
    out_ref[...] = total / (virt_ref[...] - occ_ref[...])


def on_device(amplitudes, integrals, pair_integrals, slab_index, occupied_energy, virtual_energy):
    wide_index = lax.axis_index("wide")
    narrow_index = lax.axis_index("narrow")
    height, span = amplitudes.shape
    shift = span.bit_length() - 1
    here = wide_index.astype(jnp.int32).reshape(1)
    index = slab_index.reshape(CHUNKS, LANES)
    half = height // 2

    def step(value, dz, dc=0):
        ring = [
            (z * 2 + c, (z + dz) % 8 * 2 + (c + dc) % 2) for z in range(8) for c in range(2)
        ]
        return lax.ppermute(value, "narrow", ring)

    sent, rank = pl.pallas_call(
        lambda *refs: select_kernel(shift, *refs),
        out_shape=(
            jax.ShapeDtypeStruct((CHUNKS, DEPTH, height), jnp.bfloat16),
            jax.ShapeDtypeStruct((CHUNKS, LANES), jnp.int32),
        ),
        in_specs=[SMEM, VMEM, VMEM],
        out_specs=(VMEM, VMEM),
        compiler_params=pltpu.CompilerParams(vmem_limit_bytes=24 << 20),
        cost_estimate=pl.CostEstimate(flops=2**30, bytes_accessed=2**21, transcendentals=0),
        name="select",
    )(here, index, amplitudes)
    first = lax.all_to_all(sent, "wide", 0, 0, tiled=True)

    forward, settle = pl.pallas_call(
        lambda *refs: route_kernel(shift, *refs),
        out_shape=(
            jax.ShapeDtypeStruct((CHUNKS * DEPTH, CHUNKS * DEPTH), jnp.bfloat16),
            jax.ShapeDtypeStruct((CHUNKS * DEPTH, LANES), jnp.bfloat16),
        ),
        in_specs=[SMEM, VMEM, VMEM],
        out_specs=(VMEM, VMEM),
        compiler_params=pltpu.CompilerParams(vmem_limit_bytes=16 << 20),
        cost_estimate=pl.CostEstimate(flops=2**28, bytes_accessed=2**20, transcendentals=0),
        name="route",
    )(here, index, rank)

    per = 2
    coded = pl.pallas_call(
        ladder_kernel,
        grid=(CHUNKS // per,),
        out_shape=jax.ShapeDtypeStruct((CHUNKS, height + CODE_ROWS, LANES), jnp.int16),
        in_specs=[
            pl.BlockSpec((height, span), lambda i: (0, 0)),
            pl.BlockSpec((span, per * LANES), lambda i: (0, i)),
        ],
        out_specs=pl.BlockSpec((per, height + CODE_ROWS, LANES), lambda i: (i, 0, 0)),
        compiler_params=pltpu.CompilerParams(vmem_limit_bytes=24 << 20),
        cost_estimate=pl.CostEstimate(
            flops=2 * height * span * CHUNKS * LANES, bytes_accessed=20 * 2**20, transcendentals=0
        ),
        name="ladder",
    )(amplitudes, integrals)
    shares = lax.all_to_all(coded, "wide", 0, 0, tiled=True)

    moved = bdot(forward, first.reshape(CHUNKS * DEPTH, height)).astype(jnp.bfloat16)
    second = lax.all_to_all(moved.reshape(CHUNKS, DEPTH, height), "wide", 0, 0, tiled=True)
    own = bdot(second.reshape(CHUNKS * DEPTH, height), settle, ((0,), (0,))).astype(jnp.bfloat16)

    up, down, up2, down2 = step(own, 1), step(own, -1), step(own, 2), step(own, -2)
    near = jnp.concatenate([own, up, down, up2, down2], 0)
    up3, down3 = step(up2, 1), step(down2, -1)
    up4, down4 = step(up2[:half], 2), step(down2[half:], -2)
    near_sibling = step(near, 0, 1)
    far = jnp.concatenate([up3, down3, up4, down4], 0)
    far_sibling = step(far, 0, 1)

    ladder = pl.pallas_call(
        decode_kernel,
        out_shape=jax.ShapeDtypeStruct((height, LANES), jnp.float32),
        in_specs=[VMEM],
        out_specs=VMEM,
        compiler_params=pltpu.CompilerParams(vmem_limit_bytes=16 << 20),
        cost_estimate=pl.CostEstimate(flops=2**22, bytes_accessed=5 * 2**19, transcendentals=0),
        name="decode",
    )(shares)

    where = jnp.stack([narrow_index // 2, narrow_index % 2]).astype(jnp.int32)
    return pl.pallas_call(
        finish_kernel,
        out_shape=jax.ShapeDtypeStruct((height, LANES), jnp.float32),
        in_specs=[SMEM] + [VMEM] * 8,
        out_specs=VMEM,
        compiler_params=pltpu.CompilerParams(vmem_limit_bytes=24 << 20),
        cost_estimate=pl.CostEstimate(flops=2**29, bytes_accessed=2**22, transcendentals=0),
        name="finish",
    )(
        where,
        pair_integrals,
        ladder,
        occupied_energy.reshape(height, 1),
        virtual_energy.reshape(1, LANES),
        near,
        far,
        near_sibling,
        far_sibling,
    )


def solution(mesh):
    placed = (P("narrow", "wide"), P("wide", None), P("narrow", None), P(), P("narrow"), P("wide"))
    return jax.shard_map(
        on_device, mesh=mesh, in_specs=placed, out_specs=P("narrow", "wide"), check_vma=False
    )
```

time: 261 us -> 80.9 us (0.31)
  the two profiles are of different devices: /device:TPU:1 before, /device:TPU:128 now
where the time goes in v1:
time: 80.9 us; the launch traced here: 80.4 us
  starting transfers between devices  33.1 us (41%)
  waiting for transfers between devices  18.5 us (23%)
  Pallas kernels  15 us (19%)
  local copies, waits for them, and re-layouts  11.5 us (14%)
  matrix products  1.92 us (2%)
    ppermute x10, starting transfers between devices, step(): return lax.ppermute(value, 'narrow', ring)  15.1 us
    unnamed x18, local copies, waits for them, and re-layouts  10 us
    pallas_call x1, Pallas kernels, on_device(): pl.pallas_call(ladder_kernel, grid=(CHUNKS // per,), out_shape=jax.ShapeD...  8.59 us
    all_to_all x1, waiting for transfers between devices, on_device(): first = lax.all_to_all(sent, 'wide', 0, 0, tiled=True)  8.01 us
    all_to_all x1, waiting for transfers between devices, on_device(): shares = lax.all_to_all(coded, 'wide', 0, 0, tiled=True)  7.94 us
    all_to_all x1, starting transfers between devices, on_device(): shares = lax.all_to_all(coded, 'wide', 0, 0, tiled=True)  7.21 us
    all_to_all x1, starting transfers between devices, on_device(): first = lax.all_to_all(sent, 'wide', 0, 0, tiled=True)  7.17 us
    all_to_all x1, starting transfers between devices, on_device(): lax.all_to_all(moved.reshape(CHUNKS, DEPTH, height), 'wide', 0, 0, tiled=...  3.63 us
  transfers between devices with their start and end apart: 13, of which 4 were waited for; matrix products, arithmetic and copies ran while one was open for 5% of the time, Pallas kernels for 12%

profile of v1, /device:TPU:128, one launch (start us, length us, event | category | flops | bytes accessed | tf_op | source)
XLA Modules:
  0.0 80.4 jit_solution(7652366983861354024)
XLA Ops:
  0.0 0.7 reshape.24.refs_1_
  0.7 1.2 %copy-done.2 = bf16[256,2048]{1,0:T(8,128)(2,1)S(1)} copy-done((bf16[256,2048]{1,0:T(8,128)(2,1)S(1)}, bf16[256,2048]{1,0:T(8,128)(2,1)}, u32[]{:S(2)}) %copy-start.2) | copy-done | bytes 1048600
  1.9 2.7 %select.7 = (bf16[16,32,256]{2,1,0:T(8,128)(2,1)}, s32[16,256]{1,0:T(8,128)S(1)}) custom-call(s32[1]{0:T(128)} %bitcast.4.refs_0_, s32[16,256]{1,0:T(8,128)S(1)} %reshape.24.refs_1_, bf16[256,2048]{1,0:T(8,128)(2,1)S(1)} %copy-done.2), custom_call_target="tpu_custom_call" | custom-call | flops 1073741824 | bytes 2097152 | tf_op jit(solution)/shard_map/select/pallas_call | solution.py:164
  4.6 7.2 %all-to-all-start.1 = ((bf16[16,32,256]{2,1,0:T(8,128)(2,1)}), bf16[16,32,256]{2,1,0:T(8,128)(2,1)S(1)}, u32[]{:S(2)}, u32[]{:S(2)}) async-start(bf16[16,32,256]{2,1,0:T(8,128)(2,1)} %get-tuple-element.11), calls=%async_computation.1 | async-start | bytes 524288 | tf_op jit(solution)/shard_map/all_to_all | solution.py:176
  12.3 8.0 %all-to-all-done.1 = bf16[16,32,256]{2,1,0:T(8,128)(2,1)S(1)} async-done(((bf16[16,32,256]{2,1,0:T(8,128)(2,1)}), bf16[16,32,256]{2,1,0:T(8,128)(2,1)S(1)}, u32[]{:S(2)}, u32[]{:S(2)}) %all-to-all-start.1) | async-done | bytes 262176 | tf_op jit(solution)/shard_map/all_to_all | solution.py:176
  20.3 1.0 %convolution_convert_fusion = bf16[512,256]{1,0:T(8,128)(2,1)} fusion(bf16[512,512]{1,0:T(8,128)(2,1)S(1)} %get-tuple-element.10, bf16[512,256]{1,0:T(8,128)(2,1)S(1)} %bitcast.13), kind=kOutput, calls=%fused_computation | convolution fusion | flops 134348800 | bytes 1048576 | tf_op jit(solution)/shard_map/dot_general | solution.py:27
  21.3 3.6 %all-to-all-start.2 = ((bf16[16,32,256]{2,1,0:T(8,128)(2,1)}), bf16[16,32,256]{2,1,0:T(8,128)(2,1)S(1)}, u32[]{:S(2)}, u32[]{:S(2)}) async-start(bf16[16,32,256]{2,1,0:T(8,128)(2,1)} %bitcast.6), calls=%async_computation.2 | async-start | bytes 524288 | tf_op jit(solution)/shard_map/all_to_all | solution.py:210
  25.0 5.8 %copy-done = bf16[2048,4096]{1,0:T(8,128)(2,1)S(1)} copy-done((bf16[2048,4096]{1,0:T(8,128)(2,1)S(1)}, bf16[2048,4096]{1,0:T(8,128)(2,1)}, u32[]{:S(2)}) %copy-start) | copy-done | bytes 16777240
  30.8 8.6 %ladder.1 = s16[16,272,256]{2,1,0:T(8,128)(2,1)} custom-call(bf16[256,2048]{1,0:T(8,128)(2,1)S(1)} %copy-done.3, bf16[2048,4096]{1,0:T(8,128)(2,1)S(1)} %copy-done), custom_call_target="tpu_custom_call" | custom-call | flops 4294967296 | bytes 20971520 | tf_op jit(solution)/shard_map/ladder/pallas_call | solution.py:192
  39.3 7.2 %all-to-all-start = ((s16[16,272,256]{2,1,0:T(8,128)(2,1)}), s16[16,272,256]{2,1,0:T(8,128)(2,1)S(1)}, u32[]{:S(2)}, u32[]{:S(2)}) async-start(s16[16,272,256]{2,1,0:T(8,128)(2,1)} %ladder.1), calls=%async_computation | async-start | bytes 4456448 | tf_op jit(solution)/shard_map/all_to_all | solution.py:207
  46.6 0.9 %constant_dynamic-update-slice_fusion.4 = (bf16[1280,256]{1,0:T(8,128)(2,1)}, bf16[256,256]{1,0:T(8,128)(2,1)S(1)}) fusion(bf16[512,256]{1,0:T(8,128)(2,1)S(1)} %bitcast.14, bf16[512,256]{1,0:T(8,128)(2,1)S(1)} %get-tuple-element.12), kind=kOutput, calls=%fused_computation.6 | convolution fusion | flops 67174400 | bytes 786432 | tf_op jit(solution)/shard_map/dot_general | solution.py:27
  47.5 1.5 %collective-permute-start.2 = (bf16[256,256]{1,0:T(8,128)(2,1)S(1)}, bf16[256,256]{1,0:T(8,128)(2,1)S(1)}, u32[]{:S(2)}, u32[]{:S(2)}) collective-permute-start(bf16[256,256]{1,0:T(8,128)(2,1)S(1)} %get-tuple-element.14), channel_id=1, source_target_pairs={{0,4},{1,5},{2,6},{3,7},{4,8},{5,9},{6,10},{7,11},{8,12},{9,13},{1... | collective-permute-start | bytes 393224 | tf_op jit(solution)/shard_map/ppermute | solution.py:162
  49.0 2.7 %collective-permute-start.3 = (bf16[256,256]{1,0:T(8,128)(2,1)S(1)}, bf16[256,256]{1,0:T(8,128)(2,1)S(1)}, u32[]{:S(2)}, u32[]{:S(2)}) collective-permute-start(bf16[256,256]{1,0:T(8,128)(2,1)S(1)} %get-tuple-element.14), channel_id=1, source_target_pairs={{0,12},{1,13},{2,14},{3,15},{4,0},{5,1},{6,2},{7,3},{8,4},{9,5},{1... | collective-permute-start | bytes 393224 | tf_op jit(solution)/shard_map/ppermute | solution.py:162
  51.6 1.0 %collective-permute-start = (bf16[256,256]{1,0:T(8,128)(2,1)S(1)}, bf16[256,256]{1,0:T(8,128)(2,1)S(1)}, u32[]{:S(2)}, u32[]{:S(2)}) collective-permute-start(bf16[256,256]{1,0:T(8,128)(2,1)S(1)} %get-tuple-element.14), channel_id=1, source_target_pairs={{0,2},{1,3},{2,4},{3,5},{4,6},{5,7},{6,8},{7,9},{8,10},{9,11},{10,... | collective-permute-start | bytes 393224 | tf_op jit(solution)/shard_map/ppermute | solution.py:162
  52.6 2.2 %collective-permute-start.1 = (bf16[256,256]{1,0:T(8,128)(2,1)S(1)}, bf16[256,256]{1,0:T(8,128)(2,1)S(1)}, u32[]{:S(2)}, u32[]{:S(2)}) collective-permute-start(bf16[256,256]{1,0:T(8,128)(2,1)S(1)} %get-tuple-element.14), channel_id=1, source_target_pairs={{0,14},{1,15},{2,0},{3,1},{4,2},{5,3},{6,4},{7,5},{8,6},{9,7},{10,... | collective-permute-start | bytes 393224 | tf_op jit(solution)/shard_map/ppermute | solution.py:162
  54.9 2.2 %collective-permute-done.2 = bf16[256,256]{1,0:T(8,128)(2,1)S(1)} collective-permute-done((bf16[256,256]{1,0:T(8,128)(2,1)S(1)}, bf16[256,256]{1,0:T(8,128)(2,1)S(1)}, u32[]{:S(2)}, u32[]{:S(2)}) %collective-permute-start.2) | collective-permute-done | bytes 131104 | tf_op jit(solution)/shard_map/ppermute | solution.py:162
  57.2 4.1 %collective-permute-start.7 = (bf16[128,256]{1,0:T(8,128)(2,1)S(1)}, bf16[128,256]{1,0:T(8,128)(2,1)S(1)}, u32[]{:S(2)}, u32[]{:S(2)}) collective-permute-start(bf16[128,256]{1,0:T(8,128)(2,1)S(1)} %slice.9), channel_id=1, source_target_pairs={{0,12},{1,13},{2,14},{3,15},{4,0},{5,1},{6,2},{7,3},{8,4},{9,5},{1... | collective-permute-start | bytes 196616 | tf_op jit(solution)/shard_map/ppermute | solution.py:162
  61.3 0.7 collective-permute-start.4
  62.1 2.5 %collective-permute-start.5 = (bf16[256,256]{1,0:T(8,128)(2,1)S(1)}, bf16[256,256]{1,0:T(8,128)(2,1)S(1)}, u32[]{:S(2)}, u32[]{:S(2)}) collective-permute-start(bf16[256,256]{1,0:T(8,128)(2,1)S(1)} %collective-permute-done.3), channel_id=1, source_target_pairs={{0,14},{1,15},{2,0},{3,1},{4,2},{5,3},{6,4},{7,5},{8,6},{9,7},{10,... | collective-permute-start | bytes 393224 | tf_op jit(solution)/shard_map/ppermute | solution.py:162
  65.9 0.7 constant_dynamic-update-slice_fusion.1
  66.6 0.7 constant_dynamic-update-slice_fusion.own_ref
  68.2 7.9 %all-to-all-done.coded_ref = s16[16,272,256]{2,1,0:T(8,128)(2,1)S(1)} async-done(((s16[16,272,256]{2,1,0:T(8,128)(2,1)}), s16[16,272,256]{2,1,0:T(8,128)(2,1)S(1)}, u32[]{:S(2)}, u32[]{:S(2)}) %all-to-all-start) | async-done | bytes 2228256 | tf_op jit(solution)/shard_map/all_to_all | solution.py:207
  76.7 1.0 %copy-done.1 = bf16[256,4096]{1,0:T(8,128)(2,1)S(1)} copy-done((bf16[256,4096]{1,0:T(8,128)(2,1)S(1)}, bf16[256,4096]{1,0:T(8,128)(2,1)}, u32[]{:S(2)}) %copy-start.1) | copy-done | bytes 2097176
  77.7 2.7 %finish.1 = f32[256,256]{1,0:T(8,128)} custom-call(s32[2]{0:T(128)S(1)} %pad_add_fusion.place_ref, bf16[256,4096]{1,0:T(8,128)(2,1)S(1)} %copy-done.1, f32[256,256]{1,0:T(8,128)S(1)} %decode.1.ladder_ref, f32[256,1]{1,0:T(8,128)S(1)} %copy.7.occ_ref, f32[1,256]{1,0:T(1,128)S(1)} %bitcast.12, bf16[1280,256]{1,0:T(8,128)(2,1)} %constant_dynamic-update-slice_fusion.own_ref, ...), custom_call_target="tpu_custom_call" | custom-call | flops 536870912 | bytes 4194304 | tf_op jit(solution)/shard_map/finish/pallas_call | solution.py:232
  (34 shorter events, 3.4 us)
Async XLA Ops:
  0.7 1.2 %copy-start.2 = (bf16[256,2048]{1,0:T(8,128)(2,1)S(1)}, bf16[256,2048]{1,0:T(8,128)(2,1)}, u32[]{:S(2)}) copy-start(bf16[256,2048]{1,0:T(8,128)(2,1)} %refs_2_.1) | copy-start | bytes 3145732
  4.6 20.3 %copy-start.3 = (bf16[256,2048]{1,0:T(8,128)(2,1)S(1)}, bf16[256,2048]{1,0:T(8,128)(2,1)}, u32[]{:S(2)}) copy-start(bf16[256,2048]{1,0:T(8,128)(2,1)} %refs_2_.1) | copy-start | bytes 3145732
  4.6 15.7 %all-to-all-start.1 = ((bf16[16,32,256]{2,1,0:T(8,128)(2,1)}), bf16[16,32,256]{2,1,0:T(8,128)(2,1)S(1)}, u32[]{:S(2)}, u32[]{:S(2)}) async-start(bf16[16,32,256]{2,1,0:T(8,128)(2,1)} %get-tuple-element.11), calls=%async_computation.1 | async-start | bytes 524288 | tf_op jit(solution)/shard_map/all_to_all | solution.py:176
  21.3 18.0 %all-to-all-start.2 = ((bf16[16,32,256]{2,1,0:T(8,128)(2,1)}), bf16[16,32,256]{2,1,0:T(8,128)(2,1)S(1)}, u32[]{:S(2)}, u32[]{:S(2)}) async-start(bf16[16,32,256]{2,1,0:T(8,128)(2,1)} %bitcast.6), calls=%async_computation.2 | async-start | bytes 524288 | tf_op jit(solution)/shard_map/all_to_all | solution.py:210
  25.0 5.8 %copy-start = (bf16[2048,4096]{1,0:T(8,128)(2,1)S(1)}, bf16[2048,4096]{1,0:T(8,128)(2,1)}, u32[]{:S(2)}) copy-start(bf16[2048,4096]{1,0:T(8,128)(2,1)} %int_ref.1) | copy-start | bytes 50331652
  39.3 36.8 %all-to-all-start = ((s16[16,272,256]{2,1,0:T(8,128)(2,1)}), s16[16,272,256]{2,1,0:T(8,128)(2,1)S(1)}, u32[]{:S(2)}, u32[]{:S(2)}) async-start(s16[16,272,256]{2,1,0:T(8,128)(2,1)} %ladder.1), calls=%async_computation | async-start | bytes 4456448 | tf_op jit(solution)/shard_map/all_to_all | solution.py:207
  46.6 21.4 %copy-start.5 = (f32[256]{0:T(256)S(1)}, f32[256]{0:T(256)}, u32[]{:S(2)}) copy-start(f32[256]{0:T(256)} %param.10) | copy-start | bytes 3076
  47.5 9.6 %collective-permute-start.2 = (bf16[256,256]{1,0:T(8,128)(2,1)S(1)}, bf16[256,256]{1,0:T(8,128)(2,1)S(1)}, u32[]{:S(2)}, u32[]{:S(2)}) collective-permute-start(bf16[256,256]{1,0:T(8,128)(2,1)S(1)} %get-tuple-element.14), channel_id=1, source_target_pairs={{0,4},{1,5},{2,6},{3,7},{4,8},{5,9},{6,10},{7,11},{8,12},{9,13},{1... | collective-permute-start | bytes 393224 | tf_op jit(solution)/shard_map/ppermute | solution.py:162
  49.0 8.3 %collective-permute-start.3 = (bf16[256,256]{1,0:T(8,128)(2,1)S(1)}, bf16[256,256]{1,0:T(8,128)(2,1)S(1)}, u32[]{:S(2)}, u32[]{:S(2)}) collective-permute-start(bf16[256,256]{1,0:T(8,128)(2,1)S(1)} %get-tuple-element.14), channel_id=1, source_target_pairs={{0,12},{1,13},{2,14},{3,15},{4,0},{5,1},{6,2},{7,3},{8,4},{9,5},{1... | collective-permute-start | bytes 393224 | tf_op jit(solution)/shard_map/ppermute | solution.py:162
  51.6 10.4 %collective-permute-start = (bf16[256,256]{1,0:T(8,128)(2,1)S(1)}, bf16[256,256]{1,0:T(8,128)(2,1)S(1)}, u32[]{:S(2)}, u32[]{:S(2)}) collective-permute-start(bf16[256,256]{1,0:T(8,128)(2,1)S(1)} %get-tuple-element.14), channel_id=1, source_target_pairs={{0,2},{1,3},{2,4},{3,5},{4,6},{5,7},{6,8},{7,9},{8,10},{9,11},{10,... | collective-permute-start | bytes 393224 | tf_op jit(solution)/shard_map/ppermute | solution.py:162
  52.6 12.6 %collective-permute-start.1 = (bf16[256,256]{1,0:T(8,128)(2,1)S(1)}, bf16[256,256]{1,0:T(8,128)(2,1)S(1)}, u32[]{:S(2)}, u32[]{:S(2)}) collective-permute-start(bf16[256,256]{1,0:T(8,128)(2,1)S(1)} %get-tuple-element.14), channel_id=1, source_target_pairs={{0,14},{1,15},{2,0},{3,1},{4,2},{5,3},{6,4},{7,5},{8,6},{9,7},{10,... | collective-permute-start | bytes 393224 | tf_op jit(solution)/shard_map/ppermute | solution.py:162
  57.1 10.4 %collective-permute-start.6 = (bf16[128,256]{1,0:T(8,128)(2,1)S(1)}, bf16[128,256]{1,0:T(8,128)(2,1)S(1)}, u32[]{:S(2)}, u32[]{:S(2)}) collective-permute-start(bf16[128,256]{1,0:T(8,128)(2,1)S(1)} %slice.8), channel_id=1, source_target_pairs={{0,4},{1,5},{2,6},{3,7},{4,8},{5,9},{6,10},{7,11},{8,12},{9,13},{1... | collective-permute-start | bytes 196616 | tf_op jit(solution)/shard_map/ppermute | solution.py:162
  57.2 10.4 %collective-permute-start.7 = (bf16[128,256]{1,0:T(8,128)(2,1)S(1)}, bf16[128,256]{1,0:T(8,128)(2,1)S(1)}, u32[]{:S(2)}, u32[]{:S(2)}) collective-permute-start(bf16[128,256]{1,0:T(8,128)(2,1)S(1)} %slice.9), channel_id=1, source_target_pairs={{0,12},{1,13},{2,14},{3,15},{4,0},{5,1},{6,2},{7,3},{8,4},{9,5},{1... | collective-permute-start | bytes 196616 | tf_op jit(solution)/shard_map/ppermute | solution.py:162
  61.3 6.2 %collective-permute-start.4 = (bf16[256,256]{1,0:T(8,128)(2,1)S(1)}, bf16[256,256]{1,0:T(8,128)(2,1)S(1)}, u32[]{:S(2)}, u32[]{:S(2)}) collective-permute-start(bf16[256,256]{1,0:T(8,128)(2,1)S(1)} %collective-permute-done.2), channel_id=1, source_target_pairs={{0,2},{1,3},{2,4},{3,5},{4,6},{5,7},{6,8},{7,9},{8,10},{9,11},{10,... | collective-permute-start | bytes 393224 | tf_op jit(solution)/shard_map/ppermute | solution.py:162
  62.1 5.5 %collective-permute-start.5 = (bf16[256,256]{1,0:T(8,128)(2,1)S(1)}, bf16[256,256]{1,0:T(8,128)(2,1)S(1)}, u32[]{:S(2)}, u32[]{:S(2)}) collective-permute-start(bf16[256,256]{1,0:T(8,128)(2,1)S(1)} %collective-permute-done.3), channel_id=1, source_target_pairs={{0,14},{1,15},{2,0},{3,1},{4,2},{5,3},{6,4},{7,5},{8,6},{9,7},{10,... | collective-permute-start | bytes 393224 | tf_op jit(solution)/shard_map/ppermute | solution.py:162
  64.6 12.1 %copy-start.4 = (f32[256]{0:T(256)S(1)}, f32[256]{0:T(256)}, u32[]{:S(2)}) copy-start(f32[256]{0:T(256)} %param.11) | copy-start | bytes 3076
  67.2 9.5 %collective-permute-start.8 = (bf16[1280,256]{1,0:T(8,128)(2,1)}, bf16[1280,256]{1,0:T(8,128)(2,1)S(1)}, u32[]{:S(2)}, u32[]{:S(2)}) collective-permute-start(bf16[1280,256]{1,0:T(8,128)(2,1)} %constant_dynamic-update-slice_fusion.own_ref), channel_id=1, source_target_pairs={{0,1},{1,0},{2,3},{3,2},{4,5},{5,4},{6,7},{7,6},{8,9},{9,8},{10,11... | collective-permute-start | bytes 1966088 | tf_op jit(solution)/shard_map/ppermute | solution.py:162
  67.6 9.1 %collective-permute-start.9 = (bf16[768,256]{1,0:T(8,128)(2,1)S(1)}, bf16[768,256]{1,0:T(8,128)(2,1)}, u32[]{:S(2)}, u32[]{:S(2)}) collective-permute-start(bf16[768,256]{1,0:T(8,128)(2,1)S(1)} %constant_dynamic-update-slice_fusion.5.far_ref), channel_id=1, source_target_pairs={{0,1},{1,0},{2,3},{3,2},{4,5},{5,4},{6,7},{7,6},{8,9},{9,8},{10,11... | collective-permute-start | bytes 1179656 | tf_op jit(solution)/shard_map/ppermute | solution.py:162
  76.1 1.6 %copy-start.1 = (bf16[256,4096]{1,0:T(8,128)(2,1)S(1)}, bf16[256,4096]{1,0:T(8,128)(2,1)}, u32[]{:S(2)}) copy-start(bf16[256,4096]{1,0:T(8,128)(2,1)} %pair_ref.1) | copy-start | bytes 6291460

commit v2 on v1

--- a/solution.py
+++ b/solution.py
@@ -11,7 +11,10 @@
 CODE_ROWS = 16
 STEPS = 256.0
 TOP = 32760.0
+PER = 2
+EARLY = 6
 VMEM = pl.BlockSpec(memory_space=pltpu.VMEM)
+HBM = pl.BlockSpec(memory_space=pltpu.HBM)
 SMEM = pl.BlockSpec(memory_space=pltpu.SMEM)
 
 
@@ -44,8 +47,15 @@
     return jnp.sum((member * table).reshape(CHUNKS, CHUNKS, LANES), axis=1).astype(jnp.int32)
 
 
-def select_kernel(shift, here_ref, index_ref, amp_ref, sent_ref, rank_ref):
-    index = index_ref[...]
+def widen(ref):
+    halves = [ref[pl.ds(k, CHUNKS, stride=2), :] for k in range(2)]
+    return jnp.concatenate(halves, 1)
+
+
+def select_kernel(shift, here_ref, index_ref, far_amp_ref, sent_ref, rank_ref, amp_ref, amp_sem):
+    fetch = pltpu.make_async_copy(far_amp_ref, amp_ref, amp_sem)
+    fetch.start()
+    index = widen(index_ref)
     here = here_ref[0]
     owner = jnp.right_shift(index, shift)
     member, within = count_before(owner)
@@ -67,6 +77,7 @@
     columns = (found[:DEPTH] * 64.0 + found[DEPTH:]).astype(jnp.int32)
     span = amp_ref.shape[1]
     lane = iota((DEPTH, span), 1)
+    fetch.wait()
     for k in range(0, CHUNKS, 4):
         chosen = jnp.concatenate(
             [
@@ -80,7 +91,7 @@
 
 
 def route_kernel(shift, here_ref, index_ref, rank_ref, forward_ref, settle_ref):
-    index, rank, here = index_ref[...], rank_ref[...], here_ref[0]
+    index, rank, here = widen(index_ref), rank_ref[...], here_ref[0]
     owner = jnp.right_shift(index, shift)
     middle, depth = rank & 15, jnp.right_shift(rank, 4)
     member, within = count_before(middle)
@@ -98,21 +109,54 @@
     settle_ref[...] = ones_where(iota((CHUNKS * DEPTH, LANES), 0) == wanted).astype(jnp.bfloat16)
 
 
-def ladder_kernel(amp_ref, int_ref, coded_ref):
+def forward_kernel(forward_ref, first_ref, after_ref, moved_ref):
+    del after_ref
+    arrived = first_ref[...].reshape(CHUNKS * DEPTH, first_ref.shape[2])
+    moved = bdot(forward_ref[...], arrived).astype(jnp.bfloat16)
+    moved_ref[...] = moved.reshape(moved_ref.shape)
+
+
+def settle_kernel(second_ref, settle_ref, after_ref, own_ref):
+    del after_ref
+    arrived = second_ref[...].reshape(CHUNKS * DEPTH, second_ref.shape[2])
+    own_ref[...] = bdot(arrived, settle_ref[...], ((0,), (0,))).astype(jnp.bfloat16)
+
+
+def ladder_kernel(start, count, amp_ref, int_ref, *refs):
+    coded_ref, held_ref, stage_ref, in_sems, out_sems = refs[-5:]
     height = amp_ref.shape[0]
-    for k in range(coded_ref.shape[0]):
-        part = jnp.dot(
-            amp_ref[...],
-            int_ref[:, k * LANES : (k + 1) * LANES],
-            preferred_element_type=jnp.float32,
+    width = PER * LANES
+    ins, outs = [], []
+    for b in range(count):
+        ins.append(
+            pltpu.make_async_copy(
+                int_ref.at[:, pl.ds((start + b) * width, width)], held_ref.at[b], in_sems.at[b]
+            )
         )
-        largest = jnp.max(jnp.abs(part), axis=0, keepdims=True)
-        code = jnp.ceil(jnp.log2(jnp.maximum(largest, 2.0**-120)) * STEPS) + 1.0
-        shrunk = part * jnp.exp2(code * (-1.0 / STEPS)) * TOP
-        coded_ref[k, :height, :] = jnp.round(shrunk).astype(jnp.int32).astype(jnp.int16)
-        coded_ref[k, height:, :] = jnp.broadcast_to(
-            code.astype(jnp.int32), (CODE_ROWS, LANES)
-        ).astype(jnp.int16)
+        ins[b].start()
+    for b in range(count):
+        ins[b].wait()
+        slab = jnp.dot(amp_ref[...], held_ref[b], preferred_element_type=jnp.float32)
+        for j in range(PER):
+            part = slab[:, j * LANES : (j + 1) * LANES]
+            largest = jnp.max(jnp.abs(part), axis=0, keepdims=True)
+            code = jnp.ceil(jnp.log2(jnp.maximum(largest, 2.0**-120)) * STEPS) + 1.0
+            shrunk = part * jnp.exp2(code * (-1.0 / STEPS)) * TOP
+            k = b * PER + j
+            stage_ref[k, :height, :] = jnp.round(shrunk).astype(jnp.int32).astype(jnp.int16)
+            stage_ref[k, height:, :] = jnp.broadcast_to(
+                code.astype(jnp.int32), (CODE_ROWS, LANES)
+            ).astype(jnp.int16)
+        outs.append(
+            pltpu.make_async_copy(
+                stage_ref.at[pl.ds(b * PER, PER)],
+                coded_ref.at[pl.ds((start + b) * PER, PER)],
+                out_sems.at[b],
+            )
+        )
+        outs[b].start()
+    for out in outs:
+        out.wait()
 
 
 def decode_kernel(coded_ref, sum_ref):
@@ -125,25 +169,33 @@
     sum_ref[...] = total * (1.0 / TOP)
 
 
-def finish_kernel(place_ref, pair_ref, ladder_ref, occ_ref, virt_ref, own_ref, far_ref, sib_ref, sibfar_ref, out_ref):
+def hole(place_ref, pair_ref, total, blocks):
     z, core = place_ref[0], place_ref[1]
-    rows = out_ref.shape[0]
-    half = rows // 2
-    total = ladder_ref[...]
-
-    def add(total, away, which, start, block):
+    rows = pair_ref.shape[0]
+    for away, other, start, ref in blocks:
+        which = 1 - core if other else core
         n = jnp.bitwise_and(z - away + 8, 7) * 2 + which
-        columns = pl.ds(pl.multiple_of(n * rows + start, 128), block.shape[0])
-        return total + jnp.dot(pair_ref[:, columns], block, preferred_element_type=jnp.float32)
-
-    for near, far, which in ((own_ref, far_ref, core), (sib_ref, sibfar_ref, 1 - core)):
-        for k, away in enumerate((0, 1, -1, 2, -2)):
-            total = add(total, away, which, 0, near[k * rows : (k + 1) * rows])
-        total = add(total, 3, which, 0, far[:rows])
-        total = add(total, -3, which, 0, far[rows : 2 * rows])
-        total = add(total, 4, which, 0, far[2 * rows : 2 * rows + half])
-        total = add(total, 4, which, half, far[2 * rows + half :])
-    out_ref[...] = total / (virt_ref[...] - occ_ref[...])
+        columns = pl.ds(pl.multiple_of(n * rows + start, 128), ref.shape[0])
+        total = total + jnp.dot(
+            pair_ref[:, columns], ref[...], preferred_element_type=jnp.float32
+        )
+    return total
+
+
+NEAR = (0, 1, -1, 2, -2)
+
+
+def near_kernel(place_ref, pair_ref, *refs):
+    blocks = [(NEAR[k % 5], k >= 5, 0, refs[k]) for k in range(10)]
+    refs[-1][...] = hole(place_ref, pair_ref, jnp.zeros(refs[-1].shape, jnp.float32), blocks)
+
+
+def finish_kernel(place_ref, pair_ref, ladder_ref, near_ref, occ_ref, virt_ref, *refs):
+    half = pair_ref.shape[0] // 2
+    kinds = ((3, 0), (-3, 0), (4, 0), (4, half))
+    blocks = [kinds[k % 4][:1] + (k >= 4,) + kinds[k % 4][1:] + (refs[k],) for k in range(8)]
+    total = hole(place_ref, pair_ref, ladder_ref[...] + near_ref[...], blocks)
+    refs[-1][...] = total / (virt_ref[...] - occ_ref[...])
 
 
 def on_device(amplitudes, integrals, pair_integrals, slab_index, occupied_energy, virtual_energy):
@@ -152,7 +204,7 @@
     height, span = amplitudes.shape
     shift = span.bit_length() - 1
     here = wide_index.astype(jnp.int32).reshape(1)
-    index = slab_index.reshape(CHUNKS, LANES)
+    index = slab_index.reshape(2 * CHUNKS, LANES // 2)
     half = height // 2
 
     def step(value, dz, dc=0):
@@ -167,9 +219,10 @@
             jax.ShapeDtypeStruct((CHUNKS, DEPTH, height), jnp.bfloat16),
             jax.ShapeDtypeStruct((CHUNKS, LANES), jnp.int32),
         ),
-        in_specs=[SMEM, VMEM, VMEM],
+        in_specs=[SMEM, VMEM, HBM],
         out_specs=(VMEM, VMEM),
-        compiler_params=pltpu.CompilerParams(vmem_limit_bytes=24 << 20),
+        scratch_shapes=[pltpu.VMEM((height, span), jnp.bfloat16), pltpu.SemaphoreType.DMA(())],
+        compiler_params=pltpu.CompilerParams(vmem_limit_bytes=59 << 20),
         cost_estimate=pl.CostEstimate(flops=2**30, bytes_accessed=2**21, transcendentals=0),
         name="select",
     )(here, index, amplitudes)
@@ -188,35 +241,63 @@
         name="route",
     )(here, index, rank)
 
-    per = 2
-    coded = pl.pallas_call(
-        ladder_kernel,
-        grid=(CHUNKS // per,),
-        out_shape=jax.ShapeDtypeStruct((CHUNKS, height + CODE_ROWS, LANES), jnp.int16),
-        in_specs=[
-            pl.BlockSpec((height, span), lambda i: (0, 0)),
-            pl.BlockSpec((span, per * LANES), lambda i: (0, i)),
-        ],
-        out_specs=pl.BlockSpec((per, height + CODE_ROWS, LANES), lambda i: (i, 0, 0)),
-        compiler_params=pltpu.CompilerParams(vmem_limit_bytes=24 << 20),
-        cost_estimate=pl.CostEstimate(
-            flops=2 * height * span * CHUNKS * LANES, bytes_accessed=20 * 2**20, transcendentals=0
-        ),
-        name="ladder",
-    )(amplitudes, integrals)
+    def ladder_part(start, count, extra, **kw):
+        return pl.pallas_call(
+            lambda *refs: ladder_kernel(start, count, *refs),
+            out_shape=jax.ShapeDtypeStruct((CHUNKS, height + CODE_ROWS, LANES), jnp.int16),
+            in_specs=[VMEM] + [HBM] * (1 + len(extra)),
+            out_specs=HBM,
+            scratch_shapes=[
+                pltpu.VMEM((count, span, PER * LANES), jnp.bfloat16),
+                pltpu.VMEM((count * PER, height + CODE_ROWS, LANES), jnp.int16),
+                pltpu.SemaphoreType.DMA((count,)),
+                pltpu.SemaphoreType.DMA((count,)),
+            ],
+            compiler_params=pltpu.CompilerParams(vmem_limit_bytes=50 << 20),
+            cost_estimate=pl.CostEstimate(
+                flops=2 * height * span * count * PER * LANES,
+                bytes_accessed=count * PER * 2**20,
+                transcendentals=0,
+            ),
+            **kw,
+        )(amplitudes, integrals, *extra)
+
+    slabs = CHUNKS // PER
+    early = ladder_part(0, EARLY, (rank,), name="ladder_early")
+
+    moved = pl.pallas_call(
+        forward_kernel,
+        out_shape=jax.ShapeDtypeStruct((CHUNKS, DEPTH, height), jnp.bfloat16),
+        in_specs=[VMEM, VMEM, HBM],
+        out_specs=VMEM,
+        compiler_params=pltpu.CompilerParams(vmem_limit_bytes=8 << 20),
+        cost_estimate=pl.CostEstimate(flops=2**27, bytes_accessed=2**20, transcendentals=0),
+        name="forward",
+    )(forward, first, early)
+    second = lax.all_to_all(moved, "wide", 0, 0, tiled=True)
+
+    coded = ladder_part(
+        EARLY, slabs - EARLY, (moved, early), input_output_aliases={3: 0}, name="ladder_late"
+    )
     shares = lax.all_to_all(coded, "wide", 0, 0, tiled=True)
 
-    moved = bdot(forward, first.reshape(CHUNKS * DEPTH, height)).astype(jnp.bfloat16)
-    second = lax.all_to_all(moved.reshape(CHUNKS, DEPTH, height), "wide", 0, 0, tiled=True)
-    own = bdot(second.reshape(CHUNKS * DEPTH, height), settle, ((0,), (0,))).astype(jnp.bfloat16)
+    own = pl.pallas_call(
+        settle_kernel,
+        out_shape=jax.ShapeDtypeStruct((height, LANES), jnp.bfloat16),
+        in_specs=[VMEM, VMEM, HBM],
+        out_specs=VMEM,
+        compiler_params=pltpu.CompilerParams(vmem_limit_bytes=8 << 20),
+        cost_estimate=pl.CostEstimate(flops=2**26, bytes_accessed=2**20, transcendentals=0),
+        name="settle",
+    )(second, settle, coded)
 
     up, down, up2, down2 = step(own, 1), step(own, -1), step(own, 2), step(own, -2)
-    near = jnp.concatenate([own, up, down, up2, down2], 0)
     up3, down3 = step(up2, 1), step(down2, -1)
     up4, down4 = step(up2[:half], 2), step(down2[half:], -2)
-    near_sibling = step(near, 0, 1)
-    far = jnp.concatenate([up3, down3, up4, down4], 0)
-    far_sibling = step(far, 0, 1)
+    near = [own, up, down, up2, down2]
+    far = [up3, down3, up4, down4]
+    near += [step(block, 0, 1) for block in near]
+    far += [step(block, 0, 1) for block in far]
 
     ladder = pl.pallas_call(
         decode_kernel,
@@ -228,25 +309,32 @@
         name="decode",
     )(shares)
 
-    where = jnp.stack([narrow_index // 2, narrow_index % 2]).astype(jnp.int32)
+    where = jnp.stack([narrow_index >> 1, narrow_index & 1]).astype(jnp.int32)
+    near_sum = pl.pallas_call(
+        near_kernel,
+        out_shape=jax.ShapeDtypeStruct((height, LANES), jnp.float32),
+        in_specs=[SMEM] + [VMEM] * 11,
+        out_specs=VMEM,
+        compiler_params=pltpu.CompilerParams(vmem_limit_bytes=16 << 20),
+        cost_estimate=pl.CostEstimate(flops=2**28, bytes_accessed=2**22, transcendentals=0),
+        name="near",
+    )(where, pair_integrals, *near)
     return pl.pallas_call(
         finish_kernel,
         out_shape=jax.ShapeDtypeStruct((height, LANES), jnp.float32),
-        in_specs=[SMEM] + [VMEM] * 8,
-        out_specs=VMEM,
-        compiler_params=pltpu.CompilerParams(vmem_limit_bytes=24 << 20),
-        cost_estimate=pl.CostEstimate(flops=2**29, bytes_accessed=2**22, transcendentals=0),
+        in_specs=[SMEM] + [VMEM] * 13,
+        out_specs=VMEM,
+        compiler_params=pltpu.CompilerParams(vmem_limit_bytes=16 << 20),
+        cost_estimate=pl.CostEstimate(flops=2**28, bytes_accessed=2**22, transcendentals=0),
         name="finish",
     )(
         where,
         pair_integrals,
         ladder,
+        near_sum,
         occupied_energy.reshape(height, 1),
         virtual_energy.reshape(1, LANES),
-        near,
-        far,
-        near_sibling,
-        far_sibling,
+        *far,
     )
 
 

time: 80.9 us -> 78.5 us (0.970)
  the two profiles are of different devices: /device:TPU:128 before, /device:TPU:1 now
where the time goes in v2:
time: 78.5 us; the launch traced here: 77.3 us
  starting transfers between devices  44.3 us (56%)
  Pallas kernels  21.6 us (28%)
  local copies, waits for them, and re-layouts  7.43 us (9%)
  waiting for transfers between devices  3.69 us (5%)
    ppermute x17, starting transfers between devices, step(): return lax.ppermute(value, 'narrow', ring)  26.3 us
    pallas_call x2, Pallas kernels, ladder_part(): pl.pallas_call(lambda *refs: ladder_kernel(start, count, *refs), out_shap...  11.2 us
    all_to_all x1, starting transfers between devices, on_device(): first = lax.all_to_all(sent, 'wide', 0, 0, tiled=True)  7.6 us
    unnamed x26, local copies, waits for them, and re-layouts  7.28 us
    all_to_all x1, starting transfers between devices, on_device(): second = lax.all_to_all(moved, 'wide', 0, 0, tiled=True)  6.65 us
    pallas_call x1, Pallas kernels, on_device(): pl.pallas_call(lambda *refs: select_kernel(shift, *refs), out_shape=(jax....  4.34 us
    all_to_all x1, starting transfers between devices, on_device(): shares = lax.all_to_all(coded, 'wide', 0, 0, tiled=True)  3.72 us
    all_to_all x1, waiting for transfers between devices, on_device(): second = lax.all_to_all(moved, 'wide', 0, 0, tiled=True)  3.37 us
  transfers between devices with their start and end apart: 20, of which 2 were waited for; matrix products, arithmetic and copies ran while one was open for 0% of the time, Pallas kernels for 18%

profile of v2, /device:TPU:1, one launch (start us, length us, event | category | flops | bytes accessed | tf_op | source)
XLA Modules:
  0.0 77.3 jit_solution(9416116872099833242)
XLA Ops:
  0.0 4.3 %select.1 = (bf16[16,32,256]{2,1,0:T(8,128)(2,1)}, s32[16,256]{1,0:T(8,128)}) custom-call(s32[1]{0:T(128)} %bitcast.2.refs_0_, s32[32,128]{1,0:T(8,128)} %bitcast.7, bf16[256,2048]{1,0:T(8,128)(2,1)} %refs_0_.3), custom_call_target="tpu_custom_call" | custom-call | flops 1073741824 | bytes 2097152 | tf_op jit(solution)/shard_map/select/pallas_call | solution.py:216
  4.4 7.6 %all-to-all-start = ((bf16[16,32,256]{2,1,0:T(8,128)(2,1)}), bf16[16,32,256]{2,1,0:T(8,128)(2,1)S(1)}, u32[]{:S(2)}, u32[]{:S(2)}) async-start(bf16[16,32,256]{2,1,0:T(8,128)(2,1)} %get-tuple-element.11), calls=%async_computation | async-start | bytes 524288 | tf_op jit(solution)/shard_map/all_to_all | solution.py:229
  13.2 7.3 %ladder_early.1.after_ref.refs_3_ = s16[16,272,256]{2,1,0:T(8,128)(2,1)} custom-call(bf16[256,2048]{1,0:T(8,128)(2,1)S(1)} %copy-done.2, bf16[2048,4096]{1,0:T(8,128)(2,1)} %refs_1_.3, s32[16,256]{1,0:T(8,128)S(1)} %copy-done.9), custom_call_target="tpu_custom_call" | custom-call | flops 3221225472 | bytes 12582912 | tf_op jit(solution)/shard_map/ladder_early/pallas_call | solution.py:245
  20.5 1.0 %forward.1.refs_2_ = bf16[16,32,256]{2,1,0:T(8,128)(2,1)} custom-call(bf16[512,512]{1,0:T(8,128)(2,1)S(1)} %get-tuple-element.10.forward_ref, bf16[16,32,256]{2,1,0:T(8,128)(2,1)S(1)} %all-to-all-done.first_ref, s16[16,272,256]{2,1,0:T(8,128)(2,1)} %ladder_early.1.after_ref.refs_3_), custom_call_target="tpu_custom_call" | custom-call | flops 134217728 | bytes 1048576 | tf_op jit(solution)/shard_map/forward/pallas_call | solution.py:268
  21.5 6.7 %all-to-all-start.2 = ((bf16[16,32,256]{2,1,0:T(8,128)(2,1)}), bf16[16,32,256]{2,1,0:T(8,128)(2,1)S(1)}, u32[]{:S(2)}, u32[]{:S(2)}) async-start(bf16[16,32,256]{2,1,0:T(8,128)(2,1)} %forward.1.refs_2_), calls=%async_computation.2 | async-start | bytes 524288 | tf_op jit(solution)/shard_map/all_to_all | solution.py:277
  28.1 3.9 %ladder_late.1.after_ref = s16[16,272,256]{2,1,0:T(8,128)(2,1)} custom-call(bf16[256,2048]{1,0:T(8,128)(2,1)S(1)} %copy-done.2, bf16[2048,4096]{1,0:T(8,128)(2,1)} %refs_1_.3, bf16[16,32,256]{2,1,0:T(8,128)(2,1)} %forward.1.refs_2_, s16[16,272,256]{2,1,0:T(8,128)(2,1)} %ladder_early.1.after_ref.refs_3_), custom_call_target="tpu_custom_call", output_to_operand_aliasing={{}: (3, {})} | custom-call | flops 1073741824 | bytes 4194304 | tf_op jit(solution)/shard_map/ladder_late/pallas_call | solution.py:245
  32.1 3.4 %all-to-all-done.2.second_ref = bf16[16,32,256]{2,1,0:T(8,128)(2,1)S(1)} async-done(((bf16[16,32,256]{2,1,0:T(8,128)(2,1)}), bf16[16,32,256]{2,1,0:T(8,128)(2,1)S(1)}, u32[]{:S(2)}, u32[]{:S(2)}) %all-to-all-start.2) | async-done | bytes 262176 | tf_op jit(solution)/shard_map/all_to_all | solution.py:277
  35.5 3.7 %all-to-all-start.1 = ((s16[16,272,256]{2,1,0:T(8,128)(2,1)}), s16[16,272,256]{2,1,0:T(8,128)(2,1)S(1)}, u32[]{:S(2)}, u32[]{:S(2)}) async-start(s16[16,272,256]{2,1,0:T(8,128)(2,1)} %ladder_late.1.after_ref), calls=%async_computation.1 | async-start | bytes 4456448 | tf_op jit(solution)/shard_map/all_to_all | solution.py:282
  39.5 3.1 %collective-permute-start.2 = (bf16[256,256]{1,0:T(8,128)(2,1)S(1)}, bf16[256,256]{1,0:T(8,128)(2,1)S(1)}, u32[]{:S(2)}, u32[]{:S(2)}) collective-permute-start(bf16[256,256]{1,0:T(8,128)(2,1)S(1)} %settle.1.refs_0_), channel_id=1, source_target_pairs={{0,4},{1,5},{2,6},{3,7},{4,8},{5,9},{6,10},{7,11},{8,12},{9,13},{1... | collective-permute-start | bytes 393224 | tf_op jit(solution)/shard_map/ppermute | solution.py:214
  42.5 3.1 %collective-permute-start.3 = (bf16[256,256]{1,0:T(8,128)(2,1)S(1)}, bf16[256,256]{1,0:T(8,128)(2,1)S(1)}, u32[]{:S(2)}, u32[]{:S(2)}) collective-permute-start(bf16[256,256]{1,0:T(8,128)(2,1)S(1)} %settle.1.refs_0_), channel_id=1, source_target_pairs={{0,12},{1,13},{2,14},{3,15},{4,0},{5,1},{6,2},{7,3},{8,4},{9,5},{1... | collective-permute-start | bytes 393224 | tf_op jit(solution)/shard_map/ppermute | solution.py:214
  45.7 0.7 collective-permute-start
  46.4 1.9 %collective-permute-start.1 = (bf16[256,256]{1,0:T(8,128)(2,1)S(1)}, bf16[256,256]{1,0:T(8,128)(2,1)S(1)}, u32[]{:S(2)}, u32[]{:S(2)}) collective-permute-start(bf16[256,256]{1,0:T(8,128)(2,1)S(1)} %settle.1.refs_0_), channel_id=1, source_target_pairs={{0,14},{1,15},{2,0},{3,1},{4,2},{5,3},{6,4},{7,5},{8,6},{9,7},{10,... | collective-permute-start | bytes 393224 | tf_op jit(solution)/shard_map/ppermute | solution.py:214
  48.3 3.5 %collective-permute-start.4 = (bf16[256,256]{1,0:T(8,128)(2,1)S(1)}, bf16[256,256]{1,0:T(8,128)(2,1)S(1)}, u32[]{:S(2)}, u32[]{:S(2)}) collective-permute-start(bf16[256,256]{1,0:T(8,128)(2,1)S(1)} %settle.1.refs_0_), channel_id=1, source_target_pairs={{0,1},{1,0},{2,3},{3,2},{4,5},{5,4},{6,7},{7,6},{8,9},{9,8},{10,11... | collective-permute-start | bytes 393224 | tf_op jit(solution)/shard_map/ppermute | solution.py:214
  52.0 3.8 %collective-permute-start.12 = (bf16[128,256]{1,0:T(8,128)(2,1)S(1)}, bf16[128,256]{1,0:T(8,128)(2,1)}, u32[]{:S(2)}, u32[]{:S(2)}) collective-permute-start(bf16[128,256]{1,0:T(8,128)(2,1)S(1)} %slice.9), channel_id=1, source_target_pairs={{0,12},{1,13},{2,14},{3,15},{4,0},{5,1},{6,2},{7,3},{8,4},{9,5},{1... | collective-permute-start | bytes 196616 | tf_op jit(solution)/shard_map/ppermute | solution.py:214
  55.8 2.8 %collective-permute-start.5 = (bf16[256,256]{1,0:T(8,128)(2,1)S(1)}, bf16[256,256]{1,0:T(8,128)(2,1)S(1)}, u32[]{:S(2)}, u32[]{:S(2)}) collective-permute-start(bf16[256,256]{1,0:T(8,128)(2,1)S(1)} %collective-permute-done.refs_1_), channel_id=1, source_target_pairs={{0,1},{1,0},{2,3},{3,2},{4,5},{5,4},{6,7},{7,6},{8,9},{9,8},{10,11... | collective-permute-start | bytes 393224 | tf_op jit(solution)/shard_map/ppermute | solution.py:214
  59.7 2.1 %collective-permute-start.10 = (bf16[256,256]{1,0:T(8,128)(2,1)S(1)}, bf16[256,256]{1,0:T(8,128)(2,1)}, u32[]{:S(2)}, u32[]{:S(2)}) collective-permute-start(bf16[256,256]{1,0:T(8,128)(2,1)S(1)} %collective-permute-done.3.refs_4_), channel_id=1, source_target_pairs={{0,14},{1,15},{2,0},{3,1},{4,2},{5,3},{6,4},{7,5},{8,6},{9,7},{10,... | collective-permute-start | bytes 393224 | tf_op jit(solution)/shard_map/ppermute | solution.py:214
  62.5 3.1 %collective-permute-start.8 = (bf16[256,256]{1,0:T(8,128)(2,1)S(1)}, bf16[256,256]{1,0:T(8,128)(2,1)}, u32[]{:S(2)}, u32[]{:S(2)}) collective-permute-start(bf16[256,256]{1,0:T(8,128)(2,1)S(1)} %collective-permute-done.3.refs_4_), channel_id=1, source_target_pairs={{0,1},{1,0},{2,3},{3,2},{4,5},{5,4},{6,7},{7,6},{8,9},{9,8},{10,11... | collective-permute-start | bytes 393224 | tf_op jit(solution)/shard_map/ppermute | solution.py:214
  67.7 1.6 %copy-done = bf16[256,4096]{1,0:T(8,128)(2,1)S(1)} copy-done((bf16[256,4096]{1,0:T(8,128)(2,1)S(1)}, bf16[256,4096]{1,0:T(8,128)(2,1)}, u32[]{:S(2)}) %copy-start) | copy-done | bytes 2097176
  69.3 0.9 %copy-done.4 = bf16[256,256]{1,0:T(8,128)(2,1)S(1)} copy-done((bf16[256,256]{1,0:T(8,128)(2,1)S(1)}, bf16[256,256]{1,0:T(8,128)(2,1)}, u32[]{:S(2)}) %copy-start.4) | copy-done | bytes 131096
  70.2 0.9 %copy-done.6 = bf16[256,256]{1,0:T(8,128)(2,1)S(1)} copy-done((bf16[256,256]{1,0:T(8,128)(2,1)S(1)}, bf16[256,256]{1,0:T(8,128)(2,1)}, u32[]{:S(2)}) %copy-start.6) | copy-done | bytes 131096
  71.1 0.9 %copy-done.8 = bf16[256,256]{1,0:T(8,128)(2,1)S(1)} copy-done((bf16[256,256]{1,0:T(8,128)(2,1)S(1)}, bf16[256,256]{1,0:T(8,128)(2,1)}, u32[]{:S(2)}) %copy-start.8) | copy-done | bytes 131096
  72.0 1.4 %near.1.near_ref = f32[256,256]{1,0:T(8,128)S(1)} custom-call(s32[2]{0:T(128)S(1)} %pad_add_fusion.place_ref, bf16[256,4096]{1,0:T(8,128)(2,1)S(1)} %copy-done, bf16[256,256]{1,0:T(8,128)(2,1)S(1)} %settle.1.refs_0_, bf16[256,256]{1,0:T(8,128)(2,1)S(1)} %collective-permute-done.refs_1_, bf16[256,256]{1,0:T(8,128)(2,1)S(1)} %collective-permute-done.1.refs_2_, ...), custom_call_target="tpu_custom_call" | custom-call | flops 268435456 | bytes 4194304 | tf_op jit(solution)/shard_map/near/pallas_call | solution.py:313
  74.1 1.0 %copy-done.1 = bf16[256,4096]{1,0:T(8,128)(2,1)S(1)} copy-done((bf16[256,4096]{1,0:T(8,128)(2,1)S(1)}, bf16[256,4096]{1,0:T(8,128)(2,1)}, u32[]{:S(2)}) %copy-start.1) | copy-done | bytes 2097176
  75.1 2.3 %finish.1 = f32[256,256]{1,0:T(8,128)} custom-call(s32[2]{0:T(128)S(1)} %pad_add_fusion.place_ref, bf16[256,4096]{1,0:T(8,128)(2,1)S(1)} %copy-done.1, f32[256,256]{1,0:T(8,128)S(1)} %decode.1.ladder_ref, f32[256,256]{1,0:T(8,128)S(1)} %near.1.near_ref, f32[256,1]{1,0:T(8,128)S(1)} %copy.8.occ_ref, f32[1,256]{1,0:T(1,128)S(1)} %bitcast.6, ...), custom_call_target="tpu_custom_call" | custom-call | flops 268435456 | bytes 4194304 | tf_op jit(solution)/shard_map/finish/pallas_call | solution.py:322
  (55 shorter events, 6.0 us)
Async XLA Ops:
  0.0 12.0 %copy-start.11 = (s32[4096]{0:T(1024)S(1)}, s32[4096]{0:T(1024)}, u32[]{:S(2)}) copy-start(s32[4096]{0:T(1024)} %param.9) | copy-start | bytes 49156
  0.0 13.2 %copy-start.2 = (bf16[256,2048]{1,0:T(8,128)(2,1)S(1)}, bf16[256,2048]{1,0:T(8,128)(2,1)}, u32[]{:S(2)}) copy-start(bf16[256,2048]{1,0:T(8,128)(2,1)} %refs_0_.3) | copy-start | bytes 3145732
  4.4 16.1 %all-to-all-start = ((bf16[16,32,256]{2,1,0:T(8,128)(2,1)}), bf16[16,32,256]{2,1,0:T(8,128)(2,1)S(1)}, u32[]{:S(2)}, u32[]{:S(2)}) async-start(bf16[16,32,256]{2,1,0:T(8,128)(2,1)} %get-tuple-element.11), calls=%async_computation | async-start | bytes 524288 | tf_op jit(solution)/shard_map/all_to_all | solution.py:229
  21.5 14.0 %all-to-all-start.2 = ((bf16[16,32,256]{2,1,0:T(8,128)(2,1)}), bf16[16,32,256]{2,1,0:T(8,128)(2,1)S(1)}, u32[]{:S(2)}, u32[]{:S(2)}) async-start(bf16[16,32,256]{2,1,0:T(8,128)(2,1)} %forward.1.refs_2_), calls=%async_computation.2 | async-start | bytes 524288 | tf_op jit(solution)/shard_map/all_to_all | solution.py:277
  35.5 38.0 %all-to-all-start.1 = ((s16[16,272,256]{2,1,0:T(8,128)(2,1)}), s16[16,272,256]{2,1,0:T(8,128)(2,1)S(1)}, u32[]{:S(2)}, u32[]{:S(2)}) async-start(s16[16,272,256]{2,1,0:T(8,128)(2,1)} %ladder_late.1.after_ref), calls=%async_computation.1 | async-start | bytes 4456448 | tf_op jit(solution)/shard_map/all_to_all | solution.py:282
  39.2 28.4 %copy-start.12 = (f32[256]{0:T(256)S(1)}, f32[256]{0:T(256)}, u32[]{:S(2)}) copy-start(f32[256]{0:T(256)} %param.10) | copy-start | bytes 3076
  39.5 12.4 %collective-permute-start.2 = (bf16[256,256]{1,0:T(8,128)(2,1)S(1)}, bf16[256,256]{1,0:T(8,128)(2,1)S(1)}, u32[]{:S(2)}, u32[]{:S(2)}) collective-permute-start(bf16[256,256]{1,0:T(8,128)(2,1)S(1)} %settle.1.refs_0_), channel_id=1, source_target_pairs={{0,4},{1,5},{2,6},{3,7},{4,8},{5,9},{6,10},{7,11},{8,12},{9,13},{1... | collective-permute-start | bytes 393224 | tf_op jit(solution)/shard_map/ppermute | solution.py:214
  42.5 9.4 %collective-permute-start.3 = (bf16[256,256]{1,0:T(8,128)(2,1)S(1)}, bf16[256,256]{1,0:T(8,128)(2,1)S(1)}, u32[]{:S(2)}, u32[]{:S(2)}) collective-permute-start(bf16[256,256]{1,0:T(8,128)(2,1)S(1)} %settle.1.refs_0_), channel_id=1, source_target_pairs={{0,12},{1,13},{2,14},{3,15},{4,0},{5,1},{6,2},{7,3},{8,4},{9,5},{1... | collective-permute-start | bytes 393224 | tf_op jit(solution)/shard_map/ppermute | solution.py:214
  45.7 10.2 %collective-permute-start = (bf16[256,256]{1,0:T(8,128)(2,1)S(1)}, bf16[256,256]{1,0:T(8,128)(2,1)S(1)}, u32[]{:S(2)}, u32[]{:S(2)}) collective-permute-start(bf16[256,256]{1,0:T(8,128)(2,1)S(1)} %settle.1.refs_0_), channel_id=1, source_target_pairs={{0,2},{1,3},{2,4},{3,5},{4,6},{5,7},{6,8},{7,9},{8,10},{9,11},{10,... | collective-permute-start | bytes 393224 | tf_op jit(solution)/shard_map/ppermute | solution.py:214
  46.4 12.3 %collective-permute-start.1 = (bf16[256,256]{1,0:T(8,128)(2,1)S(1)}, bf16[256,256]{1,0:T(8,128)(2,1)S(1)}, u32[]{:S(2)}, u32[]{:S(2)}) collective-permute-start(bf16[256,256]{1,0:T(8,128)(2,1)S(1)} %settle.1.refs_0_), channel_id=1, source_target_pairs={{0,14},{1,15},{2,0},{3,1},{4,2},{5,3},{6,4},{7,5},{8,6},{9,7},{10,... | collective-permute-start | bytes 393224 | tf_op jit(solution)/shard_map/ppermute | solution.py:214
  48.3 10.4 %collective-permute-start.4 = (bf16[256,256]{1,0:T(8,128)(2,1)S(1)}, bf16[256,256]{1,0:T(8,128)(2,1)S(1)}, u32[]{:S(2)}, u32[]{:S(2)}) collective-permute-start(bf16[256,256]{1,0:T(8,128)(2,1)S(1)} %settle.1.refs_0_), channel_id=1, source_target_pairs={{0,1},{1,0},{2,3},{3,2},{4,5},{5,4},{6,7},{7,6},{8,9},{9,8},{10,11... | collective-permute-start | bytes 393224 | tf_op jit(solution)/shard_map/ppermute | solution.py:214
  51.9 7.3 %collective-permute-start.11 = (bf16[128,256]{1,0:T(8,128)(2,1)S(1)}, bf16[128,256]{1,0:T(8,128)(2,1)}, u32[]{:S(2)}, u32[]{:S(2)}) collective-permute-start(bf16[128,256]{1,0:T(8,128)(2,1)S(1)} %slice.8), channel_id=1, source_target_pairs={{0,4},{1,5},{2,6},{3,7},{4,8},{5,9},{6,10},{7,11},{8,12},{9,13},{1... | collective-permute-start | bytes 196616 | tf_op jit(solution)/shard_map/ppermute | solution.py:214
  52.0 7.7 %collective-permute-start.12 = (bf16[128,256]{1,0:T(8,128)(2,1)S(1)}, bf16[128,256]{1,0:T(8,128)(2,1)}, u32[]{:S(2)}, u32[]{:S(2)}) collective-permute-start(bf16[128,256]{1,0:T(8,128)(2,1)S(1)} %slice.9), channel_id=1, source_target_pairs={{0,12},{1,13},{2,14},{3,15},{4,0},{5,1},{6,2},{7,3},{8,4},{9,5},{1... | collective-permute-start | bytes 196616 | tf_op jit(solution)/shard_map/ppermute | solution.py:214
  55.8 6.0 %collective-permute-start.5 = (bf16[256,256]{1,0:T(8,128)(2,1)S(1)}, bf16[256,256]{1,0:T(8,128)(2,1)S(1)}, u32[]{:S(2)}, u32[]{:S(2)}) collective-permute-start(bf16[256,256]{1,0:T(8,128)(2,1)S(1)} %collective-permute-done.refs_1_), channel_id=1, source_target_pairs={{0,1},{1,0},{2,3},{3,2},{4,5},{5,4},{6,7},{7,6},{8,9},{9,8},{10,11... | collective-permute-start | bytes 393224 | tf_op jit(solution)/shard_map/ppermute | solution.py:214
  58.7 6.9 %collective-permute-start.6 = (bf16[256,256]{1,0:T(8,128)(2,1)S(1)}, bf16[256,256]{1,0:T(8,128)(2,1)S(1)}, u32[]{:S(2)}, u32[]{:S(2)}) collective-permute-start(bf16[256,256]{1,0:T(8,128)(2,1)S(1)} %collective-permute-done.1.refs_2_), channel_id=1, source_target_pairs={{0,1},{1,0},{2,3},{3,2},{4,5},{5,4},{6,7},{7,6},{8,9},{9,8},{10,11... | collective-permute-start | bytes 393224 | tf_op jit(solution)/shard_map/ppermute | solution.py:214
  58.8 6.9 %collective-permute-start.7 = (bf16[256,256]{1,0:T(8,128)(2,1)S(1)}, bf16[256,256]{1,0:T(8,128)(2,1)S(1)}, u32[]{:S(2)}, u32[]{:S(2)}) collective-permute-start(bf16[256,256]{1,0:T(8,128)(2,1)S(1)} %collective-permute-done.2.refs_3_), channel_id=1, source_target_pairs={{0,1},{1,0},{2,3},{3,2},{4,5},{5,4},{6,7},{7,6},{8,9},{9,8},{10,11... | collective-permute-start | bytes 393224 | tf_op jit(solution)/shard_map/ppermute | solution.py:214
  59.2 7.6 %collective-permute-start.9 = (bf16[256,256]{1,0:T(8,128)(2,1)S(1)}, bf16[256,256]{1,0:T(8,128)(2,1)S(1)}, u32[]{:S(2)}, u32[]{:S(2)}) collective-permute-start(bf16[256,256]{1,0:T(8,128)(2,1)S(1)} %collective-permute-done.2.refs_3_), channel_id=1, source_target_pairs={{0,2},{1,3},{2,4},{3,5},{4,6},{5,7},{6,8},{7,9},{8,10},{9,11},{10,... | collective-permute-start | bytes 393224 | tf_op jit(solution)/shard_map/ppermute | solution.py:214
  59.7 7.6 %collective-permute-start.10 = (bf16[256,256]{1,0:T(8,128)(2,1)S(1)}, bf16[256,256]{1,0:T(8,128)(2,1)}, u32[]{:S(2)}, u32[]{:S(2)}) collective-permute-start(bf16[256,256]{1,0:T(8,128)(2,1)S(1)} %collective-permute-done.3.refs_4_), channel_id=1, source_target_pairs={{0,14},{1,15},{2,0},{3,1},{4,2},{5,3},{6,4},{7,5},{8,6},{9,7},{10,... | collective-permute-start | bytes 393224 | tf_op jit(solution)/shard_map/ppermute | solution.py:214
  62.5 5.2 %collective-permute-start.8 = (bf16[256,256]{1,0:T(8,128)(2,1)S(1)}, bf16[256,256]{1,0:T(8,128)(2,1)}, u32[]{:S(2)}, u32[]{:S(2)}) collective-permute-start(bf16[256,256]{1,0:T(8,128)(2,1)S(1)} %collective-permute-done.3.refs_4_), channel_id=1, source_target_pairs={{0,1},{1,0},{2,3},{3,2},{4,5},{5,4},{6,7},{7,6},{8,9},{9,8},{10,11... | collective-permute-start | bytes 393224 | tf_op jit(solution)/shard_map/ppermute | solution.py:214
  65.6 8.5 %collective-permute-start.15 = (bf16[128,256]{1,0:T(8,128)(2,1)}, bf16[128,256]{1,0:T(8,128)(2,1)}, u32[]{:S(2)}, u32[]{:S(2)}) collective-permute-start(bf16[128,256]{1,0:T(8,128)(2,1)} %collective-permute-done.11.refs_2_), channel_id=1, source_target_pairs={{0,1},{1,0},{2,3},{3,2},{4,5},{5,4},{6,7},{7,6},{8,9},{9,8},{10,11... | collective-permute-start | bytes 196616 | tf_op jit(solution)/shard_map/ppermute | solution.py:214
  66.3 7.7 %collective-permute-start.16 = (bf16[128,256]{1,0:T(8,128)(2,1)}, bf16[128,256]{1,0:T(8,128)(2,1)}, u32[]{:S(2)}, u32[]{:S(2)}) collective-permute-start(bf16[128,256]{1,0:T(8,128)(2,1)} %collective-permute-done.12.refs_3_), channel_id=1, source_target_pairs={{0,1},{1,0},{2,3},{3,2},{4,5},{5,4},{6,7},{7,6},{8,9},{9,8},{10,11... | collective-permute-start | bytes 196616 | tf_op jit(solution)/shard_map/ppermute | solution.py:214
  66.8 7.3 %collective-permute-start.13 = (bf16[256,256]{1,0:T(8,128)(2,1)S(1)}, bf16[256,256]{1,0:T(8,128)(2,1)}, u32[]{:S(2)}, u32[]{:S(2)}) collective-permute-start(bf16[256,256]{1,0:T(8,128)(2,1)S(1)} %collective-permute-done.9.refs_0_), channel_id=1, source_target_pairs={{0,1},{1,0},{2,3},{3,2},{4,5},{5,4},{6,7},{7,6},{8,9},{9,8},{10,11... | collective-permute-start | bytes 393224 | tf_op jit(solution)/shard_map/ppermute | solution.py:214
  67.4 6.7 %collective-permute-start.14 = (bf16[256,256]{1,0:T(8,128)(2,1)}, bf16[256,256]{1,0:T(8,128)(2,1)}, u32[]{:S(2)}, u32[]{:S(2)}) collective-permute-start(bf16[256,256]{1,0:T(8,128)(2,1)} %collective-permute-done.10.refs_1_), channel_id=1, source_target_pairs={{0,1},{1,0},{2,3},{3,2},{4,5},{5,4},{6,7},{7,6},{8,9},{9,8},{10,11... | collective-permute-start | bytes 393224 | tf_op jit(solution)/shard_map/ppermute | solution.py:214
  72.0 2.1 %copy-start.10 = (f32[256]{0:T(256)S(1)}, f32[256]{0:T(256)}, u32[]{:S(2)}) copy-start(f32[256]{0:T(256)} %param.11) | copy-start | bytes 3076
  (9 other events, 10.0 us)

commit v3 on v2

--- a/solution.py
+++ b/solution.py
@@ -12,7 +12,7 @@
 STEPS = 256.0
 TOP = 32760.0
 PER = 2
-EARLY = 6
+EARLY = 5
 VMEM = pl.BlockSpec(memory_space=pltpu.VMEM)
 HBM = pl.BlockSpec(memory_space=pltpu.HBM)
 SMEM = pl.BlockSpec(memory_space=pltpu.SMEM)
@@ -159,43 +159,42 @@
         out.wait()
 
 
-def decode_kernel(coded_ref, sum_ref):
-    height = sum_ref.shape[0]
-    total = jnp.zeros(sum_ref.shape, jnp.float32)
+def finish_kernel(
+    place_ref, far_pair_ref, far_coded_ref, occ_ref, virt_ref, near_ref, far_ref, *refs
+):
+    near_sibling_ref, far_sibling_ref, out_ref, pair_ref, coded_ref, sems = refs
+    fetches = [
+        pltpu.make_async_copy(far_pair_ref, pair_ref, sems.at[0]),
+        pltpu.make_async_copy(far_coded_ref, coded_ref, sems.at[1]),
+    ]
+    for fetch in fetches:
+        fetch.start()
+    z, core = place_ref[0], place_ref[1]
+    rows = out_ref.shape[0]
+    half = rows // 2
+    fetches[0].wait()
+    total = jnp.zeros(out_ref.shape, jnp.float32)
+
+    def add(total, away, which, start, block):
+        n = jnp.bitwise_and(z - away + 8, 7) * 2 + which
+        columns = pl.ds(pl.multiple_of(n * rows + start, 128), block.shape[0])
+        return total + jnp.dot(pair_ref[:, columns], block, preferred_element_type=jnp.float32)
+
+    sides = ((near_ref, far_ref, core), (near_sibling_ref, far_sibling_ref, 1 - core))
+    for near, far, which in sides:
+        for k, away in enumerate((0, 1, -1, 2, -2)):
+            total = add(total, away, which, 0, near[k * rows : (k + 1) * rows])
+        total = add(total, 3, which, 0, far[:rows])
+        total = add(total, -3, which, 0, far[rows : 2 * rows])
+        total = add(total, 4, which, 0, far[2 * rows : 2 * rows + half])
+        total = add(total, 4, which, half, far[2 * rows + half :])
+    fetches[1].wait()
+    ladder = jnp.zeros(out_ref.shape, jnp.float32)
     for k in range(CHUNKS):
-        code = coded_ref[k, height:, :].astype(jnp.int32).astype(jnp.float32)[:1, :]
-        values = coded_ref[k, :height, :].astype(jnp.int32).astype(jnp.float32)
-        total = total + values * jnp.exp2(code * (1.0 / STEPS))
-    sum_ref[...] = total * (1.0 / TOP)
-
-
-def hole(place_ref, pair_ref, total, blocks):
-    z, core = place_ref[0], place_ref[1]
-    rows = pair_ref.shape[0]
-    for away, other, start, ref in blocks:
-        which = 1 - core if other else core
-        n = jnp.bitwise_and(z - away + 8, 7) * 2 + which
-        columns = pl.ds(pl.multiple_of(n * rows + start, 128), ref.shape[0])
-        total = total + jnp.dot(
-            pair_ref[:, columns], ref[...], preferred_element_type=jnp.float32
-        )
-    return total
-
-
-NEAR = (0, 1, -1, 2, -2)
-
-
-def near_kernel(place_ref, pair_ref, *refs):
-    blocks = [(NEAR[k % 5], k >= 5, 0, refs[k]) for k in range(10)]
-    refs[-1][...] = hole(place_ref, pair_ref, jnp.zeros(refs[-1].shape, jnp.float32), blocks)
-
-
-def finish_kernel(place_ref, pair_ref, ladder_ref, near_ref, occ_ref, virt_ref, *refs):
-    half = pair_ref.shape[0] // 2
-    kinds = ((3, 0), (-3, 0), (4, 0), (4, half))
-    blocks = [kinds[k % 4][:1] + (k >= 4,) + kinds[k % 4][1:] + (refs[k],) for k in range(8)]
-    total = hole(place_ref, pair_ref, ladder_ref[...] + near_ref[...], blocks)
-    refs[-1][...] = total / (virt_ref[...] - occ_ref[...])
+        code = coded_ref[k, rows:, :].astype(jnp.int32).astype(jnp.float32)[:1, :]
+        values = coded_ref[k, :rows, :].astype(jnp.int32).astype(jnp.float32)
+        ladder = ladder + values * jnp.exp2(code * (1.0 / STEPS))
+    out_ref[...] = (ladder * (1.0 / TOP) + total) / (virt_ref[...] - occ_ref[...])
 
 
 def on_device(amplitudes, integrals, pair_integrals, slab_index, occupied_energy, virtual_energy):
@@ -294,47 +293,35 @@
     up, down, up2, down2 = step(own, 1), step(own, -1), step(own, 2), step(own, -2)
     up3, down3 = step(up2, 1), step(down2, -1)
     up4, down4 = step(up2[:half], 2), step(down2[half:], -2)
-    near = [own, up, down, up2, down2]
-    far = [up3, down3, up4, down4]
-    near += [step(block, 0, 1) for block in near]
-    far += [step(block, 0, 1) for block in far]
-
-    ladder = pl.pallas_call(
-        decode_kernel,
-        out_shape=jax.ShapeDtypeStruct((height, LANES), jnp.float32),
-        in_specs=[VMEM],
-        out_specs=VMEM,
-        compiler_params=pltpu.CompilerParams(vmem_limit_bytes=16 << 20),
-        cost_estimate=pl.CostEstimate(flops=2**22, bytes_accessed=5 * 2**19, transcendentals=0),
-        name="decode",
-    )(shares)
+    near = jnp.concatenate([own, up, down, up2, down2], 0)
+    near_sibling = step(near, 0, 1)
+    far = jnp.concatenate([up3, down3, up4, down4], 0)
+    far_sibling = step(far, 0, 1)
 
     where = jnp.stack([narrow_index >> 1, narrow_index & 1]).astype(jnp.int32)
-    near_sum = pl.pallas_call(
-        near_kernel,
-        out_shape=jax.ShapeDtypeStruct((height, LANES), jnp.float32),
-        in_specs=[SMEM] + [VMEM] * 11,
-        out_specs=VMEM,
-        compiler_params=pltpu.CompilerParams(vmem_limit_bytes=16 << 20),
-        cost_estimate=pl.CostEstimate(flops=2**28, bytes_accessed=2**22, transcendentals=0),
-        name="near",
-    )(where, pair_integrals, *near)
     return pl.pallas_call(
         finish_kernel,
         out_shape=jax.ShapeDtypeStruct((height, LANES), jnp.float32),
-        in_specs=[SMEM] + [VMEM] * 13,
+        in_specs=[SMEM, HBM, HBM] + [VMEM] * 6,
         out_specs=VMEM,
-        compiler_params=pltpu.CompilerParams(vmem_limit_bytes=16 << 20),
-        cost_estimate=pl.CostEstimate(flops=2**28, bytes_accessed=2**22, transcendentals=0),
+        scratch_shapes=[
+            pltpu.VMEM(pair_integrals.shape, jnp.bfloat16),
+            pltpu.VMEM(shares.shape, jnp.int16),
+            pltpu.SemaphoreType.DMA((2,)),
+        ],
+        compiler_params=pltpu.CompilerParams(vmem_limit_bytes=50 << 20),
+        cost_estimate=pl.CostEstimate(flops=2**30, bytes_accessed=2**23, transcendentals=0),
         name="finish",
     )(
         where,
         pair_integrals,
-        ladder,
-        near_sum,
+        shares,
         occupied_energy.reshape(height, 1),
         virtual_energy.reshape(1, LANES),
-        *far,
+        near,
+        far,
+        near_sibling,
+        far_sibling,
     )
 
 

time: 78.5 us -> 75.9 us (0.967)
  the two profiles are of different devices: /device:TPU:1 before, /device:TPU:160 now
where the time goes in v3:
time: 75.9 us; the launch traced here: 75.3 us
  starting transfers between devices  32.1 us (42%)
  Pallas kernels  22 us (29%)
  waiting for transfers between devices  19.1 us (25%)
  local copies, waits for them, and re-layouts  1.67 us (2%)
    ppermute x10, starting transfers between devices, step(): return lax.ppermute(value, 'narrow', ring)  13.4 us
    pallas_call x2, Pallas kernels, ladder_part(): pl.pallas_call(lambda *refs: ladder_kernel(start, count, *refs), out_shap...  11.3 us
    all_to_all x1, waiting for transfers between devices, on_device(): shares = lax.all_to_all(coded, 'wide', 0, 0, tiled=True)  8.52 us
    all_to_all x1, starting transfers between devices, on_device(): second = lax.all_to_all(moved, 'wide', 0, 0, tiled=True)  7.15 us
    all_to_all x1, starting transfers between devices, on_device(): first = lax.all_to_all(sent, 'wide', 0, 0, tiled=True)  7.05 us
    ppermute x10, waiting for transfers between devices, step(): return lax.ppermute(value, 'narrow', ring)  6.8 us
    pallas_call x1, Pallas kernels, on_device(): pl.pallas_call(finish_kernel, out_shape=jax.ShapeDtypeStruct((height, LAN...  4.58 us
    all_to_all x1, starting transfers between devices, on_device(): shares = lax.all_to_all(coded, 'wide', 0, 0, tiled=True)  4.44 us
  transfers between devices with their start and end apart: 13, of which 6 were waited for; matrix products, arithmetic and copies ran while one was open for 0% of the time, Pallas kernels for 16%

profile of v3, /device:TPU:160, one launch (start us, length us, event | category | flops | bytes accessed | tf_op | source)
XLA Modules:
  0.0 75.3 jit_solution(9822945675271322833)
XLA Ops:
  0.0 4.3 %select.1 = (bf16[16,32,256]{2,1,0:T(8,128)(2,1)}, s32[16,256]{1,0:T(8,128)}) custom-call(s32[1]{0:T(128)} %bitcast.2.refs_0_, s32[32,128]{1,0:T(8,128)} %bitcast.7, bf16[256,2048]{1,0:T(8,128)(2,1)} %refs_0_.3), custom_call_target="tpu_custom_call" | custom-call | flops 1073741824 | bytes 2097152 | tf_op jit(solution)/shard_map/select/pallas_call | solution.py:215
  4.4 7.0 %all-to-all-start = ((bf16[16,32,256]{2,1,0:T(8,128)(2,1)}), bf16[16,32,256]{2,1,0:T(8,128)(2,1)S(1)}, u32[]{:S(2)}, u32[]{:S(2)}) async-start(bf16[16,32,256]{2,1,0:T(8,128)(2,1)} %get-tuple-element.11), calls=%async_computation | async-start | bytes 524288 | tf_op jit(solution)/shard_map/all_to_all | solution.py:228
  11.4 0.7 copy-done.1
  12.1 0.5 route.1
  12.7 0.7 copy-done.2
  13.4 6.5 %ladder_early.1.after_ref.refs_3_ = s16[16,272,256]{2,1,0:T(8,128)(2,1)} custom-call(bf16[256,2048]{1,0:T(8,128)(2,1)S(1)} %copy-done, bf16[2048,4096]{1,0:T(8,128)(2,1)} %refs_1_.3, s32[16,256]{1,0:T(8,128)S(1)} %copy-done.2), custom_call_target="tpu_custom_call" | custom-call | flops 2684354560 | bytes 10485760 | tf_op jit(solution)/shard_map/ladder_early/pallas_call | solution.py:244
  19.9 1.0 %forward.1.refs_2_ = bf16[16,32,256]{2,1,0:T(8,128)(2,1)} custom-call(bf16[512,512]{1,0:T(8,128)(2,1)S(1)} %get-tuple-element.10.forward_ref, bf16[16,32,256]{2,1,0:T(8,128)(2,1)S(1)} %all-to-all-done.first_ref, s16[16,272,256]{2,1,0:T(8,128)(2,1)} %ladder_early.1.after_ref.refs_3_), custom_call_target="tpu_custom_call" | custom-call | flops 134217728 | bytes 1048576 | tf_op jit(solution)/shard_map/forward/pallas_call | solution.py:267
  20.9 7.2 %all-to-all-start.2 = ((bf16[16,32,256]{2,1,0:T(8,128)(2,1)}), bf16[16,32,256]{2,1,0:T(8,128)(2,1)S(1)}, u32[]{:S(2)}, u32[]{:S(2)}) async-start(bf16[16,32,256]{2,1,0:T(8,128)(2,1)} %forward.1.refs_2_), calls=%async_computation.2 | async-start | bytes 524288 | tf_op jit(solution)/shard_map/all_to_all | solution.py:276
  28.1 4.8 %ladder_late.1.after_ref = s16[16,272,256]{2,1,0:T(8,128)(2,1)} custom-call(bf16[256,2048]{1,0:T(8,128)(2,1)S(1)} %copy-done, bf16[2048,4096]{1,0:T(8,128)(2,1)} %refs_1_.3, bf16[16,32,256]{2,1,0:T(8,128)(2,1)} %forward.1.refs_2_, s16[16,272,256]{2,1,0:T(8,128)(2,1)} %ladder_early.1.after_ref.refs_3_), custom_call_target="tpu_custom_call", output_to_operand_aliasing={{}: (3, {})} | custom-call | flops 1610612736 | bytes 6291456 | tf_op jit(solution)/shard_map/ladder_late/pallas_call | solution.py:244
  32.9 3.7 %all-to-all-done.2.second_ref = bf16[16,32,256]{2,1,0:T(8,128)(2,1)S(1)} async-done(((bf16[16,32,256]{2,1,0:T(8,128)(2,1)}), bf16[16,32,256]{2,1,0:T(8,128)(2,1)S(1)}, u32[]{:S(2)}, u32[]{:S(2)}) %all-to-all-start.2) | async-done | bytes 262176 | tf_op jit(solution)/shard_map/all_to_all | solution.py:276
  36.6 4.4 %all-to-all-start.1 = ((s16[16,272,256]{2,1,0:T(8,128)(2,1)}), s16[16,272,256]{2,1,0:T(8,128)(2,1)}, u32[]{:S(2)}, u32[]{:S(2)}) async-start(s16[16,272,256]{2,1,0:T(8,128)(2,1)} %ladder_late.1.after_ref), calls=%async_computation.1 | async-start | bytes 4456448 | tf_op jit(solution)/shard_map/all_to_all | solution.py:281
  41.1 0.3 settle.1
  41.3 0.6 collective-permute-start.3
  42.0 2.4 %collective-permute-start.2 = (bf16[256,256]{1,0:T(8,128)(2,1)S(1)}, bf16[256,256]{1,0:T(8,128)(2,1)S(1)}, u32[]{:S(2)}, u32[]{:S(2)}) collective-permute-start(bf16[256,256]{1,0:T(8,128)(2,1)S(1)} %settle.1), channel_id=1, source_target_pairs={{0,4},{1,5},{2,6},{3,7},{4,8},{5,9},{6,10},{7,11},{8,12},{9,13},{1... | collective-permute-start | bytes 393224 | tf_op jit(solution)/shard_map/ppermute | solution.py:213
  44.3 2.2 %collective-permute-start = (bf16[256,256]{1,0:T(8,128)(2,1)S(1)}, bf16[256,256]{1,0:T(8,128)(2,1)S(1)}, u32[]{:S(2)}, u32[]{:S(2)}) collective-permute-start(bf16[256,256]{1,0:T(8,128)(2,1)S(1)} %settle.1), channel_id=1, source_target_pairs={{0,2},{1,3},{2,4},{3,5},{4,6},{5,7},{6,8},{7,9},{8,10},{9,11},{10,... | collective-permute-start | bytes 393224 | tf_op jit(solution)/shard_map/ppermute | solution.py:213
  46.6 2.2 %collective-permute-done.3 = bf16[256,256]{1,0:T(8,128)(2,1)S(1)} collective-permute-done((bf16[256,256]{1,0:T(8,128)(2,1)S(1)}, bf16[256,256]{1,0:T(8,128)(2,1)S(1)}, u32[]{:S(2)}, u32[]{:S(2)}) %collective-permute-start.3) | collective-permute-done | bytes 131104 | tf_op jit(solution)/shard_map/ppermute | solution.py:213
  48.8 3.5 %collective-permute-start.7 = (bf16[128,256]{1,0:T(8,128)(2,1)S(1)}, bf16[128,256]{1,0:T(8,128)(2,1)S(1)}, u32[]{:S(2)}, u32[]{:S(2)}) collective-permute-start(bf16[128,256]{1,0:T(8,128)(2,1)S(1)} %slice.9), channel_id=1, source_target_pairs={{0,12},{1,13},{2,14},{3,15},{4,0},{5,1},{6,2},{7,3},{8,4},{9,5},{1... | collective-permute-start | bytes 196616 | tf_op jit(solution)/shard_map/ppermute | solution.py:213
  52.3 0.5 collective-permute-start.6
  52.8 1.3 %collective-permute-start.5 = (bf16[256,256]{1,0:T(8,128)(2,1)S(1)}, bf16[256,256]{1,0:T(8,128)(2,1)S(1)}, u32[]{:S(2)}, u32[]{:S(2)}) collective-permute-start(bf16[256,256]{1,0:T(8,128)(2,1)S(1)} %collective-permute-done.3), channel_id=1, source_target_pairs={{0,14},{1,15},{2,0},{3,1},{4,2},{5,3},{6,4},{7,5},{8,6},{9,7},{10,... | collective-permute-start | bytes 393224 | tf_op jit(solution)/shard_map/ppermute | solution.py:213
  54.1 2.7 %collective-permute-start.4 = (bf16[256,256]{1,0:T(8,128)(2,1)S(1)}, bf16[256,256]{1,0:T(8,128)(2,1)S(1)}, u32[]{:S(2)}, u32[]{:S(2)}) collective-permute-start(bf16[256,256]{1,0:T(8,128)(2,1)S(1)} %collective-permute-done.2), channel_id=1, source_target_pairs={{0,2},{1,3},{2,4},{3,5},{4,6},{5,7},{6,8},{7,9},{8,10},{9,11},{10,... | collective-permute-start | bytes 393224 | tf_op jit(solution)/shard_map/ppermute | solution.py:213
  57.0 3.1 %collective-permute-done.4 = bf16[256,256]{1,0:T(8,128)(2,1)S(1)} collective-permute-done((bf16[256,256]{1,0:T(8,128)(2,1)S(1)}, bf16[256,256]{1,0:T(8,128)(2,1)S(1)}, u32[]{:S(2)}, u32[]{:S(2)}) %collective-permute-start.4) | collective-permute-done | bytes 131104 | tf_op jit(solution)/shard_map/ppermute | solution.py:213
  60.5 1.5 %collective-permute-done.9.refs_1_ = bf16[768,256]{1,0:T(8,128)(2,1)S(1)} collective-permute-done((bf16[768,256]{1,0:T(8,128)(2,1)S(1)}, bf16[768,256]{1,0:T(8,128)(2,1)S(1)}, u32[]{:S(2)}, u32[]{:S(2)}) %collective-permute-start.9) | collective-permute-done | bytes 393248 | tf_op jit(solution)/shard_map/ppermute | solution.py:213
  62.0 8.5 %all-to-all-done.1.far_coded_ref = s16[16,272,256]{2,1,0:T(8,128)(2,1)} async-done(((s16[16,272,256]{2,1,0:T(8,128)(2,1)}), s16[16,272,256]{2,1,0:T(8,128)(2,1)}, u32[]{:S(2)}, u32[]{:S(2)}) %all-to-all-start.1) | async-done | bytes 2228256 | tf_op jit(solution)/shard_map/all_to_all | solution.py:281
  70.5 4.6 %finish.1 = f32[256,256]{1,0:T(8,128)} custom-call(s32[2]{0:T(128)S(1)} %pad_add_fusion.place_ref, bf16[256,4096]{1,0:T(8,128)(2,1)} %far_pair_ref.1, s16[16,272,256]{2,1,0:T(8,128)(2,1)} %all-to-all-done.1.far_coded_ref, f32[256,1]{1,0:T(8,128)S(1)} %copy.8.occ_ref, f32[1,256]{1,0:T(1,128)S(1)} %bitcast.6, ...), custom_call_target="tpu_custom_call" | custom-call | flops 1073741824 | bytes 8388608 | tf_op jit(solution)/shard_map/finish/pallas_call | solution.py:302
  (34 shorter events, 0.6 us)
Async XLA Ops:
  0.0 11.4 %copy-start.4 = (s32[4096]{0:T(1024)S(1)}, s32[4096]{0:T(1024)}, u32[]{:S(2)}) copy-start(s32[4096]{0:T(1024)} %param.9) | copy-start | bytes 49156
  0.0 12.6 %copy-start = (bf16[256,2048]{1,0:T(8,128)(2,1)S(1)}, bf16[256,2048]{1,0:T(8,128)(2,1)}, u32[]{:S(2)}) copy-start(bf16[256,2048]{1,0:T(8,128)(2,1)} %refs_0_.3) | copy-start | bytes 3145732
  4.4 15.6 %all-to-all-start = ((bf16[16,32,256]{2,1,0:T(8,128)(2,1)}), bf16[16,32,256]{2,1,0:T(8,128)(2,1)S(1)}, u32[]{:S(2)}, u32[]{:S(2)}) async-start(bf16[16,32,256]{2,1,0:T(8,128)(2,1)} %get-tuple-element.11), calls=%async_computation | async-start | bytes 524288 | tf_op jit(solution)/shard_map/all_to_all | solution.py:228
  11.4 0.7 copy-start.1
  12.7 0.7 copy-start.2
  20.9 15.7 %all-to-all-start.2 = ((bf16[16,32,256]{2,1,0:T(8,128)(2,1)}), bf16[16,32,256]{2,1,0:T(8,128)(2,1)S(1)}, u32[]{:S(2)}, u32[]{:S(2)}) async-start(bf16[16,32,256]{2,1,0:T(8,128)(2,1)} %forward.1.refs_2_), calls=%async_computation.2 | async-start | bytes 524288 | tf_op jit(solution)/shard_map/all_to_all | solution.py:276
  36.6 33.9 %all-to-all-start.1 = ((s16[16,272,256]{2,1,0:T(8,128)(2,1)}), s16[16,272,256]{2,1,0:T(8,128)(2,1)}, u32[]{:S(2)}, u32[]{:S(2)}) async-start(s16[16,272,256]{2,1,0:T(8,128)(2,1)} %ladder_late.1.after_ref), calls=%async_computation.1 | async-start | bytes 4456448 | tf_op jit(solution)/shard_map/all_to_all | solution.py:281
  41.0 19.3 %copy-start.5 = (f32[256]{0:T(256)S(1)}, f32[256]{0:T(256)}, u32[]{:S(2)}) copy-start(f32[256]{0:T(256)} %param.10) | copy-start | bytes 3076
  41.1 29.5 %copy-start.3 = (f32[256]{0:T(256)S(1)}, f32[256]{0:T(256)}, u32[]{:S(2)}) copy-start(f32[256]{0:T(256)} %param.11) | copy-start | bytes 3076
  41.3 7.4 %collective-permute-start.3 = (bf16[256,256]{1,0:T(8,128)(2,1)S(1)}, bf16[256,256]{1,0:T(8,128)(2,1)S(1)}, u32[]{:S(2)}, u32[]{:S(2)}) collective-permute-start(bf16[256,256]{1,0:T(8,128)(2,1)S(1)} %settle.1), channel_id=1, source_target_pairs={{0,12},{1,13},{2,14},{3,15},{4,0},{5,1},{6,2},{7,3},{8,4},{9,5},{1... | collective-permute-start | bytes 393224 | tf_op jit(solution)/shard_map/ppermute | solution.py:213
  42.0 10.3 %collective-permute-start.2 = (bf16[256,256]{1,0:T(8,128)(2,1)S(1)}, bf16[256,256]{1,0:T(8,128)(2,1)S(1)}, u32[]{:S(2)}, u32[]{:S(2)}) collective-permute-start(bf16[256,256]{1,0:T(8,128)(2,1)S(1)} %settle.1), channel_id=1, source_target_pairs={{0,4},{1,5},{2,6},{3,7},{4,8},{5,9},{6,10},{7,11},{8,12},{9,13},{1... | collective-permute-start | bytes 393224 | tf_op jit(solution)/shard_map/ppermute | solution.py:213
  44.3 9.8 %collective-permute-start = (bf16[256,256]{1,0:T(8,128)(2,1)S(1)}, bf16[256,256]{1,0:T(8,128)(2,1)S(1)}, u32[]{:S(2)}, u32[]{:S(2)}) collective-permute-start(bf16[256,256]{1,0:T(8,128)(2,1)S(1)} %settle.1), channel_id=1, source_target_pairs={{0,2},{1,3},{2,4},{3,5},{4,6},{5,7},{6,8},{7,9},{8,10},{9,11},{10,... | collective-permute-start | bytes 393224 | tf_op jit(solution)/shard_map/ppermute | solution.py:213
  46.6 10.2 %collective-permute-start.1 = (bf16[256,256]{1,0:T(8,128)(2,1)S(1)}, bf16[256,256]{1,0:T(8,128)(2,1)S(1)}, u32[]{:S(2)}, u32[]{:S(2)}) collective-permute-start(bf16[256,256]{1,0:T(8,128)(2,1)S(1)} %settle.1), channel_id=1, source_target_pairs={{0,14},{1,15},{2,0},{3,1},{4,2},{5,3},{6,4},{7,5},{8,6},{9,7},{10,... | collective-permute-start | bytes 393224 | tf_op jit(solution)/shard_map/ppermute | solution.py:213
  48.8 11.4 %collective-permute-start.7 = (bf16[128,256]{1,0:T(8,128)(2,1)S(1)}, bf16[128,256]{1,0:T(8,128)(2,1)S(1)}, u32[]{:S(2)}, u32[]{:S(2)}) collective-permute-start(bf16[128,256]{1,0:T(8,128)(2,1)S(1)} %slice.9), channel_id=1, source_target_pairs={{0,12},{1,13},{2,14},{3,15},{4,0},{5,1},{6,2},{7,3},{8,4},{9,5},{1... | collective-permute-start | bytes 196616 | tf_op jit(solution)/shard_map/ppermute | solution.py:213
  52.3 7.9 %collective-permute-start.6 = (bf16[128,256]{1,0:T(8,128)(2,1)S(1)}, bf16[128,256]{1,0:T(8,128)(2,1)S(1)}, u32[]{:S(2)}, u32[]{:S(2)}) collective-permute-start(bf16[128,256]{1,0:T(8,128)(2,1)S(1)} %slice.8), channel_id=1, source_target_pairs={{0,4},{1,5},{2,6},{3,7},{4,8},{5,9},{6,10},{7,11},{8,12},{9,13},{1... | collective-permute-start | bytes 196616 | tf_op jit(solution)/shard_map/ppermute | solution.py:213
  52.8 7.3 %collective-permute-start.5 = (bf16[256,256]{1,0:T(8,128)(2,1)S(1)}, bf16[256,256]{1,0:T(8,128)(2,1)S(1)}, u32[]{:S(2)}, u32[]{:S(2)}) collective-permute-start(bf16[256,256]{1,0:T(8,128)(2,1)S(1)} %collective-permute-done.3), channel_id=1, source_target_pairs={{0,14},{1,15},{2,0},{3,1},{4,2},{5,3},{6,4},{7,5},{8,6},{9,7},{10,... | collective-permute-start | bytes 393224 | tf_op jit(solution)/shard_map/ppermute | solution.py:213
  54.1 6.0 %collective-permute-start.4 = (bf16[256,256]{1,0:T(8,128)(2,1)S(1)}, bf16[256,256]{1,0:T(8,128)(2,1)S(1)}, u32[]{:S(2)}, u32[]{:S(2)}) collective-permute-start(bf16[256,256]{1,0:T(8,128)(2,1)S(1)} %collective-permute-done.2), channel_id=1, source_target_pairs={{0,2},{1,3},{2,4},{3,5},{4,6},{5,7},{6,8},{7,9},{8,10},{9,11},{10,... | collective-permute-start | bytes 393224 | tf_op jit(solution)/shard_map/ppermute | solution.py:213
  56.9 5.2 %collective-permute-start.8 = (bf16[1280,256]{1,0:T(8,128)(2,1)S(1)}, bf16[1280,256]{1,0:T(8,128)(2,1)S(1)}, u32[]{:S(2)}, u32[]{:S(2)}) collective-permute-start(bf16[1280,256]{1,0:T(8,128)(2,1)S(1)} %constant_dynamic-update-slice_fusion.near_ref), channel_id=1, source_target_pairs={{0,1},{1,0},{2,3},{3,2},{4,5},{5,4},{6,7},{7,6},{8,9},{9,8},{10,11... | collective-permute-start | bytes 1966088 | tf_op jit(solution)/shard_map/ppermute | solution.py:213
  60.2 1.8 %collective-permute-start.9 = (bf16[768,256]{1,0:T(8,128)(2,1)S(1)}, bf16[768,256]{1,0:T(8,128)(2,1)S(1)}, u32[]{:S(2)}, u32[]{:S(2)}) collective-permute-start(bf16[768,256]{1,0:T(8,128)(2,1)S(1)} %constant_dynamic-update-slice_fusion.5.far_ref), channel_id=1, source_target_pairs={{0,1},{1,0},{2,3},{3,2},{4,5},{5,4},{6,7},{7,6},{8,9},{9,8},{10,11... | collective-permute-start | bytes 1179656 | tf_op jit(solution)/shard_map/ppermute | solution.py:213

commit v4 on v3

v4 whole, which is shorter than its diff:
```python
import jax
import jax.numpy as jnp
from jax import lax
from jax.experimental import pallas as pl
from jax.experimental.pallas import tpu as pltpu
from jax.sharding import PartitionSpec as P

CHUNKS = 16
DEPTH = 32
HOPS = ((0, 0), (1, 0), (3, 0), (0, 1))
ROOM = 80
LANES = 256
CODE_ROWS = 16
STEPS = 256.0
TOP = 32760.0
PER = 2
VMEM = pl.BlockSpec(memory_space=pltpu.VMEM)
HBM = pl.BlockSpec(memory_space=pltpu.HBM)
SMEM = pl.BlockSpec(memory_space=pltpu.SMEM)


def iota(shape, dim):
    return lax.broadcasted_iota(jnp.int32, shape, dim)


def ones_where(mask):
    return jnp.where(mask, 1.0, 0.0)


def bdot(left, right, dims=((1,), (0,))):
    return lax.dot_general(
        left.astype(jnp.bfloat16),
        right.astype(jnp.bfloat16),
        (dims, ((), ())),
        preferred_element_type=jnp.float32,
    )


def count_before(classes):
    member = jnp.concatenate(
        [ones_where(classes[c : c + 1, :] == iota((CHUNKS, LANES), 0)) for c in range(CHUNKS)], 0
    )
    earlier = ones_where(iota((LANES, LANES), 0) < iota((LANES, LANES), 1))
    return member, bdot(member, earlier)


def pick(member, table):
    return jnp.sum((member * table).reshape(CHUNKS, CHUNKS, LANES), axis=1).astype(jnp.int32)


def widen(ref):
    halves = [ref[pl.ds(k, CHUNKS, stride=2), :] for k in range(2)]
    return jnp.concatenate(halves, 1)


def select_kernel(shift, here_ref, index_ref, far_amp_ref, *refs):
    *sent_refs, rank_ref, amp_ref, amp_sem = refs
    fetch = pltpu.make_async_copy(far_amp_ref, amp_ref, amp_sem)
    fetch.start()
    index = widen(index_ref)
    here = here_ref[0]
    owner = jnp.right_shift(index, shift)
    member, within = count_before(owner)
    r, c = iota((LANES, LANES), 0), iota((LANES, LANES), 1)
    ahead = ones_where(((r & 15) == (c & 15)) & (jnp.right_shift(c, 4) < jnp.right_shift(r, 4)))
    base = jnp.sum(bdot(ahead, member), axis=1, keepdims=True)
    rank = pick(member, within + base)
    rank_ref[...] = rank
    middle, depth = rank & 15, jnp.right_shift(rank, 4)
    column = index & ((1 << shift) - 1)
    high, low = jnp.right_shift(column, 6).astype(jnp.float32), (column & 63).astype(jnp.float32)
    lefts, rights = [], []
    for k in range(CHUNKS):
        one = slice(k, k + 1)
        hit = ones_where((depth[one] == iota((DEPTH, LANES), 0)) & (owner[one] == here))
        lefts.append(jnp.concatenate([hit * high[one], hit * low[one]], 0))
        rights.append(ones_where(middle[one] == iota((CHUNKS, LANES), 0)))
    found = bdot(jnp.concatenate(lefts, 1), jnp.concatenate(rights, 1), ((1,), (1,)))
    columns = (found[:DEPTH] * 64.0 + found[DEPTH:]).astype(jnp.int32)
    span = amp_ref.shape[1]
    lane = iota((DEPTH, span), 1)
    fetch.wait()
    for hop, sent_ref in enumerate(sent_refs):
        chosen = jnp.concatenate(
            [
                ones_where(lane == columns[:, j : j + 1]).astype(jnp.bfloat16)
                for j in range(hop, CHUNKS, 4)
            ],
            0,
        )
        sent_ref[...] = bdot(chosen, amp_ref[...], ((1,), (1,))).astype(jnp.bfloat16)


def route_kernel(shift, here_ref, index_ref, rank_ref, forward_ref, settle_ref):
    index, rank, here = widen(index_ref), rank_ref[...], here_ref[0]
    owner = jnp.right_shift(index, shift)
    last, depth = rank & 15, jnp.right_shift(rank, 4)
    hop = rank & 3
    x, y = jnp.right_shift(owner, 2), owner & 3
    for k, (dx, dy) in enumerate(HOPS):
        x, y = jnp.where(hop == k, x + dx, x), jnp.where(hop == k, y + dy, y)
    middle = (x & 3) * 4 + (y & 3)
    member, within = count_before(middle)
    place = pick(member, within)
    source = (hop * (4 * DEPTH) + jnp.right_shift(last, 2) * DEPTH + depth).astype(jnp.float32)
    lane = iota((ROOM, CHUNKS * DEPTH), 1)
    for k in range(CHUNKS):
        one = slice(k, k + 1)
        hit = (place[one] == iota((ROOM, LANES), 0)) & (middle[one] == here)
        row = jnp.sum(jnp.where(hit, source[one], 0.0), axis=1, keepdims=True).astype(jnp.int32)
        forward_ref[k * ROOM : (k + 1) * ROOM, :] = ones_where(lane == row).astype(jnp.bfloat16)
    arrived = (middle * ROOM + place).astype(jnp.float32)
    own = iota((CHUNKS, LANES), 0) == here
    wanted = jnp.sum(jnp.where(own, arrived, 0.0), axis=0, keepdims=True).astype(jnp.int32)
    settle_ref[...] = ones_where(iota((CHUNKS * ROOM, LANES), 0) == wanted).astype(jnp.bfloat16)


def forward_kernel(forward_ref, *refs):
    *first_refs, moved_ref = refs
    arrived = jnp.concatenate([ref[...] for ref in first_refs], 0)
    moved = bdot(forward_ref[...], arrived).astype(jnp.bfloat16)
    moved_ref[...] = moved.reshape(moved_ref.shape)


def settle_kernel(second_ref, settle_ref, after_ref, own_ref):
    del after_ref
    arrived = second_ref[...].reshape(CHUNKS * ROOM, second_ref.shape[2])
    own_ref[...] = bdot(arrived, settle_ref[...], ((0,), (0,))).astype(jnp.bfloat16)


def ladder_kernel(amp_ref, int_ref, after_ref, coded_ref, held_ref, stage_ref, in_sems, out_sems):
    del after_ref
    count = CHUNKS // PER
    height = amp_ref.shape[0]
    width = PER * LANES
    ins, outs = [], []
    for b in range(count):
        ins.append(
            pltpu.make_async_copy(
                int_ref.at[:, pl.ds(b * width, width)], held_ref.at[b], in_sems.at[b]
            )
        )
        ins[b].start()
    for b in range(count):
        ins[b].wait()
        slab = jnp.dot(amp_ref[...], held_ref[b], preferred_element_type=jnp.float32)
        for j in range(PER):
            part = slab[:, j * LANES : (j + 1) * LANES]
            largest = jnp.max(jnp.abs(part), axis=0, keepdims=True)
            code = jnp.ceil(jnp.log2(jnp.maximum(largest, 2.0**-120)) * STEPS) + 1.0
            shrunk = part * jnp.exp2(code * (-1.0 / STEPS)) * TOP
            k = b * PER + j
            stage_ref[k, :height, :] = jnp.round(shrunk).astype(jnp.int32).astype(jnp.int16)
            stage_ref[k, height:, :] = jnp.broadcast_to(
                code.astype(jnp.int32), (CODE_ROWS, LANES)
            ).astype(jnp.int16)
        outs.append(
            pltpu.make_async_copy(
                stage_ref.at[pl.ds(b * PER, PER)],
                coded_ref.at[pl.ds(b * PER, PER)],
                out_sems.at[b],
            )
        )
        outs[b].start()
    for out in outs:
        out.wait()


def hole_kernel(place_ref, far_pair_ref, occ_ref, virt_ref, near_ref, far_ref, *refs):
    *away_refs, out_ref, pair_ref, near_sibling_ref, far_sibling_ref, sems = refs
    fetches = [
        pltpu.make_async_copy(source, target, sems.at[k])
        for k, (source, target) in enumerate(
            zip([far_pair_ref] + away_refs, [pair_ref, near_sibling_ref, far_sibling_ref])
        )
    ]
    for fetch in fetches:
        fetch.start()
    z, core = place_ref[0], place_ref[1]
    rows = near_ref.shape[0] // 5
    half = rows // 2
    total = jnp.zeros(out_ref.shape[1:], jnp.float32)

    def add(total, away, which, start, block):
        n = jnp.bitwise_and(z - away + 8, 7) * 2 + which
        columns = pl.ds(pl.multiple_of(n * rows + start, 128), block.shape[0])
        return total + jnp.dot(pair_ref[:, columns], block, preferred_element_type=jnp.float32)

    out_ref[1] = virt_ref[...] - occ_ref[...]
    fetches[0].wait()
    sides = ((near_ref, far_ref, core), (near_sibling_ref, far_sibling_ref, 1 - core))
    for near, far, which in sides:
        if near is near_sibling_ref:
            fetches[1].wait()
            fetches[2].wait()
        for k, away in enumerate((0, 1, -1, 2, -2)):
            total = add(total, away, which, 0, near[k * rows : (k + 1) * rows])
        total = add(total, 3, which, 0, far[:rows])
        total = add(total, -3, which, 0, far[rows : 2 * rows])
        total = add(total, 4, which, 0, far[2 * rows : 2 * rows + half])
        total = add(total, 4, which, half, far[2 * rows + half :])
    out_ref[0] = total


def finish_kernel(coded_ref, far_hole_ref, out_ref, hole_ref, hole_sem):
    fetch = pltpu.make_async_copy(far_hole_ref, hole_ref, hole_sem)
    fetch.start()
    rows = out_ref.shape[0]
    ladder = jnp.zeros(out_ref.shape, jnp.float32)
    for k in range(CHUNKS):
        code = coded_ref[k, rows:, :].astype(jnp.int32).astype(jnp.float32)[:1, :]
        values = coded_ref[k, :rows, :].astype(jnp.int32).astype(jnp.float32)
        ladder = ladder + values * jnp.exp2(code * (1.0 / STEPS))
    fetch.wait()
    out_ref[...] = (ladder * (1.0 / TOP) + hole_ref[0]) / hole_ref[1]


def on_device(amplitudes, integrals, pair_integrals, slab_index, occupied_energy, virtual_energy):
    wide_index = lax.axis_index("wide")
    narrow_index = lax.axis_index("narrow")
    height, span = amplitudes.shape
    shift = span.bit_length() - 1
    here = wide_index.astype(jnp.int32).reshape(1)
    index = slab_index.reshape(2 * CHUNKS, LANES // 2)
    half = height // 2

    def step(value, dz, dc=0):
        ring = [
            (z * 2 + c, (z + dz) % 8 * 2 + (c + dc) % 2) for z in range(8) for c in range(2)
        ]
        return lax.ppermute(value, "narrow", ring)

    *sent, rank = pl.pallas_call(
        lambda *refs: select_kernel(shift, *refs),
        out_shape=(
            *[jax.ShapeDtypeStruct((4 * DEPTH, height), jnp.bfloat16) for _ in HOPS],
            jax.ShapeDtypeStruct((CHUNKS, LANES), jnp.int32),
        ),
        in_specs=[SMEM, VMEM, HBM],
        out_specs=(VMEM,) * (len(HOPS) + 1),
        scratch_shapes=[pltpu.VMEM((height, span), jnp.bfloat16), pltpu.SemaphoreType.DMA(())],
        compiler_params=pltpu.CompilerParams(vmem_limit_bytes=59 << 20),
        cost_estimate=pl.CostEstimate(flops=2**30, bytes_accessed=2**21, transcendentals=0),
        name="select",
    )(here, index, amplitudes)
    first = sent[:1] + [
        lax.ppermute(
            sent[k],
            "wide",
            [(x * 4 + y, (x + dx) % 4 * 4 + (y + dy) % 4) for x in range(4) for y in range(4)],
        )
        for k, (dx, dy) in enumerate(HOPS)
        if k
    ]

    forward, settle = pl.pallas_call(
        lambda *refs: route_kernel(shift, *refs),
        out_shape=(
            jax.ShapeDtypeStruct((CHUNKS * ROOM, CHUNKS * DEPTH), jnp.bfloat16),
            jax.ShapeDtypeStruct((CHUNKS * ROOM, LANES), jnp.bfloat16),
        ),
        in_specs=[SMEM, VMEM, VMEM],
        out_specs=(VMEM, VMEM),
        compiler_params=pltpu.CompilerParams(vmem_limit_bytes=16 << 20),
        cost_estimate=pl.CostEstimate(flops=2**28, bytes_accessed=2**20, transcendentals=0),
        name="route",
    )(here, index, rank)

    moved = pl.pallas_call(
        forward_kernel,
        out_shape=jax.ShapeDtypeStruct((CHUNKS, ROOM, height), jnp.bfloat16),
        in_specs=[VMEM] * (len(HOPS) + 1),
        out_specs=VMEM,
        compiler_params=pltpu.CompilerParams(vmem_limit_bytes=8 << 20),
        cost_estimate=pl.CostEstimate(flops=2**28, bytes_accessed=2**20, transcendentals=0),
        name="forward",
    )(forward, *first)
    second = lax.all_to_all(moved, "wide", 0, 0, tiled=True)

    slabs = CHUNKS // PER
    coded = pl.pallas_call(
        ladder_kernel,
        out_shape=jax.ShapeDtypeStruct((CHUNKS, height + CODE_ROWS, LANES), jnp.int16),
        in_specs=[VMEM, HBM, HBM],
        out_specs=HBM,
        scratch_shapes=[
            pltpu.VMEM((slabs, span, PER * LANES), jnp.bfloat16),
            pltpu.VMEM((CHUNKS, height + CODE_ROWS, LANES), jnp.int16),
            pltpu.SemaphoreType.DMA((slabs,)),
            pltpu.SemaphoreType.DMA((slabs,)),
        ],
        compiler_params=pltpu.CompilerParams(vmem_limit_bytes=50 << 20),
        cost_estimate=pl.CostEstimate(
            flops=2 * height * span * CHUNKS * LANES, bytes_accessed=18 * 2**20, transcendentals=0
        ),
        name="ladder",
    )(amplitudes, integrals, moved)
    shares = lax.all_to_all(coded, "wide", 0, 0, tiled=True)

    own = pl.pallas_call(
        settle_kernel,
        out_shape=jax.ShapeDtypeStruct((height, LANES), jnp.bfloat16),
        in_specs=[VMEM, VMEM, HBM],
        out_specs=VMEM,
        compiler_params=pltpu.CompilerParams(vmem_limit_bytes=8 << 20),
        cost_estimate=pl.CostEstimate(flops=2**26, bytes_accessed=2**20, transcendentals=0),
        name="settle",
    )(second, settle, coded)

    up, down, up2, down2 = step(own, 1), step(own, -1), step(own, 2), step(own, -2)
    up3, down3 = step(up2, 1), step(down2, -1)
    up4, down4 = step(up2[:half], 2), step(down2[half:], -2)
    near = jnp.concatenate([own, up, down, up2, down2], 0)
    near_sibling = step(near, 0, 1)
    far = jnp.concatenate([up3, down3, up4, down4], 0)
    far_sibling = step(far, 0, 1)

    where = jnp.stack([narrow_index >> 1, narrow_index & 1]).astype(jnp.int32)
    hole = pl.pallas_call(
        hole_kernel,
        out_shape=jax.ShapeDtypeStruct((2, height, LANES), jnp.float32),
        in_specs=[SMEM, HBM] + [VMEM] * 4 + [HBM] * 2,
        out_specs=VMEM,
        scratch_shapes=[
            pltpu.VMEM(pair_integrals.shape, jnp.bfloat16),
            pltpu.VMEM(near.shape, jnp.bfloat16),
            pltpu.VMEM(far.shape, jnp.bfloat16),
            pltpu.SemaphoreType.DMA((3,)),
        ],
        compiler_params=pltpu.CompilerParams(vmem_limit_bytes=50 << 20),
        cost_estimate=pl.CostEstimate(flops=2**30, bytes_accessed=2**22, transcendentals=0),
        name="hole",
    )(
        where,
        pair_integrals,
        occupied_energy.reshape(height, 1),
        virtual_energy.reshape(1, LANES),
        near,
        far,
        near_sibling,
        far_sibling,
    )
    return pl.pallas_call(
        finish_kernel,
        out_shape=jax.ShapeDtypeStruct((height, LANES), jnp.float32),
        in_specs=[VMEM, HBM],
        out_specs=VMEM,
        scratch_shapes=[
            pltpu.VMEM((2, height, LANES), jnp.float32),
            pltpu.SemaphoreType.DMA(()),
        ],
        compiler_params=pltpu.CompilerParams(vmem_limit_bytes=20 << 20),
        cost_estimate=pl.CostEstimate(flops=2**23, bytes_accessed=2**22, transcendentals=0),
        name="finish",
    )(shares, hole)


def solution(mesh):
    placed = (P("narrow", "wide"), P("wide", None), P("narrow", None), P(), P("narrow"), P("wide"))
    return jax.shard_map(
        on_device, mesh=mesh, in_specs=placed, out_specs=P("narrow", "wide"), check_vma=False
    )
```

time: 75.9 us -> 71.6 us (0.943)
  the two profiles are of different devices: /device:TPU:160 before, /device:TPU:1 now
where the time goes in v4:
time: 71.6 us; the launch traced here: 71.2 us
  starting transfers between devices  42 us (59%)
  Pallas kernels  21 us (29%)
  waiting for transfers between devices  4.13 us (6%)
  local copies, waits for them, and re-layouts  3.56 us (5%)
    ppermute x10, starting transfers between devices, step(): return lax.ppermute(value, 'narrow', ring)  27.4 us
    pallas_call x1, Pallas kernels, on_device(): pl.pallas_call(ladder_kernel, out_shape=jax.ShapeDtypeStruct((CHUNKS, hei...  8.89 us
    all_to_all x1, starting transfers between devices, on_device(): shares = lax.all_to_all(coded, 'wide', 0, 0, tiled=True)  5.74 us
    ppermute x3, starting transfers between devices, on_device(): lax.ppermute(sent[k], 'wide', [(x * 4 + y, (x + dx) % 4 * 4 + (y + dy) %...  4.88 us
    pallas_call x1, Pallas kernels, on_device(): pl.pallas_call(lambda *refs: select_kernel(shift, *refs), out_shape=(*[ja...  4.24 us
    all_to_all x1, starting transfers between devices, on_device(): second = lax.all_to_all(moved, 'wide', 0, 0, tiled=True)  3.98 us
    pallas_call x1, Pallas kernels, on_device(): pl.pallas_call(hole_kernel, out_shape=jax.ShapeDtypeStruct((2, height, LA...  3.56 us
    unnamed x23, local copies, waits for them, and re-layouts  3.4 us
  transfers between devices with their start and end apart: 15, of which 4 were waited for; matrix products, arithmetic and copies ran while one was open for 0% of the time, Pallas kernels for 19%

profile of v4, /device:TPU:1, one launch (start us, length us, event | category | flops | bytes accessed | tf_op | source)
XLA Modules:
  0.0 71.2 jit_solution(12507823858310091023)
XLA Ops:
  0.0 4.2 %select.1 = (bf16[128,256]{1,0:T(8,128)(2,1)}, bf16[128,256]{1,0:T(8,128)(2,1)}, bf16[128,256]{1,0:T(8,128)(2,1)}, bf16[128,256]{1,0:T(8,128)(2,1)}, s32[16,256]{1,0:T(8,128)}) custom-call(s32[1]{0:T(128)} %bitcast.refs_0_, s32[32,128]{1,0:T(8,128)} %bitcast.7, bf16[256,2048]{1,0:T(8,128)(2,1)} %amp_ref.1), custom_call_target="tpu_custom_call" | custom-call | flops 1073741824 | bytes 2097152 | tf_op jit(solution)/shard_map/select/pallas_call | solution.py:233
  4.3 2.1 %collective-permute-start = (bf16[128,256]{1,0:T(8,128)(2,1)}, bf16[128,256]{1,0:T(8,128)(2,1)S(1)}, u32[]{:S(2)}, u32[]{:S(2)}) collective-permute-start(bf16[128,256]{1,0:T(8,128)(2,1)} %get-tuple-element.15), channel_id=1, source_target_pairs={{0,64},{16,80},{32,96},{48,112},{64,128},{80,144},{96,160},{112,17... | collective-permute-start | bytes 196616 | tf_op jit(solution)/shard_map/ppermute | solution.py:247
  6.4 1.4 %collective-permute-start.1 = (bf16[128,256]{1,0:T(8,128)(2,1)}, bf16[128,256]{1,0:T(8,128)(2,1)S(1)}, u32[]{:S(2)}, u32[]{:S(2)}) collective-permute-start(bf16[128,256]{1,0:T(8,128)(2,1)} %get-tuple-element.16), channel_id=1, source_target_pairs={{0,192},{16,208},{32,224},{48,240},{64,0},{80,16},{96,32},{112,48}... | collective-permute-start | bytes 196616 | tf_op jit(solution)/shard_map/ppermute | solution.py:247
  7.7 1.4 %collective-permute-start.2 = (bf16[128,256]{1,0:T(8,128)(2,1)}, bf16[128,256]{1,0:T(8,128)(2,1)S(1)}, u32[]{:S(2)}, u32[]{:S(2)}) collective-permute-start(bf16[128,256]{1,0:T(8,128)(2,1)} %get-tuple-element.17), channel_id=1, source_target_pairs={{0,16},{16,32},{32,48},{48,0},{64,80},{80,96},{96,112},{112,64},{1... | collective-permute-start | bytes 196616 | tf_op jit(solution)/shard_map/ppermute | solution.py:247
  9.9 0.9 %route.1 = (bf16[1280,512]{1,0:T(8,128)(2,1)S(1)}, bf16[1280,256]{1,0:T(8,128)(2,1)S(1)}) custom-call(s32[1]{0:T(128)} %bitcast.refs_0_, s32[32,128]{1,0:T(8,128)S(1)} %bitcast.8, s32[16,256]{1,0:T(8,128)S(1)} %copy-done.6), custom_call_target="tpu_custom_call" | custom-call | flops 268435456 | bytes 1048576 | tf_op jit(solution)/shard_map/route/pallas_call | solution.py:256
  10.8 1.9 %collective-permute-done.2.refs_3_ = bf16[128,256]{1,0:T(8,128)(2,1)S(1)} collective-permute-done((bf16[128,256]{1,0:T(8,128)(2,1)}, bf16[128,256]{1,0:T(8,128)(2,1)S(1)}, u32[]{:S(2)}, u32[]{:S(2)}) %collective-permute-start.2) | collective-permute-done | bytes 65568 | tf_op jit(solution)/shard_map/ppermute | solution.py:247
  12.7 0.8 %copy-done.3 = bf16[128,256]{1,0:T(8,128)(2,1)S(1)} copy-done((bf16[128,256]{1,0:T(8,128)(2,1)S(1)}, bf16[128,256]{1,0:T(8,128)(2,1)}, u32[]{:S(2)}) %copy-start.3) | copy-done | bytes 65560
  13.6 1.4 %forward.1.after_ref = bf16[16,80,256]{2,1,0:T(8,128)(2,1)} custom-call(bf16[1280,512]{1,0:T(8,128)(2,1)S(1)} %get-tuple-element.13.forward_ref, bf16[128,256]{1,0:T(8,128)(2,1)S(1)} %copy-done.3, bf16[128,256]{1,0:T(8,128)(2,1)S(1)} %collective-permute-done.refs_1_, bf16[128,256]{1,0:T(8,128)(2,1)S(1)} %collective-permute-done.1.refs_2_, ...), custom_call_target="tpu_custom_call" | custom-call | flops 268435456 | bytes 1048576 | tf_op jit(solution)/shard_map/forward/pallas_call | solution.py:269
  14.9 4.0 %all-to-all-start.1 = ((bf16[16,80,256]{2,1,0:T(8,128)(2,1)}), bf16[16,80,256]{2,1,0:T(8,128)(2,1)S(1)}, u32[]{:S(2)}, u32[]{:S(2)}) async-start(bf16[16,80,256]{2,1,0:T(8,128)(2,1)} %forward.1.after_ref), calls=%async_computation.1 | async-start | bytes 1310720 | tf_op jit(solution)/shard_map/all_to_all | solution.py:278
  18.9 8.9 %ladder.1.after_ref = s16[16,272,256]{2,1,0:T(8,128)(2,1)} custom-call(bf16[256,2048]{1,0:T(8,128)(2,1)S(1)} %copy-done, bf16[2048,4096]{1,0:T(8,128)(2,1)} %int_ref.1, bf16[16,80,256]{2,1,0:T(8,128)(2,1)} %forward.1.after_ref), custom_call_target="tpu_custom_call" | custom-call | flops 4294967296 | bytes 18874368 | tf_op jit(solution)/shard_map/ladder/pallas_call | solution.py:281
  27.8 0.9 %all-to-all-done.1.second_ref = bf16[16,80,256]{2,1,0:T(8,128)(2,1)S(1)} async-done(((bf16[16,80,256]{2,1,0:T(8,128)(2,1)}), bf16[16,80,256]{2,1,0:T(8,128)(2,1)S(1)}, u32[]{:S(2)}, u32[]{:S(2)}) %all-to-all-start.1) | async-done | bytes 655392 | tf_op jit(solution)/shard_map/all_to_all | solution.py:278
  28.8 5.7 %all-to-all-start = ((s16[16,272,256]{2,1,0:T(8,128)(2,1)}), s16[16,272,256]{2,1,0:T(8,128)(2,1)S(1)}, u32[]{:S(2)}, u32[]{:S(2)}) async-start(s16[16,272,256]{2,1,0:T(8,128)(2,1)} %ladder.1.after_ref), calls=%async_computation | async-start | bytes 4456448 | tf_op jit(solution)/shard_map/all_to_all | solution.py:298
  34.9 6.1 %collective-permute-start.6 = (bf16[256,256]{1,0:T(8,128)(2,1)S(1)}, bf16[256,256]{1,0:T(8,128)(2,1)S(1)}, u32[]{:S(2)}, u32[]{:S(2)}) collective-permute-start(bf16[256,256]{1,0:T(8,128)(2,1)S(1)} %settle.1), channel_id=1, source_target_pairs={{0,12},{1,13},{2,14},{3,15},{4,0},{5,1},{6,2},{7,3},{8,4},{9,5},{1... | collective-permute-start | bytes 393224 | tf_op jit(solution)/shard_map/ppermute | solution.py:231
  41.0 0.7 %collective-permute-start.3 = (bf16[256,256]{1,0:T(8,128)(2,1)S(1)}, bf16[256,256]{1,0:T(8,128)(2,1)S(1)}, u32[]{:S(2)}, u32[]{:S(2)}) collective-permute-start(bf16[256,256]{1,0:T(8,128)(2,1)S(1)} %settle.1), channel_id=1, source_target_pairs={{0,2},{1,3},{2,4},{3,5},{4,6},{5,7},{6,8},{7,9},{8,10},{9,11},{10,... | collective-permute-start | bytes 393224 | tf_op jit(solution)/shard_map/ppermute | solution.py:231
  41.8 2.4 %collective-permute-start.4 = (bf16[256,256]{1,0:T(8,128)(2,1)S(1)}, bf16[256,256]{1,0:T(8,128)(2,1)S(1)}, u32[]{:S(2)}, u32[]{:S(2)}) collective-permute-start(bf16[256,256]{1,0:T(8,128)(2,1)S(1)} %settle.1), channel_id=1, source_target_pairs={{0,14},{1,15},{2,0},{3,1},{4,2},{5,3},{6,4},{7,5},{8,6},{9,7},{10,... | collective-permute-start | bytes 393224 | tf_op jit(solution)/shard_map/ppermute | solution.py:231
  44.2 2.9 %collective-permute-start.10 = (bf16[128,256]{1,0:T(8,128)(2,1)S(1)}, bf16[128,256]{1,0:T(8,128)(2,1)S(1)}, u32[]{:S(2)}, u32[]{:S(2)}) collective-permute-start(bf16[128,256]{1,0:T(8,128)(2,1)S(1)} %slice.9), channel_id=1, source_target_pairs={{0,12},{1,13},{2,14},{3,15},{4,0},{5,1},{6,2},{7,3},{8,4},{9,5},{1... | collective-permute-start | bytes 196616 | tf_op jit(solution)/shard_map/ppermute | solution.py:231
  47.0 0.8 %collective-permute-done.5 = bf16[256,256]{1,0:T(8,128)(2,1)S(1)} collective-permute-done((bf16[256,256]{1,0:T(8,128)(2,1)S(1)}, bf16[256,256]{1,0:T(8,128)(2,1)S(1)}, u32[]{:S(2)}, u32[]{:S(2)}) %collective-permute-start.5) | collective-permute-done | bytes 131104 | tf_op jit(solution)/shard_map/ppermute | solution.py:231
  47.8 3.7 %collective-permute-start.8 = (bf16[256,256]{1,0:T(8,128)(2,1)S(1)}, bf16[256,256]{1,0:T(8,128)(2,1)S(1)}, u32[]{:S(2)}, u32[]{:S(2)}) collective-permute-start(bf16[256,256]{1,0:T(8,128)(2,1)S(1)} %collective-permute-done.6), channel_id=1, source_target_pairs={{0,14},{1,15},{2,0},{3,1},{4,2},{5,3},{6,4},{7,5},{8,6},{9,7},{10,... | collective-permute-start | bytes 393224 | tf_op jit(solution)/shard_map/ppermute | solution.py:231
  51.6 5.5 %collective-permute-start.11 = (bf16[1280,256]{1,0:T(8,128)(2,1)S(1)}, bf16[1280,256]{1,0:T(8,128)(2,1)}, u32[]{:S(2)}, u32[]{:S(2)}) collective-permute-start(bf16[1280,256]{1,0:T(8,128)(2,1)S(1)} %constant_dynamic-update-slice_fusion.near_ref), channel_id=1, source_target_pairs={{0,1},{1,0},{2,3},{3,2},{4,5},{5,4},{6,7},{7,6},{8,9},{9,8},{10,11... | collective-permute-start | bytes 1966088 | tf_op jit(solution)/shard_map/ppermute | solution.py:231
  57.2 6.1 %collective-permute-start.12 = (bf16[768,256]{1,0:T(8,128)(2,1)S(1)}, bf16[768,256]{1,0:T(8,128)(2,1)}, u32[]{:S(2)}, u32[]{:S(2)}) collective-permute-start(bf16[768,256]{1,0:T(8,128)(2,1)S(1)} %constant_dynamic-update-slice_fusion.5.far_ref), channel_id=1, source_target_pairs={{0,1},{1,0},{2,3},{3,2},{4,5},{5,4},{6,7},{7,6},{8,9},{9,8},{10,11... | collective-permute-start | bytes 1179656 | tf_op jit(solution)/shard_map/ppermute | solution.py:231
  63.3 0.8 %copy-done.1 = bf16[768,256]{1,0:T(8,128)(2,1)} copy-done((bf16[768,256]{1,0:T(8,128)(2,1)}, bf16[768,256]{1,0:T(8,128)(2,1)S(1)}, u32[]{:S(2)}) %copy-start.1) | copy-done | bytes 393240
  64.8 1.0 %copy-done.2 = bf16[768,256]{1,0:T(8,128)(2,1)S(1)} copy-done((bf16[768,256]{1,0:T(8,128)(2,1)S(1)}, bf16[768,256]{1,0:T(8,128)(2,1)}, u32[]{:S(2)}) %copy-start.2) | copy-done | bytes 393240
  65.8 3.6 %hole.1.far_hole_ref = f32[2,256,256]{2,1,0:T(8,128)S(1)} custom-call(s32[2]{0:T(128)S(1)} %pad_add_fusion.place_ref, bf16[256,4096]{1,0:T(8,128)(2,1)} %far_pair_ref.1, f32[256,1]{1,0:T(8,128)S(1)} %copy.7.occ_ref, f32[1,256]{1,0:T(1,128)S(1)} %bitcast.6, bf16[1280,256]{1,0:T(8,128)(2,1)S(1)} %constant_dynamic-update-slice_fusion.near_ref, ...), custom_call_target="tpu_custom_call" | custom-call | flops 1073741824 | bytes 4194304 | tf_op jit(solution)/shard_map/hole/pallas_call | solution.py:319
  69.4 1.6 %finish.1 = f32[256,256]{1,0:T(8,128)} custom-call(s16[16,272,256]{2,1,0:T(8,128)(2,1)S(1)} %all-to-all-done.coded_ref, f32[2,256,256]{2,1,0:T(8,128)S(1)} %hole.1.far_hole_ref), custom_call_target="tpu_custom_call" | custom-call | flops 8388608 | bytes 4194304 | tf_op jit(solution)/shard_map/finish/pallas_call | solution.py:343
  (42 shorter events, 2.0 us)
Async XLA Ops:
  0.0 9.1 %copy-start.5 = (s32[4096]{0:T(1024)S(1)}, s32[4096]{0:T(1024)}, u32[]{:S(2)}) copy-start(s32[4096]{0:T(1024)} %param.9) | copy-start | bytes 49156
  4.3 6.6 %collective-permute-start = (bf16[128,256]{1,0:T(8,128)(2,1)}, bf16[128,256]{1,0:T(8,128)(2,1)S(1)}, u32[]{:S(2)}, u32[]{:S(2)}) collective-permute-start(bf16[128,256]{1,0:T(8,128)(2,1)} %get-tuple-element.15), channel_id=1, source_target_pairs={{0,64},{16,80},{32,96},{48,112},{64,128},{80,144},{96,160},{112,17... | collective-permute-start | bytes 196616 | tf_op jit(solution)/shard_map/ppermute | solution.py:247
  6.4 4.4 %collective-permute-start.1 = (bf16[128,256]{1,0:T(8,128)(2,1)}, bf16[128,256]{1,0:T(8,128)(2,1)S(1)}, u32[]{:S(2)}, u32[]{:S(2)}) collective-permute-start(bf16[128,256]{1,0:T(8,128)(2,1)} %get-tuple-element.16), channel_id=1, source_target_pairs={{0,192},{16,208},{32,224},{48,240},{64,0},{80,16},{96,32},{112,48}... | collective-permute-start | bytes 196616 | tf_op jit(solution)/shard_map/ppermute | solution.py:247
  7.7 5.0 %collective-permute-start.2 = (bf16[128,256]{1,0:T(8,128)(2,1)}, bf16[128,256]{1,0:T(8,128)(2,1)S(1)}, u32[]{:S(2)}, u32[]{:S(2)}) collective-permute-start(bf16[128,256]{1,0:T(8,128)(2,1)} %get-tuple-element.17), channel_id=1, source_target_pairs={{0,16},{16,32},{32,48},{48,0},{64,80},{80,96},{96,112},{112,64},{1... | collective-permute-start | bytes 196616 | tf_op jit(solution)/shard_map/ppermute | solution.py:247
  9.1 0.7 %copy-start.6 = (s32[16,256]{1,0:T(8,128)S(1)}, s32[16,256]{1,0:T(8,128)}, u32[]{:S(2)}) copy-start(s32[16,256]{1,0:T(8,128)} %get-tuple-element.12.refs_2_) | copy-start | bytes 49156
  9.9 9.1 %copy-start = (bf16[256,2048]{1,0:T(8,128)(2,1)S(1)}, bf16[256,2048]{1,0:T(8,128)(2,1)}, u32[]{:S(2)}) copy-start(bf16[256,2048]{1,0:T(8,128)(2,1)} %amp_ref.1) | copy-start | bytes 3145732
  12.7 0.8 %copy-start.3 = (bf16[128,256]{1,0:T(8,128)(2,1)S(1)}, bf16[128,256]{1,0:T(8,128)(2,1)}, u32[]{:S(2)}) copy-start(bf16[128,256]{1,0:T(8,128)(2,1)} %get-tuple-element.14.refs_0_) | copy-start | bytes 196612
  14.9 13.8 %all-to-all-start.1 = ((bf16[16,80,256]{2,1,0:T(8,128)(2,1)}), bf16[16,80,256]{2,1,0:T(8,128)(2,1)S(1)}, u32[]{:S(2)}, u32[]{:S(2)}) async-start(bf16[16,80,256]{2,1,0:T(8,128)(2,1)} %forward.1.after_ref), calls=%async_computation.1 | async-start | bytes 1310720 | tf_op jit(solution)/shard_map/all_to_all | solution.py:278
  28.8 40.6 %all-to-all-start = ((s16[16,272,256]{2,1,0:T(8,128)(2,1)}), s16[16,272,256]{2,1,0:T(8,128)(2,1)S(1)}, u32[]{:S(2)}, u32[]{:S(2)}) async-start(s16[16,272,256]{2,1,0:T(8,128)(2,1)} %ladder.1.after_ref), calls=%async_computation | async-start | bytes 4456448 | tf_op jit(solution)/shard_map/all_to_all | solution.py:298
  34.5 29.6 %copy-start.7 = (f32[256]{0:T(256)S(1)}, f32[256]{0:T(256)}, u32[]{:S(2)}) copy-start(f32[256]{0:T(256)} %param.10) | copy-start | bytes 3076
  34.5 30.3 %copy-start.4 = (f32[256]{0:T(256)S(1)}, f32[256]{0:T(256)}, u32[]{:S(2)}) copy-start(f32[256]{0:T(256)} %param.11) | copy-start | bytes 3076
  34.9 9.3 %collective-permute-start.6 = (bf16[256,256]{1,0:T(8,128)(2,1)S(1)}, bf16[256,256]{1,0:T(8,128)(2,1)S(1)}, u32[]{:S(2)}, u32[]{:S(2)}) collective-permute-start(bf16[256,256]{1,0:T(8,128)(2,1)S(1)} %settle.1), channel_id=1, source_target_pairs={{0,12},{1,13},{2,14},{3,15},{4,0},{5,1},{6,2},{7,3},{8,4},{9,5},{1... | collective-permute-start | bytes 393224 | tf_op jit(solution)/shard_map/ppermute | solution.py:231
  41.0 6.8 %collective-permute-start.5 = (bf16[256,256]{1,0:T(8,128)(2,1)S(1)}, bf16[256,256]{1,0:T(8,128)(2,1)S(1)}, u32[]{:S(2)}, u32[]{:S(2)}) collective-permute-start(bf16[256,256]{1,0:T(8,128)(2,1)S(1)} %settle.1), channel_id=1, source_target_pairs={{0,4},{1,5},{2,6},{3,7},{4,8},{5,9},{6,10},{7,11},{8,12},{9,13},{1... | collective-permute-start | bytes 393224 | tf_op jit(solution)/shard_map/ppermute | solution.py:231
  41.0 10.5 %collective-permute-start.3 = (bf16[256,256]{1,0:T(8,128)(2,1)S(1)}, bf16[256,256]{1,0:T(8,128)(2,1)S(1)}, u32[]{:S(2)}, u32[]{:S(2)}) collective-permute-start(bf16[256,256]{1,0:T(8,128)(2,1)S(1)} %settle.1), channel_id=1, source_target_pairs={{0,2},{1,3},{2,4},{3,5},{4,6},{5,7},{6,8},{7,9},{8,10},{9,11},{10,... | collective-permute-start | bytes 393224 | tf_op jit(solution)/shard_map/ppermute | solution.py:231
  41.8 9.8 %collective-permute-start.4 = (bf16[256,256]{1,0:T(8,128)(2,1)S(1)}, bf16[256,256]{1,0:T(8,128)(2,1)S(1)}, u32[]{:S(2)}, u32[]{:S(2)}) collective-permute-start(bf16[256,256]{1,0:T(8,128)(2,1)S(1)} %settle.1), channel_id=1, source_target_pairs={{0,14},{1,15},{2,0},{3,1},{4,2},{5,3},{6,4},{7,5},{8,6},{9,7},{10,... | collective-permute-start | bytes 393224 | tf_op jit(solution)/shard_map/ppermute | solution.py:231
  44.2 13.0 %collective-permute-start.10 = (bf16[128,256]{1,0:T(8,128)(2,1)S(1)}, bf16[128,256]{1,0:T(8,128)(2,1)S(1)}, u32[]{:S(2)}, u32[]{:S(2)}) collective-permute-start(bf16[128,256]{1,0:T(8,128)(2,1)S(1)} %slice.9), channel_id=1, source_target_pairs={{0,12},{1,13},{2,14},{3,15},{4,0},{5,1},{6,2},{7,3},{8,4},{9,5},{1... | collective-permute-start | bytes 196616 | tf_op jit(solution)/shard_map/ppermute | solution.py:231
  47.8 9.4 %collective-permute-start.9 = (bf16[128,256]{1,0:T(8,128)(2,1)S(1)}, bf16[128,256]{1,0:T(8,128)(2,1)S(1)}, u32[]{:S(2)}, u32[]{:S(2)}) collective-permute-start(bf16[128,256]{1,0:T(8,128)(2,1)S(1)} %slice.8), channel_id=1, source_target_pairs={{0,4},{1,5},{2,6},{3,7},{4,8},{5,9},{6,10},{7,11},{8,12},{9,13},{1... | collective-permute-start | bytes 196616 | tf_op jit(solution)/shard_map/ppermute | solution.py:231
  47.8 9.3 %collective-permute-start.8 = (bf16[256,256]{1,0:T(8,128)(2,1)S(1)}, bf16[256,256]{1,0:T(8,128)(2,1)S(1)}, u32[]{:S(2)}, u32[]{:S(2)}) collective-permute-start(bf16[256,256]{1,0:T(8,128)(2,1)S(1)} %collective-permute-done.6), channel_id=1, source_target_pairs={{0,14},{1,15},{2,0},{3,1},{4,2},{5,3},{6,4},{7,5},{8,6},{9,7},{10,... | collective-permute-start | bytes 393224 | tf_op jit(solution)/shard_map/ppermute | solution.py:231
  51.5 5.6 %collective-permute-start.7 = (bf16[256,256]{1,0:T(8,128)(2,1)S(1)}, bf16[256,256]{1,0:T(8,128)(2,1)S(1)}, u32[]{:S(2)}, u32[]{:S(2)}) collective-permute-start(bf16[256,256]{1,0:T(8,128)(2,1)S(1)} %collective-permute-done.5), channel_id=1, source_target_pairs={{0,2},{1,3},{2,4},{3,5},{4,6},{5,7},{6,8},{7,9},{8,10},{9,11},{10,... | collective-permute-start | bytes 393224 | tf_op jit(solution)/shard_map/ppermute | solution.py:231
  51.6 13.2 %collective-permute-start.11 = (bf16[1280,256]{1,0:T(8,128)(2,1)S(1)}, bf16[1280,256]{1,0:T(8,128)(2,1)}, u32[]{:S(2)}, u32[]{:S(2)}) collective-permute-start(bf16[1280,256]{1,0:T(8,128)(2,1)S(1)} %constant_dynamic-update-slice_fusion.near_ref), channel_id=1, source_target_pairs={{0,1},{1,0},{2,3},{3,2},{4,5},{5,4},{6,7},{7,6},{8,9},{9,8},{10,11... | collective-permute-start | bytes 1966088 | tf_op jit(solution)/shard_map/ppermute | solution.py:231
  57.2 7.6 %collective-permute-start.12 = (bf16[768,256]{1,0:T(8,128)(2,1)S(1)}, bf16[768,256]{1,0:T(8,128)(2,1)}, u32[]{:S(2)}, u32[]{:S(2)}) collective-permute-start(bf16[768,256]{1,0:T(8,128)(2,1)S(1)} %constant_dynamic-update-slice_fusion.5.far_ref), channel_id=1, source_target_pairs={{0,1},{1,0},{2,3},{3,2},{4,5},{5,4},{6,7},{7,6},{8,9},{9,8},{10,11... | collective-permute-start | bytes 1179656 | tf_op jit(solution)/shard_map/ppermute | solution.py:231
  63.3 0.8 %copy-start.1 = (bf16[768,256]{1,0:T(8,128)(2,1)}, bf16[768,256]{1,0:T(8,128)(2,1)S(1)}, u32[]{:S(2)}) copy-start(bf16[768,256]{1,0:T(8,128)(2,1)S(1)} %constant_dynamic-update-slice_fusion.5.far_ref) | copy-start | bytes 1179652
  64.8 1.0 %copy-start.2 = (bf16[768,256]{1,0:T(8,128)(2,1)S(1)}, bf16[768,256]{1,0:T(8,128)(2,1)}, u32[]{:S(2)}) copy-start(bf16[768,256]{1,0:T(8,128)(2,1)} %copy-done.1) | copy-start | bytes 1179652

commit v5 on v4

--- a/solution.py
+++ b/solution.py
@@ -79,19 +79,19 @@
     columns = (found[:DEPTH] * 64.0 + found[DEPTH:]).astype(jnp.int32)
     span = amp_ref.shape[1]
     lane = iota((DEPTH, span), 1)
+    order = [j for hop in range(len(HOPS)) for j in range(hop, CHUNKS, len(HOPS))]
+    chosen = jnp.concatenate(
+        [ones_where(lane == columns[:, j : j + 1]).astype(jnp.bfloat16) for j in order], 0
+    )
     fetch.wait()
+    got = bdot(chosen, amp_ref[...], ((1,), (1,))).astype(jnp.bfloat16)
     for hop, sent_ref in enumerate(sent_refs):
-        chosen = jnp.concatenate(
-            [
-                ones_where(lane == columns[:, j : j + 1]).astype(jnp.bfloat16)
-                for j in range(hop, CHUNKS, 4)
-            ],
-            0,
-        )
-        sent_ref[...] = bdot(chosen, amp_ref[...], ((1,), (1,))).astype(jnp.bfloat16)
-
-
-def route_kernel(shift, here_ref, index_ref, rank_ref, forward_ref, settle_ref):
+        sent_ref[...] = got[hop * 4 * DEPTH : (hop + 1) * 4 * DEPTH]
+
+
+def route_kernel(shift, here_ref, index_ref, rank_ref, kept_ref, *refs):
+    forward_ref, settle_ref, stay_ref = refs
+    stay_ref[...] = kept_ref[...]
     index, rank, here = widen(index_ref), rank_ref[...], here_ref[0]
     owner = jnp.right_shift(index, shift)
     last, depth = rank & 15, jnp.right_shift(rank, 4)
@@ -116,8 +116,8 @@
 
 
 def forward_kernel(forward_ref, *refs):
-    *first_refs, moved_ref = refs
-    arrived = jnp.concatenate([ref[...] for ref in first_refs], 0)
+    *come_refs, moved_ref = refs
+    arrived = jnp.concatenate([ref[...] for ref in come_refs], 0)
     moved = bdot(forward_ref[...], arrived).astype(jnp.bfloat16)
     moved_ref[...] = moved.reshape(moved_ref.shape)
 
@@ -166,52 +166,66 @@
         out.wait()
 
 
+def either_kernel(core_ref, zero_ref, one_ref, out_ref):
+    @pl.when(core_ref[0] == 0)
+    def _():
+        out_ref[...] = zero_ref[...]
+
+    @pl.when(core_ref[0] != 0)
+    def _():
+        out_ref[...] = one_ref[...]
+
+
 def hole_kernel(place_ref, far_pair_ref, occ_ref, virt_ref, near_ref, far_ref, *refs):
-    *away_refs, out_ref, pair_ref, near_sibling_ref, far_sibling_ref, sems = refs
+    near_sibling_ref, far_sibling_ref, out_ref, pair_ref, sems = refs
+    z, core = place_ref[0], place_ref[1]
+    rows = near_ref.shape[0] // 5
+    blocks = [
+        (group, k, chips, which)
+        for near, far, which in (
+            (near_ref, far_ref, core),
+            (near_sibling_ref, far_sibling_ref, 1 - core),
+        )
+        for group, away in ((near, (0, 1, -1, 2, -2)), (far, (3, -3, 4)))
+        for k, chips in enumerate(away)
+    ]
+    fetches = []
+    for slot, (_, _, chips, which) in enumerate(blocks):
+        n = jnp.bitwise_and(z - chips + 8, 7) * 2 + which
+        columns = far_pair_ref.at[:, pl.ds(pl.multiple_of(n * rows, rows), rows)]
+        fetches.append(pltpu.make_async_copy(columns, pair_ref.at[slot], sems.at[slot]))
+        fetches[slot].start()
+    out_ref[1] = virt_ref[...] - occ_ref[...]
+    total = jnp.zeros(out_ref.shape[1:], jnp.float32)
+    for slot, (group, k, _, _) in enumerate(blocks):
+        fetches[slot].wait()
+        block = group[k * rows : (k + 1) * rows]
+        total = total + jnp.dot(pair_ref[slot], block, preferred_element_type=jnp.float32)
+    out_ref[0] = total
+
+
+def finish_kernel(far_coded_ref, far_hole_ref, out_ref, coded_ref, hole_ref, sems):
+    rows = out_ref.shape[0]
+    group = CHUNKS // 4
     fetches = [
-        pltpu.make_async_copy(source, target, sems.at[k])
-        for k, (source, target) in enumerate(
-            zip([far_pair_ref] + away_refs, [pair_ref, near_sibling_ref, far_sibling_ref])
-        )
+        pltpu.make_async_copy(
+            far_coded_ref.at[pl.ds(k * group, group)],
+            coded_ref.at[pl.ds(k * group, group)],
+            sems.at[k],
+        )
+        for k in range(4)
     ]
+    fetches.append(pltpu.make_async_copy(far_hole_ref, hole_ref, sems.at[4]))
     for fetch in fetches:
         fetch.start()
-    z, core = place_ref[0], place_ref[1]
-    rows = near_ref.shape[0] // 5
-    half = rows // 2
-    total = jnp.zeros(out_ref.shape[1:], jnp.float32)
-
-    def add(total, away, which, start, block):
-        n = jnp.bitwise_and(z - away + 8, 7) * 2 + which
-        columns = pl.ds(pl.multiple_of(n * rows + start, 128), block.shape[0])
-        return total + jnp.dot(pair_ref[:, columns], block, preferred_element_type=jnp.float32)
-
-    out_ref[1] = virt_ref[...] - occ_ref[...]
-    fetches[0].wait()
-    sides = ((near_ref, far_ref, core), (near_sibling_ref, far_sibling_ref, 1 - core))
-    for near, far, which in sides:
-        if near is near_sibling_ref:
-            fetches[1].wait()
-            fetches[2].wait()
-        for k, away in enumerate((0, 1, -1, 2, -2)):
-            total = add(total, away, which, 0, near[k * rows : (k + 1) * rows])
-        total = add(total, 3, which, 0, far[:rows])
-        total = add(total, -3, which, 0, far[rows : 2 * rows])
-        total = add(total, 4, which, 0, far[2 * rows : 2 * rows + half])
-        total = add(total, 4, which, half, far[2 * rows + half :])
-    out_ref[0] = total
-
-
-def finish_kernel(coded_ref, far_hole_ref, out_ref, hole_ref, hole_sem):
-    fetch = pltpu.make_async_copy(far_hole_ref, hole_ref, hole_sem)
-    fetch.start()
-    rows = out_ref.shape[0]
     ladder = jnp.zeros(out_ref.shape, jnp.float32)
     for k in range(CHUNKS):
+        if k % group == 0:
+            fetches[k // group].wait()
         code = coded_ref[k, rows:, :].astype(jnp.int32).astype(jnp.float32)[:1, :]
         values = coded_ref[k, :rows, :].astype(jnp.int32).astype(jnp.float32)
         ladder = ladder + values * jnp.exp2(code * (1.0 / STEPS))
-    fetch.wait()
+    fetches[4].wait()
     out_ref[...] = (ladder * (1.0 / TOP) + hole_ref[0]) / hole_ref[1]
 
 
@@ -222,11 +236,13 @@
     shift = span.bit_length() - 1
     here = wide_index.astype(jnp.int32).reshape(1)
     index = slab_index.reshape(2 * CHUNKS, LANES // 2)
-    half = height // 2
-
-    def step(value, dz, dc=0):
+    core = narrow_index & 1
+
+    def step(value, dz, dc=0, turn=1):
         ring = [
-            (z * 2 + c, (z + dz) % 8 * 2 + (c + dc) % 2) for z in range(8) for c in range(2)
+            (z * 2 + c, (z + (turn if c else 1) * dz) % 8 * 2 + (c + dc) % 2)
+            for z in range(8)
+            for c in range(2)
         ]
         return lax.ppermute(value, "narrow", ring)
 
@@ -243,7 +259,7 @@
         cost_estimate=pl.CostEstimate(flops=2**30, bytes_accessed=2**21, transcendentals=0),
         name="select",
     )(here, index, amplitudes)
-    first = sent[:1] + [
+    came = [
         lax.ppermute(
             sent[k],
             "wide",
@@ -253,18 +269,19 @@
         if k
     ]
 
-    forward, settle = pl.pallas_call(
+    forward, settle, stay = pl.pallas_call(
         lambda *refs: route_kernel(shift, *refs),
         out_shape=(
             jax.ShapeDtypeStruct((CHUNKS * ROOM, CHUNKS * DEPTH), jnp.bfloat16),
             jax.ShapeDtypeStruct((CHUNKS * ROOM, LANES), jnp.bfloat16),
+            jax.ShapeDtypeStruct(sent[0].shape, jnp.bfloat16),
         ),
-        in_specs=[SMEM, VMEM, VMEM],
-        out_specs=(VMEM, VMEM),
+        in_specs=[SMEM, VMEM, VMEM, VMEM],
+        out_specs=(VMEM, VMEM, VMEM),
         compiler_params=pltpu.CompilerParams(vmem_limit_bytes=16 << 20),
         cost_estimate=pl.CostEstimate(flops=2**28, bytes_accessed=2**20, transcendentals=0),
         name="route",
-    )(here, index, rank)
+    )(here, index, rank, sent[0])
 
     moved = pl.pallas_call(
         forward_kernel,
@@ -274,7 +291,7 @@
         compiler_params=pltpu.CompilerParams(vmem_limit_bytes=8 << 20),
         cost_estimate=pl.CostEstimate(flops=2**28, bytes_accessed=2**20, transcendentals=0),
         name="forward",
-    )(forward, *first)
+    )(forward, stay, *came)
     second = lax.all_to_all(moved, "wide", 0, 0, tiled=True)
 
     slabs = CHUNKS // PER
@@ -309,23 +326,30 @@
 
     up, down, up2, down2 = step(own, 1), step(own, -1), step(own, 2), step(own, -2)
     up3, down3 = step(up2, 1), step(down2, -1)
-    up4, down4 = step(up2[:half], 2), step(down2[half:], -2)
+    two = pl.pallas_call(
+        either_kernel,
+        out_shape=jax.ShapeDtypeStruct(up2.shape, jnp.bfloat16),
+        in_specs=[SMEM, VMEM, VMEM],
+        out_specs=VMEM,
+        compiler_params=pltpu.CompilerParams(vmem_limit_bytes=4 << 20),
+        cost_estimate=pl.CostEstimate(flops=0, bytes_accessed=2**18, transcendentals=0),
+        name="either",
+    )(core.astype(jnp.int32).reshape(1), up2, down2)
+    four = step(two, 2, turn=-1)
     near = jnp.concatenate([own, up, down, up2, down2], 0)
     near_sibling = step(near, 0, 1)
-    far = jnp.concatenate([up3, down3, up4, down4], 0)
+    far = jnp.concatenate([up3, down3, four], 0)
     far_sibling = step(far, 0, 1)
 
-    where = jnp.stack([narrow_index >> 1, narrow_index & 1]).astype(jnp.int32)
+    where = jnp.stack([narrow_index >> 1, core]).astype(jnp.int32)
     hole = pl.pallas_call(
         hole_kernel,
         out_shape=jax.ShapeDtypeStruct((2, height, LANES), jnp.float32),
-        in_specs=[SMEM, HBM] + [VMEM] * 4 + [HBM] * 2,
+        in_specs=[SMEM, HBM] + [VMEM] * 6,
         out_specs=VMEM,
         scratch_shapes=[
-            pltpu.VMEM(pair_integrals.shape, jnp.bfloat16),
-            pltpu.VMEM(near.shape, jnp.bfloat16),
-            pltpu.VMEM(far.shape, jnp.bfloat16),
-            pltpu.SemaphoreType.DMA((3,)),
+            pltpu.VMEM((CHUNKS, height, height), jnp.bfloat16),
+            pltpu.SemaphoreType.DMA((CHUNKS,)),
         ],
         compiler_params=pltpu.CompilerParams(vmem_limit_bytes=50 << 20),
         cost_estimate=pl.CostEstimate(flops=2**30, bytes_accessed=2**22, transcendentals=0),
@@ -343,13 +367,14 @@
     return pl.pallas_call(
         finish_kernel,
         out_shape=jax.ShapeDtypeStruct((height, LANES), jnp.float32),
-        in_specs=[VMEM, HBM],
+        in_specs=[HBM] * 2,
         out_specs=VMEM,
         scratch_shapes=[
-            pltpu.VMEM((2, height, LANES), jnp.float32),
-            pltpu.SemaphoreType.DMA(()),
+            pltpu.VMEM(shares.shape, jnp.int16),
+            pltpu.VMEM(hole.shape, jnp.float32),
+            pltpu.SemaphoreType.DMA((5,)),
         ],
-        compiler_params=pltpu.CompilerParams(vmem_limit_bytes=20 << 20),
+        compiler_params=pltpu.CompilerParams(vmem_limit_bytes=54 << 20),
         cost_estimate=pl.CostEstimate(flops=2**23, bytes_accessed=2**22, transcendentals=0),
         name="finish",
     )(shares, hole)

time: 71.6 us -> 71.3 us (level)
  waiting for transfers between devices: 4.13 us -> 7.43 us
  starting transfers between devices: 42 us -> 38.8 us
  local copies, waits for them, and re-layouts: 3.56 us -> 2.58 us
    ppermute x10 -> x9, waiting for transfers between devices: 1.28 us -> 5.21 us  [step(): return lax.ppermute(value, 'narrow', ring)]
    ppermute x10 -> x9, starting transfers between devices: 27.4 us -> 24.2 us  [step(): return lax.ppermute(value, 'narrow', ring)]
    pallas_call x1, Pallas kernels: 1.63 us -> 2.74 us  [on_device(): pl.pallas_call(finish_kernel, out_shape=jax.ShapeDtypeStruct((height, LAN...]
    unnamed x23 -> x20, local copies, waits for them, and re-layouts: 3.4 us -> 2.42 us
    ppermute x3, waiting for transfers between devices: 1.91 us -> 1.07 us  [on_device(): lax.ppermute(sent[k], 'wide', [(x * 4 + y, (x + dx) % 4 * 4 + (y + dy) %...]
  transfers between devices with their start and end apart: 15 -> 14, of which waited for: 4 -> 5; matrix products, arithmetic and copies ran while one was open for 0% -> 0% of each run, Pallas kernels for 19% -> 19%
where the time goes in v5:
time: 71.3 us; the launch traced here: 70.9 us
  starting transfers between devices  38.8 us (54%)
  Pallas kernels  21.6 us (30%)
  waiting for transfers between devices  7.43 us (10%)
  local copies, waits for them, and re-layouts  2.58 us (4%)
    ppermute x9, starting transfers between devices, step(): return lax.ppermute(value, 'narrow', ring)  24.2 us
    pallas_call x1, Pallas kernels, on_device(): pl.pallas_call(ladder_kernel, out_shape=jax.ShapeDtypeStruct((CHUNKS, hei...  8.9 us
    all_to_all x1, starting transfers between devices, on_device(): shares = lax.all_to_all(coded, 'wide', 0, 0, tiled=True)  5.57 us
    ppermute x9, waiting for transfers between devices, step(): return lax.ppermute(value, 'narrow', ring)  5.21 us
    ppermute x3, starting transfers between devices, on_device(): lax.ppermute(sent[k], 'wide', [(x * 4 + y, (x + dx) % 4 * 4 + (y + dy) %...  4.88 us
    all_to_all x1, starting transfers between devices, on_device(): second = lax.all_to_all(moved, 'wide', 0, 0, tiled=True)  4.2 us
    pallas_call x1, Pallas kernels, on_device(): pl.pallas_call(lambda *refs: select_kernel(shift, *refs), out_shape=(*[ja...  3.79 us
    pallas_call x1, Pallas kernels, on_device(): pl.pallas_call(hole_kernel, out_shape=jax.ShapeDtypeStruct((2, height, LA...  3.48 us
  transfers between devices with their start and end apart: 14, of which 5 were waited for; matrix products, arithmetic and copies ran while one was open for 0% of the time, Pallas kernels for 19%

profile of v5, /device:TPU:1, one launch (start us, length us, event | category | flops | bytes accessed | tf_op | source)
XLA Modules:
  0.0 70.9 jit_solution(8216910553705470885)
XLA Ops:
  0.0 3.8 %select.1 = (bf16[128,256]{1,0:T(8,128)(2,1)}, bf16[128,256]{1,0:T(8,128)(2,1)}, bf16[128,256]{1,0:T(8,128)(2,1)}, bf16[128,256]{1,0:T(8,128)(2,1)}, s32[16,256]{1,0:T(8,128)}) custom-call(s32[1]{0:T(128)} %bitcast.refs_0_, s32[32,128]{1,0:T(8,128)} %bitcast.7, bf16[256,2048]{1,0:T(8,128)(2,1)} %amp_ref.1), custom_call_target="tpu_custom_call" | custom-call | flops 1073741824 | bytes 2097152 | tf_op jit(solution)/shard_map/select/pallas_call | solution.py:249
  3.8 2.1 %collective-permute-start = (bf16[128,256]{1,0:T(8,128)(2,1)}, bf16[128,256]{1,0:T(8,128)(2,1)S(1)}, u32[]{:S(2)}, u32[]{:S(2)}) collective-permute-start(bf16[128,256]{1,0:T(8,128)(2,1)} %get-tuple-element.17), channel_id=1, source_target_pairs={{0,64},{16,80},{32,96},{48,112},{64,128},{80,144},{96,160},{112,17... | collective-permute-start | bytes 196616 | tf_op jit(solution)/shard_map/ppermute | solution.py:263
  5.9 1.4 %collective-permute-start.1 = (bf16[128,256]{1,0:T(8,128)(2,1)}, bf16[128,256]{1,0:T(8,128)(2,1)S(1)}, u32[]{:S(2)}, u32[]{:S(2)}) collective-permute-start(bf16[128,256]{1,0:T(8,128)(2,1)} %get-tuple-element.18), channel_id=1, source_target_pairs={{0,192},{16,208},{32,224},{48,240},{64,0},{80,16},{96,32},{112,48}... | collective-permute-start | bytes 196616 | tf_op jit(solution)/shard_map/ppermute | solution.py:263
  7.3 1.4 %collective-permute-start.2 = (bf16[128,256]{1,0:T(8,128)(2,1)}, bf16[128,256]{1,0:T(8,128)(2,1)S(1)}, u32[]{:S(2)}, u32[]{:S(2)}) collective-permute-start(bf16[128,256]{1,0:T(8,128)(2,1)} %get-tuple-element.19), channel_id=1, source_target_pairs={{0,16},{16,32},{32,48},{48,0},{64,80},{80,96},{96,112},{112,64},{1... | collective-permute-start | bytes 196616 | tf_op jit(solution)/shard_map/ppermute | solution.py:263
  8.7 0.8 %copy-done.4 = bf16[128,256]{1,0:T(8,128)(2,1)S(1)} copy-done((bf16[128,256]{1,0:T(8,128)(2,1)S(1)}, bf16[128,256]{1,0:T(8,128)(2,1)}, u32[]{:S(2)}) %copy-start.4) | copy-done | bytes 65560
  9.5 0.7 %copy-done.5 = s32[16,256]{1,0:T(8,128)S(1)} copy-done((s32[16,256]{1,0:T(8,128)S(1)}, s32[16,256]{1,0:T(8,128)}, u32[]{:S(2)}) %copy-start.5) | copy-done | bytes 16408
  10.2 0.9 %route.1 = (bf16[1280,512]{1,0:T(8,128)(2,1)S(1)}, bf16[1280,256]{1,0:T(8,128)(2,1)S(1)}, bf16[128,256]{1,0:T(8,128)(2,1)S(1)}) custom-call(s32[1]{0:T(128)} %bitcast.refs_0_, s32[32,128]{1,0:T(8,128)S(1)} %bitcast.8, s32[16,256]{1,0:T(8,128)S(1)} %copy-done.5, bf16[128,256]{1,0:T(8,128)(2,1)S(1)} %copy-done.4), custom_call_target="tpu_custom_call" | custom-call | flops 268435456 | bytes 1048576 | tf_op jit(solution)/shard_map/route/pallas_call | solution.py:272
  11.2 1.1 %collective-permute-done.2.refs_3_ = bf16[128,256]{1,0:T(8,128)(2,1)S(1)} collective-permute-done((bf16[128,256]{1,0:T(8,128)(2,1)}, bf16[128,256]{1,0:T(8,128)(2,1)S(1)}, u32[]{:S(2)}, u32[]{:S(2)}) %collective-permute-start.2) | collective-permute-done | bytes 65568 | tf_op jit(solution)/shard_map/ppermute | solution.py:263
  12.3 1.3 %forward.1.after_ref = bf16[16,80,256]{2,1,0:T(8,128)(2,1)} custom-call(bf16[1280,512]{1,0:T(8,128)(2,1)S(1)} %get-tuple-element.15.forward_ref, bf16[128,256]{1,0:T(8,128)(2,1)S(1)} %get-tuple-element.16.refs_0_, bf16[128,256]{1,0:T(8,128)(2,1)S(1)} %collective-permute-done.refs_1_, bf16[128,256]{1,0:T(8,128)(2,1)S(1)} %collective-permute-done.1.refs_2_, ...), custom_call_target="tpu_custom_call" | custom-call | flops 268435456 | bytes 1048576 | tf_op jit(solution)/shard_map/forward/pallas_call | solution.py:286
  13.6 4.2 %all-to-all-start.1 = ((bf16[16,80,256]{2,1,0:T(8,128)(2,1)}), bf16[16,80,256]{2,1,0:T(8,128)(2,1)S(1)}, u32[]{:S(2)}, u32[]{:S(2)}) async-start(bf16[16,80,256]{2,1,0:T(8,128)(2,1)} %forward.1.after_ref), calls=%async_computation.1 | async-start | bytes 1310720 | tf_op jit(solution)/shard_map/all_to_all | solution.py:295
  17.8 8.9 %ladder.1.after_ref = s16[16,272,256]{2,1,0:T(8,128)(2,1)} custom-call(bf16[256,2048]{1,0:T(8,128)(2,1)S(1)} %copy-done.1, bf16[2048,4096]{1,0:T(8,128)(2,1)} %int_ref.1, bf16[16,80,256]{2,1,0:T(8,128)(2,1)} %forward.1.after_ref), custom_call_target="tpu_custom_call" | custom-call | flops 4294967296 | bytes 18874368 | tf_op jit(solution)/shard_map/ladder/pallas_call | solution.py:298
  26.7 1.2 %all-to-all-done.1.second_ref = bf16[16,80,256]{2,1,0:T(8,128)(2,1)S(1)} async-done(((bf16[16,80,256]{2,1,0:T(8,128)(2,1)}), bf16[16,80,256]{2,1,0:T(8,128)(2,1)S(1)}, u32[]{:S(2)}, u32[]{:S(2)}) %all-to-all-start.1) | async-done | bytes 655392 | tf_op jit(solution)/shard_map/all_to_all | solution.py:295
  27.9 5.6 %all-to-all-start = ((s16[16,272,256]{2,1,0:T(8,128)(2,1)}), s16[16,272,256]{2,1,0:T(8,128)(2,1)}, u32[]{:S(2)}, u32[]{:S(2)}) async-start(s16[16,272,256]{2,1,0:T(8,128)(2,1)} %ladder.1.after_ref), calls=%async_computation | async-start | bytes 4456448 | tf_op jit(solution)/shard_map/all_to_all | solution.py:315
  33.9 6.1 %collective-permute-start.6 = (bf16[256,256]{1,0:T(8,128)(2,1)S(1)}, bf16[256,256]{1,0:T(8,128)(2,1)S(1)}, u32[]{:S(2)}, u32[]{:S(2)}) collective-permute-start(bf16[256,256]{1,0:T(8,128)(2,1)S(1)} %settle.1), channel_id=1, source_target_pairs={{0,12},{1,13},{2,14},{3,15},{4,0},{5,1},{6,2},{7,3},{8,4},{9,5},{1... | collective-permute-start | bytes 393224 | tf_op jit(solution)/shard_map/ppermute | solution.py:247
  40.0 0.7 %collective-permute-start.3 = (bf16[256,256]{1,0:T(8,128)(2,1)S(1)}, bf16[256,256]{1,0:T(8,128)(2,1)S(1)}, u32[]{:S(2)}, u32[]{:S(2)}) collective-permute-start(bf16[256,256]{1,0:T(8,128)(2,1)S(1)} %settle.1), channel_id=1, source_target_pairs={{0,2},{1,3},{2,4},{3,5},{4,6},{5,7},{6,8},{7,9},{8,10},{9,11},{10,... | collective-permute-start | bytes 393224 | tf_op jit(solution)/shard_map/ppermute | solution.py:247
  40.7 2.4 %collective-permute-start.4 = (bf16[256,256]{1,0:T(8,128)(2,1)S(1)}, bf16[256,256]{1,0:T(8,128)(2,1)S(1)}, u32[]{:S(2)}, u32[]{:S(2)}) collective-permute-start(bf16[256,256]{1,0:T(8,128)(2,1)S(1)} %settle.1), channel_id=1, source_target_pairs={{0,14},{1,15},{2,0},{3,1},{4,2},{5,3},{6,4},{7,5},{8,6},{9,7},{10,... | collective-permute-start | bytes 393224 | tf_op jit(solution)/shard_map/ppermute | solution.py:247
  43.1 3.6 %collective-permute-done.5.zero_ref = bf16[256,256]{1,0:T(8,128)(2,1)S(1)} collective-permute-done((bf16[256,256]{1,0:T(8,128)(2,1)S(1)}, bf16[256,256]{1,0:T(8,128)(2,1)S(1)}, u32[]{:S(2)}, u32[]{:S(2)}) %collective-permute-start.5) | collective-permute-done | bytes 131104 | tf_op jit(solution)/shard_map/ppermute | solution.py:247
  47.2 1.6 %collective-permute-start.8 = (bf16[256,256]{1,0:T(8,128)(2,1)S(1)}, bf16[256,256]{1,0:T(8,128)(2,1)S(1)}, u32[]{:S(2)}, u32[]{:S(2)}) collective-permute-start(bf16[256,256]{1,0:T(8,128)(2,1)S(1)} %collective-permute-done.6.one_ref), channel_id=1, source_target_pairs={{0,14},{1,15},{2,0},{3,1},{4,2},{5,3},{6,4},{7,5},{8,6},{9,7},{10,... | collective-permute-start | bytes 393224 | tf_op jit(solution)/shard_map/ppermute | solution.py:247
  49.3 6.9 %collective-permute-start.10 = (bf16[1280,256]{1,0:T(8,128)(2,1)S(1)}, bf16[1280,256]{1,0:T(8,128)(2,1)S(1)}, u32[]{:S(2)}, u32[]{:S(2)}) collective-permute-start(bf16[1280,256]{1,0:T(8,128)(2,1)S(1)} %constant_dynamic-update-slice_fusion.near_ref), channel_id=1, source_target_pairs={{0,1},{1,0},{2,3},{3,2},{4,5},{5,4},{6,7},{7,6},{8,9},{9,8},{10,11... | collective-permute-start | bytes 1966088 | tf_op jit(solution)/shard_map/ppermute | solution.py:247
  56.3 6.1 %collective-permute-start.11 = (bf16[768,256]{1,0:T(8,128)(2,1)S(1)}, bf16[768,256]{1,0:T(8,128)(2,1)S(1)}, u32[]{:S(2)}, u32[]{:S(2)}) collective-permute-start(bf16[768,256]{1,0:T(8,128)(2,1)S(1)} %constant_dynamic-update-slice_fusion.5.far_ref), channel_id=1, source_target_pairs={{0,1},{1,0},{2,3},{3,2},{4,5},{5,4},{6,7},{7,6},{8,9},{9,8},{10,11... | collective-permute-start | bytes 1179656 | tf_op jit(solution)/shard_map/ppermute | solution.py:247
  62.6 1.1 %collective-permute-done.11.refs_1_ = bf16[768,256]{1,0:T(8,128)(2,1)S(1)} collective-permute-done((bf16[768,256]{1,0:T(8,128)(2,1)S(1)}, bf16[768,256]{1,0:T(8,128)(2,1)S(1)}, u32[]{:S(2)}, u32[]{:S(2)}) %collective-permute-start.11) | collective-permute-done | bytes 393248 | tf_op jit(solution)/shard_map/ppermute | solution.py:247
  63.7 3.5 %hole.1.far_hole_ref = f32[2,256,256]{2,1,0:T(8,128)S(1)} custom-call(s32[2]{0:T(128)S(1)} %pad_add_fusion.place_ref, bf16[256,4096]{1,0:T(8,128)(2,1)} %far_pair_ref.1, f32[256,1]{1,0:T(8,128)S(1)} %copy.7.occ_ref, f32[1,256]{1,0:T(1,128)S(1)} %bitcast.6, bf16[1280,256]{1,0:T(8,128)(2,1)S(1)} %constant_dynamic-update-slice_fusion.near_ref, ...), custom_call_target="tpu_custom_call" | custom-call | flops 1073741824 | bytes 4194304 | tf_op jit(solution)/shard_map/hole/pallas_call | solution.py:345
  67.2 0.8 %copy-done = f32[2,256,256]{2,1,0:T(8,128)} copy-done((f32[2,256,256]{2,1,0:T(8,128)}, f32[2,256,256]{2,1,0:T(8,128)S(1)}, u32[]{:S(2)}) %copy-start) | copy-done | bytes 524312
  68.0 2.7 %finish.1 = f32[256,256]{1,0:T(8,128)} custom-call(s16[16,272,256]{2,1,0:T(8,128)(2,1)} %all-to-all-done.far_coded_ref, f32[2,256,256]{2,1,0:T(8,128)} %copy-done), custom_call_target="tpu_custom_call" | custom-call | flops 8388608 | bytes 4194304 | tf_op jit(solution)/shard_map/finish/pallas_call | solution.py:367
  (36 shorter events, 1.6 us)
Async XLA Ops:
  0.0 8.7 %copy-start.3 = (s32[4096]{0:T(1024)S(1)}, s32[4096]{0:T(1024)}, u32[]{:S(2)}) copy-start(s32[4096]{0:T(1024)} %param.9) | copy-start | bytes 49156
  3.8 7.4 %collective-permute-start = (bf16[128,256]{1,0:T(8,128)(2,1)}, bf16[128,256]{1,0:T(8,128)(2,1)S(1)}, u32[]{:S(2)}, u32[]{:S(2)}) collective-permute-start(bf16[128,256]{1,0:T(8,128)(2,1)} %get-tuple-element.17), channel_id=1, source_target_pairs={{0,64},{16,80},{32,96},{48,112},{64,128},{80,144},{96,160},{112,17... | collective-permute-start | bytes 196616 | tf_op jit(solution)/shard_map/ppermute | solution.py:263
  5.9 5.3 %collective-permute-start.1 = (bf16[128,256]{1,0:T(8,128)(2,1)}, bf16[128,256]{1,0:T(8,128)(2,1)S(1)}, u32[]{:S(2)}, u32[]{:S(2)}) collective-permute-start(bf16[128,256]{1,0:T(8,128)(2,1)} %get-tuple-element.18), channel_id=1, source_target_pairs={{0,192},{16,208},{32,224},{48,240},{64,0},{80,16},{96,32},{112,48}... | collective-permute-start | bytes 196616 | tf_op jit(solution)/shard_map/ppermute | solution.py:263
  7.3 5.0 %collective-permute-start.2 = (bf16[128,256]{1,0:T(8,128)(2,1)}, bf16[128,256]{1,0:T(8,128)(2,1)S(1)}, u32[]{:S(2)}, u32[]{:S(2)}) collective-permute-start(bf16[128,256]{1,0:T(8,128)(2,1)} %get-tuple-element.19), channel_id=1, source_target_pairs={{0,16},{16,32},{32,48},{48,0},{64,80},{80,96},{96,112},{112,64},{1... | collective-permute-start | bytes 196616 | tf_op jit(solution)/shard_map/ppermute | solution.py:263
  8.7 0.8 %copy-start.4 = (bf16[128,256]{1,0:T(8,128)(2,1)S(1)}, bf16[128,256]{1,0:T(8,128)(2,1)}, u32[]{:S(2)}) copy-start(bf16[128,256]{1,0:T(8,128)(2,1)} %get-tuple-element.14.refs_3_) | copy-start | bytes 196612
  9.5 0.7 %copy-start.5 = (s32[16,256]{1,0:T(8,128)S(1)}, s32[16,256]{1,0:T(8,128)}, u32[]{:S(2)}) copy-start(s32[16,256]{1,0:T(8,128)} %get-tuple-element.13.refs_2_) | copy-start | bytes 49156
  10.2 7.6 %copy-start.1 = (bf16[256,2048]{1,0:T(8,128)(2,1)S(1)}, bf16[256,2048]{1,0:T(8,128)(2,1)}, u32[]{:S(2)}) copy-start(bf16[256,2048]{1,0:T(8,128)(2,1)} %amp_ref.1) | copy-start | bytes 3145732
  13.6 14.3 %all-to-all-start.1 = ((bf16[16,80,256]{2,1,0:T(8,128)(2,1)}), bf16[16,80,256]{2,1,0:T(8,128)(2,1)S(1)}, u32[]{:S(2)}, u32[]{:S(2)}) async-start(bf16[16,80,256]{2,1,0:T(8,128)(2,1)} %forward.1.after_ref), calls=%async_computation.1 | async-start | bytes 1310720 | tf_op jit(solution)/shard_map/all_to_all | solution.py:295
  27.9 40.1 %all-to-all-start = ((s16[16,272,256]{2,1,0:T(8,128)(2,1)}), s16[16,272,256]{2,1,0:T(8,128)(2,1)}, u32[]{:S(2)}, u32[]{:S(2)}) async-start(s16[16,272,256]{2,1,0:T(8,128)(2,1)} %ladder.1.after_ref), calls=%async_computation | async-start | bytes 4456448 | tf_op jit(solution)/shard_map/all_to_all | solution.py:315
  33.5 28.9 %copy-start.6 = (f32[256]{0:T(256)S(1)}, f32[256]{0:T(256)}, u32[]{:S(2)}) copy-start(f32[256]{0:T(256)} %param.10) | copy-start | bytes 3076
  33.9 29.8 %copy-start.2 = (f32[256]{0:T(256)S(1)}, f32[256]{0:T(256)}, u32[]{:S(2)}) copy-start(f32[256]{0:T(256)} %param.11) | copy-start | bytes 3076
  33.9 9.2 %collective-permute-start.6 = (bf16[256,256]{1,0:T(8,128)(2,1)S(1)}, bf16[256,256]{1,0:T(8,128)(2,1)S(1)}, u32[]{:S(2)}, u32[]{:S(2)}) collective-permute-start(bf16[256,256]{1,0:T(8,128)(2,1)S(1)} %settle.1), channel_id=1, source_target_pairs={{0,12},{1,13},{2,14},{3,15},{4,0},{5,1},{6,2},{7,3},{8,4},{9,5},{1... | collective-permute-start | bytes 393224 | tf_op jit(solution)/shard_map/ppermute | solution.py:247
  40.0 6.8 %collective-permute-start.5 = (bf16[256,256]{1,0:T(8,128)(2,1)S(1)}, bf16[256,256]{1,0:T(8,128)(2,1)S(1)}, u32[]{:S(2)}, u32[]{:S(2)}) collective-permute-start(bf16[256,256]{1,0:T(8,128)(2,1)S(1)} %settle.1), channel_id=1, source_target_pairs={{0,4},{1,5},{2,6},{3,7},{4,8},{5,9},{6,10},{7,11},{8,12},{9,13},{1... | collective-permute-start | bytes 393224 | tf_op jit(solution)/shard_map/ppermute | solution.py:247
  40.0 9.2 %collective-permute-start.3 = (bf16[256,256]{1,0:T(8,128)(2,1)S(1)}, bf16[256,256]{1,0:T(8,128)(2,1)S(1)}, u32[]{:S(2)}, u32[]{:S(2)}) collective-permute-start(bf16[256,256]{1,0:T(8,128)(2,1)S(1)} %settle.1), channel_id=1, source_target_pairs={{0,2},{1,3},{2,4},{3,5},{4,6},{5,7},{6,8},{7,9},{8,10},{9,11},{10,... | collective-permute-start | bytes 393224 | tf_op jit(solution)/shard_map/ppermute | solution.py:247
  40.7 8.5 %collective-permute-start.4 = (bf16[256,256]{1,0:T(8,128)(2,1)S(1)}, bf16[256,256]{1,0:T(8,128)(2,1)S(1)}, u32[]{:S(2)}, u32[]{:S(2)}) collective-permute-start(bf16[256,256]{1,0:T(8,128)(2,1)S(1)} %settle.1), channel_id=1, source_target_pairs={{0,14},{1,15},{2,0},{3,1},{4,2},{5,3},{6,4},{7,5},{8,6},{9,7},{10,... | collective-permute-start | bytes 393224 | tf_op jit(solution)/shard_map/ppermute | solution.py:247
  46.8 9.4 %collective-permute-start.9 = (bf16[256,256]{1,0:T(8,128)(2,1)S(1)}, bf16[256,256]{1,0:T(8,128)(2,1)S(1)}, u32[]{:S(2)}, u32[]{:S(2)}) collective-permute-start(bf16[256,256]{1,0:T(8,128)(2,1)S(1)} %either.1), channel_id=1, source_target_pairs={{0,4},{1,13},{2,6},{3,15},{4,8},{5,1},{6,10},{7,3},{8,12},{9,5},{1... | collective-permute-start | bytes 393224 | tf_op jit(solution)/shard_map/ppermute | solution.py:247
  47.2 9.0 %collective-permute-start.8 = (bf16[256,256]{1,0:T(8,128)(2,1)S(1)}, bf16[256,256]{1,0:T(8,128)(2,1)S(1)}, u32[]{:S(2)}, u32[]{:S(2)}) collective-permute-start(bf16[256,256]{1,0:T(8,128)(2,1)S(1)} %collective-permute-done.6.one_ref), channel_id=1, source_target_pairs={{0,14},{1,15},{2,0},{3,1},{4,2},{5,3},{6,4},{7,5},{8,6},{9,7},{10,... | collective-permute-start | bytes 393224 | tf_op jit(solution)/shard_map/ppermute | solution.py:247
  48.8 7.4 %collective-permute-start.7 = (bf16[256,256]{1,0:T(8,128)(2,1)S(1)}, bf16[256,256]{1,0:T(8,128)(2,1)S(1)}, u32[]{:S(2)}, u32[]{:S(2)}) collective-permute-start(bf16[256,256]{1,0:T(8,128)(2,1)S(1)} %collective-permute-done.5.zero_ref), channel_id=1, source_target_pairs={{0,2},{1,3},{2,4},{3,5},{4,6},{5,7},{6,8},{7,9},{8,10},{9,11},{10,... | collective-permute-start | bytes 393224 | tf_op jit(solution)/shard_map/ppermute | solution.py:247
  49.3 14.4 %collective-permute-start.10 = (bf16[1280,256]{1,0:T(8,128)(2,1)S(1)}, bf16[1280,256]{1,0:T(8,128)(2,1)S(1)}, u32[]{:S(2)}, u32[]{:S(2)}) collective-permute-start(bf16[1280,256]{1,0:T(8,128)(2,1)S(1)} %constant_dynamic-update-slice_fusion.near_ref), channel_id=1, source_target_pairs={{0,1},{1,0},{2,3},{3,2},{4,5},{5,4},{6,7},{7,6},{8,9},{9,8},{10,11... | collective-permute-start | bytes 1966088 | tf_op jit(solution)/shard_map/ppermute | solution.py:247
  56.3 7.4 %collective-permute-start.11 = (bf16[768,256]{1,0:T(8,128)(2,1)S(1)}, bf16[768,256]{1,0:T(8,128)(2,1)S(1)}, u32[]{:S(2)}, u32[]{:S(2)}) collective-permute-start(bf16[768,256]{1,0:T(8,128)(2,1)S(1)} %constant_dynamic-update-slice_fusion.5.far_ref), channel_id=1, source_target_pairs={{0,1},{1,0},{2,3},{3,2},{4,5},{5,4},{6,7},{7,6},{8,9},{9,8},{10,11... | collective-permute-start | bytes 1179656 | tf_op jit(solution)/shard_map/ppermute | solution.py:247
  67.2 0.8 %copy-start = (f32[2,256,256]{2,1,0:T(8,128)}, f32[2,256,256]{2,1,0:T(8,128)S(1)}, u32[]{:S(2)}) copy-start(f32[2,256,256]{2,1,0:T(8,128)S(1)} %hole.1.far_hole_ref) | copy-start | bytes 1572868

commit v6 on v5

--- a/solution.py
+++ b/solution.py
@@ -176,57 +176,53 @@
         out_ref[...] = one_ref[...]
 
 
-def hole_kernel(place_ref, far_pair_ref, occ_ref, virt_ref, near_ref, far_ref, *refs):
-    near_sibling_ref, far_sibling_ref, out_ref, pair_ref, sems = refs
+def finish_kernel(place_ref, far_coded_ref, far_pair_ref, occ_ref, virt_ref, *refs):
+    *groups, out_ref, coded_ref, pair_ref, coded_sems, pair_sems = refs
     z, core = place_ref[0], place_ref[1]
-    rows = near_ref.shape[0] // 5
-    blocks = [
-        (group, k, chips, which)
-        for near, far, which in (
-            (near_ref, far_ref, core),
-            (near_sibling_ref, far_sibling_ref, 1 - core),
-        )
-        for group, away in ((near, (0, 1, -1, 2, -2)), (far, (3, -3, 4)))
-        for k, chips in enumerate(away)
-    ]
-    fetches = []
-    for slot, (_, _, chips, which) in enumerate(blocks):
-        n = jnp.bitwise_and(z - chips + 8, 7) * 2 + which
-        columns = far_pair_ref.at[:, pl.ds(pl.multiple_of(n * rows, rows), rows)]
-        fetches.append(pltpu.make_async_copy(columns, pair_ref.at[slot], sems.at[slot]))
-        fetches[slot].start()
-    out_ref[1] = virt_ref[...] - occ_ref[...]
-    total = jnp.zeros(out_ref.shape[1:], jnp.float32)
-    for slot, (group, k, _, _) in enumerate(blocks):
-        fetches[slot].wait()
-        block = group[k * rows : (k + 1) * rows]
-        total = total + jnp.dot(pair_ref[slot], block, preferred_element_type=jnp.float32)
-    out_ref[0] = total
-
-
-def finish_kernel(far_coded_ref, far_hole_ref, out_ref, coded_ref, hole_ref, sems):
     rows = out_ref.shape[0]
-    group = CHUNKS // 4
-    fetches = [
+    piece = CHUNKS // 4
+    shares = [
         pltpu.make_async_copy(
-            far_coded_ref.at[pl.ds(k * group, group)],
-            coded_ref.at[pl.ds(k * group, group)],
-            sems.at[k],
+            far_coded_ref.at[pl.ds(k * piece, piece)],
+            coded_ref.at[pl.ds(k * piece, piece)],
+            coded_sems.at[k],
         )
         for k in range(4)
     ]
-    fetches.append(pltpu.make_async_copy(far_hole_ref, hole_ref, sems.at[4]))
-    for fetch in fetches:
-        fetch.start()
-    ladder = jnp.zeros(out_ref.shape, jnp.float32)
+    chips = (0, 1, -1, 2, -2, 3, -3, 4)
+    pairs = []
+    for slot in range(2 * len(chips)):
+        which = core if slot < len(chips) else 1 - core
+        n = jnp.bitwise_and(z - chips[slot % len(chips)] + 8, 7) * 2 + which
+        pairs.append(
+            pltpu.make_async_copy(
+                far_pair_ref.at[:, pl.ds(pl.multiple_of(n * rows, rows), rows)],
+                pair_ref.at[:, pl.ds(slot * rows, rows)],
+                pair_sems.at[slot],
+            )
+        )
+    for copy in shares + pairs:
+        copy.start()
+    total = jnp.zeros(out_ref.shape, jnp.float32)
     for k in range(CHUNKS):
-        if k % group == 0:
-            fetches[k // group].wait()
+        if k % piece == 0:
+            shares[k // piece].wait()
         code = coded_ref[k, rows:, :].astype(jnp.int32).astype(jnp.float32)[:1, :]
         values = coded_ref[k, :rows, :].astype(jnp.int32).astype(jnp.float32)
-        ladder = ladder + values * jnp.exp2(code * (1.0 / STEPS))
-    fetches[4].wait()
-    out_ref[...] = (ladder * (1.0 / TOP) + hole_ref[0]) / hole_ref[1]
+        total = total + values * jnp.exp2(code * (1.0 / STEPS))
+    total = total * (1.0 / TOP)
+    start = 0
+    for group_ref in groups:
+        count = group_ref.shape[0] // rows
+        for copy in pairs[start : start + count]:
+            copy.wait()
+        total = total + jnp.dot(
+            pair_ref[:, start * rows : (start + count) * rows],
+            group_ref[...],
+            preferred_element_type=jnp.float32,
+        )
+        start += count
+    out_ref[...] = total / (virt_ref[...] - occ_ref[...])
 
 
 def on_device(amplitudes, integrals, pair_integrals, slab_index, occupied_energy, virtual_energy):
@@ -342,20 +338,23 @@
     far_sibling = step(far, 0, 1)
 
     where = jnp.stack([narrow_index >> 1, core]).astype(jnp.int32)
-    hole = pl.pallas_call(
-        hole_kernel,
-        out_shape=jax.ShapeDtypeStruct((2, height, LANES), jnp.float32),
-        in_specs=[SMEM, HBM] + [VMEM] * 6,
+    return pl.pallas_call(
+        finish_kernel,
+        out_shape=jax.ShapeDtypeStruct((height, LANES), jnp.float32),
+        in_specs=[SMEM, HBM, HBM] + [VMEM] * 6,
         out_specs=VMEM,
         scratch_shapes=[
-            pltpu.VMEM((CHUNKS, height, height), jnp.bfloat16),
+            pltpu.VMEM(shares.shape, jnp.int16),
+            pltpu.VMEM(pair_integrals.shape, jnp.bfloat16),
+            pltpu.SemaphoreType.DMA((4,)),
             pltpu.SemaphoreType.DMA((CHUNKS,)),
         ],
-        compiler_params=pltpu.CompilerParams(vmem_limit_bytes=50 << 20),
-        cost_estimate=pl.CostEstimate(flops=2**30, bytes_accessed=2**22, transcendentals=0),
-        name="hole",
+        compiler_params=pltpu.CompilerParams(vmem_limit_bytes=51 << 20),
+        cost_estimate=pl.CostEstimate(flops=2**30, bytes_accessed=2**23, transcendentals=0),
+        name="finish",
     )(
         where,
+        shares,
         pair_integrals,
         occupied_energy.reshape(height, 1),
         virtual_energy.reshape(1, LANES),
@@ -364,20 +363,6 @@
         near_sibling,
         far_sibling,
     )
-    return pl.pallas_call(
-        finish_kernel,
-        out_shape=jax.ShapeDtypeStruct((height, LANES), jnp.float32),
-        in_specs=[HBM] * 2,
-        out_specs=VMEM,
-        scratch_shapes=[
-            pltpu.VMEM(shares.shape, jnp.int16),
-            pltpu.VMEM(hole.shape, jnp.float32),
-            pltpu.SemaphoreType.DMA((5,)),
-        ],
-        compiler_params=pltpu.CompilerParams(vmem_limit_bytes=54 << 20),
-        cost_estimate=pl.CostEstimate(flops=2**23, bytes_accessed=2**22, transcendentals=0),
-        name="finish",
-    )(shares, hole)
 
 
 def solution(mesh):

time: 71.3 us -> 70.3 us (0.986)
  Pallas kernels: 21.6 us -> 20.8 us
  local copies, waits for them, and re-layouts: 2.58 us -> 1.79 us
    pallas_call x1 -> x0, Pallas kernels: 3.48 us -> none  [on_device(): pl.pallas_call(hole_kernel, out_shape=jax.ShapeDtypeStruct((2, height, LA...]
    pallas_call x1, Pallas kernels: 2.74 us -> 5.46 us  [on_device(): pl.pallas_call(finish_kernel, out_shape=jax.ShapeDtypeStruct((height, LAN...]
    unnamed x20 -> x18, local copies, waits for them, and re-layouts: 2.42 us -> 1.64 us
  transfers between devices with their start and end apart: 14 -> 14, of which waited for: 5 -> 5; matrix products, arithmetic and copies ran while one was open for 0% -> 0% of each run, Pallas kernels for 19% -> 15%
where the time goes in v6:
time: 70.3 us; the launch traced here: 69.3 us
  starting transfers between devices  38.8 us (55%)
  Pallas kernels  20.8 us (30%)
  waiting for transfers between devices  7.45 us (11%)
  local copies, waits for them, and re-layouts  1.79 us (3%)
    ppermute x9, starting transfers between devices, step(): return lax.ppermute(value, 'narrow', ring)  24.2 us
    pallas_call x1, Pallas kernels, on_device(): pl.pallas_call(ladder_kernel, out_shape=jax.ShapeDtypeStruct((CHUNKS, hei...  8.89 us
    all_to_all x1, starting transfers between devices, on_device(): shares = lax.all_to_all(coded, 'wide', 0, 0, tiled=True)  5.56 us
    pallas_call x1, Pallas kernels, on_device(): pl.pallas_call(finish_kernel, out_shape=jax.ShapeDtypeStruct((height, LAN...  5.46 us
    ppermute x9, waiting for transfers between devices, step(): return lax.ppermute(value, 'narrow', ring)  5.22 us
    ppermute x3, starting transfers between devices, on_device(): lax.ppermute(sent[k], 'wide', [(x * 4 + y, (x + dx) % 4 * 4 + (y + dy) %...  4.88 us
    all_to_all x1, starting transfers between devices, on_device(): second = lax.all_to_all(moved, 'wide', 0, 0, tiled=True)  4.2 us
    pallas_call x1, Pallas kernels, on_device(): pl.pallas_call(lambda *refs: select_kernel(shift, *refs), out_shape=(*[ja...  3.77 us
  transfers between devices with their start and end apart: 14, of which 5 were waited for; matrix products, arithmetic and copies ran while one was open for 0% of the time, Pallas kernels for 15%

profile of v6, /device:TPU:1, one launch (start us, length us, event | category | flops | bytes accessed | tf_op | source)
XLA Modules:
  0.0 69.3 jit_solution(9152048580173468857)
XLA Ops:
  0.0 3.8 %select.1 = (bf16[128,256]{1,0:T(8,128)(2,1)}, bf16[128,256]{1,0:T(8,128)(2,1)}, bf16[128,256]{1,0:T(8,128)(2,1)}, bf16[128,256]{1,0:T(8,128)(2,1)}, s32[16,256]{1,0:T(8,128)}) custom-call(s32[1]{0:T(128)} %bitcast.2.refs_0_, s32[32,128]{1,0:T(8,128)} %bitcast.7, bf16[256,2048]{1,0:T(8,128)(2,1)} %amp_ref.1), custom_call_target="tpu_custom_call" | custom-call | flops 1073741824 | bytes 2097152 | tf_op jit(solution)/shard_map/select/pallas_call | solution.py:245
  3.8 2.1 %collective-permute-start = (bf16[128,256]{1,0:T(8,128)(2,1)}, bf16[128,256]{1,0:T(8,128)(2,1)S(1)}, u32[]{:S(2)}, u32[]{:S(2)}) collective-permute-start(bf16[128,256]{1,0:T(8,128)(2,1)} %get-tuple-element.17), channel_id=1, source_target_pairs={{0,64},{16,80},{32,96},{48,112},{64,128},{80,144},{96,160},{112,17... | collective-permute-start | bytes 196616 | tf_op jit(solution)/shard_map/ppermute | solution.py:259
  5.9 1.4 %collective-permute-start.1 = (bf16[128,256]{1,0:T(8,128)(2,1)}, bf16[128,256]{1,0:T(8,128)(2,1)S(1)}, u32[]{:S(2)}, u32[]{:S(2)}) collective-permute-start(bf16[128,256]{1,0:T(8,128)(2,1)} %get-tuple-element.18), channel_id=1, source_target_pairs={{0,192},{16,208},{32,224},{48,240},{64,0},{80,16},{96,32},{112,48}... | collective-permute-start | bytes 196616 | tf_op jit(solution)/shard_map/ppermute | solution.py:259
  7.3 1.4 %collective-permute-start.2 = (bf16[128,256]{1,0:T(8,128)(2,1)}, bf16[128,256]{1,0:T(8,128)(2,1)S(1)}, u32[]{:S(2)}, u32[]{:S(2)}) collective-permute-start(bf16[128,256]{1,0:T(8,128)(2,1)} %get-tuple-element.19), channel_id=1, source_target_pairs={{0,16},{16,32},{32,48},{48,0},{64,80},{80,96},{96,112},{112,64},{1... | collective-permute-start | bytes 196616 | tf_op jit(solution)/shard_map/ppermute | solution.py:259
  8.7 0.8 %copy-done.3 = bf16[128,256]{1,0:T(8,128)(2,1)S(1)} copy-done((bf16[128,256]{1,0:T(8,128)(2,1)S(1)}, bf16[128,256]{1,0:T(8,128)(2,1)}, u32[]{:S(2)}) %copy-start.3) | copy-done | bytes 65560
  9.5 0.7 %copy-done.4 = s32[16,256]{1,0:T(8,128)S(1)} copy-done((s32[16,256]{1,0:T(8,128)S(1)}, s32[16,256]{1,0:T(8,128)}, u32[]{:S(2)}) %copy-start.4) | copy-done | bytes 16408
  10.2 0.9 %route.1 = (bf16[1280,512]{1,0:T(8,128)(2,1)S(1)}, bf16[1280,256]{1,0:T(8,128)(2,1)S(1)}, bf16[128,256]{1,0:T(8,128)(2,1)S(1)}) custom-call(s32[1]{0:T(128)} %bitcast.2.refs_0_, s32[32,128]{1,0:T(8,128)S(1)} %bitcast.8, s32[16,256]{1,0:T(8,128)S(1)} %copy-done.4, bf16[128,256]{1,0:T(8,128)(2,1)S(1)} %copy-done.3), custom_call_target="tpu_custom_call" | custom-call | flops 268435456 | bytes 1048576 | tf_op jit(solution)/shard_map/route/pallas_call | solution.py:268
  11.2 1.1 %collective-permute-done.2.refs_3_ = bf16[128,256]{1,0:T(8,128)(2,1)S(1)} collective-permute-done((bf16[128,256]{1,0:T(8,128)(2,1)}, bf16[128,256]{1,0:T(8,128)(2,1)S(1)}, u32[]{:S(2)}, u32[]{:S(2)}) %collective-permute-start.2) | collective-permute-done | bytes 65568 | tf_op jit(solution)/shard_map/ppermute | solution.py:259
  12.3 1.3 %forward.1.after_ref = bf16[16,80,256]{2,1,0:T(8,128)(2,1)} custom-call(bf16[1280,512]{1,0:T(8,128)(2,1)S(1)} %get-tuple-element.15.forward_ref, bf16[128,256]{1,0:T(8,128)(2,1)S(1)} %get-tuple-element.16.refs_0_, bf16[128,256]{1,0:T(8,128)(2,1)S(1)} %collective-permute-done.refs_1_, bf16[128,256]{1,0:T(8,128)(2,1)S(1)} %collective-permute-done.1.refs_2_, ...), custom_call_target="tpu_custom_call" | custom-call | flops 268435456 | bytes 1048576 | tf_op jit(solution)/shard_map/forward/pallas_call | solution.py:282
  13.6 4.2 %all-to-all-start.1 = ((bf16[16,80,256]{2,1,0:T(8,128)(2,1)}), bf16[16,80,256]{2,1,0:T(8,128)(2,1)S(1)}, u32[]{:S(2)}, u32[]{:S(2)}) async-start(bf16[16,80,256]{2,1,0:T(8,128)(2,1)} %forward.1.after_ref), calls=%async_computation.1 | async-start | bytes 1310720 | tf_op jit(solution)/shard_map/all_to_all | solution.py:291
  17.8 8.9 %ladder.1.after_ref = s16[16,272,256]{2,1,0:T(8,128)(2,1)} custom-call(bf16[256,2048]{1,0:T(8,128)(2,1)S(1)} %copy-done, bf16[2048,4096]{1,0:T(8,128)(2,1)} %int_ref.1, bf16[16,80,256]{2,1,0:T(8,128)(2,1)} %forward.1.after_ref), custom_call_target="tpu_custom_call" | custom-call | flops 4294967296 | bytes 18874368 | tf_op jit(solution)/shard_map/ladder/pallas_call | solution.py:294
  26.7 1.2 %all-to-all-done.1.second_ref = bf16[16,80,256]{2,1,0:T(8,128)(2,1)S(1)} async-done(((bf16[16,80,256]{2,1,0:T(8,128)(2,1)}), bf16[16,80,256]{2,1,0:T(8,128)(2,1)S(1)}, u32[]{:S(2)}, u32[]{:S(2)}) %all-to-all-start.1) | async-done | bytes 655392 | tf_op jit(solution)/shard_map/all_to_all | solution.py:291
  27.9 5.6 %all-to-all-start = ((s16[16,272,256]{2,1,0:T(8,128)(2,1)}), s16[16,272,256]{2,1,0:T(8,128)(2,1)}, u32[]{:S(2)}, u32[]{:S(2)}) async-start(s16[16,272,256]{2,1,0:T(8,128)(2,1)} %ladder.1.after_ref), calls=%async_computation | async-start | bytes 4456448 | tf_op jit(solution)/shard_map/all_to_all | solution.py:311
  33.9 6.1 %collective-permute-start.6 = (bf16[256,256]{1,0:T(8,128)(2,1)S(1)}, bf16[256,256]{1,0:T(8,128)(2,1)S(1)}, u32[]{:S(2)}, u32[]{:S(2)}) collective-permute-start(bf16[256,256]{1,0:T(8,128)(2,1)S(1)} %settle.1), channel_id=1, source_target_pairs={{0,12},{1,13},{2,14},{3,15},{4,0},{5,1},{6,2},{7,3},{8,4},{9,5},{1... | collective-permute-start | bytes 393224 | tf_op jit(solution)/shard_map/ppermute | solution.py:243
  40.0 0.7 %collective-permute-start.3 = (bf16[256,256]{1,0:T(8,128)(2,1)S(1)}, bf16[256,256]{1,0:T(8,128)(2,1)S(1)}, u32[]{:S(2)}, u32[]{:S(2)}) collective-permute-start(bf16[256,256]{1,0:T(8,128)(2,1)S(1)} %settle.1), channel_id=1, source_target_pairs={{0,2},{1,3},{2,4},{3,5},{4,6},{5,7},{6,8},{7,9},{8,10},{9,11},{10,... | collective-permute-start | bytes 393224 | tf_op jit(solution)/shard_map/ppermute | solution.py:243
  40.7 2.4 %collective-permute-start.4 = (bf16[256,256]{1,0:T(8,128)(2,1)S(1)}, bf16[256,256]{1,0:T(8,128)(2,1)S(1)}, u32[]{:S(2)}, u32[]{:S(2)}) collective-permute-start(bf16[256,256]{1,0:T(8,128)(2,1)S(1)} %settle.1), channel_id=1, source_target_pairs={{0,14},{1,15},{2,0},{3,1},{4,2},{5,3},{6,4},{7,5},{8,6},{9,7},{10,... | collective-permute-start | bytes 393224 | tf_op jit(solution)/shard_map/ppermute | solution.py:243
  43.1 3.6 %collective-permute-done.5.zero_ref = bf16[256,256]{1,0:T(8,128)(2,1)S(1)} collective-permute-done((bf16[256,256]{1,0:T(8,128)(2,1)S(1)}, bf16[256,256]{1,0:T(8,128)(2,1)S(1)}, u32[]{:S(2)}, u32[]{:S(2)}) %collective-permute-start.5) | collective-permute-done | bytes 131104 | tf_op jit(solution)/shard_map/ppermute | solution.py:243
  46.8 0.4 collective-permute-start.9
  47.2 1.6 %collective-permute-start.8 = (bf16[256,256]{1,0:T(8,128)(2,1)S(1)}, bf16[256,256]{1,0:T(8,128)(2,1)S(1)}, u32[]{:S(2)}, u32[]{:S(2)}) collective-permute-start(bf16[256,256]{1,0:T(8,128)(2,1)S(1)} %collective-permute-done.6.one_ref), channel_id=1, source_target_pairs={{0,14},{1,15},{2,0},{3,1},{4,2},{5,3},{6,4},{7,5},{8,6},{9,7},{10,... | collective-permute-start | bytes 393224 | tf_op jit(solution)/shard_map/ppermute | solution.py:243
  48.8 0.4 collective-permute-done.3
  49.3 6.9 %collective-permute-start.10 = (bf16[1280,256]{1,0:T(8,128)(2,1)S(1)}, bf16[1280,256]{1,0:T(8,128)(2,1)S(1)}, u32[]{:S(2)}, u32[]{:S(2)}) collective-permute-start(bf16[1280,256]{1,0:T(8,128)(2,1)S(1)} %constant_dynamic-update-slice_fusion.refs_0_), channel_id=1, source_target_pairs={{0,1},{1,0},{2,3},{3,2},{4,5},{5,4},{6,7},{7,6},{8,9},{9,8},{10,11... | collective-permute-start | bytes 1966088 | tf_op jit(solution)/shard_map/ppermute | solution.py:243
  56.2 6.1 %collective-permute-start.11 = (bf16[768,256]{1,0:T(8,128)(2,1)S(1)}, bf16[768,256]{1,0:T(8,128)(2,1)S(1)}, u32[]{:S(2)}, u32[]{:S(2)}) collective-permute-start(bf16[768,256]{1,0:T(8,128)(2,1)S(1)} %constant_dynamic-update-slice_fusion.5.refs_1_), channel_id=1, source_target_pairs={{0,1},{1,0},{2,3},{3,2},{4,5},{5,4},{6,7},{7,6},{8,9},{9,8},{10,11... | collective-permute-start | bytes 1179656 | tf_op jit(solution)/shard_map/ppermute | solution.py:243
  62.6 1.1 %collective-permute-done.11.refs_3_ = bf16[768,256]{1,0:T(8,128)(2,1)S(1)} collective-permute-done((bf16[768,256]{1,0:T(8,128)(2,1)S(1)}, bf16[768,256]{1,0:T(8,128)(2,1)S(1)}, u32[]{:S(2)}, u32[]{:S(2)}) %collective-permute-start.11) | collective-permute-done | bytes 393248 | tf_op jit(solution)/shard_map/ppermute | solution.py:243
  63.7 5.5 %finish.1 = f32[256,256]{1,0:T(8,128)} custom-call(s32[2]{0:T(128)S(1)} %pad_add_fusion.place_ref, s16[16,272,256]{2,1,0:T(8,128)(2,1)} %all-to-all-done.far_coded_ref, bf16[256,4096]{1,0:T(8,128)(2,1)} %far_pair_ref.1, f32[256,1]{1,0:T(8,128)S(1)} %copy.7.occ_ref, f32[1,256]{1,0:T(1,128)S(1)} %bitcast.6, ...), custom_call_target="tpu_custom_call" | custom-call | flops 1073741824 | bytes 8388608 | tf_op jit(solution)/shard_map/finish/pallas_call | solution.py:341
  (33 shorter events, 0.7 us)
Async XLA Ops:
  0.0 8.7 %copy-start.2 = (s32[4096]{0:T(1024)S(1)}, s32[4096]{0:T(1024)}, u32[]{:S(2)}) copy-start(s32[4096]{0:T(1024)} %param.9) | copy-start | bytes 49156
  3.8 7.4 %collective-permute-start = (bf16[128,256]{1,0:T(8,128)(2,1)}, bf16[128,256]{1,0:T(8,128)(2,1)S(1)}, u32[]{:S(2)}, u32[]{:S(2)}) collective-permute-start(bf16[128,256]{1,0:T(8,128)(2,1)} %get-tuple-element.17), channel_id=1, source_target_pairs={{0,64},{16,80},{32,96},{48,112},{64,128},{80,144},{96,160},{112,17... | collective-permute-start | bytes 196616 | tf_op jit(solution)/shard_map/ppermute | solution.py:259
  5.9 5.3 %collective-permute-start.1 = (bf16[128,256]{1,0:T(8,128)(2,1)}, bf16[128,256]{1,0:T(8,128)(2,1)S(1)}, u32[]{:S(2)}, u32[]{:S(2)}) collective-permute-start(bf16[128,256]{1,0:T(8,128)(2,1)} %get-tuple-element.18), channel_id=1, source_target_pairs={{0,192},{16,208},{32,224},{48,240},{64,0},{80,16},{96,32},{112,48}... | collective-permute-start | bytes 196616 | tf_op jit(solution)/shard_map/ppermute | solution.py:259
  7.3 5.0 %collective-permute-start.2 = (bf16[128,256]{1,0:T(8,128)(2,1)}, bf16[128,256]{1,0:T(8,128)(2,1)S(1)}, u32[]{:S(2)}, u32[]{:S(2)}) collective-permute-start(bf16[128,256]{1,0:T(8,128)(2,1)} %get-tuple-element.19), channel_id=1, source_target_pairs={{0,16},{16,32},{32,48},{48,0},{64,80},{80,96},{96,112},{112,64},{1... | collective-permute-start | bytes 196616 | tf_op jit(solution)/shard_map/ppermute | solution.py:259
  8.7 0.8 %copy-start.3 = (bf16[128,256]{1,0:T(8,128)(2,1)S(1)}, bf16[128,256]{1,0:T(8,128)(2,1)}, u32[]{:S(2)}) copy-start(bf16[128,256]{1,0:T(8,128)(2,1)} %get-tuple-element.14.refs_3_) | copy-start | bytes 196612
  9.5 0.7 %copy-start.4 = (s32[16,256]{1,0:T(8,128)S(1)}, s32[16,256]{1,0:T(8,128)}, u32[]{:S(2)}) copy-start(s32[16,256]{1,0:T(8,128)} %get-tuple-element.13.refs_2_) | copy-start | bytes 49156
  10.2 7.6 %copy-start = (bf16[256,2048]{1,0:T(8,128)(2,1)S(1)}, bf16[256,2048]{1,0:T(8,128)(2,1)}, u32[]{:S(2)}) copy-start(bf16[256,2048]{1,0:T(8,128)(2,1)} %amp_ref.1) | copy-start | bytes 3145732
  13.6 14.3 %all-to-all-start.1 = ((bf16[16,80,256]{2,1,0:T(8,128)(2,1)}), bf16[16,80,256]{2,1,0:T(8,128)(2,1)S(1)}, u32[]{:S(2)}, u32[]{:S(2)}) async-start(bf16[16,80,256]{2,1,0:T(8,128)(2,1)} %forward.1.after_ref), calls=%async_computation.1 | async-start | bytes 1310720 | tf_op jit(solution)/shard_map/all_to_all | solution.py:291
  27.9 35.8 %all-to-all-start = ((s16[16,272,256]{2,1,0:T(8,128)(2,1)}), s16[16,272,256]{2,1,0:T(8,128)(2,1)}, u32[]{:S(2)}, u32[]{:S(2)}) async-start(s16[16,272,256]{2,1,0:T(8,128)(2,1)} %ladder.1.after_ref), calls=%async_computation | async-start | bytes 4456448 | tf_op jit(solution)/shard_map/all_to_all | solution.py:311
  33.5 28.9 %copy-start.5 = (f32[256]{0:T(256)S(1)}, f32[256]{0:T(256)}, u32[]{:S(2)}) copy-start(f32[256]{0:T(256)} %param.10) | copy-start | bytes 3076
  33.9 29.8 %copy-start.1 = (f32[256]{0:T(256)S(1)}, f32[256]{0:T(256)}, u32[]{:S(2)}) copy-start(f32[256]{0:T(256)} %param.11) | copy-start | bytes 3076
  33.9 9.2 %collective-permute-start.6 = (bf16[256,256]{1,0:T(8,128)(2,1)S(1)}, bf16[256,256]{1,0:T(8,128)(2,1)S(1)}, u32[]{:S(2)}, u32[]{:S(2)}) collective-permute-start(bf16[256,256]{1,0:T(8,128)(2,1)S(1)} %settle.1), channel_id=1, source_target_pairs={{0,12},{1,13},{2,14},{3,15},{4,0},{5,1},{6,2},{7,3},{8,4},{9,5},{1... | collective-permute-start | bytes 393224 | tf_op jit(solution)/shard_map/ppermute | solution.py:243
  40.0 6.8 %collective-permute-start.5 = (bf16[256,256]{1,0:T(8,128)(2,1)S(1)}, bf16[256,256]{1,0:T(8,128)(2,1)S(1)}, u32[]{:S(2)}, u32[]{:S(2)}) collective-permute-start(bf16[256,256]{1,0:T(8,128)(2,1)S(1)} %settle.1), channel_id=1, source_target_pairs={{0,4},{1,5},{2,6},{3,7},{4,8},{5,9},{6,10},{7,11},{8,12},{9,13},{1... | collective-permute-start | bytes 393224 | tf_op jit(solution)/shard_map/ppermute | solution.py:243
  40.0 9.3 %collective-permute-start.3 = (bf16[256,256]{1,0:T(8,128)(2,1)S(1)}, bf16[256,256]{1,0:T(8,128)(2,1)S(1)}, u32[]{:S(2)}, u32[]{:S(2)}) collective-permute-start(bf16[256,256]{1,0:T(8,128)(2,1)S(1)} %settle.1), channel_id=1, source_target_pairs={{0,2},{1,3},{2,4},{3,5},{4,6},{5,7},{6,8},{7,9},{8,10},{9,11},{10,... | collective-permute-start | bytes 393224 | tf_op jit(solution)/shard_map/ppermute | solution.py:243
  40.7 8.5 %collective-permute-start.4 = (bf16[256,256]{1,0:T(8,128)(2,1)S(1)}, bf16[256,256]{1,0:T(8,128)(2,1)S(1)}, u32[]{:S(2)}, u32[]{:S(2)}) collective-permute-start(bf16[256,256]{1,0:T(8,128)(2,1)S(1)} %settle.1), channel_id=1, source_target_pairs={{0,14},{1,15},{2,0},{3,1},{4,2},{5,3},{6,4},{7,5},{8,6},{9,7},{10,... | collective-permute-start | bytes 393224 | tf_op jit(solution)/shard_map/ppermute | solution.py:243
  46.8 9.4 %collective-permute-start.9 = (bf16[256,256]{1,0:T(8,128)(2,1)S(1)}, bf16[256,256]{1,0:T(8,128)(2,1)S(1)}, u32[]{:S(2)}, u32[]{:S(2)}) collective-permute-start(bf16[256,256]{1,0:T(8,128)(2,1)S(1)} %either.1), channel_id=1, source_target_pairs={{0,4},{1,13},{2,6},{3,15},{4,8},{5,1},{6,10},{7,3},{8,12},{9,5},{1... | collective-permute-start | bytes 393224 | tf_op jit(solution)/shard_map/ppermute | solution.py:243
  47.2 9.0 %collective-permute-start.8 = (bf16[256,256]{1,0:T(8,128)(2,1)S(1)}, bf16[256,256]{1,0:T(8,128)(2,1)S(1)}, u32[]{:S(2)}, u32[]{:S(2)}) collective-permute-start(bf16[256,256]{1,0:T(8,128)(2,1)S(1)} %collective-permute-done.6.one_ref), channel_id=1, source_target_pairs={{0,14},{1,15},{2,0},{3,1},{4,2},{5,3},{6,4},{7,5},{8,6},{9,7},{10,... | collective-permute-start | bytes 393224 | tf_op jit(solution)/shard_map/ppermute | solution.py:243
  48.8 7.4 %collective-permute-start.7 = (bf16[256,256]{1,0:T(8,128)(2,1)S(1)}, bf16[256,256]{1,0:T(8,128)(2,1)S(1)}, u32[]{:S(2)}, u32[]{:S(2)}) collective-permute-start(bf16[256,256]{1,0:T(8,128)(2,1)S(1)} %collective-permute-done.5.zero_ref), channel_id=1, source_target_pairs={{0,2},{1,3},{2,4},{3,5},{4,6},{5,7},{6,8},{7,9},{8,10},{9,11},{10,... | collective-permute-start | bytes 393224 | tf_op jit(solution)/shard_map/ppermute | solution.py:243
  49.3 14.4 %collective-permute-start.10 = (bf16[1280,256]{1,0:T(8,128)(2,1)S(1)}, bf16[1280,256]{1,0:T(8,128)(2,1)S(1)}, u32[]{:S(2)}, u32[]{:S(2)}) collective-permute-start(bf16[1280,256]{1,0:T(8,128)(2,1)S(1)} %constant_dynamic-update-slice_fusion.refs_0_), channel_id=1, source_target_pairs={{0,1},{1,0},{2,3},{3,2},{4,5},{5,4},{6,7},{7,6},{8,9},{9,8},{10,11... | collective-permute-start | bytes 1966088 | tf_op jit(solution)/shard_map/ppermute | solution.py:243
  56.2 7.4 %collective-permute-start.11 = (bf16[768,256]{1,0:T(8,128)(2,1)S(1)}, bf16[768,256]{1,0:T(8,128)(2,1)S(1)}, u32[]{:S(2)}, u32[]{:S(2)}) collective-permute-start(bf16[768,256]{1,0:T(8,128)(2,1)S(1)} %constant_dynamic-update-slice_fusion.5.refs_1_), channel_id=1, source_target_pairs={{0,1},{1,0},{2,3},{3,2},{4,5},{5,4},{6,7},{7,6},{8,9},{9,8},{10,11... | collective-permute-start | bytes 1179656 | tf_op jit(solution)/shard_map/ppermute | solution.py:243

commit v7 on v6

--- a/solution.py
+++ b/solution.py
@@ -13,6 +13,7 @@
 CODE_ROWS = 16
 STEPS = 256.0
 TOP = 32760.0
+PIECES = 4
 PER = 2
 VMEM = pl.BlockSpec(memory_space=pltpu.VMEM)
 HBM = pl.BlockSpec(memory_space=pltpu.HBM)
@@ -176,53 +177,38 @@
         out_ref[...] = one_ref[...]
 
 
-def finish_kernel(place_ref, far_coded_ref, far_pair_ref, occ_ref, virt_ref, *refs):
-    *groups, out_ref, coded_ref, pair_ref, coded_sems, pair_sems = refs
+def finish_kernel(place_ref, far_pair_ref, far_coded_ref, occ_ref, virt_ref, *refs):
+    *groups, out_ref, pair_ref, coded_ref, ordered_ref, sems = refs
+    piece = CHUNKS // PIECES
+    fetches = [pltpu.make_async_copy(far_pair_ref, pair_ref, sems.at[PIECES])]
+    for k in range(PIECES):
+        some = pl.ds(k * piece, piece)
+        fetches.append(
+            pltpu.make_async_copy(far_coded_ref.at[some], coded_ref.at[some], sems.at[k])
+        )
+    for fetch in fetches:
+        fetch.start()
     z, core = place_ref[0], place_ref[1]
     rows = out_ref.shape[0]
-    piece = CHUNKS // 4
-    shares = [
-        pltpu.make_async_copy(
-            far_coded_ref.at[pl.ds(k * piece, piece)],
-            coded_ref.at[pl.ds(k * piece, piece)],
-            coded_sems.at[k],
-        )
-        for k in range(4)
-    ]
     chips = (0, 1, -1, 2, -2, 3, -3, 4)
-    pairs = []
-    for slot in range(2 * len(chips)):
-        which = core if slot < len(chips) else 1 - core
-        n = jnp.bitwise_and(z - chips[slot % len(chips)] + 8, 7) * 2 + which
-        pairs.append(
-            pltpu.make_async_copy(
-                far_pair_ref.at[:, pl.ds(pl.multiple_of(n * rows, rows), rows)],
-                pair_ref.at[:, pl.ds(slot * rows, rows)],
-                pair_sems.at[slot],
-            )
-        )
-    for copy in shares + pairs:
-        copy.start()
+    slot = 0
+    for group_ref in groups:
+        for k in range(group_ref.shape[0] // rows):
+            which = core if slot < len(chips) else 1 - core
+            n = jnp.bitwise_and(z - chips[slot % len(chips)] + 8, 7) * 2 + which
+            held = pl.ds(pl.multiple_of(n * rows, rows), rows)
+            ordered_ref[held, :] = group_ref[k * rows : (k + 1) * rows, :]
+            slot += 1
+    fetches[0].wait()
+    hole = jnp.dot(pair_ref[...], ordered_ref[...], preferred_element_type=jnp.float32)
     total = jnp.zeros(out_ref.shape, jnp.float32)
     for k in range(CHUNKS):
         if k % piece == 0:
-            shares[k // piece].wait()
+            fetches[1 + k // piece].wait()
         code = coded_ref[k, rows:, :].astype(jnp.int32).astype(jnp.float32)[:1, :]
         values = coded_ref[k, :rows, :].astype(jnp.int32).astype(jnp.float32)
         total = total + values * jnp.exp2(code * (1.0 / STEPS))
-    total = total * (1.0 / TOP)
-    start = 0
-    for group_ref in groups:
-        count = group_ref.shape[0] // rows
-        for copy in pairs[start : start + count]:
-            copy.wait()
-        total = total + jnp.dot(
-            pair_ref[:, start * rows : (start + count) * rows],
-            group_ref[...],
-            preferred_element_type=jnp.float32,
-        )
-        start += count
-    out_ref[...] = total / (virt_ref[...] - occ_ref[...])
+    out_ref[...] = (total * (1.0 / TOP) + hole) / (virt_ref[...] - occ_ref[...])
 
 
 def on_device(amplitudes, integrals, pair_integrals, slab_index, occupied_energy, virtual_energy):
@@ -344,18 +330,18 @@
         in_specs=[SMEM, HBM, HBM] + [VMEM] * 6,
         out_specs=VMEM,
         scratch_shapes=[
+            pltpu.VMEM(pair_integrals.shape, jnp.bfloat16),
             pltpu.VMEM(shares.shape, jnp.int16),
-            pltpu.VMEM(pair_integrals.shape, jnp.bfloat16),
-            pltpu.SemaphoreType.DMA((4,)),
-            pltpu.SemaphoreType.DMA((CHUNKS,)),
+            pltpu.VMEM((CHUNKS * height, LANES), jnp.bfloat16),
+            pltpu.SemaphoreType.DMA((PIECES + 1,)),
         ],
         compiler_params=pltpu.CompilerParams(vmem_limit_bytes=51 << 20),
         cost_estimate=pl.CostEstimate(flops=2**30, bytes_accessed=2**23, transcendentals=0),
         name="finish",
     )(
         where,
+        pair_integrals,
         shares,
-        pair_integrals,
         occupied_energy.reshape(height, 1),
         virtual_energy.reshape(1, LANES),
         near,

time: 70.3 us -> 69.3 us (0.986)
  Pallas kernels: 20.8 us -> 19.8 us
    pallas_call x1, Pallas kernels: 5.46 us -> 4.46 us  [on_device(): pl.pallas_call(finish_kernel, out_shape=jax.ShapeDtypeStruct((height, LAN...]
where the time goes in v7:
time: 69.3 us; the launch traced here: 68.3 us
  starting transfers between devices  38.8 us (56%)
  Pallas kernels  19.8 us (29%)
  waiting for transfers between devices  7.45 us (11%)
  local copies, waits for them, and re-layouts  1.79 us (3%)
    ppermute x9, starting transfers between devices, step(): return lax.ppermute(value, 'narrow', ring)  24.2 us
    pallas_call x1, Pallas kernels, on_device(): pl.pallas_call(ladder_kernel, out_shape=jax.ShapeDtypeStruct((CHUNKS, hei...  8.89 us
    all_to_all x1, starting transfers between devices, on_device(): shares = lax.all_to_all(coded, 'wide', 0, 0, tiled=True)  5.56 us
    ppermute x9, waiting for transfers between devices, step(): return lax.ppermute(value, 'narrow', ring)  5.22 us
    ppermute x3, starting transfers between devices, on_device(): lax.ppermute(sent[k], 'wide', [(x * 4 + y, (x + dx) % 4 * 4 + (y + dy) %...  4.88 us
    pallas_call x1, Pallas kernels, on_device(): pl.pallas_call(finish_kernel, out_shape=jax.ShapeDtypeStruct((height, LAN...  4.46 us
    all_to_all x1, starting transfers between devices, on_device(): second = lax.all_to_all(moved, 'wide', 0, 0, tiled=True)  4.2 us
    pallas_call x1, Pallas kernels, on_device(): pl.pallas_call(lambda *refs: select_kernel(shift, *refs), out_shape=(*[ja...  3.77 us
  transfers between devices with their start and end apart: 14, of which 5 were waited for; matrix products, arithmetic and copies ran while one was open for 0% of the time, Pallas kernels for 15%

profile of v7, /device:TPU:1, one launch (start us, length us, event | category | flops | bytes accessed | tf_op | source)
XLA Modules:
  0.0 68.3 jit_solution(1000577514160674894)
XLA Ops:
  0.0 3.8 %select.1 = (bf16[128,256]{1,0:T(8,128)(2,1)}, bf16[128,256]{1,0:T(8,128)(2,1)}, bf16[128,256]{1,0:T(8,128)(2,1)}, bf16[128,256]{1,0:T(8,128)(2,1)}, s32[16,256]{1,0:T(8,128)}) custom-call(s32[1]{0:T(128)} %bitcast.2.refs_0_, s32[32,128]{1,0:T(8,128)} %bitcast.7, bf16[256,2048]{1,0:T(8,128)(2,1)} %amp_ref.1), custom_call_target="tpu_custom_call" | custom-call | flops 1073741824 | bytes 2097152 | tf_op jit(solution)/shard_map/select/pallas_call | solution.py:231
  3.8 2.1 %collective-permute-start = (bf16[128,256]{1,0:T(8,128)(2,1)}, bf16[128,256]{1,0:T(8,128)(2,1)S(1)}, u32[]{:S(2)}, u32[]{:S(2)}) collective-permute-start(bf16[128,256]{1,0:T(8,128)(2,1)} %get-tuple-element.17), channel_id=1, source_target_pairs={{0,64},{16,80},{32,96},{48,112},{64,128},{80,144},{96,160},{112,17... | collective-permute-start | bytes 196616 | tf_op jit(solution)/shard_map/ppermute | solution.py:245
  5.9 1.4 %collective-permute-start.1 = (bf16[128,256]{1,0:T(8,128)(2,1)}, bf16[128,256]{1,0:T(8,128)(2,1)S(1)}, u32[]{:S(2)}, u32[]{:S(2)}) collective-permute-start(bf16[128,256]{1,0:T(8,128)(2,1)} %get-tuple-element.18), channel_id=1, source_target_pairs={{0,192},{16,208},{32,224},{48,240},{64,0},{80,16},{96,32},{112,48}... | collective-permute-start | bytes 196616 | tf_op jit(solution)/shard_map/ppermute | solution.py:245
  7.3 1.4 %collective-permute-start.2 = (bf16[128,256]{1,0:T(8,128)(2,1)}, bf16[128,256]{1,0:T(8,128)(2,1)S(1)}, u32[]{:S(2)}, u32[]{:S(2)}) collective-permute-start(bf16[128,256]{1,0:T(8,128)(2,1)} %get-tuple-element.19), channel_id=1, source_target_pairs={{0,16},{16,32},{32,48},{48,0},{64,80},{80,96},{96,112},{112,64},{1... | collective-permute-start | bytes 196616 | tf_op jit(solution)/shard_map/ppermute | solution.py:245
  8.7 0.8 %copy-done.3 = bf16[128,256]{1,0:T(8,128)(2,1)S(1)} copy-done((bf16[128,256]{1,0:T(8,128)(2,1)S(1)}, bf16[128,256]{1,0:T(8,128)(2,1)}, u32[]{:S(2)}) %copy-start.3) | copy-done | bytes 65560
  9.5 0.7 %copy-done.4 = s32[16,256]{1,0:T(8,128)S(1)} copy-done((s32[16,256]{1,0:T(8,128)S(1)}, s32[16,256]{1,0:T(8,128)}, u32[]{:S(2)}) %copy-start.4) | copy-done | bytes 16408
  10.2 0.9 %route.1 = (bf16[1280,512]{1,0:T(8,128)(2,1)S(1)}, bf16[1280,256]{1,0:T(8,128)(2,1)S(1)}, bf16[128,256]{1,0:T(8,128)(2,1)S(1)}) custom-call(s32[1]{0:T(128)} %bitcast.2.refs_0_, s32[32,128]{1,0:T(8,128)S(1)} %bitcast.8, s32[16,256]{1,0:T(8,128)S(1)} %copy-done.4, bf16[128,256]{1,0:T(8,128)(2,1)S(1)} %copy-done.3), custom_call_target="tpu_custom_call" | custom-call | flops 268435456 | bytes 1048576 | tf_op jit(solution)/shard_map/route/pallas_call | solution.py:254
  11.2 1.1 %collective-permute-done.2.refs_3_ = bf16[128,256]{1,0:T(8,128)(2,1)S(1)} collective-permute-done((bf16[128,256]{1,0:T(8,128)(2,1)}, bf16[128,256]{1,0:T(8,128)(2,1)S(1)}, u32[]{:S(2)}, u32[]{:S(2)}) %collective-permute-start.2) | collective-permute-done | bytes 65568 | tf_op jit(solution)/shard_map/ppermute | solution.py:245
  12.3 1.3 %forward.1.after_ref = bf16[16,80,256]{2,1,0:T(8,128)(2,1)} custom-call(bf16[1280,512]{1,0:T(8,128)(2,1)S(1)} %get-tuple-element.15.forward_ref, bf16[128,256]{1,0:T(8,128)(2,1)S(1)} %get-tuple-element.16.refs_0_, bf16[128,256]{1,0:T(8,128)(2,1)S(1)} %collective-permute-done.refs_1_, bf16[128,256]{1,0:T(8,128)(2,1)S(1)} %collective-permute-done.1.refs_2_, ...), custom_call_target="tpu_custom_call" | custom-call | flops 268435456 | bytes 1048576 | tf_op jit(solution)/shard_map/forward/pallas_call | solution.py:268
  13.6 4.2 %all-to-all-start.1 = ((bf16[16,80,256]{2,1,0:T(8,128)(2,1)}), bf16[16,80,256]{2,1,0:T(8,128)(2,1)S(1)}, u32[]{:S(2)}, u32[]{:S(2)}) async-start(bf16[16,80,256]{2,1,0:T(8,128)(2,1)} %forward.1.after_ref), calls=%async_computation.1 | async-start | bytes 1310720 | tf_op jit(solution)/shard_map/all_to_all | solution.py:277
  17.8 8.9 %ladder.1.after_ref = s16[16,272,256]{2,1,0:T(8,128)(2,1)} custom-call(bf16[256,2048]{1,0:T(8,128)(2,1)S(1)} %copy-done, bf16[2048,4096]{1,0:T(8,128)(2,1)} %int_ref.1, bf16[16,80,256]{2,1,0:T(8,128)(2,1)} %forward.1.after_ref), custom_call_target="tpu_custom_call" | custom-call | flops 4294967296 | bytes 18874368 | tf_op jit(solution)/shard_map/ladder/pallas_call | solution.py:280
  26.7 1.2 %all-to-all-done.1.second_ref = bf16[16,80,256]{2,1,0:T(8,128)(2,1)S(1)} async-done(((bf16[16,80,256]{2,1,0:T(8,128)(2,1)}), bf16[16,80,256]{2,1,0:T(8,128)(2,1)S(1)}, u32[]{:S(2)}, u32[]{:S(2)}) %all-to-all-start.1) | async-done | bytes 655392 | tf_op jit(solution)/shard_map/all_to_all | solution.py:277
  27.9 5.6 %all-to-all-start = ((s16[16,272,256]{2,1,0:T(8,128)(2,1)}), s16[16,272,256]{2,1,0:T(8,128)(2,1)}, u32[]{:S(2)}, u32[]{:S(2)}) async-start(s16[16,272,256]{2,1,0:T(8,128)(2,1)} %ladder.1.after_ref), calls=%async_computation | async-start | bytes 4456448 | tf_op jit(solution)/shard_map/all_to_all | solution.py:297
  33.9 6.1 %collective-permute-start.6 = (bf16[256,256]{1,0:T(8,128)(2,1)S(1)}, bf16[256,256]{1,0:T(8,128)(2,1)S(1)}, u32[]{:S(2)}, u32[]{:S(2)}) collective-permute-start(bf16[256,256]{1,0:T(8,128)(2,1)S(1)} %settle.1), channel_id=1, source_target_pairs={{0,12},{1,13},{2,14},{3,15},{4,0},{5,1},{6,2},{7,3},{8,4},{9,5},{1... | collective-permute-start | bytes 393224 | tf_op jit(solution)/shard_map/ppermute | solution.py:229
  40.0 0.7 %collective-permute-start.3 = (bf16[256,256]{1,0:T(8,128)(2,1)S(1)}, bf16[256,256]{1,0:T(8,128)(2,1)S(1)}, u32[]{:S(2)}, u32[]{:S(2)}) collective-permute-start(bf16[256,256]{1,0:T(8,128)(2,1)S(1)} %settle.1), channel_id=1, source_target_pairs={{0,2},{1,3},{2,4},{3,5},{4,6},{5,7},{6,8},{7,9},{8,10},{9,11},{10,... | collective-permute-start | bytes 393224 | tf_op jit(solution)/shard_map/ppermute | solution.py:229
  40.7 2.4 %collective-permute-start.4 = (bf16[256,256]{1,0:T(8,128)(2,1)S(1)}, bf16[256,256]{1,0:T(8,128)(2,1)S(1)}, u32[]{:S(2)}, u32[]{:S(2)}) collective-permute-start(bf16[256,256]{1,0:T(8,128)(2,1)S(1)} %settle.1), channel_id=1, source_target_pairs={{0,14},{1,15},{2,0},{3,1},{4,2},{5,3},{6,4},{7,5},{8,6},{9,7},{10,... | collective-permute-start | bytes 393224 | tf_op jit(solution)/shard_map/ppermute | solution.py:229
  43.1 3.6 %collective-permute-done.5.zero_ref = bf16[256,256]{1,0:T(8,128)(2,1)S(1)} collective-permute-done((bf16[256,256]{1,0:T(8,128)(2,1)S(1)}, bf16[256,256]{1,0:T(8,128)(2,1)S(1)}, u32[]{:S(2)}, u32[]{:S(2)}) %collective-permute-start.5) | collective-permute-done | bytes 131104 | tf_op jit(solution)/shard_map/ppermute | solution.py:229
  46.8 0.4 collective-permute-start.9
  47.2 1.6 %collective-permute-start.8 = (bf16[256,256]{1,0:T(8,128)(2,1)S(1)}, bf16[256,256]{1,0:T(8,128)(2,1)S(1)}, u32[]{:S(2)}, u32[]{:S(2)}) collective-permute-start(bf16[256,256]{1,0:T(8,128)(2,1)S(1)} %collective-permute-done.6.one_ref), channel_id=1, source_target_pairs={{0,14},{1,15},{2,0},{3,1},{4,2},{5,3},{6,4},{7,5},{8,6},{9,7},{10,... | collective-permute-start | bytes 393224 | tf_op jit(solution)/shard_map/ppermute | solution.py:229
  48.8 0.4 collective-permute-done.3
  49.3 6.9 %collective-permute-start.10 = (bf16[1280,256]{1,0:T(8,128)(2,1)S(1)}, bf16[1280,256]{1,0:T(8,128)(2,1)S(1)}, u32[]{:S(2)}, u32[]{:S(2)}) collective-permute-start(bf16[1280,256]{1,0:T(8,128)(2,1)S(1)} %constant_dynamic-update-slice_fusion.refs_0_), channel_id=1, source_target_pairs={{0,1},{1,0},{2,3},{3,2},{4,5},{5,4},{6,7},{7,6},{8,9},{9,8},{10,11... | collective-permute-start | bytes 1966088 | tf_op jit(solution)/shard_map/ppermute | solution.py:229
  56.2 6.1 %collective-permute-start.11 = (bf16[768,256]{1,0:T(8,128)(2,1)S(1)}, bf16[768,256]{1,0:T(8,128)(2,1)S(1)}, u32[]{:S(2)}, u32[]{:S(2)}) collective-permute-start(bf16[768,256]{1,0:T(8,128)(2,1)S(1)} %constant_dynamic-update-slice_fusion.5.refs_1_), channel_id=1, source_target_pairs={{0,1},{1,0},{2,3},{3,2},{4,5},{5,4},{6,7},{7,6},{8,9},{9,8},{10,11... | collective-permute-start | bytes 1179656 | tf_op jit(solution)/shard_map/ppermute | solution.py:229
  62.6 1.1 %collective-permute-done.11.refs_3_ = bf16[768,256]{1,0:T(8,128)(2,1)S(1)} collective-permute-done((bf16[768,256]{1,0:T(8,128)(2,1)S(1)}, bf16[768,256]{1,0:T(8,128)(2,1)S(1)}, u32[]{:S(2)}, u32[]{:S(2)}) %collective-permute-start.11) | collective-permute-done | bytes 393248 | tf_op jit(solution)/shard_map/ppermute | solution.py:229
  63.7 4.5 %finish.1 = f32[256,256]{1,0:T(8,128)} custom-call(s32[2]{0:T(128)S(1)} %pad_add_fusion.place_ref, bf16[256,4096]{1,0:T(8,128)(2,1)} %far_pair_ref.1, s16[16,272,256]{2,1,0:T(8,128)(2,1)} %all-to-all-done.far_coded_ref, f32[256,1]{1,0:T(8,128)S(1)} %copy.7.occ_ref, f32[1,256]{1,0:T(1,128)S(1)} %bitcast.6, ...), custom_call_target="tpu_custom_call" | custom-call | flops 1073741824 | bytes 8388608 | tf_op jit(solution)/shard_map/finish/pallas_call | solution.py:327
  (33 shorter events, 0.7 us)
Async XLA Ops:
  0.0 8.7 %copy-start.2 = (s32[4096]{0:T(1024)S(1)}, s32[4096]{0:T(1024)}, u32[]{:S(2)}) copy-start(s32[4096]{0:T(1024)} %param.9) | copy-start | bytes 49156
  3.8 7.4 %collective-permute-start = (bf16[128,256]{1,0:T(8,128)(2,1)}, bf16[128,256]{1,0:T(8,128)(2,1)S(1)}, u32[]{:S(2)}, u32[]{:S(2)}) collective-permute-start(bf16[128,256]{1,0:T(8,128)(2,1)} %get-tuple-element.17), channel_id=1, source_target_pairs={{0,64},{16,80},{32,96},{48,112},{64,128},{80,144},{96,160},{112,17... | collective-permute-start | bytes 196616 | tf_op jit(solution)/shard_map/ppermute | solution.py:245
  5.9 5.3 %collective-permute-start.1 = (bf16[128,256]{1,0:T(8,128)(2,1)}, bf16[128,256]{1,0:T(8,128)(2,1)S(1)}, u32[]{:S(2)}, u32[]{:S(2)}) collective-permute-start(bf16[128,256]{1,0:T(8,128)(2,1)} %get-tuple-element.18), channel_id=1, source_target_pairs={{0,192},{16,208},{32,224},{48,240},{64,0},{80,16},{96,32},{112,48}... | collective-permute-start | bytes 196616 | tf_op jit(solution)/shard_map/ppermute | solution.py:245
  7.3 5.0 %collective-permute-start.2 = (bf16[128,256]{1,0:T(8,128)(2,1)}, bf16[128,256]{1,0:T(8,128)(2,1)S(1)}, u32[]{:S(2)}, u32[]{:S(2)}) collective-permute-start(bf16[128,256]{1,0:T(8,128)(2,1)} %get-tuple-element.19), channel_id=1, source_target_pairs={{0,16},{16,32},{32,48},{48,0},{64,80},{80,96},{96,112},{112,64},{1... | collective-permute-start | bytes 196616 | tf_op jit(solution)/shard_map/ppermute | solution.py:245
  8.7 0.8 %copy-start.3 = (bf16[128,256]{1,0:T(8,128)(2,1)S(1)}, bf16[128,256]{1,0:T(8,128)(2,1)}, u32[]{:S(2)}) copy-start(bf16[128,256]{1,0:T(8,128)(2,1)} %get-tuple-element.14.refs_3_) | copy-start | bytes 196612
  9.5 0.7 %copy-start.4 = (s32[16,256]{1,0:T(8,128)S(1)}, s32[16,256]{1,0:T(8,128)}, u32[]{:S(2)}) copy-start(s32[16,256]{1,0:T(8,128)} %get-tuple-element.13.refs_2_) | copy-start | bytes 49156
  10.2 7.6 %copy-start = (bf16[256,2048]{1,0:T(8,128)(2,1)S(1)}, bf16[256,2048]{1,0:T(8,128)(2,1)}, u32[]{:S(2)}) copy-start(bf16[256,2048]{1,0:T(8,128)(2,1)} %amp_ref.1) | copy-start | bytes 3145732
  13.6 14.3 %all-to-all-start.1 = ((bf16[16,80,256]{2,1,0:T(8,128)(2,1)}), bf16[16,80,256]{2,1,0:T(8,128)(2,1)S(1)}, u32[]{:S(2)}, u32[]{:S(2)}) async-start(bf16[16,80,256]{2,1,0:T(8,128)(2,1)} %forward.1.after_ref), calls=%async_computation.1 | async-start | bytes 1310720 | tf_op jit(solution)/shard_map/all_to_all | solution.py:277
  27.9 35.8 %all-to-all-start = ((s16[16,272,256]{2,1,0:T(8,128)(2,1)}), s16[16,272,256]{2,1,0:T(8,128)(2,1)}, u32[]{:S(2)}, u32[]{:S(2)}) async-start(s16[16,272,256]{2,1,0:T(8,128)(2,1)} %ladder.1.after_ref), calls=%async_computation | async-start | bytes 4456448 | tf_op jit(solution)/shard_map/all_to_all | solution.py:297
  33.5 28.9 %copy-start.5 = (f32[256]{0:T(256)S(1)}, f32[256]{0:T(256)}, u32[]{:S(2)}) copy-start(f32[256]{0:T(256)} %param.10) | copy-start | bytes 3076
  33.9 29.8 %copy-start.1 = (f32[256]{0:T(256)S(1)}, f32[256]{0:T(256)}, u32[]{:S(2)}) copy-start(f32[256]{0:T(256)} %param.11) | copy-start | bytes 3076
  33.9 9.2 %collective-permute-start.6 = (bf16[256,256]{1,0:T(8,128)(2,1)S(1)}, bf16[256,256]{1,0:T(8,128)(2,1)S(1)}, u32[]{:S(2)}, u32[]{:S(2)}) collective-permute-start(bf16[256,256]{1,0:T(8,128)(2,1)S(1)} %settle.1), channel_id=1, source_target_pairs={{0,12},{1,13},{2,14},{3,15},{4,0},{5,1},{6,2},{7,3},{8,4},{9,5},{1... | collective-permute-start | bytes 393224 | tf_op jit(solution)/shard_map/ppermute | solution.py:229
  40.0 6.8 %collective-permute-start.5 = (bf16[256,256]{1,0:T(8,128)(2,1)S(1)}, bf16[256,256]{1,0:T(8,128)(2,1)S(1)}, u32[]{:S(2)}, u32[]{:S(2)}) collective-permute-start(bf16[256,256]{1,0:T(8,128)(2,1)S(1)} %settle.1), channel_id=1, source_target_pairs={{0,4},{1,5},{2,6},{3,7},{4,8},{5,9},{6,10},{7,11},{8,12},{9,13},{1... | collective-permute-start | bytes 393224 | tf_op jit(solution)/shard_map/ppermute | solution.py:229
  40.0 9.3 %collective-permute-start.3 = (bf16[256,256]{1,0:T(8,128)(2,1)S(1)}, bf16[256,256]{1,0:T(8,128)(2,1)S(1)}, u32[]{:S(2)}, u32[]{:S(2)}) collective-permute-start(bf16[256,256]{1,0:T(8,128)(2,1)S(1)} %settle.1), channel_id=1, source_target_pairs={{0,2},{1,3},{2,4},{3,5},{4,6},{5,7},{6,8},{7,9},{8,10},{9,11},{10,... | collective-permute-start | bytes 393224 | tf_op jit(solution)/shard_map/ppermute | solution.py:229
  40.7 8.5 %collective-permute-start.4 = (bf16[256,256]{1,0:T(8,128)(2,1)S(1)}, bf16[256,256]{1,0:T(8,128)(2,1)S(1)}, u32[]{:S(2)}, u32[]{:S(2)}) collective-permute-start(bf16[256,256]{1,0:T(8,128)(2,1)S(1)} %settle.1), channel_id=1, source_target_pairs={{0,14},{1,15},{2,0},{3,1},{4,2},{5,3},{6,4},{7,5},{8,6},{9,7},{10,... | collective-permute-start | bytes 393224 | tf_op jit(solution)/shard_map/ppermute | solution.py:229
  46.8 9.4 %collective-permute-start.9 = (bf16[256,256]{1,0:T(8,128)(2,1)S(1)}, bf16[256,256]{1,0:T(8,128)(2,1)S(1)}, u32[]{:S(2)}, u32[]{:S(2)}) collective-permute-start(bf16[256,256]{1,0:T(8,128)(2,1)S(1)} %either.1), channel_id=1, source_target_pairs={{0,4},{1,13},{2,6},{3,15},{4,8},{5,1},{6,10},{7,3},{8,12},{9,5},{1... | collective-permute-start | bytes 393224 | tf_op jit(solution)/shard_map/ppermute | solution.py:229
  47.2 9.0 %collective-permute-start.8 = (bf16[256,256]{1,0:T(8,128)(2,1)S(1)}, bf16[256,256]{1,0:T(8,128)(2,1)S(1)}, u32[]{:S(2)}, u32[]{:S(2)}) collective-permute-start(bf16[256,256]{1,0:T(8,128)(2,1)S(1)} %collective-permute-done.6.one_ref), channel_id=1, source_target_pairs={{0,14},{1,15},{2,0},{3,1},{4,2},{5,3},{6,4},{7,5},{8,6},{9,7},{10,... | collective-permute-start | bytes 393224 | tf_op jit(solution)/shard_map/ppermute | solution.py:229
  48.8 7.4 %collective-permute-start.7 = (bf16[256,256]{1,0:T(8,128)(2,1)S(1)}, bf16[256,256]{1,0:T(8,128)(2,1)S(1)}, u32[]{:S(2)}, u32[]{:S(2)}) collective-permute-start(bf16[256,256]{1,0:T(8,128)(2,1)S(1)} %collective-permute-done.5.zero_ref), channel_id=1, source_target_pairs={{0,2},{1,3},{2,4},{3,5},{4,6},{5,7},{6,8},{7,9},{8,10},{9,11},{10,... | collective-permute-start | bytes 393224 | tf_op jit(solution)/shard_map/ppermute | solution.py:229
  49.3 14.4 %collective-permute-start.10 = (bf16[1280,256]{1,0:T(8,128)(2,1)S(1)}, bf16[1280,256]{1,0:T(8,128)(2,1)S(1)}, u32[]{:S(2)}, u32[]{:S(2)}) collective-permute-start(bf16[1280,256]{1,0:T(8,128)(2,1)S(1)} %constant_dynamic-update-slice_fusion.refs_0_), channel_id=1, source_target_pairs={{0,1},{1,0},{2,3},{3,2},{4,5},{5,4},{6,7},{7,6},{8,9},{9,8},{10,11... | collective-permute-start | bytes 1966088 | tf_op jit(solution)/shard_map/ppermute | solution.py:229
  56.2 7.4 %collective-permute-start.11 = (bf16[768,256]{1,0:T(8,128)(2,1)S(1)}, bf16[768,256]{1,0:T(8,128)(2,1)S(1)}, u32[]{:S(2)}, u32[]{:S(2)}) collective-permute-start(bf16[768,256]{1,0:T(8,128)(2,1)S(1)} %constant_dynamic-update-slice_fusion.5.refs_1_), channel_id=1, source_target_pairs={{0,1},{1,0},{2,3},{3,2},{4,5},{5,4},{6,7},{7,6},{8,9},{9,8},{10,11... | collective-permute-start | bytes 1179656 | tf_op jit(solution)/shard_map/ppermute | solution.py:229

commit v8 on v7

--- a/solution.py
+++ b/solution.py
@@ -177,34 +177,39 @@
         out_ref[...] = one_ref[...]
 
 
-def finish_kernel(place_ref, far_pair_ref, far_coded_ref, occ_ref, virt_ref, *refs):
-    *groups, out_ref, pair_ref, coded_ref, ordered_ref, sems = refs
-    piece = CHUNKS // PIECES
-    fetches = [pltpu.make_async_copy(far_pair_ref, pair_ref, sems.at[PIECES])]
-    for k in range(PIECES):
-        some = pl.ds(k * piece, piece)
-        fetches.append(
-            pltpu.make_async_copy(far_coded_ref.at[some], coded_ref.at[some], sems.at[k])
-        )
-    for fetch in fetches:
-        fetch.start()
+def finish_kernel(place_ref, pair_ref, far_coded_ref, occ_ref, virt_ref, *refs):
+    *groups, out_ref, coded_ref, ordered_ref, coded_sems, block_sems = refs
     z, core = place_ref[0], place_ref[1]
     rows = out_ref.shape[0]
     chips = (0, 1, -1, 2, -2, 3, -3, 4)
-    slot = 0
+    blocks = []
     for group_ref in groups:
         for k in range(group_ref.shape[0] // rows):
+            slot = len(blocks)
             which = core if slot < len(chips) else 1 - core
             n = jnp.bitwise_and(z - chips[slot % len(chips)] + 8, 7) * 2 + which
             held = pl.ds(pl.multiple_of(n * rows, rows), rows)
-            ordered_ref[held, :] = group_ref[k * rows : (k + 1) * rows, :]
-            slot += 1
-    fetches[0].wait()
+            blocks.append(
+                pltpu.make_async_copy(
+                    group_ref.at[pl.ds(k * rows, rows)], ordered_ref.at[held], block_sems.at[slot]
+                )
+            )
+    piece = CHUNKS // PIECES
+    shares = []
+    for k in range(PIECES):
+        some = pl.ds(k * piece, piece)
+        shares.append(
+            pltpu.make_async_copy(far_coded_ref.at[some], coded_ref.at[some], coded_sems.at[k])
+        )
+    for copy in blocks + shares:
+        copy.start()
+    for copy in blocks:
+        copy.wait()
     hole = jnp.dot(pair_ref[...], ordered_ref[...], preferred_element_type=jnp.float32)
     total = jnp.zeros(out_ref.shape, jnp.float32)
     for k in range(CHUNKS):
         if k % piece == 0:
-            fetches[1 + k // piece].wait()
+            shares[k // piece].wait()
         code = coded_ref[k, rows:, :].astype(jnp.int32).astype(jnp.float32)[:1, :]
         values = coded_ref[k, :rows, :].astype(jnp.int32).astype(jnp.float32)
         total = total + values * jnp.exp2(code * (1.0 / STEPS))
@@ -327,15 +332,15 @@
     return pl.pallas_call(
         finish_kernel,
         out_shape=jax.ShapeDtypeStruct((height, LANES), jnp.float32),
-        in_specs=[SMEM, HBM, HBM] + [VMEM] * 6,
+        in_specs=[SMEM, VMEM, HBM, VMEM, VMEM] + [HBM] * 4,
         out_specs=VMEM,
         scratch_shapes=[
-            pltpu.VMEM(pair_integrals.shape, jnp.bfloat16),
             pltpu.VMEM(shares.shape, jnp.int16),
             pltpu.VMEM((CHUNKS * height, LANES), jnp.bfloat16),
-            pltpu.SemaphoreType.DMA((PIECES + 1,)),
+            pltpu.SemaphoreType.DMA((PIECES,)),
+            pltpu.SemaphoreType.DMA((CHUNKS,)),
         ],
-        compiler_params=pltpu.CompilerParams(vmem_limit_bytes=51 << 20),
+        compiler_params=pltpu.CompilerParams(vmem_limit_bytes=48 << 20),
         cost_estimate=pl.CostEstimate(flops=2**30, bytes_accessed=2**23, transcendentals=0),
         name="finish",
     )(

time: 69.3 us -> 71.2 us (1.027)
  Pallas kernels: 19.8 us -> 21.6 us
    pallas_call x1, Pallas kernels: 4.46 us -> 6.26 us  [on_device(): pl.pallas_call(finish_kernel, out_shape=jax.ShapeDtypeStruct((height, LAN...]
    unnamed x18 -> x20, local copies, waits for them, and re-layouts: 1.64 us -> 1.64 us
where the time goes in v8:
time: 71.2 us; the launch traced here: 70.3 us
  starting transfers between devices  38.8 us (54%)
  Pallas kernels  21.6 us (30%)
  waiting for transfers between devices  7.57 us (11%)
  local copies, waits for them, and re-layouts  1.8 us (3%)
    ppermute x9, starting transfers between devices, step(): return lax.ppermute(value, 'narrow', ring)  24.2 us
    pallas_call x1, Pallas kernels, on_device(): pl.pallas_call(ladder_kernel, out_shape=jax.ShapeDtypeStruct((CHUNKS, hei...  8.9 us
    pallas_call x1, Pallas kernels, on_device(): pl.pallas_call(finish_kernel, out_shape=jax.ShapeDtypeStruct((height, LAN...  6.26 us
    all_to_all x1, starting transfers between devices, on_device(): shares = lax.all_to_all(coded, 'wide', 0, 0, tiled=True)  5.57 us
    ppermute x9, waiting for transfers between devices, step(): return lax.ppermute(value, 'narrow', ring)  5.35 us
    ppermute x3, starting transfers between devices, on_device(): lax.ppermute(sent[k], 'wide', [(x * 4 + y, (x + dx) % 4 * 4 + (y + dy) %...  4.88 us
    all_to_all x1, starting transfers between devices, on_device(): second = lax.all_to_all(moved, 'wide', 0, 0, tiled=True)  4.2 us
    pallas_call x1, Pallas kernels, on_device(): pl.pallas_call(lambda *refs: select_kernel(shift, *refs), out_shape=(*[ja...  3.79 us
  transfers between devices with their start and end apart: 14, of which 5 were waited for; matrix products, arithmetic and copies ran while one was open for 0% of the time, Pallas kernels for 15%

profile of v8, /device:TPU:1, one launch (start us, length us, event | category | flops | bytes accessed | tf_op | source)
XLA Modules:
  0.0 70.3 jit_solution(13044076676038924597)
XLA Ops:
  0.0 3.8 %select.1 = (bf16[128,256]{1,0:T(8,128)(2,1)}, bf16[128,256]{1,0:T(8,128)(2,1)}, bf16[128,256]{1,0:T(8,128)(2,1)}, bf16[128,256]{1,0:T(8,128)(2,1)}, s32[16,256]{1,0:T(8,128)}) custom-call(s32[1]{0:T(128)} %bitcast.2.refs_0_, s32[32,128]{1,0:T(8,128)} %bitcast.7, bf16[256,2048]{1,0:T(8,128)(2,1)} %amp_ref.1), custom_call_target="tpu_custom_call" | custom-call | flops 1073741824 | bytes 2097152 | tf_op jit(solution)/shard_map/select/pallas_call | solution.py:236
  3.8 2.1 %collective-permute-start = (bf16[128,256]{1,0:T(8,128)(2,1)}, bf16[128,256]{1,0:T(8,128)(2,1)S(1)}, u32[]{:S(2)}, u32[]{:S(2)}) collective-permute-start(bf16[128,256]{1,0:T(8,128)(2,1)} %get-tuple-element.17), channel_id=1, source_target_pairs={{0,64},{16,80},{32,96},{48,112},{64,128},{80,144},{96,160},{112,17... | collective-permute-start | bytes 196616 | tf_op jit(solution)/shard_map/ppermute | solution.py:250
  5.9 1.4 %collective-permute-start.1 = (bf16[128,256]{1,0:T(8,128)(2,1)}, bf16[128,256]{1,0:T(8,128)(2,1)S(1)}, u32[]{:S(2)}, u32[]{:S(2)}) collective-permute-start(bf16[128,256]{1,0:T(8,128)(2,1)} %get-tuple-element.18), channel_id=1, source_target_pairs={{0,192},{16,208},{32,224},{48,240},{64,0},{80,16},{96,32},{112,48}... | collective-permute-start | bytes 196616 | tf_op jit(solution)/shard_map/ppermute | solution.py:250
  7.3 1.4 %collective-permute-start.2 = (bf16[128,256]{1,0:T(8,128)(2,1)}, bf16[128,256]{1,0:T(8,128)(2,1)S(1)}, u32[]{:S(2)}, u32[]{:S(2)}) collective-permute-start(bf16[128,256]{1,0:T(8,128)(2,1)} %get-tuple-element.19), channel_id=1, source_target_pairs={{0,16},{16,32},{32,48},{48,0},{64,80},{80,96},{96,112},{112,64},{1... | collective-permute-start | bytes 196616 | tf_op jit(solution)/shard_map/ppermute | solution.py:250
  8.7 0.8 %copy-done.4 = bf16[128,256]{1,0:T(8,128)(2,1)S(1)} copy-done((bf16[128,256]{1,0:T(8,128)(2,1)S(1)}, bf16[128,256]{1,0:T(8,128)(2,1)}, u32[]{:S(2)}) %copy-start.4) | copy-done | bytes 65560
  9.5 0.7 %copy-done.5 = s32[16,256]{1,0:T(8,128)S(1)} copy-done((s32[16,256]{1,0:T(8,128)S(1)}, s32[16,256]{1,0:T(8,128)}, u32[]{:S(2)}) %copy-start.5) | copy-done | bytes 16408
  10.2 0.9 %route.1 = (bf16[1280,512]{1,0:T(8,128)(2,1)S(1)}, bf16[1280,256]{1,0:T(8,128)(2,1)S(1)}, bf16[128,256]{1,0:T(8,128)(2,1)S(1)}) custom-call(s32[1]{0:T(128)} %bitcast.2.refs_0_, s32[32,128]{1,0:T(8,128)S(1)} %bitcast.8, s32[16,256]{1,0:T(8,128)S(1)} %copy-done.5, bf16[128,256]{1,0:T(8,128)(2,1)S(1)} %copy-done.4), custom_call_target="tpu_custom_call" | custom-call | flops 268435456 | bytes 1048576 | tf_op jit(solution)/shard_map/route/pallas_call | solution.py:259
  11.2 1.1 %collective-permute-done.2.refs_3_ = bf16[128,256]{1,0:T(8,128)(2,1)S(1)} collective-permute-done((bf16[128,256]{1,0:T(8,128)(2,1)}, bf16[128,256]{1,0:T(8,128)(2,1)S(1)}, u32[]{:S(2)}, u32[]{:S(2)}) %collective-permute-start.2) | collective-permute-done | bytes 65568 | tf_op jit(solution)/shard_map/ppermute | solution.py:250
  12.3 1.3 %forward.1.after_ref = bf16[16,80,256]{2,1,0:T(8,128)(2,1)} custom-call(bf16[1280,512]{1,0:T(8,128)(2,1)S(1)} %get-tuple-element.15.forward_ref, bf16[128,256]{1,0:T(8,128)(2,1)S(1)} %get-tuple-element.16.refs_0_, bf16[128,256]{1,0:T(8,128)(2,1)S(1)} %collective-permute-done.refs_1_, bf16[128,256]{1,0:T(8,128)(2,1)S(1)} %collective-permute-done.1.refs_2_, ...), custom_call_target="tpu_custom_call" | custom-call | flops 268435456 | bytes 1048576 | tf_op jit(solution)/shard_map/forward/pallas_call | solution.py:273
  13.6 4.2 %all-to-all-start.1 = ((bf16[16,80,256]{2,1,0:T(8,128)(2,1)}), bf16[16,80,256]{2,1,0:T(8,128)(2,1)S(1)}, u32[]{:S(2)}, u32[]{:S(2)}) async-start(bf16[16,80,256]{2,1,0:T(8,128)(2,1)} %forward.1.after_ref), calls=%async_computation.1 | async-start | bytes 1310720 | tf_op jit(solution)/shard_map/all_to_all | solution.py:282
  17.8 8.9 %ladder.1.after_ref = s16[16,272,256]{2,1,0:T(8,128)(2,1)} custom-call(bf16[256,2048]{1,0:T(8,128)(2,1)S(1)} %copy-done.1, bf16[2048,4096]{1,0:T(8,128)(2,1)} %int_ref.1, bf16[16,80,256]{2,1,0:T(8,128)(2,1)} %forward.1.after_ref), custom_call_target="tpu_custom_call" | custom-call | flops 4294967296 | bytes 18874368 | tf_op jit(solution)/shard_map/ladder/pallas_call | solution.py:285
  26.7 1.2 %all-to-all-done.1.second_ref = bf16[16,80,256]{2,1,0:T(8,128)(2,1)S(1)} async-done(((bf16[16,80,256]{2,1,0:T(8,128)(2,1)}), bf16[16,80,256]{2,1,0:T(8,128)(2,1)S(1)}, u32[]{:S(2)}, u32[]{:S(2)}) %all-to-all-start.1) | async-done | bytes 655392 | tf_op jit(solution)/shard_map/all_to_all | solution.py:282
  27.9 5.6 %all-to-all-start = ((s16[16,272,256]{2,1,0:T(8,128)(2,1)}), s16[16,272,256]{2,1,0:T(8,128)(2,1)}, u32[]{:S(2)}, u32[]{:S(2)}) async-start(s16[16,272,256]{2,1,0:T(8,128)(2,1)} %ladder.1.after_ref), calls=%async_computation | async-start | bytes 4456448 | tf_op jit(solution)/shard_map/all_to_all | solution.py:302
  33.9 6.1 %collective-permute-start.6 = (bf16[256,256]{1,0:T(8,128)(2,1)S(1)}, bf16[256,256]{1,0:T(8,128)(2,1)S(1)}, u32[]{:S(2)}, u32[]{:S(2)}) collective-permute-start(bf16[256,256]{1,0:T(8,128)(2,1)S(1)} %settle.1), channel_id=1, source_target_pairs={{0,12},{1,13},{2,14},{3,15},{4,0},{5,1},{6,2},{7,3},{8,4},{9,5},{1... | collective-permute-start | bytes 393224 | tf_op jit(solution)/shard_map/ppermute | solution.py:234
  40.0 0.7 %collective-permute-start.3 = (bf16[256,256]{1,0:T(8,128)(2,1)S(1)}, bf16[256,256]{1,0:T(8,128)(2,1)S(1)}, u32[]{:S(2)}, u32[]{:S(2)}) collective-permute-start(bf16[256,256]{1,0:T(8,128)(2,1)S(1)} %settle.1), channel_id=1, source_target_pairs={{0,2},{1,3},{2,4},{3,5},{4,6},{5,7},{6,8},{7,9},{8,10},{9,11},{10,... | collective-permute-start | bytes 393224 | tf_op jit(solution)/shard_map/ppermute | solution.py:234
  40.7 2.4 %collective-permute-start.4 = (bf16[256,256]{1,0:T(8,128)(2,1)S(1)}, bf16[256,256]{1,0:T(8,128)(2,1)S(1)}, u32[]{:S(2)}, u32[]{:S(2)}) collective-permute-start(bf16[256,256]{1,0:T(8,128)(2,1)S(1)} %settle.1), channel_id=1, source_target_pairs={{0,14},{1,15},{2,0},{3,1},{4,2},{5,3},{6,4},{7,5},{8,6},{9,7},{10,... | collective-permute-start | bytes 393224 | tf_op jit(solution)/shard_map/ppermute | solution.py:234
  43.1 3.6 %collective-permute-done.5.zero_ref = bf16[256,256]{1,0:T(8,128)(2,1)S(1)} collective-permute-done((bf16[256,256]{1,0:T(8,128)(2,1)S(1)}, bf16[256,256]{1,0:T(8,128)(2,1)S(1)}, u32[]{:S(2)}, u32[]{:S(2)}) %collective-permute-start.5) | collective-permute-done | bytes 131104 | tf_op jit(solution)/shard_map/ppermute | solution.py:234
  46.8 0.4 collective-permute-start.9
  47.2 1.6 %collective-permute-start.8 = (bf16[256,256]{1,0:T(8,128)(2,1)S(1)}, bf16[256,256]{1,0:T(8,128)(2,1)S(1)}, u32[]{:S(2)}, u32[]{:S(2)}) collective-permute-start(bf16[256,256]{1,0:T(8,128)(2,1)S(1)} %collective-permute-done.6.one_ref), channel_id=1, source_target_pairs={{0,14},{1,15},{2,0},{3,1},{4,2},{5,3},{6,4},{7,5},{8,6},{9,7},{10,... | collective-permute-start | bytes 393224 | tf_op jit(solution)/shard_map/ppermute | solution.py:234
  48.8 0.4 collective-permute-done.3
  49.3 6.9 %collective-permute-start.10 = (bf16[1280,256]{1,0:T(8,128)(2,1)S(1)}, bf16[1280,256]{1,0:T(8,128)(2,1)}, u32[]{:S(2)}, u32[]{:S(2)}) collective-permute-start(bf16[1280,256]{1,0:T(8,128)(2,1)S(1)} %constant_dynamic-update-slice_fusion.refs_0_), channel_id=1, source_target_pairs={{0,1},{1,0},{2,3},{3,2},{4,5},{5,4},{6,7},{7,6},{8,9},{9,8},{10,11... | collective-permute-start | bytes 1966088 | tf_op jit(solution)/shard_map/ppermute | solution.py:234
  56.3 6.1 %collective-permute-start.11 = (bf16[768,256]{1,0:T(8,128)(2,1)S(1)}, bf16[768,256]{1,0:T(8,128)(2,1)}, u32[]{:S(2)}, u32[]{:S(2)}) collective-permute-start(bf16[768,256]{1,0:T(8,128)(2,1)S(1)} %constant_dynamic-update-slice_fusion.5.refs_1_), channel_id=1, source_target_pairs={{0,1},{1,0},{2,3},{3,2},{4,5},{5,4},{6,7},{7,6},{8,9},{9,8},{10,11... | collective-permute-start | bytes 1179656 | tf_op jit(solution)/shard_map/ppermute | solution.py:234
  62.6 1.3 %collective-permute-done.11.refs_3_ = bf16[768,256]{1,0:T(8,128)(2,1)} collective-permute-done((bf16[768,256]{1,0:T(8,128)(2,1)S(1)}, bf16[768,256]{1,0:T(8,128)(2,1)}, u32[]{:S(2)}, u32[]{:S(2)}) %collective-permute-start.11) | collective-permute-done | bytes 393248 | tf_op jit(solution)/shard_map/ppermute | solution.py:234
  63.9 6.3 %finish.1 = f32[256,256]{1,0:T(8,128)} custom-call(s32[2]{0:T(128)S(1)} %pad_add_fusion.place_ref, bf16[256,4096]{1,0:T(8,128)(2,1)S(1)} %copy-done, s16[16,272,256]{2,1,0:T(8,128)(2,1)} %all-to-all-done.far_coded_ref, f32[256,1]{1,0:T(8,128)S(1)} %copy.7.occ_ref, f32[1,256]{1,0:T(1,128)S(1)} %bitcast.6, ...), custom_call_target="tpu_custom_call" | custom-call | flops 1073741824 | bytes 8388608 | tf_op jit(solution)/shard_map/finish/pallas_call | solution.py:332
  (35 shorter events, 0.7 us)
Async XLA Ops:
  0.0 8.7 %copy-start.3 = (s32[4096]{0:T(1024)S(1)}, s32[4096]{0:T(1024)}, u32[]{:S(2)}) copy-start(s32[4096]{0:T(1024)} %param.9) | copy-start | bytes 49156
  3.8 7.4 %collective-permute-start = (bf16[128,256]{1,0:T(8,128)(2,1)}, bf16[128,256]{1,0:T(8,128)(2,1)S(1)}, u32[]{:S(2)}, u32[]{:S(2)}) collective-permute-start(bf16[128,256]{1,0:T(8,128)(2,1)} %get-tuple-element.17), channel_id=1, source_target_pairs={{0,64},{16,80},{32,96},{48,112},{64,128},{80,144},{96,160},{112,17... | collective-permute-start | bytes 196616 | tf_op jit(solution)/shard_map/ppermute | solution.py:250
  5.9 5.3 %collective-permute-start.1 = (bf16[128,256]{1,0:T(8,128)(2,1)}, bf16[128,256]{1,0:T(8,128)(2,1)S(1)}, u32[]{:S(2)}, u32[]{:S(2)}) collective-permute-start(bf16[128,256]{1,0:T(8,128)(2,1)} %get-tuple-element.18), channel_id=1, source_target_pairs={{0,192},{16,208},{32,224},{48,240},{64,0},{80,16},{96,32},{112,48}... | collective-permute-start | bytes 196616 | tf_op jit(solution)/shard_map/ppermute | solution.py:250
  7.3 5.0 %collective-permute-start.2 = (bf16[128,256]{1,0:T(8,128)(2,1)}, bf16[128,256]{1,0:T(8,128)(2,1)S(1)}, u32[]{:S(2)}, u32[]{:S(2)}) collective-permute-start(bf16[128,256]{1,0:T(8,128)(2,1)} %get-tuple-element.19), channel_id=1, source_target_pairs={{0,16},{16,32},{32,48},{48,0},{64,80},{80,96},{96,112},{112,64},{1... | collective-permute-start | bytes 196616 | tf_op jit(solution)/shard_map/ppermute | solution.py:250
  8.7 0.8 %copy-start.4 = (bf16[128,256]{1,0:T(8,128)(2,1)S(1)}, bf16[128,256]{1,0:T(8,128)(2,1)}, u32[]{:S(2)}) copy-start(bf16[128,256]{1,0:T(8,128)(2,1)} %get-tuple-element.14.refs_3_) | copy-start | bytes 196612
  9.5 0.7 %copy-start.5 = (s32[16,256]{1,0:T(8,128)S(1)}, s32[16,256]{1,0:T(8,128)}, u32[]{:S(2)}) copy-start(s32[16,256]{1,0:T(8,128)} %get-tuple-element.13.refs_2_) | copy-start | bytes 49156
  10.2 7.6 %copy-start.1 = (bf16[256,2048]{1,0:T(8,128)(2,1)S(1)}, bf16[256,2048]{1,0:T(8,128)(2,1)}, u32[]{:S(2)}) copy-start(bf16[256,2048]{1,0:T(8,128)(2,1)} %amp_ref.1) | copy-start | bytes 3145732
  13.6 14.3 %all-to-all-start.1 = ((bf16[16,80,256]{2,1,0:T(8,128)(2,1)}), bf16[16,80,256]{2,1,0:T(8,128)(2,1)S(1)}, u32[]{:S(2)}, u32[]{:S(2)}) async-start(bf16[16,80,256]{2,1,0:T(8,128)(2,1)} %forward.1.after_ref), calls=%async_computation.1 | async-start | bytes 1310720 | tf_op jit(solution)/shard_map/all_to_all | solution.py:282
  27.9 35.9 %all-to-all-start = ((s16[16,272,256]{2,1,0:T(8,128)(2,1)}), s16[16,272,256]{2,1,0:T(8,128)(2,1)}, u32[]{:S(2)}, u32[]{:S(2)}) async-start(s16[16,272,256]{2,1,0:T(8,128)(2,1)} %ladder.1.after_ref), calls=%async_computation | async-start | bytes 4456448 | tf_op jit(solution)/shard_map/all_to_all | solution.py:302
  33.5 28.9 %copy-start.6 = (f32[256]{0:T(256)S(1)}, f32[256]{0:T(256)}, u32[]{:S(2)}) copy-start(f32[256]{0:T(256)} %param.10) | copy-start | bytes 3076
  33.9 30.0 %copy-start = (bf16[256,4096]{1,0:T(8,128)(2,1)S(1)}, bf16[256,4096]{1,0:T(8,128)(2,1)}, u32[]{:S(2)}) copy-start(bf16[256,4096]{1,0:T(8,128)(2,1)} %pair_ref.1) | copy-start | bytes 6291460
  33.9 30.0 %copy-start.2 = (f32[256]{0:T(256)S(1)}, f32[256]{0:T(256)}, u32[]{:S(2)}) copy-start(f32[256]{0:T(256)} %param.11) | copy-start | bytes 3076
  33.9 9.2 %collective-permute-start.6 = (bf16[256,256]{1,0:T(8,128)(2,1)S(1)}, bf16[256,256]{1,0:T(8,128)(2,1)S(1)}, u32[]{:S(2)}, u32[]{:S(2)}) collective-permute-start(bf16[256,256]{1,0:T(8,128)(2,1)S(1)} %settle.1), channel_id=1, source_target_pairs={{0,12},{1,13},{2,14},{3,15},{4,0},{5,1},{6,2},{7,3},{8,4},{9,5},{1... | collective-permute-start | bytes 393224 | tf_op jit(solution)/shard_map/ppermute | solution.py:234
  40.0 6.8 %collective-permute-start.5 = (bf16[256,256]{1,0:T(8,128)(2,1)S(1)}, bf16[256,256]{1,0:T(8,128)(2,1)S(1)}, u32[]{:S(2)}, u32[]{:S(2)}) collective-permute-start(bf16[256,256]{1,0:T(8,128)(2,1)S(1)} %settle.1), channel_id=1, source_target_pairs={{0,4},{1,5},{2,6},{3,7},{4,8},{5,9},{6,10},{7,11},{8,12},{9,13},{1... | collective-permute-start | bytes 393224 | tf_op jit(solution)/shard_map/ppermute | solution.py:234
  40.0 9.2 %collective-permute-start.3 = (bf16[256,256]{1,0:T(8,128)(2,1)S(1)}, bf16[256,256]{1,0:T(8,128)(2,1)S(1)}, u32[]{:S(2)}, u32[]{:S(2)}) collective-permute-start(bf16[256,256]{1,0:T(8,128)(2,1)S(1)} %settle.1), channel_id=1, source_target_pairs={{0,2},{1,3},{2,4},{3,5},{4,6},{5,7},{6,8},{7,9},{8,10},{9,11},{10,... | collective-permute-start | bytes 393224 | tf_op jit(solution)/shard_map/ppermute | solution.py:234
  40.7 8.5 %collective-permute-start.4 = (bf16[256,256]{1,0:T(8,128)(2,1)S(1)}, bf16[256,256]{1,0:T(8,128)(2,1)S(1)}, u32[]{:S(2)}, u32[]{:S(2)}) collective-permute-start(bf16[256,256]{1,0:T(8,128)(2,1)S(1)} %settle.1), channel_id=1, source_target_pairs={{0,14},{1,15},{2,0},{3,1},{4,2},{5,3},{6,4},{7,5},{8,6},{9,7},{10,... | collective-permute-start | bytes 393224 | tf_op jit(solution)/shard_map/ppermute | solution.py:234
  46.8 9.4 %collective-permute-start.9 = (bf16[256,256]{1,0:T(8,128)(2,1)S(1)}, bf16[256,256]{1,0:T(8,128)(2,1)S(1)}, u32[]{:S(2)}, u32[]{:S(2)}) collective-permute-start(bf16[256,256]{1,0:T(8,128)(2,1)S(1)} %either.1), channel_id=1, source_target_pairs={{0,4},{1,13},{2,6},{3,15},{4,8},{5,1},{6,10},{7,3},{8,12},{9,5},{1... | collective-permute-start | bytes 393224 | tf_op jit(solution)/shard_map/ppermute | solution.py:234
  47.2 9.0 %collective-permute-start.8 = (bf16[256,256]{1,0:T(8,128)(2,1)S(1)}, bf16[256,256]{1,0:T(8,128)(2,1)S(1)}, u32[]{:S(2)}, u32[]{:S(2)}) collective-permute-start(bf16[256,256]{1,0:T(8,128)(2,1)S(1)} %collective-permute-done.6.one_ref), channel_id=1, source_target_pairs={{0,14},{1,15},{2,0},{3,1},{4,2},{5,3},{6,4},{7,5},{8,6},{9,7},{10,... | collective-permute-start | bytes 393224 | tf_op jit(solution)/shard_map/ppermute | solution.py:234
  48.8 7.4 %collective-permute-start.7 = (bf16[256,256]{1,0:T(8,128)(2,1)S(1)}, bf16[256,256]{1,0:T(8,128)(2,1)S(1)}, u32[]{:S(2)}, u32[]{:S(2)}) collective-permute-start(bf16[256,256]{1,0:T(8,128)(2,1)S(1)} %collective-permute-done.5.zero_ref), channel_id=1, source_target_pairs={{0,2},{1,3},{2,4},{3,5},{4,6},{5,7},{6,8},{7,9},{8,10},{9,11},{10,... | collective-permute-start | bytes 393224 | tf_op jit(solution)/shard_map/ppermute | solution.py:234
  49.3 14.5 %collective-permute-start.10 = (bf16[1280,256]{1,0:T(8,128)(2,1)S(1)}, bf16[1280,256]{1,0:T(8,128)(2,1)}, u32[]{:S(2)}, u32[]{:S(2)}) collective-permute-start(bf16[1280,256]{1,0:T(8,128)(2,1)S(1)} %constant_dynamic-update-slice_fusion.refs_0_), channel_id=1, source_target_pairs={{0,1},{1,0},{2,3},{3,2},{4,5},{5,4},{6,7},{7,6},{8,9},{9,8},{10,11... | collective-permute-start | bytes 1966088 | tf_op jit(solution)/shard_map/ppermute | solution.py:234
  56.3 7.6 %collective-permute-start.11 = (bf16[768,256]{1,0:T(8,128)(2,1)S(1)}, bf16[768,256]{1,0:T(8,128)(2,1)}, u32[]{:S(2)}, u32[]{:S(2)}) collective-permute-start(bf16[768,256]{1,0:T(8,128)(2,1)S(1)} %constant_dynamic-update-slice_fusion.5.refs_1_), channel_id=1, source_target_pairs={{0,1},{1,0},{2,3},{3,2},{4,5},{5,4},{6,7},{7,6},{8,9},{9,8},{10,11... | collective-permute-start | bytes 1179656 | tf_op jit(solution)/shard_map/ppermute | solution.py:234

commit v9 on v7

--- a/solution.py
+++ b/solution.py
@@ -13,7 +13,7 @@
 CODE_ROWS = 16
 STEPS = 256.0
 TOP = 32760.0
-PIECES = 4
+PIECES = 2
 PER = 2
 VMEM = pl.BlockSpec(memory_space=pltpu.VMEM)
 HBM = pl.BlockSpec(memory_space=pltpu.HBM)
@@ -177,34 +177,42 @@
         out_ref[...] = one_ref[...]
 
 
-def finish_kernel(place_ref, far_pair_ref, far_coded_ref, occ_ref, virt_ref, *refs):
-    *groups, out_ref, pair_ref, coded_ref, ordered_ref, sems = refs
+def finish_kernel(
+    place_ref, pair_ref, far_coded_ref, occ_ref, virt_ref, near_ref, far_ref, *refs
+):
+    *away_refs, out_ref, coded_ref, near_sibling_ref, far_sibling_ref, ordered_ref, sems = refs
     piece = CHUNKS // PIECES
-    fetches = [pltpu.make_async_copy(far_pair_ref, pair_ref, sems.at[PIECES])]
+    siblings = [
+        pltpu.make_async_copy(away_refs[0], near_sibling_ref, sems.at[PIECES]),
+        pltpu.make_async_copy(away_refs[1], far_sibling_ref, sems.at[PIECES + 1]),
+    ]
+    shares = []
     for k in range(PIECES):
         some = pl.ds(k * piece, piece)
-        fetches.append(
+        shares.append(
             pltpu.make_async_copy(far_coded_ref.at[some], coded_ref.at[some], sems.at[k])
         )
-    for fetch in fetches:
-        fetch.start()
+    for copy in siblings + shares:
+        copy.start()
     z, core = place_ref[0], place_ref[1]
     rows = out_ref.shape[0]
     chips = (0, 1, -1, 2, -2, 3, -3, 4)
     slot = 0
-    for group_ref in groups:
+    for group_ref in (near_ref, far_ref, near_sibling_ref, far_sibling_ref):
+        if group_ref is near_sibling_ref:
+            for copy in siblings:
+                copy.wait()
         for k in range(group_ref.shape[0] // rows):
             which = core if slot < len(chips) else 1 - core
             n = jnp.bitwise_and(z - chips[slot % len(chips)] + 8, 7) * 2 + which
             held = pl.ds(pl.multiple_of(n * rows, rows), rows)
             ordered_ref[held, :] = group_ref[k * rows : (k + 1) * rows, :]
             slot += 1
-    fetches[0].wait()
     hole = jnp.dot(pair_ref[...], ordered_ref[...], preferred_element_type=jnp.float32)
     total = jnp.zeros(out_ref.shape, jnp.float32)
     for k in range(CHUNKS):
         if k % piece == 0:
-            fetches[1 + k // piece].wait()
+            shares[k // piece].wait()
         code = coded_ref[k, rows:, :].astype(jnp.int32).astype(jnp.float32)[:1, :]
         values = coded_ref[k, :rows, :].astype(jnp.int32).astype(jnp.float32)
         total = total + values * jnp.exp2(code * (1.0 / STEPS))
@@ -327,15 +335,16 @@
     return pl.pallas_call(
         finish_kernel,
         out_shape=jax.ShapeDtypeStruct((height, LANES), jnp.float32),
-        in_specs=[SMEM, HBM, HBM] + [VMEM] * 6,
+        in_specs=[SMEM, VMEM, HBM, VMEM, VMEM, VMEM, VMEM, HBM, HBM],
         out_specs=VMEM,
         scratch_shapes=[
-            pltpu.VMEM(pair_integrals.shape, jnp.bfloat16),
             pltpu.VMEM(shares.shape, jnp.int16),
+            pltpu.VMEM(near.shape, jnp.bfloat16),
+            pltpu.VMEM(far.shape, jnp.bfloat16),
             pltpu.VMEM((CHUNKS * height, LANES), jnp.bfloat16),
-            pltpu.SemaphoreType.DMA((PIECES + 1,)),
+            pltpu.SemaphoreType.DMA((PIECES + 2,)),
         ],
-        compiler_params=pltpu.CompilerParams(vmem_limit_bytes=51 << 20),
+        compiler_params=pltpu.CompilerParams(vmem_limit_bytes=48 << 20),
         cost_estimate=pl.CostEstimate(flops=2**30, bytes_accessed=2**23, transcendentals=0),
         name="finish",
     )(

time: 69.3 us -> 68.9 us (level)
    unnamed x18 -> x20, local copies, waits for them, and re-layouts: 1.64 us -> 1.64 us
where the time goes in v9:
time: 68.9 us; the launch traced here: 68 us
  starting transfers between devices  38.8 us (56%)
  Pallas kernels  19.4 us (28%)
  waiting for transfers between devices  7.57 us (11%)
  local copies, waits for them, and re-layouts  1.8 us (3%)
    ppermute x9, starting transfers between devices, step(): return lax.ppermute(value, 'narrow', ring)  24.2 us
    pallas_call x1, Pallas kernels, on_device(): pl.pallas_call(ladder_kernel, out_shape=jax.ShapeDtypeStruct((CHUNKS, hei...  8.9 us
    all_to_all x1, starting transfers between devices, on_device(): shares = lax.all_to_all(coded, 'wide', 0, 0, tiled=True)  5.57 us
    ppermute x9, waiting for transfers between devices, step(): return lax.ppermute(value, 'narrow', ring)  5.35 us
    ppermute x3, starting transfers between devices, on_device(): lax.ppermute(sent[k], 'wide', [(x * 4 + y, (x + dx) % 4 * 4 + (y + dy) %...  4.88 us
    all_to_all x1, starting transfers between devices, on_device(): second = lax.all_to_all(moved, 'wide', 0, 0, tiled=True)  4.2 us
    pallas_call x1, Pallas kernels, on_device(): pl.pallas_call(finish_kernel, out_shape=jax.ShapeDtypeStruct((height, LAN...  4.02 us
    pallas_call x1, Pallas kernels, on_device(): pl.pallas_call(lambda *refs: select_kernel(shift, *refs), out_shape=(*[ja...  3.79 us
  transfers between devices with their start and end apart: 14, of which 5 were waited for; matrix products, arithmetic and copies ran while one was open for 0% of the time, Pallas kernels for 15%

profile of v9, /device:TPU:1, one launch (start us, length us, event | category | flops | bytes accessed | tf_op | source)
XLA Modules:
  0.0 68.0 jit_solution(13438201055837315629)
XLA Ops:
  0.0 3.8 %select.1 = (bf16[128,256]{1,0:T(8,128)(2,1)}, bf16[128,256]{1,0:T(8,128)(2,1)}, bf16[128,256]{1,0:T(8,128)(2,1)}, bf16[128,256]{1,0:T(8,128)(2,1)}, s32[16,256]{1,0:T(8,128)}) custom-call(s32[1]{0:T(128)} %bitcast.2.refs_0_, s32[32,128]{1,0:T(8,128)} %bitcast.7, bf16[256,2048]{1,0:T(8,128)(2,1)} %amp_ref.1), custom_call_target="tpu_custom_call" | custom-call | flops 1073741824 | bytes 2097152 | tf_op jit(solution)/shard_map/select/pallas_call | solution.py:239
  3.8 2.1 %collective-permute-start = (bf16[128,256]{1,0:T(8,128)(2,1)}, bf16[128,256]{1,0:T(8,128)(2,1)S(1)}, u32[]{:S(2)}, u32[]{:S(2)}) collective-permute-start(bf16[128,256]{1,0:T(8,128)(2,1)} %get-tuple-element.17), channel_id=1, source_target_pairs={{0,64},{16,80},{32,96},{48,112},{64,128},{80,144},{96,160},{112,17... | collective-permute-start | bytes 196616 | tf_op jit(solution)/shard_map/ppermute | solution.py:253
  5.9 1.4 %collective-permute-start.1 = (bf16[128,256]{1,0:T(8,128)(2,1)}, bf16[128,256]{1,0:T(8,128)(2,1)S(1)}, u32[]{:S(2)}, u32[]{:S(2)}) collective-permute-start(bf16[128,256]{1,0:T(8,128)(2,1)} %get-tuple-element.18), channel_id=1, source_target_pairs={{0,192},{16,208},{32,224},{48,240},{64,0},{80,16},{96,32},{112,48}... | collective-permute-start | bytes 196616 | tf_op jit(solution)/shard_map/ppermute | solution.py:253
  7.3 1.4 %collective-permute-start.2 = (bf16[128,256]{1,0:T(8,128)(2,1)}, bf16[128,256]{1,0:T(8,128)(2,1)S(1)}, u32[]{:S(2)}, u32[]{:S(2)}) collective-permute-start(bf16[128,256]{1,0:T(8,128)(2,1)} %get-tuple-element.19), channel_id=1, source_target_pairs={{0,16},{16,32},{32,48},{48,0},{64,80},{80,96},{96,112},{112,64},{1... | collective-permute-start | bytes 196616 | tf_op jit(solution)/shard_map/ppermute | solution.py:253
  8.7 0.8 %copy-done.4 = bf16[128,256]{1,0:T(8,128)(2,1)S(1)} copy-done((bf16[128,256]{1,0:T(8,128)(2,1)S(1)}, bf16[128,256]{1,0:T(8,128)(2,1)}, u32[]{:S(2)}) %copy-start.4) | copy-done | bytes 65560
  9.5 0.7 %copy-done.5 = s32[16,256]{1,0:T(8,128)S(1)} copy-done((s32[16,256]{1,0:T(8,128)S(1)}, s32[16,256]{1,0:T(8,128)}, u32[]{:S(2)}) %copy-start.5) | copy-done | bytes 16408
  10.2 0.9 %route.1 = (bf16[1280,512]{1,0:T(8,128)(2,1)S(1)}, bf16[1280,256]{1,0:T(8,128)(2,1)S(1)}, bf16[128,256]{1,0:T(8,128)(2,1)S(1)}) custom-call(s32[1]{0:T(128)} %bitcast.2.refs_0_, s32[32,128]{1,0:T(8,128)S(1)} %bitcast.8, s32[16,256]{1,0:T(8,128)S(1)} %copy-done.5, bf16[128,256]{1,0:T(8,128)(2,1)S(1)} %copy-done.4), custom_call_target="tpu_custom_call" | custom-call | flops 268435456 | bytes 1048576 | tf_op jit(solution)/shard_map/route/pallas_call | solution.py:262
  11.2 1.1 %collective-permute-done.2.refs_3_ = bf16[128,256]{1,0:T(8,128)(2,1)S(1)} collective-permute-done((bf16[128,256]{1,0:T(8,128)(2,1)}, bf16[128,256]{1,0:T(8,128)(2,1)S(1)}, u32[]{:S(2)}, u32[]{:S(2)}) %collective-permute-start.2) | collective-permute-done | bytes 65568 | tf_op jit(solution)/shard_map/ppermute | solution.py:253
  12.3 1.3 %forward.1.after_ref = bf16[16,80,256]{2,1,0:T(8,128)(2,1)} custom-call(bf16[1280,512]{1,0:T(8,128)(2,1)S(1)} %get-tuple-element.15.forward_ref, bf16[128,256]{1,0:T(8,128)(2,1)S(1)} %get-tuple-element.16.refs_0_, bf16[128,256]{1,0:T(8,128)(2,1)S(1)} %collective-permute-done.refs_1_, bf16[128,256]{1,0:T(8,128)(2,1)S(1)} %collective-permute-done.1.refs_2_, ...), custom_call_target="tpu_custom_call" | custom-call | flops 268435456 | bytes 1048576 | tf_op jit(solution)/shard_map/forward/pallas_call | solution.py:276
  13.6 4.2 %all-to-all-start.1 = ((bf16[16,80,256]{2,1,0:T(8,128)(2,1)}), bf16[16,80,256]{2,1,0:T(8,128)(2,1)S(1)}, u32[]{:S(2)}, u32[]{:S(2)}) async-start(bf16[16,80,256]{2,1,0:T(8,128)(2,1)} %forward.1.after_ref), calls=%async_computation.1 | async-start | bytes 1310720 | tf_op jit(solution)/shard_map/all_to_all | solution.py:285
  17.8 8.9 %ladder.1.after_ref = s16[16,272,256]{2,1,0:T(8,128)(2,1)} custom-call(bf16[256,2048]{1,0:T(8,128)(2,1)S(1)} %copy-done.1, bf16[2048,4096]{1,0:T(8,128)(2,1)} %int_ref.1, bf16[16,80,256]{2,1,0:T(8,128)(2,1)} %forward.1.after_ref), custom_call_target="tpu_custom_call" | custom-call | flops 4294967296 | bytes 18874368 | tf_op jit(solution)/shard_map/ladder/pallas_call | solution.py:288
  26.7 1.2 %all-to-all-done.1.second_ref = bf16[16,80,256]{2,1,0:T(8,128)(2,1)S(1)} async-done(((bf16[16,80,256]{2,1,0:T(8,128)(2,1)}), bf16[16,80,256]{2,1,0:T(8,128)(2,1)S(1)}, u32[]{:S(2)}, u32[]{:S(2)}) %all-to-all-start.1) | async-done | bytes 655392 | tf_op jit(solution)/shard_map/all_to_all | solution.py:285
  27.9 5.6 %all-to-all-start = ((s16[16,272,256]{2,1,0:T(8,128)(2,1)}), s16[16,272,256]{2,1,0:T(8,128)(2,1)}, u32[]{:S(2)}, u32[]{:S(2)}) async-start(s16[16,272,256]{2,1,0:T(8,128)(2,1)} %ladder.1.after_ref), calls=%async_computation | async-start | bytes 4456448 | tf_op jit(solution)/shard_map/all_to_all | solution.py:305
  33.9 6.1 %collective-permute-start.6 = (bf16[256,256]{1,0:T(8,128)(2,1)S(1)}, bf16[256,256]{1,0:T(8,128)(2,1)S(1)}, u32[]{:S(2)}, u32[]{:S(2)}) collective-permute-start(bf16[256,256]{1,0:T(8,128)(2,1)S(1)} %settle.1), channel_id=1, source_target_pairs={{0,12},{1,13},{2,14},{3,15},{4,0},{5,1},{6,2},{7,3},{8,4},{9,5},{1... | collective-permute-start | bytes 393224 | tf_op jit(solution)/shard_map/ppermute | solution.py:237
  40.0 0.7 %collective-permute-start.3 = (bf16[256,256]{1,0:T(8,128)(2,1)S(1)}, bf16[256,256]{1,0:T(8,128)(2,1)S(1)}, u32[]{:S(2)}, u32[]{:S(2)}) collective-permute-start(bf16[256,256]{1,0:T(8,128)(2,1)S(1)} %settle.1), channel_id=1, source_target_pairs={{0,2},{1,3},{2,4},{3,5},{4,6},{5,7},{6,8},{7,9},{8,10},{9,11},{10,... | collective-permute-start | bytes 393224 | tf_op jit(solution)/shard_map/ppermute | solution.py:237
  40.7 2.4 %collective-permute-start.4 = (bf16[256,256]{1,0:T(8,128)(2,1)S(1)}, bf16[256,256]{1,0:T(8,128)(2,1)S(1)}, u32[]{:S(2)}, u32[]{:S(2)}) collective-permute-start(bf16[256,256]{1,0:T(8,128)(2,1)S(1)} %settle.1), channel_id=1, source_target_pairs={{0,14},{1,15},{2,0},{3,1},{4,2},{5,3},{6,4},{7,5},{8,6},{9,7},{10,... | collective-permute-start | bytes 393224 | tf_op jit(solution)/shard_map/ppermute | solution.py:237
  43.1 3.6 %collective-permute-done.5.zero_ref = bf16[256,256]{1,0:T(8,128)(2,1)S(1)} collective-permute-done((bf16[256,256]{1,0:T(8,128)(2,1)S(1)}, bf16[256,256]{1,0:T(8,128)(2,1)S(1)}, u32[]{:S(2)}, u32[]{:S(2)}) %collective-permute-start.5) | collective-permute-done | bytes 131104 | tf_op jit(solution)/shard_map/ppermute | solution.py:237
  46.8 0.4 collective-permute-start.9
  47.2 1.6 %collective-permute-start.8 = (bf16[256,256]{1,0:T(8,128)(2,1)S(1)}, bf16[256,256]{1,0:T(8,128)(2,1)S(1)}, u32[]{:S(2)}, u32[]{:S(2)}) collective-permute-start(bf16[256,256]{1,0:T(8,128)(2,1)S(1)} %collective-permute-done.6.one_ref), channel_id=1, source_target_pairs={{0,14},{1,15},{2,0},{3,1},{4,2},{5,3},{6,4},{7,5},{8,6},{9,7},{10,... | collective-permute-start | bytes 393224 | tf_op jit(solution)/shard_map/ppermute | solution.py:237
  48.8 0.4 collective-permute-done.3
  49.3 6.9 %collective-permute-start.10 = (bf16[1280,256]{1,0:T(8,128)(2,1)S(1)}, bf16[1280,256]{1,0:T(8,128)(2,1)}, u32[]{:S(2)}, u32[]{:S(2)}) collective-permute-start(bf16[1280,256]{1,0:T(8,128)(2,1)S(1)} %constant_dynamic-update-slice_fusion.near_ref), channel_id=1, source_target_pairs={{0,1},{1,0},{2,3},{3,2},{4,5},{5,4},{6,7},{7,6},{8,9},{9,8},{10,11... | collective-permute-start | bytes 1966088 | tf_op jit(solution)/shard_map/ppermute | solution.py:237
  56.3 6.1 %collective-permute-start.11 = (bf16[768,256]{1,0:T(8,128)(2,1)S(1)}, bf16[768,256]{1,0:T(8,128)(2,1)}, u32[]{:S(2)}, u32[]{:S(2)}) collective-permute-start(bf16[768,256]{1,0:T(8,128)(2,1)S(1)} %constant_dynamic-update-slice_fusion.5.far_ref), channel_id=1, source_target_pairs={{0,1},{1,0},{2,3},{3,2},{4,5},{5,4},{6,7},{7,6},{8,9},{9,8},{10,11... | collective-permute-start | bytes 1179656 | tf_op jit(solution)/shard_map/ppermute | solution.py:237
  62.6 1.3 %collective-permute-done.11.refs_1_ = bf16[768,256]{1,0:T(8,128)(2,1)} collective-permute-done((bf16[768,256]{1,0:T(8,128)(2,1)S(1)}, bf16[768,256]{1,0:T(8,128)(2,1)}, u32[]{:S(2)}, u32[]{:S(2)}) %collective-permute-start.11) | collective-permute-done | bytes 393248 | tf_op jit(solution)/shard_map/ppermute | solution.py:237
  63.9 4.0 %finish.1 = f32[256,256]{1,0:T(8,128)} custom-call(s32[2]{0:T(128)S(1)} %pad_add_fusion.place_ref, bf16[256,4096]{1,0:T(8,128)(2,1)S(1)} %copy-done, s16[16,272,256]{2,1,0:T(8,128)(2,1)} %all-to-all-done.far_coded_ref, f32[256,1]{1,0:T(8,128)S(1)} %copy.7.occ_ref, f32[1,256]{1,0:T(1,128)S(1)} %bitcast.6, ...), custom_call_target="tpu_custom_call" | custom-call | flops 1073741824 | bytes 8388608 | tf_op jit(solution)/shard_map/finish/pallas_call | solution.py:335
  (35 shorter events, 0.7 us)
Async XLA Ops:
  0.0 8.7 %copy-start.3 = (s32[4096]{0:T(1024)S(1)}, s32[4096]{0:T(1024)}, u32[]{:S(2)}) copy-start(s32[4096]{0:T(1024)} %param.9) | copy-start | bytes 49156
  3.8 7.4 %collective-permute-start = (bf16[128,256]{1,0:T(8,128)(2,1)}, bf16[128,256]{1,0:T(8,128)(2,1)S(1)}, u32[]{:S(2)}, u32[]{:S(2)}) collective-permute-start(bf16[128,256]{1,0:T(8,128)(2,1)} %get-tuple-element.17), channel_id=1, source_target_pairs={{0,64},{16,80},{32,96},{48,112},{64,128},{80,144},{96,160},{112,17... | collective-permute-start | bytes 196616 | tf_op jit(solution)/shard_map/ppermute | solution.py:253
  5.9 5.3 %collective-permute-start.1 = (bf16[128,256]{1,0:T(8,128)(2,1)}, bf16[128,256]{1,0:T(8,128)(2,1)S(1)}, u32[]{:S(2)}, u32[]{:S(2)}) collective-permute-start(bf16[128,256]{1,0:T(8,128)(2,1)} %get-tuple-element.18), channel_id=1, source_target_pairs={{0,192},{16,208},{32,224},{48,240},{64,0},{80,16},{96,32},{112,48}... | collective-permute-start | bytes 196616 | tf_op jit(solution)/shard_map/ppermute | solution.py:253
  7.3 5.0 %collective-permute-start.2 = (bf16[128,256]{1,0:T(8,128)(2,1)}, bf16[128,256]{1,0:T(8,128)(2,1)S(1)}, u32[]{:S(2)}, u32[]{:S(2)}) collective-permute-start(bf16[128,256]{1,0:T(8,128)(2,1)} %get-tuple-element.19), channel_id=1, source_target_pairs={{0,16},{16,32},{32,48},{48,0},{64,80},{80,96},{96,112},{112,64},{1... | collective-permute-start | bytes 196616 | tf_op jit(solution)/shard_map/ppermute | solution.py:253
  8.7 0.8 %copy-start.4 = (bf16[128,256]{1,0:T(8,128)(2,1)S(1)}, bf16[128,256]{1,0:T(8,128)(2,1)}, u32[]{:S(2)}) copy-start(bf16[128,256]{1,0:T(8,128)(2,1)} %get-tuple-element.14.refs_3_) | copy-start | bytes 196612
  9.5 0.7 %copy-start.5 = (s32[16,256]{1,0:T(8,128)S(1)}, s32[16,256]{1,0:T(8,128)}, u32[]{:S(2)}) copy-start(s32[16,256]{1,0:T(8,128)} %get-tuple-element.13.refs_2_) | copy-start | bytes 49156
  10.2 7.6 %copy-start.1 = (bf16[256,2048]{1,0:T(8,128)(2,1)S(1)}, bf16[256,2048]{1,0:T(8,128)(2,1)}, u32[]{:S(2)}) copy-start(bf16[256,2048]{1,0:T(8,128)(2,1)} %amp_ref.1) | copy-start | bytes 3145732
  13.6 14.3 %all-to-all-start.1 = ((bf16[16,80,256]{2,1,0:T(8,128)(2,1)}), bf16[16,80,256]{2,1,0:T(8,128)(2,1)S(1)}, u32[]{:S(2)}, u32[]{:S(2)}) async-start(bf16[16,80,256]{2,1,0:T(8,128)(2,1)} %forward.1.after_ref), calls=%async_computation.1 | async-start | bytes 1310720 | tf_op jit(solution)/shard_map/all_to_all | solution.py:285
  27.9 35.9 %all-to-all-start = ((s16[16,272,256]{2,1,0:T(8,128)(2,1)}), s16[16,272,256]{2,1,0:T(8,128)(2,1)}, u32[]{:S(2)}, u32[]{:S(2)}) async-start(s16[16,272,256]{2,1,0:T(8,128)(2,1)} %ladder.1.after_ref), calls=%async_computation | async-start | bytes 4456448 | tf_op jit(solution)/shard_map/all_to_all | solution.py:305
  33.5 28.9 %copy-start.6 = (f32[256]{0:T(256)S(1)}, f32[256]{0:T(256)}, u32[]{:S(2)}) copy-start(f32[256]{0:T(256)} %param.10) | copy-start | bytes 3076
  33.9 30.0 %copy-start = (bf16[256,4096]{1,0:T(8,128)(2,1)S(1)}, bf16[256,4096]{1,0:T(8,128)(2,1)}, u32[]{:S(2)}) copy-start(bf16[256,4096]{1,0:T(8,128)(2,1)} %pair_ref.1) | copy-start | bytes 6291460
  33.9 30.0 %copy-start.2 = (f32[256]{0:T(256)S(1)}, f32[256]{0:T(256)}, u32[]{:S(2)}) copy-start(f32[256]{0:T(256)} %param.11) | copy-start | bytes 3076
  33.9 9.2 %collective-permute-start.6 = (bf16[256,256]{1,0:T(8,128)(2,1)S(1)}, bf16[256,256]{1,0:T(8,128)(2,1)S(1)}, u32[]{:S(2)}, u32[]{:S(2)}) collective-permute-start(bf16[256,256]{1,0:T(8,128)(2,1)S(1)} %settle.1), channel_id=1, source_target_pairs={{0,12},{1,13},{2,14},{3,15},{4,0},{5,1},{6,2},{7,3},{8,4},{9,5},{1... | collective-permute-start | bytes 393224 | tf_op jit(solution)/shard_map/ppermute | solution.py:237
  40.0 6.8 %collective-permute-start.5 = (bf16[256,256]{1,0:T(8,128)(2,1)S(1)}, bf16[256,256]{1,0:T(8,128)(2,1)S(1)}, u32[]{:S(2)}, u32[]{:S(2)}) collective-permute-start(bf16[256,256]{1,0:T(8,128)(2,1)S(1)} %settle.1), channel_id=1, source_target_pairs={{0,4},{1,5},{2,6},{3,7},{4,8},{5,9},{6,10},{7,11},{8,12},{9,13},{1... | collective-permute-start | bytes 393224 | tf_op jit(solution)/shard_map/ppermute | solution.py:237
  40.0 9.2 %collective-permute-start.3 = (bf16[256,256]{1,0:T(8,128)(2,1)S(1)}, bf16[256,256]{1,0:T(8,128)(2,1)S(1)}, u32[]{:S(2)}, u32[]{:S(2)}) collective-permute-start(bf16[256,256]{1,0:T(8,128)(2,1)S(1)} %settle.1), channel_id=1, source_target_pairs={{0,2},{1,3},{2,4},{3,5},{4,6},{5,7},{6,8},{7,9},{8,10},{9,11},{10,... | collective-permute-start | bytes 393224 | tf_op jit(solution)/shard_map/ppermute | solution.py:237
  40.7 8.5 %collective-permute-start.4 = (bf16[256,256]{1,0:T(8,128)(2,1)S(1)}, bf16[256,256]{1,0:T(8,128)(2,1)S(1)}, u32[]{:S(2)}, u32[]{:S(2)}) collective-permute-start(bf16[256,256]{1,0:T(8,128)(2,1)S(1)} %settle.1), channel_id=1, source_target_pairs={{0,14},{1,15},{2,0},{3,1},{4,2},{5,3},{6,4},{7,5},{8,6},{9,7},{10,... | collective-permute-start | bytes 393224 | tf_op jit(solution)/shard_map/ppermute | solution.py:237
  46.8 9.4 %collective-permute-start.9 = (bf16[256,256]{1,0:T(8,128)(2,1)S(1)}, bf16[256,256]{1,0:T(8,128)(2,1)S(1)}, u32[]{:S(2)}, u32[]{:S(2)}) collective-permute-start(bf16[256,256]{1,0:T(8,128)(2,1)S(1)} %either.1), channel_id=1, source_target_pairs={{0,4},{1,13},{2,6},{3,15},{4,8},{5,1},{6,10},{7,3},{8,12},{9,5},{1... | collective-permute-start | bytes 393224 | tf_op jit(solution)/shard_map/ppermute | solution.py:237
  47.2 9.0 %collective-permute-start.8 = (bf16[256,256]{1,0:T(8,128)(2,1)S(1)}, bf16[256,256]{1,0:T(8,128)(2,1)S(1)}, u32[]{:S(2)}, u32[]{:S(2)}) collective-permute-start(bf16[256,256]{1,0:T(8,128)(2,1)S(1)} %collective-permute-done.6.one_ref), channel_id=1, source_target_pairs={{0,14},{1,15},{2,0},{3,1},{4,2},{5,3},{6,4},{7,5},{8,6},{9,7},{10,... | collective-permute-start | bytes 393224 | tf_op jit(solution)/shard_map/ppermute | solution.py:237
  48.8 7.4 %collective-permute-start.7 = (bf16[256,256]{1,0:T(8,128)(2,1)S(1)}, bf16[256,256]{1,0:T(8,128)(2,1)S(1)}, u32[]{:S(2)}, u32[]{:S(2)}) collective-permute-start(bf16[256,256]{1,0:T(8,128)(2,1)S(1)} %collective-permute-done.5.zero_ref), channel_id=1, source_target_pairs={{0,2},{1,3},{2,4},{3,5},{4,6},{5,7},{6,8},{7,9},{8,10},{9,11},{10,... | collective-permute-start | bytes 393224 | tf_op jit(solution)/shard_map/ppermute | solution.py:237
  49.3 14.5 %collective-permute-start.10 = (bf16[1280,256]{1,0:T(8,128)(2,1)S(1)}, bf16[1280,256]{1,0:T(8,128)(2,1)}, u32[]{:S(2)}, u32[]{:S(2)}) collective-permute-start(bf16[1280,256]{1,0:T(8,128)(2,1)S(1)} %constant_dynamic-update-slice_fusion.near_ref), channel_id=1, source_target_pairs={{0,1},{1,0},{2,3},{3,2},{4,5},{5,4},{6,7},{7,6},{8,9},{9,8},{10,11... | collective-permute-start | bytes 1966088 | tf_op jit(solution)/shard_map/ppermute | solution.py:237
  56.3 7.6 %collective-permute-start.11 = (bf16[768,256]{1,0:T(8,128)(2,1)S(1)}, bf16[768,256]{1,0:T(8,128)(2,1)}, u32[]{:S(2)}, u32[]{:S(2)}) collective-permute-start(bf16[768,256]{1,0:T(8,128)(2,1)S(1)} %constant_dynamic-update-slice_fusion.5.far_ref), channel_id=1, source_target_pairs={{0,1},{1,0},{2,3},{3,2},{4,5},{5,4},{6,7},{7,6},{8,9},{9,8},{10,11... | collective-permute-start | bytes 1179656 | tf_op jit(solution)/shard_map/ppermute | solution.py:237

commit v10 on v9

--- a/solution.py
+++ b/solution.py
@@ -49,24 +49,27 @@
     return jnp.sum((member * table).reshape(CHUNKS, CHUNKS, LANES), axis=1).astype(jnp.int32)
 
 
+def rank_in_owner(owner):
+    member, within = count_before(owner)
+    r, c = iota((LANES, LANES), 0), iota((LANES, LANES), 1)
+    ahead = ones_where(((r & 15) == (c & 15)) & (jnp.right_shift(c, 4) < jnp.right_shift(r, 4)))
+    base = jnp.sum(bdot(ahead, member), axis=1, keepdims=True)
+    return pick(member, within + base)
+
+
 def widen(ref):
     halves = [ref[pl.ds(k, CHUNKS, stride=2), :] for k in range(2)]
     return jnp.concatenate(halves, 1)
 
 
 def select_kernel(shift, here_ref, index_ref, far_amp_ref, *refs):
-    *sent_refs, rank_ref, amp_ref, amp_sem = refs
+    *sent_refs, amp_ref, amp_sem = refs
     fetch = pltpu.make_async_copy(far_amp_ref, amp_ref, amp_sem)
     fetch.start()
     index = widen(index_ref)
     here = here_ref[0]
     owner = jnp.right_shift(index, shift)
-    member, within = count_before(owner)
-    r, c = iota((LANES, LANES), 0), iota((LANES, LANES), 1)
-    ahead = ones_where(((r & 15) == (c & 15)) & (jnp.right_shift(c, 4) < jnp.right_shift(r, 4)))
-    base = jnp.sum(bdot(ahead, member), axis=1, keepdims=True)
-    rank = pick(member, within + base)
-    rank_ref[...] = rank
+    rank = rank_in_owner(owner)
     middle, depth = rank & 15, jnp.right_shift(rank, 4)
     column = index & ((1 << shift) - 1)
     high, low = jnp.right_shift(column, 6).astype(jnp.float32), (column & 63).astype(jnp.float32)
@@ -90,11 +93,12 @@
         sent_ref[...] = got[hop * 4 * DEPTH : (hop + 1) * 4 * DEPTH]
 
 
-def route_kernel(shift, here_ref, index_ref, rank_ref, kept_ref, *refs):
+def route_kernel(shift, here_ref, index_ref, kept_ref, *refs):
     forward_ref, settle_ref, stay_ref = refs
     stay_ref[...] = kept_ref[...]
-    index, rank, here = widen(index_ref), rank_ref[...], here_ref[0]
+    index, here = widen(index_ref), here_ref[0]
     owner = jnp.right_shift(index, shift)
+    rank = rank_in_owner(owner)
     last, depth = rank & 15, jnp.right_shift(rank, 4)
     hop = rank & 3
     x, y = jnp.right_shift(owner, 2), owner & 3
@@ -236,14 +240,13 @@
         ]
         return lax.ppermute(value, "narrow", ring)
 
-    *sent, rank = pl.pallas_call(
+    sent = pl.pallas_call(
         lambda *refs: select_kernel(shift, *refs),
         out_shape=(
             *[jax.ShapeDtypeStruct((4 * DEPTH, height), jnp.bfloat16) for _ in HOPS],
-            jax.ShapeDtypeStruct((CHUNKS, LANES), jnp.int32),
         ),
         in_specs=[SMEM, VMEM, HBM],
-        out_specs=(VMEM,) * (len(HOPS) + 1),
+        out_specs=(VMEM,) * len(HOPS),
         scratch_shapes=[pltpu.VMEM((height, span), jnp.bfloat16), pltpu.SemaphoreType.DMA(())],
         compiler_params=pltpu.CompilerParams(vmem_limit_bytes=59 << 20),
         cost_estimate=pl.CostEstimate(flops=2**30, bytes_accessed=2**21, transcendentals=0),
@@ -266,12 +269,12 @@
             jax.ShapeDtypeStruct((CHUNKS * ROOM, LANES), jnp.bfloat16),
             jax.ShapeDtypeStruct(sent[0].shape, jnp.bfloat16),
         ),
-        in_specs=[SMEM, VMEM, VMEM, VMEM],
+        in_specs=[SMEM, VMEM, VMEM],
         out_specs=(VMEM, VMEM, VMEM),
         compiler_params=pltpu.CompilerParams(vmem_limit_bytes=16 << 20),
         cost_estimate=pl.CostEstimate(flops=2**28, bytes_accessed=2**20, transcendentals=0),
         name="route",
-    )(here, index, rank, sent[0])
+    )(here, index, sent[0])
 
     moved = pl.pallas_call(
         forward_kernel,

time: 68.9 us -> 68.8 us (level)
  local copies, waits for them, and re-layouts: 1.8 us -> 1.08 us
    unnamed x20 -> x18, local copies, waits for them, and re-layouts: 1.64 us -> 0.93 us
  transfers between devices with their start and end apart: 14 -> 14, of which waited for: 5 -> 4; matrix products, arithmetic and copies ran while one was open for 0% -> 0% of each run, Pallas kernels for 15% -> 16%
where the time goes in v10:
time: 68.8 us; the launch traced here: 67.8 us
  starting transfers between devices  39.3 us (57%)
  Pallas kernels  19.8 us (29%)
  waiting for transfers between devices  7.27 us (11%)
  local copies, waits for them, and re-layouts  1.08 us (2%)
    ppermute x9, starting transfers between devices, step(): return lax.ppermute(value, 'narrow', ring)  24.6 us
    pallas_call x1, Pallas kernels, on_device(): pl.pallas_call(ladder_kernel, out_shape=jax.ShapeDtypeStruct((CHUNKS, hei...  8.89 us
    all_to_all x1, starting transfers between devices, on_device(): shares = lax.all_to_all(coded, 'wide', 0, 0, tiled=True)  5.79 us
    ppermute x9, waiting for transfers between devices, step(): return lax.ppermute(value, 'narrow', ring)  4.95 us
    ppermute x3, starting transfers between devices, on_device(): lax.ppermute(sent[k], 'wide', [(x * 4 + y, (x + dx) % 4 * 4 + (y + dy) %...  4.88 us
    pallas_call x1, Pallas kernels, on_device(): pl.pallas_call(finish_kernel, out_shape=jax.ShapeDtypeStruct((height, LAN...  4.02 us
    all_to_all x1, starting transfers between devices, on_device(): second = lax.all_to_all(moved, 'wide', 0, 0, tiled=True)  3.97 us
    pallas_call x1, Pallas kernels, on_device(): pl.pallas_call(lambda *refs: select_kernel(shift, *refs), out_shape=(*[ja...  3.77 us
  transfers between devices with their start and end apart: 14, of which 4 were waited for; matrix products, arithmetic and copies ran while one was open for 0% of the time, Pallas kernels for 16%

profile of v10, /device:TPU:1, one launch (start us, length us, event | category | flops | bytes accessed | tf_op | source)
XLA Modules:
  0.0 67.8 jit_solution(6865922220073325700)
XLA Ops:
  0.0 3.8 %select.1 = (bf16[128,256]{1,0:T(8,128)(2,1)}, bf16[128,256]{1,0:T(8,128)(2,1)}, bf16[128,256]{1,0:T(8,128)(2,1)}, bf16[128,256]{1,0:T(8,128)(2,1)}) custom-call(s32[1]{0:T(128)} %bitcast.2.refs_0_, s32[32,128]{1,0:T(8,128)} %bitcast.7, bf16[256,2048]{1,0:T(8,128)(2,1)} %amp_ref.1), custom_call_target="tpu_custom_call" | custom-call | flops 1073741824 | bytes 2097152 | tf_op jit(solution)/shard_map/select/pallas_call | solution.py:243
  3.8 2.1 %collective-permute-start = (bf16[128,256]{1,0:T(8,128)(2,1)}, bf16[128,256]{1,0:T(8,128)(2,1)S(1)}, u32[]{:S(2)}, u32[]{:S(2)}) collective-permute-start(bf16[128,256]{1,0:T(8,128)(2,1)} %get-tuple-element.15), channel_id=1, source_target_pairs={{0,64},{16,80},{32,96},{48,112},{64,128},{80,144},{96,160},{112,17... | collective-permute-start | bytes 196616 | tf_op jit(solution)/shard_map/ppermute | solution.py:256
  5.9 1.4 %collective-permute-start.1 = (bf16[128,256]{1,0:T(8,128)(2,1)}, bf16[128,256]{1,0:T(8,128)(2,1)S(1)}, u32[]{:S(2)}, u32[]{:S(2)}) collective-permute-start(bf16[128,256]{1,0:T(8,128)(2,1)} %get-tuple-element.16), channel_id=1, source_target_pairs={{0,192},{16,208},{32,224},{48,240},{64,0},{80,16},{96,32},{112,48}... | collective-permute-start | bytes 196616 | tf_op jit(solution)/shard_map/ppermute | solution.py:256
  7.3 1.4 %collective-permute-start.2 = (bf16[128,256]{1,0:T(8,128)(2,1)}, bf16[128,256]{1,0:T(8,128)(2,1)S(1)}, u32[]{:S(2)}, u32[]{:S(2)}) collective-permute-start(bf16[128,256]{1,0:T(8,128)(2,1)} %get-tuple-element.17), channel_id=1, source_target_pairs={{0,16},{16,32},{32,48},{48,0},{64,80},{80,96},{96,112},{112,64},{1... | collective-permute-start | bytes 196616 | tf_op jit(solution)/shard_map/ppermute | solution.py:256
  8.7 0.8 %copy-done.4 = bf16[128,256]{1,0:T(8,128)(2,1)S(1)} copy-done((bf16[128,256]{1,0:T(8,128)(2,1)S(1)}, bf16[128,256]{1,0:T(8,128)(2,1)}, u32[]{:S(2)}) %copy-start.4) | copy-done | bytes 65560
  9.5 1.3 %route.1 = (bf16[1280,512]{1,0:T(8,128)(2,1)S(1)}, bf16[1280,256]{1,0:T(8,128)(2,1)S(1)}, bf16[128,256]{1,0:T(8,128)(2,1)S(1)}) custom-call(s32[1]{0:T(128)} %bitcast.2.refs_0_, s32[32,128]{1,0:T(8,128)S(1)} %bitcast.8, bf16[128,256]{1,0:T(8,128)(2,1)S(1)} %copy-done.4), custom_call_target="tpu_custom_call" | custom-call | flops 268435456 | bytes 1048576 | tf_op jit(solution)/shard_map/route/pallas_call | solution.py:265
  10.9 1.4 %collective-permute-done.2.refs_3_ = bf16[128,256]{1,0:T(8,128)(2,1)S(1)} collective-permute-done((bf16[128,256]{1,0:T(8,128)(2,1)}, bf16[128,256]{1,0:T(8,128)(2,1)S(1)}, u32[]{:S(2)}, u32[]{:S(2)}) %collective-permute-start.2) | collective-permute-done | bytes 65568 | tf_op jit(solution)/shard_map/ppermute | solution.py:256
  12.3 1.4 %forward.1.after_ref = bf16[16,80,256]{2,1,0:T(8,128)(2,1)} custom-call(bf16[1280,512]{1,0:T(8,128)(2,1)S(1)} %get-tuple-element.13.forward_ref, bf16[128,256]{1,0:T(8,128)(2,1)S(1)} %get-tuple-element.14.refs_0_, bf16[128,256]{1,0:T(8,128)(2,1)S(1)} %collective-permute-done.refs_1_, bf16[128,256]{1,0:T(8,128)(2,1)S(1)} %collective-permute-done.1.refs_2_, ...), custom_call_target="tpu_custom_call" | custom-call | flops 268435456 | bytes 1048576 | tf_op jit(solution)/shard_map/forward/pallas_call | solution.py:279
  13.6 4.0 %all-to-all-start.1 = ((bf16[16,80,256]{2,1,0:T(8,128)(2,1)}), bf16[16,80,256]{2,1,0:T(8,128)(2,1)S(1)}, u32[]{:S(2)}, u32[]{:S(2)}) async-start(bf16[16,80,256]{2,1,0:T(8,128)(2,1)} %forward.1.after_ref), calls=%async_computation.1 | async-start | bytes 1310720 | tf_op jit(solution)/shard_map/all_to_all | solution.py:288
  17.6 8.9 %ladder.1.after_ref = s16[16,272,256]{2,1,0:T(8,128)(2,1)} custom-call(bf16[256,2048]{1,0:T(8,128)(2,1)S(1)} %copy-done.1, bf16[2048,4096]{1,0:T(8,128)(2,1)} %int_ref.1, bf16[16,80,256]{2,1,0:T(8,128)(2,1)} %forward.1.after_ref), custom_call_target="tpu_custom_call" | custom-call | flops 4294967296 | bytes 18874368 | tf_op jit(solution)/shard_map/ladder/pallas_call | solution.py:291
  26.5 0.9 %all-to-all-done.1.second_ref = bf16[16,80,256]{2,1,0:T(8,128)(2,1)S(1)} async-done(((bf16[16,80,256]{2,1,0:T(8,128)(2,1)}), bf16[16,80,256]{2,1,0:T(8,128)(2,1)S(1)}, u32[]{:S(2)}, u32[]{:S(2)}) %all-to-all-start.1) | async-done | bytes 655392 | tf_op jit(solution)/shard_map/all_to_all | solution.py:288
  27.4 5.8 %all-to-all-start = ((s16[16,272,256]{2,1,0:T(8,128)(2,1)}), s16[16,272,256]{2,1,0:T(8,128)(2,1)}, u32[]{:S(2)}, u32[]{:S(2)}) async-start(s16[16,272,256]{2,1,0:T(8,128)(2,1)} %ladder.1.after_ref), calls=%async_computation | async-start | bytes 4456448 | tf_op jit(solution)/shard_map/all_to_all | solution.py:308
  33.2 0.4 settle.1
  33.6 6.1 %collective-permute-start.6 = (bf16[256,256]{1,0:T(8,128)(2,1)S(1)}, bf16[256,256]{1,0:T(8,128)(2,1)S(1)}, u32[]{:S(2)}, u32[]{:S(2)}) collective-permute-start(bf16[256,256]{1,0:T(8,128)(2,1)S(1)} %settle.1), channel_id=1, source_target_pairs={{0,12},{1,13},{2,14},{3,15},{4,0},{5,1},{6,2},{7,3},{8,4},{9,5},{1... | collective-permute-start | bytes 393224 | tf_op jit(solution)/shard_map/ppermute | solution.py:241
  39.8 0.7 %collective-permute-start.3 = (bf16[256,256]{1,0:T(8,128)(2,1)S(1)}, bf16[256,256]{1,0:T(8,128)(2,1)S(1)}, u32[]{:S(2)}, u32[]{:S(2)}) collective-permute-start(bf16[256,256]{1,0:T(8,128)(2,1)S(1)} %settle.1), channel_id=1, source_target_pairs={{0,2},{1,3},{2,4},{3,5},{4,6},{5,7},{6,8},{7,9},{8,10},{9,11},{10,... | collective-permute-start | bytes 393224 | tf_op jit(solution)/shard_map/ppermute | solution.py:241
  40.5 2.4 %collective-permute-start.4 = (bf16[256,256]{1,0:T(8,128)(2,1)S(1)}, bf16[256,256]{1,0:T(8,128)(2,1)S(1)}, u32[]{:S(2)}, u32[]{:S(2)}) collective-permute-start(bf16[256,256]{1,0:T(8,128)(2,1)S(1)} %settle.1), channel_id=1, source_target_pairs={{0,14},{1,15},{2,0},{3,1},{4,2},{5,3},{6,4},{7,5},{8,6},{9,7},{10,... | collective-permute-start | bytes 393224 | tf_op jit(solution)/shard_map/ppermute | solution.py:241
  42.9 3.6 %collective-permute-done.5.zero_ref = bf16[256,256]{1,0:T(8,128)(2,1)S(1)} collective-permute-done((bf16[256,256]{1,0:T(8,128)(2,1)S(1)}, bf16[256,256]{1,0:T(8,128)(2,1)S(1)}, u32[]{:S(2)}, u32[]{:S(2)}) %collective-permute-start.5) | collective-permute-done | bytes 131104 | tf_op jit(solution)/shard_map/ppermute | solution.py:241
  46.5 0.1 collective-permute-start.9
  46.7 1.9 %collective-permute-start.8 = (bf16[256,256]{1,0:T(8,128)(2,1)S(1)}, bf16[256,256]{1,0:T(8,128)(2,1)S(1)}, u32[]{:S(2)}, u32[]{:S(2)}) collective-permute-start(bf16[256,256]{1,0:T(8,128)(2,1)S(1)} %collective-permute-done.6.one_ref), channel_id=1, source_target_pairs={{0,14},{1,15},{2,0},{3,1},{4,2},{5,3},{6,4},{7,5},{8,6},{9,7},{10,... | collective-permute-start | bytes 393224 | tf_op jit(solution)/shard_map/ppermute | solution.py:241
  48.7 7.3 %collective-permute-start.10 = (bf16[1280,256]{1,0:T(8,128)(2,1)S(1)}, bf16[1280,256]{1,0:T(8,128)(2,1)}, u32[]{:S(2)}, u32[]{:S(2)}) collective-permute-start(bf16[1280,256]{1,0:T(8,128)(2,1)S(1)} %constant_dynamic-update-slice_fusion.near_ref), channel_id=1, source_target_pairs={{0,1},{1,0},{2,3},{3,2},{4,5},{5,4},{6,7},{7,6},{8,9},{9,8},{10,11... | collective-permute-start | bytes 1966088 | tf_op jit(solution)/shard_map/ppermute | solution.py:241
  56.0 6.1 %collective-permute-start.11 = (bf16[768,256]{1,0:T(8,128)(2,1)S(1)}, bf16[768,256]{1,0:T(8,128)(2,1)}, u32[]{:S(2)}, u32[]{:S(2)}) collective-permute-start(bf16[768,256]{1,0:T(8,128)(2,1)S(1)} %constant_dynamic-update-slice_fusion.5.far_ref), channel_id=1, source_target_pairs={{0,1},{1,0},{2,3},{3,2},{4,5},{5,4},{6,7},{7,6},{8,9},{9,8},{10,11... | collective-permute-start | bytes 1179656 | tf_op jit(solution)/shard_map/ppermute | solution.py:241
  62.1 0.1 copy.7.occ_ref
  62.3 1.3 %collective-permute-done.11.refs_1_ = bf16[768,256]{1,0:T(8,128)(2,1)} collective-permute-done((bf16[768,256]{1,0:T(8,128)(2,1)S(1)}, bf16[768,256]{1,0:T(8,128)(2,1)}, u32[]{:S(2)}, u32[]{:S(2)}) %collective-permute-start.11) | collective-permute-done | bytes 393248 | tf_op jit(solution)/shard_map/ppermute | solution.py:241
  63.6 4.0 %finish.1 = f32[256,256]{1,0:T(8,128)} custom-call(s32[2]{0:T(128)S(1)} %pad_add_fusion.place_ref, bf16[256,4096]{1,0:T(8,128)(2,1)S(1)} %copy-done, s16[16,272,256]{2,1,0:T(8,128)(2,1)} %all-to-all-done.far_coded_ref, f32[256,1]{1,0:T(8,128)S(1)} %copy.7.occ_ref, f32[1,256]{1,0:T(1,128)S(1)} %bitcast.6, ...), custom_call_target="tpu_custom_call" | custom-call | flops 1073741824 | bytes 8388608 | tf_op jit(solution)/shard_map/finish/pallas_call | solution.py:338
  (33 shorter events, 0.3 us)
Async XLA Ops:
  0.0 8.7 %copy-start.3 = (s32[4096]{0:T(1024)S(1)}, s32[4096]{0:T(1024)}, u32[]{:S(2)}) copy-start(s32[4096]{0:T(1024)} %param.9) | copy-start | bytes 49156
  3.8 7.1 %collective-permute-start = (bf16[128,256]{1,0:T(8,128)(2,1)}, bf16[128,256]{1,0:T(8,128)(2,1)S(1)}, u32[]{:S(2)}, u32[]{:S(2)}) collective-permute-start(bf16[128,256]{1,0:T(8,128)(2,1)} %get-tuple-element.15), channel_id=1, source_target_pairs={{0,64},{16,80},{32,96},{48,112},{64,128},{80,144},{96,160},{112,17... | collective-permute-start | bytes 196616 | tf_op jit(solution)/shard_map/ppermute | solution.py:256
  5.9 5.0 %collective-permute-start.1 = (bf16[128,256]{1,0:T(8,128)(2,1)}, bf16[128,256]{1,0:T(8,128)(2,1)S(1)}, u32[]{:S(2)}, u32[]{:S(2)}) collective-permute-start(bf16[128,256]{1,0:T(8,128)(2,1)} %get-tuple-element.16), channel_id=1, source_target_pairs={{0,192},{16,208},{32,224},{48,240},{64,0},{80,16},{96,32},{112,48}... | collective-permute-start | bytes 196616 | tf_op jit(solution)/shard_map/ppermute | solution.py:256
  7.3 5.0 %collective-permute-start.2 = (bf16[128,256]{1,0:T(8,128)(2,1)}, bf16[128,256]{1,0:T(8,128)(2,1)S(1)}, u32[]{:S(2)}, u32[]{:S(2)}) collective-permute-start(bf16[128,256]{1,0:T(8,128)(2,1)} %get-tuple-element.17), channel_id=1, source_target_pairs={{0,16},{16,32},{32,48},{48,0},{64,80},{80,96},{96,112},{112,64},{1... | collective-permute-start | bytes 196616 | tf_op jit(solution)/shard_map/ppermute | solution.py:256
  8.7 0.8 %copy-start.4 = (bf16[128,256]{1,0:T(8,128)(2,1)S(1)}, bf16[128,256]{1,0:T(8,128)(2,1)}, u32[]{:S(2)}) copy-start(bf16[128,256]{1,0:T(8,128)(2,1)} %get-tuple-element.12.refs_2_) | copy-start | bytes 196612
  9.5 8.1 %copy-start.1 = (bf16[256,2048]{1,0:T(8,128)(2,1)S(1)}, bf16[256,2048]{1,0:T(8,128)(2,1)}, u32[]{:S(2)}) copy-start(bf16[256,2048]{1,0:T(8,128)(2,1)} %amp_ref.1) | copy-start | bytes 3145732
  13.6 13.8 %all-to-all-start.1 = ((bf16[16,80,256]{2,1,0:T(8,128)(2,1)}), bf16[16,80,256]{2,1,0:T(8,128)(2,1)S(1)}, u32[]{:S(2)}, u32[]{:S(2)}) async-start(bf16[16,80,256]{2,1,0:T(8,128)(2,1)} %forward.1.after_ref), calls=%async_computation.1 | async-start | bytes 1310720 | tf_op jit(solution)/shard_map/all_to_all | solution.py:288
  27.4 36.2 %all-to-all-start = ((s16[16,272,256]{2,1,0:T(8,128)(2,1)}), s16[16,272,256]{2,1,0:T(8,128)(2,1)}, u32[]{:S(2)}, u32[]{:S(2)}) async-start(s16[16,272,256]{2,1,0:T(8,128)(2,1)} %ladder.1.after_ref), calls=%async_computation | async-start | bytes 4456448 | tf_op jit(solution)/shard_map/all_to_all | solution.py:308
  33.2 28.9 %copy-start.5 = (f32[256]{0:T(256)S(1)}, f32[256]{0:T(256)}, u32[]{:S(2)}) copy-start(f32[256]{0:T(256)} %param.10) | copy-start | bytes 3076
  33.6 30.0 %copy-start = (bf16[256,4096]{1,0:T(8,128)(2,1)S(1)}, bf16[256,4096]{1,0:T(8,128)(2,1)}, u32[]{:S(2)}) copy-start(bf16[256,4096]{1,0:T(8,128)(2,1)} %pair_ref.1) | copy-start | bytes 6291460
  33.6 30.0 %copy-start.2 = (f32[256]{0:T(256)S(1)}, f32[256]{0:T(256)}, u32[]{:S(2)}) copy-start(f32[256]{0:T(256)} %param.11) | copy-start | bytes 3076
  33.6 9.3 %collective-permute-start.6 = (bf16[256,256]{1,0:T(8,128)(2,1)S(1)}, bf16[256,256]{1,0:T(8,128)(2,1)S(1)}, u32[]{:S(2)}, u32[]{:S(2)}) collective-permute-start(bf16[256,256]{1,0:T(8,128)(2,1)S(1)} %settle.1), channel_id=1, source_target_pairs={{0,12},{1,13},{2,14},{3,15},{4,0},{5,1},{6,2},{7,3},{8,4},{9,5},{1... | collective-permute-start | bytes 393224 | tf_op jit(solution)/shard_map/ppermute | solution.py:241
  39.8 6.8 %collective-permute-start.5 = (bf16[256,256]{1,0:T(8,128)(2,1)S(1)}, bf16[256,256]{1,0:T(8,128)(2,1)S(1)}, u32[]{:S(2)}, u32[]{:S(2)}) collective-permute-start(bf16[256,256]{1,0:T(8,128)(2,1)S(1)} %settle.1), channel_id=1, source_target_pairs={{0,4},{1,5},{2,6},{3,7},{4,8},{5,9},{6,10},{7,11},{8,12},{9,13},{1... | collective-permute-start | bytes 393224 | tf_op jit(solution)/shard_map/ppermute | solution.py:241
  39.8 8.9 %collective-permute-start.3 = (bf16[256,256]{1,0:T(8,128)(2,1)S(1)}, bf16[256,256]{1,0:T(8,128)(2,1)S(1)}, u32[]{:S(2)}, u32[]{:S(2)}) collective-permute-start(bf16[256,256]{1,0:T(8,128)(2,1)S(1)} %settle.1), channel_id=1, source_target_pairs={{0,2},{1,3},{2,4},{3,5},{4,6},{5,7},{6,8},{7,9},{8,10},{9,11},{10,... | collective-permute-start | bytes 393224 | tf_op jit(solution)/shard_map/ppermute | solution.py:241
  40.5 8.1 %collective-permute-start.4 = (bf16[256,256]{1,0:T(8,128)(2,1)S(1)}, bf16[256,256]{1,0:T(8,128)(2,1)S(1)}, u32[]{:S(2)}, u32[]{:S(2)}) collective-permute-start(bf16[256,256]{1,0:T(8,128)(2,1)S(1)} %settle.1), channel_id=1, source_target_pairs={{0,14},{1,15},{2,0},{3,1},{4,2},{5,3},{6,4},{7,5},{8,6},{9,7},{10,... | collective-permute-start | bytes 393224 | tf_op jit(solution)/shard_map/ppermute | solution.py:241
  46.5 9.5 %collective-permute-start.9 = (bf16[256,256]{1,0:T(8,128)(2,1)S(1)}, bf16[256,256]{1,0:T(8,128)(2,1)S(1)}, u32[]{:S(2)}, u32[]{:S(2)}) collective-permute-start(bf16[256,256]{1,0:T(8,128)(2,1)S(1)} %either.1), channel_id=1, source_target_pairs={{0,4},{1,13},{2,6},{3,15},{4,8},{5,1},{6,10},{7,3},{8,12},{9,5},{1... | collective-permute-start | bytes 393224 | tf_op jit(solution)/shard_map/ppermute | solution.py:241
  46.7 9.3 %collective-permute-start.8 = (bf16[256,256]{1,0:T(8,128)(2,1)S(1)}, bf16[256,256]{1,0:T(8,128)(2,1)S(1)}, u32[]{:S(2)}, u32[]{:S(2)}) collective-permute-start(bf16[256,256]{1,0:T(8,128)(2,1)S(1)} %collective-permute-done.6.one_ref), channel_id=1, source_target_pairs={{0,14},{1,15},{2,0},{3,1},{4,2},{5,3},{6,4},{7,5},{8,6},{9,7},{10,... | collective-permute-start | bytes 393224 | tf_op jit(solution)/shard_map/ppermute | solution.py:241
  48.6 7.4 %collective-permute-start.7 = (bf16[256,256]{1,0:T(8,128)(2,1)S(1)}, bf16[256,256]{1,0:T(8,128)(2,1)S(1)}, u32[]{:S(2)}, u32[]{:S(2)}) collective-permute-start(bf16[256,256]{1,0:T(8,128)(2,1)S(1)} %collective-permute-done.5.zero_ref), channel_id=1, source_target_pairs={{0,2},{1,3},{2,4},{3,5},{4,6},{5,7},{6,8},{7,9},{8,10},{9,11},{10,... | collective-permute-start | bytes 393224 | tf_op jit(solution)/shard_map/ppermute | solution.py:241
  48.7 14.9 %collective-permute-start.10 = (bf16[1280,256]{1,0:T(8,128)(2,1)S(1)}, bf16[1280,256]{1,0:T(8,128)(2,1)}, u32[]{:S(2)}, u32[]{:S(2)}) collective-permute-start(bf16[1280,256]{1,0:T(8,128)(2,1)S(1)} %constant_dynamic-update-slice_fusion.near_ref), channel_id=1, source_target_pairs={{0,1},{1,0},{2,3},{3,2},{4,5},{5,4},{6,7},{7,6},{8,9},{9,8},{10,11... | collective-permute-start | bytes 1966088 | tf_op jit(solution)/shard_map/ppermute | solution.py:241
  56.0 7.6 %collective-permute-start.11 = (bf16[768,256]{1,0:T(8,128)(2,1)S(1)}, bf16[768,256]{1,0:T(8,128)(2,1)}, u32[]{:S(2)}, u32[]{:S(2)}) collective-permute-start(bf16[768,256]{1,0:T(8,128)(2,1)S(1)} %constant_dynamic-update-slice_fusion.5.far_ref), channel_id=1, source_target_pairs={{0,1},{1,0},{2,3},{3,2},{4,5},{5,4},{6,7},{7,6},{8,9},{9,8},{10,11... | collective-permute-start | bytes 1179656 | tf_op jit(solution)/shard_map/ppermute | solution.py:241

commit v11 on v10

--- a/solution.py
+++ b/solution.py
@@ -13,7 +13,7 @@
 CODE_ROWS = 16
 STEPS = 256.0
 TOP = 32760.0
-PIECES = 2
+PIECES = 4
 PER = 2
 VMEM = pl.BlockSpec(memory_space=pltpu.VMEM)
 HBM = pl.BlockSpec(memory_space=pltpu.HBM)

time: 68.8 us -> 68.9 us (level)
  no operation moved by 1% of the time
where the time goes in v11:
time: 68.9 us; the launch traced here: 67.9 us
  starting transfers between devices  39.3 us (57%)
  Pallas kernels  19.9 us (29%)
  waiting for transfers between devices  7.27 us (11%)
  local copies, waits for them, and re-layouts  1.08 us (2%)
    ppermute x9, starting transfers between devices, step(): return lax.ppermute(value, 'narrow', ring)  24.6 us
    pallas_call x1, Pallas kernels, on_device(): pl.pallas_call(ladder_kernel, out_shape=jax.ShapeDtypeStruct((CHUNKS, hei...  8.89 us
    all_to_all x1, starting transfers between devices, on_device(): shares = lax.all_to_all(coded, 'wide', 0, 0, tiled=True)  5.79 us
    ppermute x9, waiting for transfers between devices, step(): return lax.ppermute(value, 'narrow', ring)  4.95 us
    ppermute x3, starting transfers between devices, on_device(): lax.ppermute(sent[k], 'wide', [(x * 4 + y, (x + dx) % 4 * 4 + (y + dy) %...  4.88 us
    pallas_call x1, Pallas kernels, on_device(): pl.pallas_call(finish_kernel, out_shape=jax.ShapeDtypeStruct((height, LAN...  4.14 us
    all_to_all x1, starting transfers between devices, on_device(): second = lax.all_to_all(moved, 'wide', 0, 0, tiled=True)  3.97 us
    pallas_call x1, Pallas kernels, on_device(): pl.pallas_call(lambda *refs: select_kernel(shift, *refs), out_shape=(*[ja...  3.77 us
  transfers between devices with their start and end apart: 14, of which 4 were waited for; matrix products, arithmetic and copies ran while one was open for 0% of the time, Pallas kernels for 16%

profile of v11, /device:TPU:1, one launch (start us, length us, event | category | flops | bytes accessed | tf_op | source)
XLA Modules:
  0.0 67.9 jit_solution(16046621266764072150)
XLA Ops:
  0.0 3.8 %select.1 = (bf16[128,256]{1,0:T(8,128)(2,1)}, bf16[128,256]{1,0:T(8,128)(2,1)}, bf16[128,256]{1,0:T(8,128)(2,1)}, bf16[128,256]{1,0:T(8,128)(2,1)}) custom-call(s32[1]{0:T(128)} %bitcast.2.refs_0_, s32[32,128]{1,0:T(8,128)} %bitcast.7, bf16[256,2048]{1,0:T(8,128)(2,1)} %amp_ref.1), custom_call_target="tpu_custom_call" | custom-call | flops 1073741824 | bytes 2097152 | tf_op jit(solution)/shard_map/select/pallas_call | solution.py:243
  3.8 2.1 %collective-permute-start = (bf16[128,256]{1,0:T(8,128)(2,1)}, bf16[128,256]{1,0:T(8,128)(2,1)S(1)}, u32[]{:S(2)}, u32[]{:S(2)}) collective-permute-start(bf16[128,256]{1,0:T(8,128)(2,1)} %get-tuple-element.15), channel_id=1, source_target_pairs={{0,64},{16,80},{32,96},{48,112},{64,128},{80,144},{96,160},{112,17... | collective-permute-start | bytes 196616 | tf_op jit(solution)/shard_map/ppermute | solution.py:256
  5.9 1.4 %collective-permute-start.1 = (bf16[128,256]{1,0:T(8,128)(2,1)}, bf16[128,256]{1,0:T(8,128)(2,1)S(1)}, u32[]{:S(2)}, u32[]{:S(2)}) collective-permute-start(bf16[128,256]{1,0:T(8,128)(2,1)} %get-tuple-element.16), channel_id=1, source_target_pairs={{0,192},{16,208},{32,224},{48,240},{64,0},{80,16},{96,32},{112,48}... | collective-permute-start | bytes 196616 | tf_op jit(solution)/shard_map/ppermute | solution.py:256
  7.3 1.4 %collective-permute-start.2 = (bf16[128,256]{1,0:T(8,128)(2,1)}, bf16[128,256]{1,0:T(8,128)(2,1)S(1)}, u32[]{:S(2)}, u32[]{:S(2)}) collective-permute-start(bf16[128,256]{1,0:T(8,128)(2,1)} %get-tuple-element.17), channel_id=1, source_target_pairs={{0,16},{16,32},{32,48},{48,0},{64,80},{80,96},{96,112},{112,64},{1... | collective-permute-start | bytes 196616 | tf_op jit(solution)/shard_map/ppermute | solution.py:256
  8.7 0.8 %copy-done.4 = bf16[128,256]{1,0:T(8,128)(2,1)S(1)} copy-done((bf16[128,256]{1,0:T(8,128)(2,1)S(1)}, bf16[128,256]{1,0:T(8,128)(2,1)}, u32[]{:S(2)}) %copy-start.4) | copy-done | bytes 65560
  9.5 1.3 %route.1 = (bf16[1280,512]{1,0:T(8,128)(2,1)S(1)}, bf16[1280,256]{1,0:T(8,128)(2,1)S(1)}, bf16[128,256]{1,0:T(8,128)(2,1)S(1)}) custom-call(s32[1]{0:T(128)} %bitcast.2.refs_0_, s32[32,128]{1,0:T(8,128)S(1)} %bitcast.8, bf16[128,256]{1,0:T(8,128)(2,1)S(1)} %copy-done.4), custom_call_target="tpu_custom_call" | custom-call | flops 268435456 | bytes 1048576 | tf_op jit(solution)/shard_map/route/pallas_call | solution.py:265
  10.9 1.4 %collective-permute-done.2.refs_3_ = bf16[128,256]{1,0:T(8,128)(2,1)S(1)} collective-permute-done((bf16[128,256]{1,0:T(8,128)(2,1)}, bf16[128,256]{1,0:T(8,128)(2,1)S(1)}, u32[]{:S(2)}, u32[]{:S(2)}) %collective-permute-start.2) | collective-permute-done | bytes 65568 | tf_op jit(solution)/shard_map/ppermute | solution.py:256
  12.3 1.4 %forward.1.after_ref = bf16[16,80,256]{2,1,0:T(8,128)(2,1)} custom-call(bf16[1280,512]{1,0:T(8,128)(2,1)S(1)} %get-tuple-element.13.forward_ref, bf16[128,256]{1,0:T(8,128)(2,1)S(1)} %get-tuple-element.14.refs_0_, bf16[128,256]{1,0:T(8,128)(2,1)S(1)} %collective-permute-done.refs_1_, bf16[128,256]{1,0:T(8,128)(2,1)S(1)} %collective-permute-done.1.refs_2_, ...), custom_call_target="tpu_custom_call" | custom-call | flops 268435456 | bytes 1048576 | tf_op jit(solution)/shard_map/forward/pallas_call | solution.py:279
  13.6 4.0 %all-to-all-start.1 = ((bf16[16,80,256]{2,1,0:T(8,128)(2,1)}), bf16[16,80,256]{2,1,0:T(8,128)(2,1)S(1)}, u32[]{:S(2)}, u32[]{:S(2)}) async-start(bf16[16,80,256]{2,1,0:T(8,128)(2,1)} %forward.1.after_ref), calls=%async_computation.1 | async-start | bytes 1310720 | tf_op jit(solution)/shard_map/all_to_all | solution.py:288
  17.6 8.9 %ladder.1.after_ref = s16[16,272,256]{2,1,0:T(8,128)(2,1)} custom-call(bf16[256,2048]{1,0:T(8,128)(2,1)S(1)} %copy-done.1, bf16[2048,4096]{1,0:T(8,128)(2,1)} %int_ref.1, bf16[16,80,256]{2,1,0:T(8,128)(2,1)} %forward.1.after_ref), custom_call_target="tpu_custom_call" | custom-call | flops 4294967296 | bytes 18874368 | tf_op jit(solution)/shard_map/ladder/pallas_call | solution.py:291
  26.5 0.9 %all-to-all-done.1.second_ref = bf16[16,80,256]{2,1,0:T(8,128)(2,1)S(1)} async-done(((bf16[16,80,256]{2,1,0:T(8,128)(2,1)}), bf16[16,80,256]{2,1,0:T(8,128)(2,1)S(1)}, u32[]{:S(2)}, u32[]{:S(2)}) %all-to-all-start.1) | async-done | bytes 655392 | tf_op jit(solution)/shard_map/all_to_all | solution.py:288
  27.4 5.8 %all-to-all-start = ((s16[16,272,256]{2,1,0:T(8,128)(2,1)}), s16[16,272,256]{2,1,0:T(8,128)(2,1)}, u32[]{:S(2)}, u32[]{:S(2)}) async-start(s16[16,272,256]{2,1,0:T(8,128)(2,1)} %ladder.1.after_ref), calls=%async_computation | async-start | bytes 4456448 | tf_op jit(solution)/shard_map/all_to_all | solution.py:308
  33.2 0.4 settle.1
  33.6 6.1 %collective-permute-start.6 = (bf16[256,256]{1,0:T(8,128)(2,1)S(1)}, bf16[256,256]{1,0:T(8,128)(2,1)S(1)}, u32[]{:S(2)}, u32[]{:S(2)}) collective-permute-start(bf16[256,256]{1,0:T(8,128)(2,1)S(1)} %settle.1), channel_id=1, source_target_pairs={{0,12},{1,13},{2,14},{3,15},{4,0},{5,1},{6,2},{7,3},{8,4},{9,5},{1... | collective-permute-start | bytes 393224 | tf_op jit(solution)/shard_map/ppermute | solution.py:241
  39.8 0.7 %collective-permute-start.3 = (bf16[256,256]{1,0:T(8,128)(2,1)S(1)}, bf16[256,256]{1,0:T(8,128)(2,1)S(1)}, u32[]{:S(2)}, u32[]{:S(2)}) collective-permute-start(bf16[256,256]{1,0:T(8,128)(2,1)S(1)} %settle.1), channel_id=1, source_target_pairs={{0,2},{1,3},{2,4},{3,5},{4,6},{5,7},{6,8},{7,9},{8,10},{9,11},{10,... | collective-permute-start | bytes 393224 | tf_op jit(solution)/shard_map/ppermute | solution.py:241
  40.5 2.4 %collective-permute-start.4 = (bf16[256,256]{1,0:T(8,128)(2,1)S(1)}, bf16[256,256]{1,0:T(8,128)(2,1)S(1)}, u32[]{:S(2)}, u32[]{:S(2)}) collective-permute-start(bf16[256,256]{1,0:T(8,128)(2,1)S(1)} %settle.1), channel_id=1, source_target_pairs={{0,14},{1,15},{2,0},{3,1},{4,2},{5,3},{6,4},{7,5},{8,6},{9,7},{10,... | collective-permute-start | bytes 393224 | tf_op jit(solution)/shard_map/ppermute | solution.py:241
  42.9 3.6 %collective-permute-done.5.zero_ref = bf16[256,256]{1,0:T(8,128)(2,1)S(1)} collective-permute-done((bf16[256,256]{1,0:T(8,128)(2,1)S(1)}, bf16[256,256]{1,0:T(8,128)(2,1)S(1)}, u32[]{:S(2)}, u32[]{:S(2)}) %collective-permute-start.5) | collective-permute-done | bytes 131104 | tf_op jit(solution)/shard_map/ppermute | solution.py:241
  46.5 0.1 collective-permute-start.9
  46.7 1.9 %collective-permute-start.8 = (bf16[256,256]{1,0:T(8,128)(2,1)S(1)}, bf16[256,256]{1,0:T(8,128)(2,1)S(1)}, u32[]{:S(2)}, u32[]{:S(2)}) collective-permute-start(bf16[256,256]{1,0:T(8,128)(2,1)S(1)} %collective-permute-done.6.one_ref), channel_id=1, source_target_pairs={{0,14},{1,15},{2,0},{3,1},{4,2},{5,3},{6,4},{7,5},{8,6},{9,7},{10,... | collective-permute-start | bytes 393224 | tf_op jit(solution)/shard_map/ppermute | solution.py:241
  48.7 7.3 %collective-permute-start.10 = (bf16[1280,256]{1,0:T(8,128)(2,1)S(1)}, bf16[1280,256]{1,0:T(8,128)(2,1)}, u32[]{:S(2)}, u32[]{:S(2)}) collective-permute-start(bf16[1280,256]{1,0:T(8,128)(2,1)S(1)} %constant_dynamic-update-slice_fusion.near_ref), channel_id=1, source_target_pairs={{0,1},{1,0},{2,3},{3,2},{4,5},{5,4},{6,7},{7,6},{8,9},{9,8},{10,11... | collective-permute-start | bytes 1966088 | tf_op jit(solution)/shard_map/ppermute | solution.py:241
  56.0 6.1 %collective-permute-start.11 = (bf16[768,256]{1,0:T(8,128)(2,1)S(1)}, bf16[768,256]{1,0:T(8,128)(2,1)}, u32[]{:S(2)}, u32[]{:S(2)}) collective-permute-start(bf16[768,256]{1,0:T(8,128)(2,1)S(1)} %constant_dynamic-update-slice_fusion.5.far_ref), channel_id=1, source_target_pairs={{0,1},{1,0},{2,3},{3,2},{4,5},{5,4},{6,7},{7,6},{8,9},{9,8},{10,11... | collective-permute-start | bytes 1179656 | tf_op jit(solution)/shard_map/ppermute | solution.py:241
  62.1 0.1 copy.7.occ_ref
  62.3 1.3 %collective-permute-done.11.refs_1_ = bf16[768,256]{1,0:T(8,128)(2,1)} collective-permute-done((bf16[768,256]{1,0:T(8,128)(2,1)S(1)}, bf16[768,256]{1,0:T(8,128)(2,1)}, u32[]{:S(2)}, u32[]{:S(2)}) %collective-permute-start.11) | collective-permute-done | bytes 393248 | tf_op jit(solution)/shard_map/ppermute | solution.py:241
  63.6 4.1 %finish.1 = f32[256,256]{1,0:T(8,128)} custom-call(s32[2]{0:T(128)S(1)} %pad_add_fusion.place_ref, bf16[256,4096]{1,0:T(8,128)(2,1)S(1)} %copy-done, s16[16,272,256]{2,1,0:T(8,128)(2,1)} %all-to-all-done.far_coded_ref, f32[256,1]{1,0:T(8,128)S(1)} %copy.7.occ_ref, f32[1,256]{1,0:T(1,128)S(1)} %bitcast.6, ...), custom_call_target="tpu_custom_call" | custom-call | flops 1073741824 | bytes 8388608 | tf_op jit(solution)/shard_map/finish/pallas_call | solution.py:338
  (33 shorter events, 0.3 us)
Async XLA Ops:
  0.0 8.7 %copy-start.3 = (s32[4096]{0:T(1024)S(1)}, s32[4096]{0:T(1024)}, u32[]{:S(2)}) copy-start(s32[4096]{0:T(1024)} %param.9) | copy-start | bytes 49156
  3.8 7.1 %collective-permute-start = (bf16[128,256]{1,0:T(8,128)(2,1)}, bf16[128,256]{1,0:T(8,128)(2,1)S(1)}, u32[]{:S(2)}, u32[]{:S(2)}) collective-permute-start(bf16[128,256]{1,0:T(8,128)(2,1)} %get-tuple-element.15), channel_id=1, source_target_pairs={{0,64},{16,80},{32,96},{48,112},{64,128},{80,144},{96,160},{112,17... | collective-permute-start | bytes 196616 | tf_op jit(solution)/shard_map/ppermute | solution.py:256
  5.9 5.0 %collective-permute-start.1 = (bf16[128,256]{1,0:T(8,128)(2,1)}, bf16[128,256]{1,0:T(8,128)(2,1)S(1)}, u32[]{:S(2)}, u32[]{:S(2)}) collective-permute-start(bf16[128,256]{1,0:T(8,128)(2,1)} %get-tuple-element.16), channel_id=1, source_target_pairs={{0,192},{16,208},{32,224},{48,240},{64,0},{80,16},{96,32},{112,48}... | collective-permute-start | bytes 196616 | tf_op jit(solution)/shard_map/ppermute | solution.py:256
  7.3 5.0 %collective-permute-start.2 = (bf16[128,256]{1,0:T(8,128)(2,1)}, bf16[128,256]{1,0:T(8,128)(2,1)S(1)}, u32[]{:S(2)}, u32[]{:S(2)}) collective-permute-start(bf16[128,256]{1,0:T(8,128)(2,1)} %get-tuple-element.17), channel_id=1, source_target_pairs={{0,16},{16,32},{32,48},{48,0},{64,80},{80,96},{96,112},{112,64},{1... | collective-permute-start | bytes 196616 | tf_op jit(solution)/shard_map/ppermute | solution.py:256
  8.7 0.8 %copy-start.4 = (bf16[128,256]{1,0:T(8,128)(2,1)S(1)}, bf16[128,256]{1,0:T(8,128)(2,1)}, u32[]{:S(2)}) copy-start(bf16[128,256]{1,0:T(8,128)(2,1)} %get-tuple-element.12.refs_2_) | copy-start | bytes 196612
  9.5 8.1 %copy-start.1 = (bf16[256,2048]{1,0:T(8,128)(2,1)S(1)}, bf16[256,2048]{1,0:T(8,128)(2,1)}, u32[]{:S(2)}) copy-start(bf16[256,2048]{1,0:T(8,128)(2,1)} %amp_ref.1) | copy-start | bytes 3145732
  13.6 13.8 %all-to-all-start.1 = ((bf16[16,80,256]{2,1,0:T(8,128)(2,1)}), bf16[16,80,256]{2,1,0:T(8,128)(2,1)S(1)}, u32[]{:S(2)}, u32[]{:S(2)}) async-start(bf16[16,80,256]{2,1,0:T(8,128)(2,1)} %forward.1.after_ref), calls=%async_computation.1 | async-start | bytes 1310720 | tf_op jit(solution)/shard_map/all_to_all | solution.py:288
  27.4 36.2 %all-to-all-start = ((s16[16,272,256]{2,1,0:T(8,128)(2,1)}), s16[16,272,256]{2,1,0:T(8,128)(2,1)}, u32[]{:S(2)}, u32[]{:S(2)}) async-start(s16[16,272,256]{2,1,0:T(8,128)(2,1)} %ladder.1.after_ref), calls=%async_computation | async-start | bytes 4456448 | tf_op jit(solution)/shard_map/all_to_all | solution.py:308
  33.2 28.9 %copy-start.5 = (f32[256]{0:T(256)S(1)}, f32[256]{0:T(256)}, u32[]{:S(2)}) copy-start(f32[256]{0:T(256)} %param.10) | copy-start | bytes 3076
  33.6 30.0 %copy-start = (bf16[256,4096]{1,0:T(8,128)(2,1)S(1)}, bf16[256,4096]{1,0:T(8,128)(2,1)}, u32[]{:S(2)}) copy-start(bf16[256,4096]{1,0:T(8,128)(2,1)} %pair_ref.1) | copy-start | bytes 6291460
  33.6 30.0 %copy-start.2 = (f32[256]{0:T(256)S(1)}, f32[256]{0:T(256)}, u32[]{:S(2)}) copy-start(f32[256]{0:T(256)} %param.11) | copy-start | bytes 3076
  33.6 9.3 %collective-permute-start.6 = (bf16[256,256]{1,0:T(8,128)(2,1)S(1)}, bf16[256,256]{1,0:T(8,128)(2,1)S(1)}, u32[]{:S(2)}, u32[]{:S(2)}) collective-permute-start(bf16[256,256]{1,0:T(8,128)(2,1)S(1)} %settle.1), channel_id=1, source_target_pairs={{0,12},{1,13},{2,14},{3,15},{4,0},{5,1},{6,2},{7,3},{8,4},{9,5},{1... | collective-permute-start | bytes 393224 | tf_op jit(solution)/shard_map/ppermute | solution.py:241
  39.8 6.8 %collective-permute-start.5 = (bf16[256,256]{1,0:T(8,128)(2,1)S(1)}, bf16[256,256]{1,0:T(8,128)(2,1)S(1)}, u32[]{:S(2)}, u32[]{:S(2)}) collective-permute-start(bf16[256,256]{1,0:T(8,128)(2,1)S(1)} %settle.1), channel_id=1, source_target_pairs={{0,4},{1,5},{2,6},{3,7},{4,8},{5,9},{6,10},{7,11},{8,12},{9,13},{1... | collective-permute-start | bytes 393224 | tf_op jit(solution)/shard_map/ppermute | solution.py:241
  39.8 8.9 %collective-permute-start.3 = (bf16[256,256]{1,0:T(8,128)(2,1)S(1)}, bf16[256,256]{1,0:T(8,128)(2,1)S(1)}, u32[]{:S(2)}, u32[]{:S(2)}) collective-permute-start(bf16[256,256]{1,0:T(8,128)(2,1)S(1)} %settle.1), channel_id=1, source_target_pairs={{0,2},{1,3},{2,4},{3,5},{4,6},{5,7},{6,8},{7,9},{8,10},{9,11},{10,... | collective-permute-start | bytes 393224 | tf_op jit(solution)/shard_map/ppermute | solution.py:241
  40.5 8.1 %collective-permute-start.4 = (bf16[256,256]{1,0:T(8,128)(2,1)S(1)}, bf16[256,256]{1,0:T(8,128)(2,1)S(1)}, u32[]{:S(2)}, u32[]{:S(2)}) collective-permute-start(bf16[256,256]{1,0:T(8,128)(2,1)S(1)} %settle.1), channel_id=1, source_target_pairs={{0,14},{1,15},{2,0},{3,1},{4,2},{5,3},{6,4},{7,5},{8,6},{9,7},{10,... | collective-permute-start | bytes 393224 | tf_op jit(solution)/shard_map/ppermute | solution.py:241
  46.5 9.5 %collective-permute-start.9 = (bf16[256,256]{1,0:T(8,128)(2,1)S(1)}, bf16[256,256]{1,0:T(8,128)(2,1)S(1)}, u32[]{:S(2)}, u32[]{:S(2)}) collective-permute-start(bf16[256,256]{1,0:T(8,128)(2,1)S(1)} %either.1), channel_id=1, source_target_pairs={{0,4},{1,13},{2,6},{3,15},{4,8},{5,1},{6,10},{7,3},{8,12},{9,5},{1... | collective-permute-start | bytes 393224 | tf_op jit(solution)/shard_map/ppermute | solution.py:241
  46.7 9.3 %collective-permute-start.8 = (bf16[256,256]{1,0:T(8,128)(2,1)S(1)}, bf16[256,256]{1,0:T(8,128)(2,1)S(1)}, u32[]{:S(2)}, u32[]{:S(2)}) collective-permute-start(bf16[256,256]{1,0:T(8,128)(2,1)S(1)} %collective-permute-done.6.one_ref), channel_id=1, source_target_pairs={{0,14},{1,15},{2,0},{3,1},{4,2},{5,3},{6,4},{7,5},{8,6},{9,7},{10,... | collective-permute-start | bytes 393224 | tf_op jit(solution)/shard_map/ppermute | solution.py:241
  48.6 7.4 %collective-permute-start.7 = (bf16[256,256]{1,0:T(8,128)(2,1)S(1)}, bf16[256,256]{1,0:T(8,128)(2,1)S(1)}, u32[]{:S(2)}, u32[]{:S(2)}) collective-permute-start(bf16[256,256]{1,0:T(8,128)(2,1)S(1)} %collective-permute-done.5.zero_ref), channel_id=1, source_target_pairs={{0,2},{1,3},{2,4},{3,5},{4,6},{5,7},{6,8},{7,9},{8,10},{9,11},{10,... | collective-permute-start | bytes 393224 | tf_op jit(solution)/shard_map/ppermute | solution.py:241
  48.7 14.9 %collective-permute-start.10 = (bf16[1280,256]{1,0:T(8,128)(2,1)S(1)}, bf16[1280,256]{1,0:T(8,128)(2,1)}, u32[]{:S(2)}, u32[]{:S(2)}) collective-permute-start(bf16[1280,256]{1,0:T(8,128)(2,1)S(1)} %constant_dynamic-update-slice_fusion.near_ref), channel_id=1, source_target_pairs={{0,1},{1,0},{2,3},{3,2},{4,5},{5,4},{6,7},{7,6},{8,9},{9,8},{10,11... | collective-permute-start | bytes 1966088 | tf_op jit(solution)/shard_map/ppermute | solution.py:241
  56.0 7.6 %collective-permute-start.11 = (bf16[768,256]{1,0:T(8,128)(2,1)S(1)}, bf16[768,256]{1,0:T(8,128)(2,1)}, u32[]{:S(2)}, u32[]{:S(2)}) collective-permute-start(bf16[768,256]{1,0:T(8,128)(2,1)S(1)} %constant_dynamic-update-slice_fusion.5.far_ref), channel_id=1, source_target_pairs={{0,1},{1,0},{2,3},{3,2},{4,5},{5,4},{6,7},{7,6},{8,9},{9,8},{10,11... | collective-permute-start | bytes 1179656 | tf_op jit(solution)/shard_map/ppermute | solution.py:241

commit v12 on v10

--- a/solution.py
+++ b/solution.py
@@ -121,10 +121,20 @@
 
 
 def forward_kernel(forward_ref, *refs):
-    *come_refs, moved_ref = refs
+    *come_refs, far_moved_ref, moved_ref, sems = refs
     arrived = jnp.concatenate([ref[...] for ref in come_refs], 0)
-    moved = bdot(forward_ref[...], arrived).astype(jnp.bfloat16)
-    moved_ref[...] = moved.reshape(moved_ref.shape)
+    half = CHUNKS // 2
+    copies = []
+    for k in range(2):
+        moved = bdot(forward_ref[k * half * ROOM : (k + 1) * half * ROOM, :], arrived)
+        some = pl.ds(k * half, half)
+        moved_ref[some] = moved.astype(jnp.bfloat16).reshape(half, ROOM, moved.shape[1])
+        copies.append(
+            pltpu.make_async_copy(moved_ref.at[some], far_moved_ref.at[some], sems.at[k])
+        )
+        copies[k].start()
+    for copy in copies:
+        copy.wait()
 
 
 def settle_kernel(second_ref, settle_ref, after_ref, own_ref):
@@ -280,7 +290,11 @@
         forward_kernel,
         out_shape=jax.ShapeDtypeStruct((CHUNKS, ROOM, height), jnp.bfloat16),
         in_specs=[VMEM] * (len(HOPS) + 1),
-        out_specs=VMEM,
+        out_specs=HBM,
+        scratch_shapes=[
+            pltpu.VMEM((CHUNKS, ROOM, height), jnp.bfloat16),
+            pltpu.SemaphoreType.DMA((2,)),
+        ],
         compiler_params=pltpu.CompilerParams(vmem_limit_bytes=8 << 20),
         cost_estimate=pl.CostEstimate(flops=2**28, bytes_accessed=2**20, transcendentals=0),
         name="forward",

time: 68.8 us -> 68.8 us (level)
  no operation moved by 1% of the time
where the time goes in v12:
time: 68.8 us; the launch traced here: 67.9 us
  starting transfers between devices  39.3 us (57%)
  Pallas kernels  19.8 us (29%)
  waiting for transfers between devices  7.27 us (11%)
  local copies, waits for them, and re-layouts  1.08 us (2%)
    ppermute x9, starting transfers between devices, step(): return lax.ppermute(value, 'narrow', ring)  24.6 us
    pallas_call x1, Pallas kernels, on_device(): pl.pallas_call(ladder_kernel, out_shape=jax.ShapeDtypeStruct((CHUNKS, hei...  8.89 us
    all_to_all x1, starting transfers between devices, on_device(): shares = lax.all_to_all(coded, 'wide', 0, 0, tiled=True)  5.78 us
    ppermute x9, waiting for transfers between devices, step(): return lax.ppermute(value, 'narrow', ring)  4.93 us
    ppermute x3, starting transfers between devices, on_device(): lax.ppermute(sent[k], 'wide', [(x * 4 + y, (x + dx) % 4 * 4 + (y + dy) %...  4.88 us
    pallas_call x1, Pallas kernels, on_device(): pl.pallas_call(finish_kernel, out_shape=jax.ShapeDtypeStruct((height, LAN...  4.02 us
    all_to_all x1, starting transfers between devices, on_device(): second = lax.all_to_all(moved, 'wide', 0, 0, tiled=True)  3.99 us
    pallas_call x1, Pallas kernels, on_device(): pl.pallas_call(lambda *refs: select_kernel(shift, *refs), out_shape=(*[ja...  3.77 us
  transfers between devices with their start and end apart: 14, of which 4 were waited for; matrix products, arithmetic and copies ran while one was open for 0% of the time, Pallas kernels for 16%

profile of v12, /device:TPU:1, one launch (start us, length us, event | category | flops | bytes accessed | tf_op | source)
XLA Modules:
  0.0 67.9 jit_solution(903309582956224496)
XLA Ops:
  0.0 3.8 %select.1 = (bf16[128,256]{1,0:T(8,128)(2,1)}, bf16[128,256]{1,0:T(8,128)(2,1)}, bf16[128,256]{1,0:T(8,128)(2,1)}, bf16[128,256]{1,0:T(8,128)(2,1)}) custom-call(s32[1]{0:T(128)} %bitcast.2.refs_0_, s32[32,128]{1,0:T(8,128)} %bitcast.7, bf16[256,2048]{1,0:T(8,128)(2,1)} %amp_ref.1), custom_call_target="tpu_custom_call" | custom-call | flops 1073741824 | bytes 2097152 | tf_op jit(solution)/shard_map/select/pallas_call | solution.py:253
  3.8 2.1 %collective-permute-start = (bf16[128,256]{1,0:T(8,128)(2,1)}, bf16[128,256]{1,0:T(8,128)(2,1)S(1)}, u32[]{:S(2)}, u32[]{:S(2)}) collective-permute-start(bf16[128,256]{1,0:T(8,128)(2,1)} %get-tuple-element.15), channel_id=1, source_target_pairs={{0,64},{16,80},{32,96},{48,112},{64,128},{80,144},{96,160},{112,17... | collective-permute-start | bytes 196616 | tf_op jit(solution)/shard_map/ppermute | solution.py:266
  5.9 1.4 %collective-permute-start.1 = (bf16[128,256]{1,0:T(8,128)(2,1)}, bf16[128,256]{1,0:T(8,128)(2,1)S(1)}, u32[]{:S(2)}, u32[]{:S(2)}) collective-permute-start(bf16[128,256]{1,0:T(8,128)(2,1)} %get-tuple-element.16), channel_id=1, source_target_pairs={{0,192},{16,208},{32,224},{48,240},{64,0},{80,16},{96,32},{112,48}... | collective-permute-start | bytes 196616 | tf_op jit(solution)/shard_map/ppermute | solution.py:266
  7.3 1.4 %collective-permute-start.2 = (bf16[128,256]{1,0:T(8,128)(2,1)}, bf16[128,256]{1,0:T(8,128)(2,1)S(1)}, u32[]{:S(2)}, u32[]{:S(2)}) collective-permute-start(bf16[128,256]{1,0:T(8,128)(2,1)} %get-tuple-element.17), channel_id=1, source_target_pairs={{0,16},{16,32},{32,48},{48,0},{64,80},{80,96},{96,112},{112,64},{1... | collective-permute-start | bytes 196616 | tf_op jit(solution)/shard_map/ppermute | solution.py:266
  8.7 0.8 %copy-done.4 = bf16[128,256]{1,0:T(8,128)(2,1)S(1)} copy-done((bf16[128,256]{1,0:T(8,128)(2,1)S(1)}, bf16[128,256]{1,0:T(8,128)(2,1)}, u32[]{:S(2)}) %copy-start.4) | copy-done | bytes 65560
  9.5 1.3 %route.1 = (bf16[1280,512]{1,0:T(8,128)(2,1)S(1)}, bf16[1280,256]{1,0:T(8,128)(2,1)S(1)}, bf16[128,256]{1,0:T(8,128)(2,1)S(1)}) custom-call(s32[1]{0:T(128)} %bitcast.2.refs_0_, s32[32,128]{1,0:T(8,128)S(1)} %bitcast.8, bf16[128,256]{1,0:T(8,128)(2,1)S(1)} %copy-done.4), custom_call_target="tpu_custom_call" | custom-call | flops 268435456 | bytes 1048576 | tf_op jit(solution)/shard_map/route/pallas_call | solution.py:275
  10.9 1.4 %collective-permute-done.2.refs_3_ = bf16[128,256]{1,0:T(8,128)(2,1)S(1)} collective-permute-done((bf16[128,256]{1,0:T(8,128)(2,1)}, bf16[128,256]{1,0:T(8,128)(2,1)S(1)}, u32[]{:S(2)}, u32[]{:S(2)}) %collective-permute-start.2) | collective-permute-done | bytes 65568 | tf_op jit(solution)/shard_map/ppermute | solution.py:266
  12.3 1.4 %forward.1.after_ref = bf16[16,80,256]{2,1,0:T(8,128)(2,1)} custom-call(bf16[1280,512]{1,0:T(8,128)(2,1)S(1)} %get-tuple-element.13.forward_ref, bf16[128,256]{1,0:T(8,128)(2,1)S(1)} %get-tuple-element.14.refs_0_, bf16[128,256]{1,0:T(8,128)(2,1)S(1)} %collective-permute-done.refs_1_, bf16[128,256]{1,0:T(8,128)(2,1)S(1)} %collective-permute-done.1.refs_2_, ...), custom_call_target="tpu_custom_call" | custom-call | flops 268435456 | bytes 1048576 | tf_op jit(solution)/shard_map/forward/pallas_call | solution.py:289
  13.6 4.0 %all-to-all-start.1 = ((bf16[16,80,256]{2,1,0:T(8,128)(2,1)}), bf16[16,80,256]{2,1,0:T(8,128)(2,1)S(1)}, u32[]{:S(2)}, u32[]{:S(2)}) async-start(bf16[16,80,256]{2,1,0:T(8,128)(2,1)} %forward.1.after_ref), calls=%async_computation.1 | async-start | bytes 1310720 | tf_op jit(solution)/shard_map/all_to_all | solution.py:302
  17.6 8.9 %ladder.1.after_ref = s16[16,272,256]{2,1,0:T(8,128)(2,1)} custom-call(bf16[256,2048]{1,0:T(8,128)(2,1)S(1)} %copy-done.1, bf16[2048,4096]{1,0:T(8,128)(2,1)} %int_ref.1, bf16[16,80,256]{2,1,0:T(8,128)(2,1)} %forward.1.after_ref), custom_call_target="tpu_custom_call" | custom-call | flops 4294967296 | bytes 18874368 | tf_op jit(solution)/shard_map/ladder/pallas_call | solution.py:305
  26.5 0.9 %all-to-all-done.1.second_ref = bf16[16,80,256]{2,1,0:T(8,128)(2,1)S(1)} async-done(((bf16[16,80,256]{2,1,0:T(8,128)(2,1)}), bf16[16,80,256]{2,1,0:T(8,128)(2,1)S(1)}, u32[]{:S(2)}, u32[]{:S(2)}) %all-to-all-start.1) | async-done | bytes 655392 | tf_op jit(solution)/shard_map/all_to_all | solution.py:302
  27.5 5.8 %all-to-all-start = ((s16[16,272,256]{2,1,0:T(8,128)(2,1)}), s16[16,272,256]{2,1,0:T(8,128)(2,1)}, u32[]{:S(2)}, u32[]{:S(2)}) async-start(s16[16,272,256]{2,1,0:T(8,128)(2,1)} %ladder.1.after_ref), calls=%async_computation | async-start | bytes 4456448 | tf_op jit(solution)/shard_map/all_to_all | solution.py:322
  33.3 0.4 settle.1
  33.7 6.1 %collective-permute-start.6 = (bf16[256,256]{1,0:T(8,128)(2,1)S(1)}, bf16[256,256]{1,0:T(8,128)(2,1)S(1)}, u32[]{:S(2)}, u32[]{:S(2)}) collective-permute-start(bf16[256,256]{1,0:T(8,128)(2,1)S(1)} %settle.1), channel_id=1, source_target_pairs={{0,12},{1,13},{2,14},{3,15},{4,0},{5,1},{6,2},{7,3},{8,4},{9,5},{1... | collective-permute-start | bytes 393224 | tf_op jit(solution)/shard_map/ppermute | solution.py:251
  39.8 0.7 %collective-permute-start.3 = (bf16[256,256]{1,0:T(8,128)(2,1)S(1)}, bf16[256,256]{1,0:T(8,128)(2,1)S(1)}, u32[]{:S(2)}, u32[]{:S(2)}) collective-permute-start(bf16[256,256]{1,0:T(8,128)(2,1)S(1)} %settle.1), channel_id=1, source_target_pairs={{0,2},{1,3},{2,4},{3,5},{4,6},{5,7},{6,8},{7,9},{8,10},{9,11},{10,... | collective-permute-start | bytes 393224 | tf_op jit(solution)/shard_map/ppermute | solution.py:251
  40.5 2.4 %collective-permute-start.4 = (bf16[256,256]{1,0:T(8,128)(2,1)S(1)}, bf16[256,256]{1,0:T(8,128)(2,1)S(1)}, u32[]{:S(2)}, u32[]{:S(2)}) collective-permute-start(bf16[256,256]{1,0:T(8,128)(2,1)S(1)} %settle.1), channel_id=1, source_target_pairs={{0,14},{1,15},{2,0},{3,1},{4,2},{5,3},{6,4},{7,5},{8,6},{9,7},{10,... | collective-permute-start | bytes 393224 | tf_op jit(solution)/shard_map/ppermute | solution.py:251
  42.9 3.6 %collective-permute-done.5.zero_ref = bf16[256,256]{1,0:T(8,128)(2,1)S(1)} collective-permute-done((bf16[256,256]{1,0:T(8,128)(2,1)S(1)}, bf16[256,256]{1,0:T(8,128)(2,1)S(1)}, u32[]{:S(2)}, u32[]{:S(2)}) %collective-permute-start.5) | collective-permute-done | bytes 131104 | tf_op jit(solution)/shard_map/ppermute | solution.py:251
  46.6 0.1 collective-permute-start.9
  46.7 1.9 %collective-permute-start.8 = (bf16[256,256]{1,0:T(8,128)(2,1)S(1)}, bf16[256,256]{1,0:T(8,128)(2,1)S(1)}, u32[]{:S(2)}, u32[]{:S(2)}) collective-permute-start(bf16[256,256]{1,0:T(8,128)(2,1)S(1)} %collective-permute-done.6.one_ref), channel_id=1, source_target_pairs={{0,14},{1,15},{2,0},{3,1},{4,2},{5,3},{6,4},{7,5},{8,6},{9,7},{10,... | collective-permute-start | bytes 393224 | tf_op jit(solution)/shard_map/ppermute | solution.py:251
  48.7 7.3 %collective-permute-start.10 = (bf16[1280,256]{1,0:T(8,128)(2,1)S(1)}, bf16[1280,256]{1,0:T(8,128)(2,1)}, u32[]{:S(2)}, u32[]{:S(2)}) collective-permute-start(bf16[1280,256]{1,0:T(8,128)(2,1)S(1)} %constant_dynamic-update-slice_fusion.near_ref), channel_id=1, source_target_pairs={{0,1},{1,0},{2,3},{3,2},{4,5},{5,4},{6,7},{7,6},{8,9},{9,8},{10,11... | collective-permute-start | bytes 1966088 | tf_op jit(solution)/shard_map/ppermute | solution.py:251
  56.1 6.1 %collective-permute-start.11 = (bf16[768,256]{1,0:T(8,128)(2,1)S(1)}, bf16[768,256]{1,0:T(8,128)(2,1)}, u32[]{:S(2)}, u32[]{:S(2)}) collective-permute-start(bf16[768,256]{1,0:T(8,128)(2,1)S(1)} %constant_dynamic-update-slice_fusion.5.far_ref), channel_id=1, source_target_pairs={{0,1},{1,0},{2,3},{3,2},{4,5},{5,4},{6,7},{7,6},{8,9},{9,8},{10,11... | collective-permute-start | bytes 1179656 | tf_op jit(solution)/shard_map/ppermute | solution.py:251
  62.2 0.1 copy.7.occ_ref
  62.4 1.3 %collective-permute-done.11.refs_1_ = bf16[768,256]{1,0:T(8,128)(2,1)} collective-permute-done((bf16[768,256]{1,0:T(8,128)(2,1)S(1)}, bf16[768,256]{1,0:T(8,128)(2,1)}, u32[]{:S(2)}, u32[]{:S(2)}) %collective-permute-start.11) | collective-permute-done | bytes 393248 | tf_op jit(solution)/shard_map/ppermute | solution.py:251
  63.7 4.0 %finish.1 = f32[256,256]{1,0:T(8,128)} custom-call(s32[2]{0:T(128)S(1)} %pad_add_fusion.place_ref, bf16[256,4096]{1,0:T(8,128)(2,1)S(1)} %copy-done, s16[16,272,256]{2,1,0:T(8,128)(2,1)} %all-to-all-done.far_coded_ref, f32[256,1]{1,0:T(8,128)S(1)} %copy.7.occ_ref, f32[1,256]{1,0:T(1,128)S(1)} %bitcast.6, ...), custom_call_target="tpu_custom_call" | custom-call | flops 1073741824 | bytes 8388608 | tf_op jit(solution)/shard_map/finish/pallas_call | solution.py:352
  (33 shorter events, 0.3 us)
Async XLA Ops:
  0.0 8.7 %copy-start.3 = (s32[4096]{0:T(1024)S(1)}, s32[4096]{0:T(1024)}, u32[]{:S(2)}) copy-start(s32[4096]{0:T(1024)} %param.9) | copy-start | bytes 49156
  3.8 7.1 %collective-permute-start = (bf16[128,256]{1,0:T(8,128)(2,1)}, bf16[128,256]{1,0:T(8,128)(2,1)S(1)}, u32[]{:S(2)}, u32[]{:S(2)}) collective-permute-start(bf16[128,256]{1,0:T(8,128)(2,1)} %get-tuple-element.15), channel_id=1, source_target_pairs={{0,64},{16,80},{32,96},{48,112},{64,128},{80,144},{96,160},{112,17... | collective-permute-start | bytes 196616 | tf_op jit(solution)/shard_map/ppermute | solution.py:266
  5.9 5.0 %collective-permute-start.1 = (bf16[128,256]{1,0:T(8,128)(2,1)}, bf16[128,256]{1,0:T(8,128)(2,1)S(1)}, u32[]{:S(2)}, u32[]{:S(2)}) collective-permute-start(bf16[128,256]{1,0:T(8,128)(2,1)} %get-tuple-element.16), channel_id=1, source_target_pairs={{0,192},{16,208},{32,224},{48,240},{64,0},{80,16},{96,32},{112,48}... | collective-permute-start | bytes 196616 | tf_op jit(solution)/shard_map/ppermute | solution.py:266
  7.3 5.0 %collective-permute-start.2 = (bf16[128,256]{1,0:T(8,128)(2,1)}, bf16[128,256]{1,0:T(8,128)(2,1)S(1)}, u32[]{:S(2)}, u32[]{:S(2)}) collective-permute-start(bf16[128,256]{1,0:T(8,128)(2,1)} %get-tuple-element.17), channel_id=1, source_target_pairs={{0,16},{16,32},{32,48},{48,0},{64,80},{80,96},{96,112},{112,64},{1... | collective-permute-start | bytes 196616 | tf_op jit(solution)/shard_map/ppermute | solution.py:266
  8.7 0.8 %copy-start.4 = (bf16[128,256]{1,0:T(8,128)(2,1)S(1)}, bf16[128,256]{1,0:T(8,128)(2,1)}, u32[]{:S(2)}) copy-start(bf16[128,256]{1,0:T(8,128)(2,1)} %get-tuple-element.12.refs_2_) | copy-start | bytes 196612
  9.5 8.1 %copy-start.1 = (bf16[256,2048]{1,0:T(8,128)(2,1)S(1)}, bf16[256,2048]{1,0:T(8,128)(2,1)}, u32[]{:S(2)}) copy-start(bf16[256,2048]{1,0:T(8,128)(2,1)} %amp_ref.1) | copy-start | bytes 3145732
  13.6 13.8 %all-to-all-start.1 = ((bf16[16,80,256]{2,1,0:T(8,128)(2,1)}), bf16[16,80,256]{2,1,0:T(8,128)(2,1)S(1)}, u32[]{:S(2)}, u32[]{:S(2)}) async-start(bf16[16,80,256]{2,1,0:T(8,128)(2,1)} %forward.1.after_ref), calls=%async_computation.1 | async-start | bytes 1310720 | tf_op jit(solution)/shard_map/all_to_all | solution.py:302
  27.5 36.2 %all-to-all-start = ((s16[16,272,256]{2,1,0:T(8,128)(2,1)}), s16[16,272,256]{2,1,0:T(8,128)(2,1)}, u32[]{:S(2)}, u32[]{:S(2)}) async-start(s16[16,272,256]{2,1,0:T(8,128)(2,1)} %ladder.1.after_ref), calls=%async_computation | async-start | bytes 4456448 | tf_op jit(solution)/shard_map/all_to_all | solution.py:322
  33.3 28.9 %copy-start.5 = (f32[256]{0:T(256)S(1)}, f32[256]{0:T(256)}, u32[]{:S(2)}) copy-start(f32[256]{0:T(256)} %param.10) | copy-start | bytes 3076
  33.7 30.0 %copy-start = (bf16[256,4096]{1,0:T(8,128)(2,1)S(1)}, bf16[256,4096]{1,0:T(8,128)(2,1)}, u32[]{:S(2)}) copy-start(bf16[256,4096]{1,0:T(8,128)(2,1)} %pair_ref.1) | copy-start | bytes 6291460
  33.7 30.0 %copy-start.2 = (f32[256]{0:T(256)S(1)}, f32[256]{0:T(256)}, u32[]{:S(2)}) copy-start(f32[256]{0:T(256)} %param.11) | copy-start | bytes 3076
  33.7 9.2 %collective-permute-start.6 = (bf16[256,256]{1,0:T(8,128)(2,1)S(1)}, bf16[256,256]{1,0:T(8,128)(2,1)S(1)}, u32[]{:S(2)}, u32[]{:S(2)}) collective-permute-start(bf16[256,256]{1,0:T(8,128)(2,1)S(1)} %settle.1), channel_id=1, source_target_pairs={{0,12},{1,13},{2,14},{3,15},{4,0},{5,1},{6,2},{7,3},{8,4},{9,5},{1... | collective-permute-start | bytes 393224 | tf_op jit(solution)/shard_map/ppermute | solution.py:251
  39.8 6.8 %collective-permute-start.5 = (bf16[256,256]{1,0:T(8,128)(2,1)S(1)}, bf16[256,256]{1,0:T(8,128)(2,1)S(1)}, u32[]{:S(2)}, u32[]{:S(2)}) collective-permute-start(bf16[256,256]{1,0:T(8,128)(2,1)S(1)} %settle.1), channel_id=1, source_target_pairs={{0,4},{1,5},{2,6},{3,7},{4,8},{5,9},{6,10},{7,11},{8,12},{9,13},{1... | collective-permute-start | bytes 393224 | tf_op jit(solution)/shard_map/ppermute | solution.py:251
  39.8 8.9 %collective-permute-start.3 = (bf16[256,256]{1,0:T(8,128)(2,1)S(1)}, bf16[256,256]{1,0:T(8,128)(2,1)S(1)}, u32[]{:S(2)}, u32[]{:S(2)}) collective-permute-start(bf16[256,256]{1,0:T(8,128)(2,1)S(1)} %settle.1), channel_id=1, source_target_pairs={{0,2},{1,3},{2,4},{3,5},{4,6},{5,7},{6,8},{7,9},{8,10},{9,11},{10,... | collective-permute-start | bytes 393224 | tf_op jit(solution)/shard_map/ppermute | solution.py:251
  40.5 8.1 %collective-permute-start.4 = (bf16[256,256]{1,0:T(8,128)(2,1)S(1)}, bf16[256,256]{1,0:T(8,128)(2,1)S(1)}, u32[]{:S(2)}, u32[]{:S(2)}) collective-permute-start(bf16[256,256]{1,0:T(8,128)(2,1)S(1)} %settle.1), channel_id=1, source_target_pairs={{0,14},{1,15},{2,0},{3,1},{4,2},{5,3},{6,4},{7,5},{8,6},{9,7},{10,... | collective-permute-start | bytes 393224 | tf_op jit(solution)/shard_map/ppermute | solution.py:251
  46.6 9.5 %collective-permute-start.9 = (bf16[256,256]{1,0:T(8,128)(2,1)S(1)}, bf16[256,256]{1,0:T(8,128)(2,1)S(1)}, u32[]{:S(2)}, u32[]{:S(2)}) collective-permute-start(bf16[256,256]{1,0:T(8,128)(2,1)S(1)} %either.1), channel_id=1, source_target_pairs={{0,4},{1,13},{2,6},{3,15},{4,8},{5,1},{6,10},{7,3},{8,12},{9,5},{1... | collective-permute-start | bytes 393224 | tf_op jit(solution)/shard_map/ppermute | solution.py:251
  46.7 9.4 %collective-permute-start.8 = (bf16[256,256]{1,0:T(8,128)(2,1)S(1)}, bf16[256,256]{1,0:T(8,128)(2,1)S(1)}, u32[]{:S(2)}, u32[]{:S(2)}) collective-permute-start(bf16[256,256]{1,0:T(8,128)(2,1)S(1)} %collective-permute-done.6.one_ref), channel_id=1, source_target_pairs={{0,14},{1,15},{2,0},{3,1},{4,2},{5,3},{6,4},{7,5},{8,6},{9,7},{10,... | collective-permute-start | bytes 393224 | tf_op jit(solution)/shard_map/ppermute | solution.py:251
  48.6 7.4 %collective-permute-start.7 = (bf16[256,256]{1,0:T(8,128)(2,1)S(1)}, bf16[256,256]{1,0:T(8,128)(2,1)S(1)}, u32[]{:S(2)}, u32[]{:S(2)}) collective-permute-start(bf16[256,256]{1,0:T(8,128)(2,1)S(1)} %collective-permute-done.5.zero_ref), channel_id=1, source_target_pairs={{0,2},{1,3},{2,4},{3,5},{4,6},{5,7},{6,8},{7,9},{8,10},{9,11},{10,... | collective-permute-start | bytes 393224 | tf_op jit(solution)/shard_map/ppermute | solution.py:251
  48.7 14.9 %collective-permute-start.10 = (bf16[1280,256]{1,0:T(8,128)(2,1)S(1)}, bf16[1280,256]{1,0:T(8,128)(2,1)}, u32[]{:S(2)}, u32[]{:S(2)}) collective-permute-start(bf16[1280,256]{1,0:T(8,128)(2,1)S(1)} %constant_dynamic-update-slice_fusion.near_ref), channel_id=1, source_target_pairs={{0,1},{1,0},{2,3},{3,2},{4,5},{5,4},{6,7},{7,6},{8,9},{9,8},{10,11... | collective-permute-start | bytes 1966088 | tf_op jit(solution)/shard_map/ppermute | solution.py:251
  56.1 7.6 %collective-permute-start.11 = (bf16[768,256]{1,0:T(8,128)(2,1)S(1)}, bf16[768,256]{1,0:T(8,128)(2,1)}, u32[]{:S(2)}, u32[]{:S(2)}) collective-permute-start(bf16[768,256]{1,0:T(8,128)(2,1)S(1)} %constant_dynamic-update-slice_fusion.5.far_ref), channel_id=1, source_target_pairs={{0,1},{1,0},{2,3},{3,2},{4,5},{5,4},{6,7},{7,6},{8,9},{9,8},{10,11... | collective-permute-start | bytes 1179656 | tf_op jit(solution)/shard_map/ppermute | solution.py:251
